TPU v7x, 32 devices: a whole 2x2x4 slice. The times are simulated.
32 devices in a mesh: groups: 2 (over y), expert: 8 (over z, core), helper: 2 (over x), dp: 1.
Axes of the slice: x: 2, y: 2, z: 4, core: 2. Of those that a mesh axis runs over, the one named last changes fastest.
Arguments:
- tokens: bfloat16 [2048, 2048], P(('groups', 'expert', 'dp')), parts along dimension 0, may hold values from -6 to 6
- expert_ids: int32 [2048, 4], P(('groups', 'expert', 'dp')), parts along dimension 0, may hold values from 0 to 7, all different within a row; in each aligned block of 128 rows (0 to 127, 128 to 255, ...) at most 80 rows name the same one
- pick_counts: int32 [2048], P(('groups', 'expert', 'dp')), parts along dimension 0, may hold values from 1 to 4
- gate_scores: float32 [2048, 4], P(('groups', 'expert', 'dp')), parts along dimension 0, may hold values from 0.05 to 1
- w_gate: bfloat16 [8, 2048, 2048], P('expert', None, 'helper'), may hold values from -0.125 to 0.125
- w_up: bfloat16 [8, 2048, 2048], P('expert', None, 'helper'), may hold values from -0.125 to 0.125
- w_down: bfloat16 [8, 2048, 2048], P('expert', 'helper'), may hold values from -0.125 to 0.125
- grad_out: bfloat16 [2048, 2048], P(('groups', 'expert', 'dp')), parts along dimension 0, may hold values from -6 to 6
Outputs:
- outputs: bfloat16 [2048, 2048], P(('groups', 'expert', 'dp'), 'helper'), parts along dimension 0
- input_grads: bfloat16 [2048, 2048], P(('groups', 'expert', 'dp'), 'helper'), parts along dimension 0
- d_scores: float32 [2048, 4], P(('groups', 'expert', 'dp')), parts along dimension 0
- grad_w_gate: bfloat16 [16, 2048, 2048], P(('groups', 'expert'), 'dp', 'helper'), parts along dimension 0
- grad_w_up: bfloat16 [16, 2048, 2048], P(('groups', 'expert'), 'dp', 'helper'), parts along dimension 0
- grad_w_down: bfloat16 [16, 2048, 2048], P(('groups', 'expert'), 'helper', 'dp'), parts along dimension 0
There are 2 independent parts, one for each index of `groups`. A program takes and returns all parts, laid end to end along the dimension named above; an argument that names none is the same for every part. Nothing has to cross between parts.
Inputs may be any that keep to these rules, and one draw needn't show every extreme that they name: `expert_ids`: in each aligned block of 128 rows (the rows of one device), no expert is named by more than 80 rows over all 4 columns; the entries of a row are distinct.
All inputs are finite; a program needn't handle non-finite values.
Results may differ from a plain program's by a relative error of at most 0.015.
Values may be sent and summed in bfloat16 or wider, within the bound.
No kernel may reach another device: no remote copies, remote signals or barrier semaphores. Data moves between devices by JAX's collectives and lax.ppermute only.
A program may use at most 128 MiB of HBM per device.

v0:
```python
import jax
import jax.numpy as jnp
from jax import lax
from jax.sharding import PartitionSpec as P


def product(first_mat, second_mat):
    return jnp.dot(first_mat, second_mat, preferred_element_type=jnp.float32)


def transposed_product(first_mat, second_mat):
    return lax.dot_general(
        first_mat, second_mat, (((0,), (0,)), ((), ())), preferred_element_type=jnp.float32
    )


def right_transposed(first_mat, second_mat):
    return lax.dot_general(
        first_mat, second_mat, (((1,), (1,)), ((), ())), preferred_element_type=jnp.float32
    )


def swap_halves(rows):
    half = rows.shape[-2] // 2
    return jnp.concatenate([rows[..., half:, :], rows[..., :half, :]], axis=-2)


class WholeAxis:
    def __init__(self, tok_rows):
        self.tok_rows = tok_rows

    def dispatch(self, rows):
        return lax.all_gather(rows, "expert", tiled=True)

    def order(self, by_device):
        return by_device.reshape(-1)

    def unorder(self, rows):
        return rows.reshape(-1, self.tok_rows)

    def combine(self, partial):
        summed = lax.psum_scatter(partial, "expert", scatter_dimension=0, tiled=True)
        return lax.psum_scatter(summed, "helper", scatter_dimension=1, tiled=True)


class FourChips:
    def __init__(self, tok_rows):
        self.tok_rows = tok_rows
        self.half = tok_rows // 2
        me = lax.axis_index("expert")
        self.chip, self.core = me // 2, me % 2
        self.side = lax.axis_index("helper")
        both = lambda pairs: [(2 * a + c, 2 * b + c) for a, b in pairs for c in (0, 1)]
        self.near = both([(z, z ^ 1) for z in range(4)])
        self.far = both([(z, z ^ 2) for z in range(4)])
        self.middle = both([(1, 2), (2, 1)])
        self.outward = both([(1, 0), (2, 3)])
        self.inward = both([(0, 1), (3, 2)])
        self.cores = [(i, i ^ 1) for i in range(8)]
        self.sides = [(0, 1), (1, 0)]

    def own_first(self, rows):
        return jnp.where(self.side == 0, rows, swap_halves(rows))

    def dispatch(self, rows):
        own = lax.dynamic_slice_in_dim(rows, self.side * self.half, self.half, 0)
        far = lax.ppermute(own, "expert", self.far)
        near = lax.ppermute(own, "expert", self.near)
        middle = lax.ppermute(own, "expert", self.middle)
        last = middle + lax.ppermute(far, "expert", self.outward)
        pieces = [self.own_first(rows)]
        for piece in (near, far, last):
            pieces = pieces + [piece, lax.ppermute(piece, "helper", self.sides)]
        own_core = jnp.concatenate(pieces, axis=0)
        other_core = lax.ppermute(own_core, "expert", self.cores)
        return jnp.concatenate([own_core, other_core], axis=0)

    def devices(self):
        slot = jnp.arange(4)
        return jnp.concatenate([(self.chip ^ slot) * 2 + self.core, (self.chip ^ slot) * 2 + 1 - self.core])

    def order(self, by_device):
        rows = by_device[self.devices()][..., None]
        return self.own_first(rows).reshape(-1)

    def unorder(self, rows):
        rows = self.own_first(rows.reshape(8, self.tok_rows, 1))[..., 0]
        everyone = jnp.arange(8)
        place = (everyone % 2 != self.core) * 4 + (everyone // 2 ^ self.chip)
        return rows[place]

    def combine(self, partial):
        rows, width = partial.shape
        received = lax.ppermute(partial[rows // 2 :], "expert", self.cores)
        kept = partial[: rows // 2]
        columns = width // 2

        def part_of(side):
            first = lax.dynamic_slice_in_dim(kept, side * columns, columns, 1)
            second = lax.dynamic_slice_in_dim(received, side * columns, columns, 1)
            total = first.astype(jnp.float32) + second.astype(jnp.float32)
            return total.reshape(4, self.tok_rows, columns)

        sent = part_of(1 - self.side).astype(jnp.bfloat16)
        mine = part_of(self.side)
        slots = [None] * 4
        for s in (3, 2, 1, 0):
            arrived = swap_halves(lax.ppermute(sent[s], "helper", self.sides))
            slots[s] = mine[s] + arrived.astype(jnp.float32)
        relay = lax.ppermute(slots[3].astype(jnp.bfloat16), "expert", self.inward)
        far = lax.ppermute(
            (slots[2] + relay.astype(jnp.float32)).astype(jnp.bfloat16), "expert", self.far
        )
        near = lax.ppermute(slots[1].astype(jnp.bfloat16), "expert", self.near)
        middle = lax.ppermute(slots[3].astype(jnp.bfloat16), "expert", self.middle)
        total = slots[0] + far.astype(jnp.float32) + near.astype(jnp.float32) + middle.astype(jnp.float32)
        return self.own_first(total).astype(jnp.bfloat16)


def on_device(tokens, expert_ids, pick_counts, gate_scores, w_gate, w_up, w_down, grad_out):
    tok_rows = tokens.shape[0]
    pick_width = expert_ids.shape[1]
    experts = lax.axis_size("expert")
    lined = experts == 8 and lax.axis_size("helper") == 2 and lax.axis_size("dp") == 1
    plan = FourChips(tok_rows) if lined else WholeAxis(tok_rows)
    gate_local, up_local, down_local = w_gate[0], w_up[0], w_down[0]
    active_mask = lax.broadcasted_iota(jnp.int32, (tok_rows, pick_width), 1) < pick_counts[:, None]
    active_float = active_mask.astype(jnp.float32)
    weighted = gate_scores * active_float
    score_sum = jnp.sum(weighted, axis=1, keepdims=True)
    gate_weights = weighted / score_sum
    picked = (expert_ids[:, :, None] == lax.broadcasted_iota(jnp.int32, (1, 1, experts), 2)).astype(
        jnp.float32
    )
    gate_table = jnp.sum(gate_weights[:, :, None] * picked, axis=1)

    rows = plan.dispatch(tokens)
    tables = lax.all_gather(gate_table.T, "expert", tiled=False)
    gates = plan.order(jnp.take(tables, lax.axis_index("expert"), axis=1))[:, None]
    grads = plan.dispatch(grad_out)

    pre_gate = product(rows, gate_local)
    pre_up = product(rows, up_local)
    sigmoid_part = jax.nn.sigmoid(pre_gate)
    silu_value = pre_gate * sigmoid_part
    silu_slope = sigmoid_part * (1.0 + pre_gate * (1.0 - sigmoid_part))
    hidden_act = silu_value * pre_up
    gated_act = (gates * hidden_act).astype(jnp.bfloat16)
    partial_out = product(gated_act, down_local).astype(jnp.bfloat16)
    output_cols = plan.combine(partial_out)

    raw_act = right_transposed(grads, down_local)
    gate_part = jnp.sum(raw_act * hidden_act, axis=1)
    d_act = gates * raw_act
    d_pre_gate = (d_act * pre_up * silu_slope).astype(jnp.bfloat16)
    d_pre_up = (d_act * silu_value).astype(jnp.bfloat16)
    partial_in = (
        right_transposed(d_pre_gate, gate_local) + right_transposed(d_pre_up, up_local)
    ).astype(jnp.bfloat16)
    input_cols = plan.combine(partial_in)

    gate_parts = lax.all_gather(plan.unorder(gate_part), ("expert", "helper"), tiled=False)
    own_parts = jnp.take(gate_parts, lax.axis_index("expert"), axis=1)
    by_expert = jnp.sum(own_parts.reshape(experts, -1, tok_rows), axis=1).T
    d_gates = jnp.sum(by_expert[:, None, :] * picked, axis=2)
    d_scores = (
        active_float
        * (d_gates - jnp.sum(gate_weights * d_gates, axis=1, keepdims=True))
        / score_sum
    )

    def over_dp(product_of, dimension):
        product_of = product_of.astype(jnp.bfloat16)
        if lax.axis_size("dp") > 1:
            product_of = lax.psum_scatter(
                product_of, "dp", scatter_dimension=dimension, tiled=True
            )
        return product_of[None]

    grad_w_gate = over_dp(transposed_product(rows, d_pre_gate), 0)
    grad_w_up = over_dp(transposed_product(rows, d_pre_up), 0)
    grad_w_down = over_dp(transposed_product(gated_act, grads), 1)
    return output_cols, input_cols, d_scores, grad_w_gate, grad_w_up, grad_w_down


def solution(mesh):
    in_specs = (
        P(("groups", "expert", "dp"), None),
        P(("groups", "expert", "dp"), None),
        P(("groups", "expert", "dp")),
        P(("groups", "expert", "dp"), None),
        P("expert", None, "helper"),
        P("expert", None, "helper"),
        P("expert", "helper", None),
        P(("groups", "expert", "dp"), None),
    )
    out_specs = (
        P(("groups", "expert", "dp"), "helper"),
        P(("groups", "expert", "dp"), "helper"),
        P(("groups", "expert", "dp"), None),
        P(("groups", "expert"), "dp", "helper"),
        P(("groups", "expert"), "dp", "helper"),
        P(("groups", "expert"), "helper", "dp"),
    )
    return jax.shard_map(
        on_device, mesh=mesh, in_specs=in_specs, out_specs=out_specs, check_vma=False
    )
```

profile of v0, /device:TPU:0, one launch (start us, length us, event | category | flops | bytes accessed | tf_op | source)
XLA Modules:
  0.0 277.1 jit_solution(18444869022288523445)
XLA Ops:
  2.6 5.8 %collective-permute-start.2 = (bf16[64,2048]{1,0:T(8,128)(2,1)S(1)}, bf16[64,2048]{1,0:T(8,128)(2,1)S(1)}, u32[]{:S(2)}, u32[]{:S(2)}) collective-permute-start(bf16[64,2048]{1,0:T(8,128)(2,1)S(1)} %get-tuple-element.61), channel_id=1, source_target_pairs={{0,8},{2,10},{4,12},{6,14},{8,0},{10,2},{12,4},{14,6},{1,9},{3,11}... | collective-permute-start | bytes 786440 | tf_op jit(solution)/shard_map/ppermute | solution.py:67
  10.5 4.6 %collective-permute-start.19 = (bf16[64,2048]{1,0:T(8,128)(2,1)S(1)}, bf16[64,2048]{1,0:T(8,128)(2,1)S(1)}, u32[]{:S(2)}, u32[]{:S(2)}) collective-permute-start(bf16[64,2048]{1,0:T(8,128)(2,1)S(1)} %get-tuple-element.64), channel_id=1, source_target_pairs={{0,8},{2,10},{4,12},{6,14},{8,0},{10,2},{12,4},{14,6},{1,9},{3,11}... | collective-permute-start | bytes 786440 | tf_op jit(solution)/shard_map/ppermute | solution.py:67
  15.8 2.2 constant_dynamic-update-slice_fusion.21
  19.2 1.6 collective-permute-done
  20.7 1.5 collective-permute-start.1
  22.3 10.0 %collective-permute-done.2 = bf16[64,2048]{1,0:T(8,128)(2,1)S(1)} collective-permute-done((bf16[64,2048]{1,0:T(8,128)(2,1)S(1)}, bf16[64,2048]{1,0:T(8,128)(2,1)S(1)}, u32[]{:S(2)}, u32[]{:S(2)}) %collective-permute-start.2) | collective-permute-done | bytes 262176 | tf_op jit(solution)/shard_map/ppermute | solution.py:67
  32.3 1.3 collective-permute-start.5
  34.4 1.5 collective-permute-start.3
  37.6 3.2 %collective-permute-done.3 = bf16[64,2048]{1,0:T(8,128)(2,1)S(1)} collective-permute-done((bf16[64,2048]{1,0:T(8,128)(2,1)S(1)}, bf16[64,2048]{1,0:T(8,128)(2,1)S(1)}, u32[]{:S(2)}, u32[]{:S(2)}) %collective-permute-start.3) | collective-permute-done | bytes 262176 | tf_op jit(solution)/shard_map/ppermute | solution.py:73
  40.8 2.7 collective-permute-start.17
  44.3 3.7 %collective-permute-done.5 = bf16[64,2048]{1,0:T(8,128)(2,1)S(1)} collective-permute-done((bf16[64,2048]{1,0:T(8,128)(2,1)S(1)}, bf16[64,2048]{1,0:T(8,128)(2,1)S(1)}, u32[]{:S(2)}, u32[]{:S(2)}) %collective-permute-start.5) | collective-permute-done | bytes 262176 | tf_op jit(solution)/shard_map/ppermute | solution.py:70
  48.8 1.5 collective-permute-start.6
  51.4 1.5 collective-permute-start.18
  53.7 4.0 %collective-permute-done.6 = bf16[64,2048]{1,0:T(8,128)(2,1)S(1)} collective-permute-done((bf16[64,2048]{1,0:T(8,128)(2,1)S(1)}, bf16[64,2048]{1,0:T(8,128)(2,1)S(1)}, u32[]{:S(2)}, u32[]{:S(2)}) %collective-permute-start.6) | collective-permute-done | bytes 262176 | tf_op jit(solution)/shard_map/ppermute | solution.py:73
  58.5 1.3 collective-permute-start.22
  59.8 1.6 collective-permute-start.20
  63.8 4.7 %collective-permute-done.20 = bf16[64,2048]{1,0:T(8,128)(2,1)S(1)} collective-permute-done((bf16[64,2048]{1,0:T(8,128)(2,1)S(1)}, bf16[64,2048]{1,0:T(8,128)(2,1)S(1)}, u32[]{:S(2)}, u32[]{:S(2)}) %collective-permute-start.20) | collective-permute-done | bytes 262176 | tf_op jit(solution)/shard_map/ppermute | solution.py:73
  70.2 1.5 collective-permute-start.23
  72.4 5.7 %collective-permute-done.23 = bf16[64,2048]{1,0:T(8,128)(2,1)S(1)} collective-permute-done((bf16[64,2048]{1,0:T(8,128)(2,1)S(1)}, bf16[64,2048]{1,0:T(8,128)(2,1)S(1)}, u32[]{:S(2)}, u32[]{:S(2)}) %collective-permute-start.23) | collective-permute-done | bytes 262176 | tf_op jit(solution)/shard_map/ppermute | solution.py:73
  79.0 1.6 constant_dynamic-update-slice_fusion.7
  80.6 6.5 %fusion.6 = f32[1024,1024]{0,1:T(8,128)S(1)} fusion(bf16[1024,2048]{1,0:T(8,128)(2,1)} %constant_dynamic-update-slice_fusion.7, bf16[1,2048,1024]{2,1,0:T(8,128)(2,1)S(1)} %copy-done.13), kind=kOutput, calls=%fused_computation.9 | convolution fusion | flops 4294967296 | bytes 12582912 | tf_op jit(solution)/shard_map/dot_general | solution.py:8
  87.1 4.6 %fusion.10 = f32[1024,1024]{0,1:T(8,128)S(1)} fusion(bf16[1024,2048]{1,0:T(8,128)(2,1)S(1)} %copy-done.6, bf16[1,2048,1024]{2,1,0:T(8,128)(2,1)S(1)} %copy-done.15), kind=kOutput, calls=%fused_computation.13 | convolution fusion | flops 4294967296 | bytes 12582912 | tf_op jit(solution)/shard_map/dot_general | solution.py:8
  92.0 3.4 %copy-done.11 = bf16[1,1024,2048]{2,1,0:T(8,128)(2,1)S(1)} copy-done((bf16[1,1024,2048]{2,1,0:T(8,128)(2,1)S(1)}, bf16[1,1024,2048]{2,1,0:T(8,128)(2,1)}, u32[]{:S(2)}) %copy-start.11) | copy-done | bytes 4194328
  95.4 6.5 %multiply_reduce_fusion = (f32[1024]{0:T(1024)S(1)}, f32[1024,1024]{0,1:T(8,128)}) fusion(f32[1024,1024]{0,1:T(8,128)S(1)} %fusion.6, f32[1024,1024]{0,1:T(8,128)S(1)} %fusion.10, bf16[1024,2048]{1,0:T(8,128)(2,1)S(1)} %constant_dynamic-update-slice_fusion.22, bf16[1,1024,2048]{2,1,0:T(8,128)(2,1)S(1)} %copy-done.11), kind=kOutput, calls=%fused_computation.18 | convolution fusion | flops 4302306304 | bytes 20975616 | tf_op jit(solution)/shard_map/dot_general | solution.py:18
  102.6 32.2 %all-gather.1 = f32[128,128]{1,0:T(8,128)S(1)} all-gather(f32[8,128]{1,0:T(8,128)S(1)} %gather_fusion.1), channel_id=3, replica_groups=mesh['groups'=2,'expert'=8,'helper'=2,'dp'=1] {'expert','helper'}, dimensions={0}, use_global_device_ids=true | all-gather | bytes 69632 | tf_op jit(solution)/shard_map/all_gather | solution.py:162
  134.9 14.2 %all-gather = f32[64,128]{1,0:T(8,128)S(1)} all-gather(f32[8,128]{1,0:T(8,128)S(1)} %bitcast.75), channel_id=2, replica_groups=mesh['groups'=2,'expert'=8,'helper'=2,'dp'=1] {'expert'}, dimensions={0}, use_global_device_ids=true | all-gather | bytes 36864 | tf_op jit(solution)/shard_map/all_gather | solution.py:138
  149.9 6.2 %multiply_convert_fusion.1 = (bf16[1024,1024]{0,1:T(8,128)(2,1)S(1)}, bf16[1024,1024]{0,1:T(8,128)(2,1)S(1)}, bf16[1024,1024]{0,1:T(8,128)(2,1)S(1)}) fusion(f32[1024,1024]{0,1:T(8,128)} %copy-done.1, f32[1024,1024]{0,1:T(8,128)} %copy-done, f32[1024,1024]{0,1:T(8,128)} %get-tuple-element.112, f32[1024]{0:T(1024)S(1)} %fusion.34), kind=kLoop, calls=%fused_computation.20 | loop fusion | flops 17825792 | bytes 18878464 | tf_op jit(solution)/shard_map/convert_element_type | solution.py:155
  156.1 6.0 %convert_bitcast_fusion = bf16[1,1024,2048]{2,1,0:T(8,128)(2,1)} fusion(bf16[1024,1024]{0,1:T(8,128)(2,1)S(1)} %get-tuple-element.36, bf16[1024,2048]{1,0:T(8,128)(2,1)S(1)} %copy-done.5), kind=kOutput, calls=%fused_computation.15 | convolution fusion | flops 4297064448 | bytes 10485760 | tf_op jit(solution)/shard_map/dot_general | solution.py:12
  162.1 5.0 %fusion.13 = bf16[1024,2048]{1,0:T(8,128)(2,1)S(1)} fusion(bf16[1024,1024]{0,1:T(8,128)(2,1)S(1)} %get-tuple-element.36, bf16[1,1024,2048]{2,1,0:T(8,128)(2,1)S(1)} %copy-done.12), kind=kOutput, calls=%fused_computation.24 | convolution fusion | flops 4297064448 | bytes 10485760 | tf_op jit(solution)/shard_map/dot_general | solution.py:8
  168.0 1.3 copy-done.14
  169.3 6.8 %fusion.4 = f32[1024,2048]{1,0:T(8,128)} fusion(bf16[1024,1024]{0,1:T(8,128)(2,1)S(1)} %get-tuple-element.35, bf16[1,2048,1024]{2,1,0:T(8,128)(2,1)S(1)} %copy-done.14), kind=kOutput, calls=%fused_computation.7 | convolution fusion | flops 4294967296 | bytes 14680064 | tf_op jit(solution)/shard_map/dot_general | solution.py:18
  176.1 7.1 %add_convert_fusion = bf16[1024,2048]{1,0:T(8,128)(2,1)S(1)} fusion(f32[1024,2048]{1,0:T(8,128)} %fusion.4, bf16[1024,1024]{0,1:T(8,128)(2,1)S(1)} %get-tuple-element.34, bf16[1,2048,1024]{2,1,0:T(8,128)(2,1)S(1)} %copy-done.16), kind=kOutput, calls=%fused_computation.2 | convolution fusion | flops 4299161600 | bytes 18874368 | tf_op jit(solution)/shard_map/dot_general | solution.py:18
  185.3 6.3 %convert_bitcast_fusion.2 = bf16[1,2048,1024]{2,1,0:T(8,128)(2,1)} fusion(bf16[1024,2048]{1,0:T(8,128)(2,1)S(1)} %copy-done.7, bf16[1024,1024]{0,1:T(8,128)(2,1)S(1)} %get-tuple-element.34), kind=kOutput, calls=%fused_computation.17 | convolution fusion | flops 4297064448 | bytes 10485760 | tf_op jit(solution)/shard_map/dot_general | solution.py:12
  191.6 6.3 %convert_bitcast_fusion.1 = bf16[1,2048,1024]{2,1,0:T(8,128)(2,1)} fusion(bf16[1024,2048]{1,0:T(8,128)(2,1)S(1)} %copy-done.7, bf16[1024,1024]{0,1:T(8,128)(2,1)S(1)} %get-tuple-element.35), kind=kOutput, calls=%fused_computation.16 | convolution fusion | flops 4297064448 | bytes 10485760 | tf_op jit(solution)/shard_map/dot_general | solution.py:12
  199.0 2.0 collective-permute-start.14
  201.1 2.0 collective-permute-start.10
  204.2 15.2 %collective-permute-done.11 = bf16[128,1024]{1,0:T(8,128)(2,1)S(1)} collective-permute-done((bf16[128,1024]{1,0:T(8,128)(2,1)S(1)}, bf16[128,1024]{1,0:T(8,128)(2,1)S(1)}, u32[]{:S(2)}, u32[]{:S(2)}) %collective-permute-start.11) | collective-permute-done | bytes 262176 | tf_op jit(solution)/shard_map/ppermute | solution.py:108
  219.5 16.1 %collective-permute-done.28 = bf16[128,1024]{1,0:T(8,128)(2,1)S(1)} collective-permute-done((bf16[128,1024]{1,0:T(8,128)(2,1)S(1)}, bf16[128,1024]{1,0:T(8,128)(2,1)S(1)}, u32[]{:S(2)}, u32[]{:S(2)}) %collective-permute-start.28) | collective-permute-done | bytes 262176 | tf_op jit(solution)/shard_map/ppermute | solution.py:108
  236.0 1.8 collective-permute-start.27
  238.5 4.3 %collective-permute-start.12 = (bf16[128,1024]{1,0:T(8,128)(2,1)S(1)}, bf16[128,1024]{1,0:T(8,128)(2,1)S(1)}, u32[]{:S(2)}, u32[]{:S(2)}) collective-permute-start(bf16[128,1024]{1,0:T(8,128)(2,1)S(1)} %fusion.26), channel_id=1, source_target_pairs={{0,4},{2,6},{12,8},{14,10},{1,5},{3,7},{13,9},{15,11},{16,20},{18,... | collective-permute-start | bytes 786440 | tf_op jit(solution)/shard_map/ppermute | solution.py:110
  244.8 1.3 collective-permute-start.29
  246.2 3.3 %collective-permute-done.12 = bf16[128,1024]{1,0:T(8,128)(2,1)S(1)} collective-permute-done((bf16[128,1024]{1,0:T(8,128)(2,1)S(1)}, bf16[128,1024]{1,0:T(8,128)(2,1)S(1)}, u32[]{:S(2)}, u32[]{:S(2)}) %collective-permute-start.12) | collective-permute-done | bytes 262176 | tf_op jit(solution)/shard_map/ppermute | solution.py:110
  250.5 1.9 collective-permute-start.15
  252.4 2.8 collective-permute-done.29
  255.3 1.7 collective-permute-start.30
  258.0 7.6 %collective-permute-done.13 = bf16[128,1024]{1,0:T(8,128)(2,1)S(1)} collective-permute-done((bf16[128,1024]{1,0:T(8,128)(2,1)S(1)}, bf16[128,1024]{1,0:T(8,128)(2,1)S(1)}, u32[]{:S(2)}, u32[]{:S(2)}) %collective-permute-start.13) | collective-permute-done | bytes 262176 | tf_op jit(solution)/shard_map/ppermute | solution.py:111
  266.6 7.2 %collective-permute-done.30 = bf16[128,1024]{1,0:T(8,128)(2,1)S(1)} collective-permute-done((bf16[128,1024]{1,0:T(8,128)(2,1)S(1)}, bf16[128,1024]{1,0:T(8,128)(2,1)S(1)}, u32[]{:S(2)}, u32[]{:S(2)}) %collective-permute-start.30) | collective-permute-done | bytes 262176 | tf_op jit(solution)/shard_map/ppermute | solution.py:111
  273.8 1.5 collective-permute-done.32
  (130 shorter events, 33.7 us)
Async XLA Ops:
  0.6 17.3 %copy-start.2 = (bf16[128,2048]{1,0:T(8,128)(2,1)S(1)}, bf16[128,2048]{1,0:T(8,128)(2,1)}, u32[]{:S(2)}) copy-start(bf16[128,2048]{1,0:T(8,128)(2,1)} %param.8) | copy-start | bytes 1572868
  0.6 18.5 %copy-start.9 = (s32[128]{0:T(128)S(1)}, s32[128]{0:T(128)}, u32[]{:S(2)}) copy-start(s32[128]{0:T(128)} %param.10) | copy-start | bytes 1540
  0.7 18.5 %copy-start.8 = (f32[128,4]{0,1:T(4,128)S(1)}, f32[128,4]{0,1:T(4,128)}, u32[]{:S(2)}) copy-start(f32[128,4]{0,1:T(4,128)} %param.11) | copy-start | bytes 6148
  1.9 42.4 %collective-permute-start.4 = (bf16[64,2048]{1,0:T(8,128)(2,1)S(1)}, bf16[64,2048]{1,0:T(8,128)(2,1)S(1)}, u32[]{:S(2)}, u32[]{:S(2)}) collective-permute-start(bf16[64,2048]{1,0:T(8,128)(2,1)S(1)} %get-tuple-element.61), channel_id=1, source_target_pairs={{4,8},{6,10},{8,4},{10,6},{5,9},{7,11},{9,5},{11,7},{20,24},{22,26... | collective-permute-start | bytes 786440 | tf_op jit(solution)/shard_map/ppermute | solution.py:69
  2.6 29.7 %collective-permute-start.2 = (bf16[64,2048]{1,0:T(8,128)(2,1)S(1)}, bf16[64,2048]{1,0:T(8,128)(2,1)S(1)}, u32[]{:S(2)}, u32[]{:S(2)}) collective-permute-start(bf16[64,2048]{1,0:T(8,128)(2,1)S(1)} %get-tuple-element.61), channel_id=1, source_target_pairs={{0,8},{2,10},{4,12},{6,14},{8,0},{10,2},{12,4},{14,6},{1,9},{3,11}... | collective-permute-start | bytes 786440 | tf_op jit(solution)/shard_map/ppermute | solution.py:67
  8.4 12.4 %collective-permute-start = (bf16[64,2048]{1,0:T(8,128)(2,1)S(1)}, bf16[64,2048]{1,0:T(8,128)(2,1)S(1)}, u32[]{:S(2)}, u32[]{:S(2)}) collective-permute-start(bf16[64,2048]{1,0:T(8,128)(2,1)S(1)} %get-tuple-element.61), channel_id=1, source_target_pairs={{0,4},{2,6},{4,0},{6,2},{8,12},{10,14},{12,8},{14,10},{1,5},{3,7},... | collective-permute-start | bytes 786440 | tf_op jit(solution)/shard_map/ppermute | solution.py:68
  9.8 59.6 %collective-permute-start.21 = (bf16[64,2048]{1,0:T(8,128)(2,1)S(1)}, bf16[64,2048]{1,0:T(8,128)(2,1)S(1)}, u32[]{:S(2)}, u32[]{:S(2)}) collective-permute-start(bf16[64,2048]{1,0:T(8,128)(2,1)S(1)} %get-tuple-element.64), channel_id=1, source_target_pairs={{4,8},{6,10},{8,4},{10,6},{5,9},{7,11},{9,5},{11,7},{20,24},{22,26... | collective-permute-start | bytes 786440 | tf_op jit(solution)/shard_map/ppermute | solution.py:69
  10.5 48.0 %collective-permute-start.19 = (bf16[64,2048]{1,0:T(8,128)(2,1)S(1)}, bf16[64,2048]{1,0:T(8,128)(2,1)S(1)}, u32[]{:S(2)}, u32[]{:S(2)}) collective-permute-start(bf16[64,2048]{1,0:T(8,128)(2,1)S(1)} %get-tuple-element.64), channel_id=1, source_target_pairs={{0,8},{2,10},{4,12},{6,14},{8,0},{10,2},{12,4},{14,6},{1,9},{3,11}... | collective-permute-start | bytes 786440 | tf_op jit(solution)/shard_map/ppermute | solution.py:67
  20.7 13.7 %collective-permute-start.1 = (bf16[64,2048]{1,0:T(8,128)(2,1)S(1)}, bf16[64,2048]{1,0:T(8,128)(2,1)S(1)}, u32[]{:S(2)}, u32[]{:S(2)}) collective-permute-start(bf16[64,2048]{1,0:T(8,128)(2,1)S(1)} %collective-permute-done), channel_id=1, source_target_pairs={{0,1},{1,0},{2,3},{3,2},{4,5},{5,4},{6,7},{7,6},{8,9},{9,8},{10,11... | collective-permute-start | bytes 786440 | tf_op jit(solution)/shard_map/ppermute | solution.py:73
  32.3 15.7 %collective-permute-start.5 = (bf16[64,2048]{1,0:T(8,128)(2,1)S(1)}, bf16[64,2048]{1,0:T(8,128)(2,1)S(1)}, u32[]{:S(2)}, u32[]{:S(2)}) collective-permute-start(bf16[64,2048]{1,0:T(8,128)(2,1)S(1)} %collective-permute-done.2), channel_id=1, source_target_pairs={{4,0},{6,2},{8,12},{10,14},{5,1},{7,3},{9,13},{11,15},{20,16},{22,... | collective-permute-start | bytes 786440 | tf_op jit(solution)/shard_map/ppermute | solution.py:70
  34.4 6.4 %collective-permute-start.3 = (bf16[64,2048]{1,0:T(8,128)(2,1)S(1)}, bf16[64,2048]{1,0:T(8,128)(2,1)S(1)}, u32[]{:S(2)}, u32[]{:S(2)}) collective-permute-start(bf16[64,2048]{1,0:T(8,128)(2,1)S(1)} %collective-permute-done.2), channel_id=1, source_target_pairs={{0,1},{1,0},{2,3},{3,2},{4,5},{5,4},{6,7},{7,6},{8,9},{9,8},{10,11... | collective-permute-start | bytes 786440 | tf_op jit(solution)/shard_map/ppermute | solution.py:73
  40.8 10.6 %collective-permute-start.17 = (bf16[64,2048]{1,0:T(8,128)(2,1)S(1)}, bf16[64,2048]{1,0:T(8,128)(2,1)S(1)}, u32[]{:S(2)}, u32[]{:S(2)}) collective-permute-start(bf16[64,2048]{1,0:T(8,128)(2,1)S(1)} %get-tuple-element.64), channel_id=1, source_target_pairs={{0,4},{2,6},{4,0},{6,2},{8,12},{10,14},{12,8},{14,10},{1,5},{3,7},... | collective-permute-start | bytes 786440 | tf_op jit(solution)/shard_map/ppermute | solution.py:68
  48.8 8.8 %collective-permute-start.6 = (bf16[64,2048]{1,0:T(8,128)(2,1)S(1)}, bf16[64,2048]{1,0:T(8,128)(2,1)S(1)}, u32[]{:S(2)}, u32[]{:S(2)}) collective-permute-start(bf16[64,2048]{1,0:T(8,128)(2,1)S(1)} %get-tuple-element.31), channel_id=1, source_target_pairs={{0,1},{1,0},{2,3},{3,2},{4,5},{5,4},{6,7},{7,6},{8,9},{9,8},{10,11... | collective-permute-start | bytes 786440 | tf_op jit(solution)/shard_map/ppermute | solution.py:73
  51.4 10.7 %collective-permute-start.18 = (bf16[64,2048]{1,0:T(8,128)(2,1)S(1)}, bf16[64,2048]{1,0:T(8,128)(2,1)S(1)}, u32[]{:S(2)}, u32[]{:S(2)}) collective-permute-start(bf16[64,2048]{1,0:T(8,128)(2,1)S(1)} %collective-permute-done.17), channel_id=1, source_target_pairs={{0,1},{1,0},{2,3},{3,2},{4,5},{5,4},{6,7},{7,6},{8,9},{9,8},{10,11... | collective-permute-start | bytes 786440 | tf_op jit(solution)/shard_map/ppermute | solution.py:73
  58.5 20.5 %collective-permute-start.7 = (bf16[512,2048]{1,0:T(8,128)(2,1)}, bf16[512,2048]{1,0:T(8,128)(2,1)S(1)}, u32[]{:S(2)}, u32[]{:S(2)}) collective-permute-start(bf16[512,2048]{1,0:T(8,128)(2,1)} %get-tuple-element.87), channel_id=1, source_target_pairs={{0,2},{2,0},{4,6},{6,4},{8,10},{10,8},{12,14},{14,12},{1,3},{3,1},... | collective-permute-start | bytes 6291464 | tf_op jit(solution)/shard_map/ppermute | solution.py:75
  58.5 10.9 %collective-permute-start.22 = (bf16[64,2048]{1,0:T(8,128)(2,1)S(1)}, bf16[64,2048]{1,0:T(8,128)(2,1)S(1)}, u32[]{:S(2)}, u32[]{:S(2)}) collective-permute-start(bf16[64,2048]{1,0:T(8,128)(2,1)S(1)} %collective-permute-done.19), channel_id=1, source_target_pairs={{4,0},{6,2},{8,12},{10,14},{5,1},{7,3},{9,13},{11,15},{20,16},{22,... | collective-permute-start | bytes 786440 | tf_op jit(solution)/shard_map/ppermute | solution.py:70
  59.8 8.8 %collective-permute-start.20 = (bf16[64,2048]{1,0:T(8,128)(2,1)S(1)}, bf16[64,2048]{1,0:T(8,128)(2,1)S(1)}, u32[]{:S(2)}, u32[]{:S(2)}) collective-permute-start(bf16[64,2048]{1,0:T(8,128)(2,1)S(1)} %collective-permute-done.19), channel_id=1, source_target_pairs={{0,1},{1,0},{2,3},{3,2},{4,5},{5,4},{6,7},{7,6},{8,9},{9,8},{10,11... | collective-permute-start | bytes 786440 | tf_op jit(solution)/shard_map/ppermute | solution.py:73
  70.2 7.9 %collective-permute-start.23 = (bf16[64,2048]{1,0:T(8,128)(2,1)S(1)}, bf16[64,2048]{1,0:T(8,128)(2,1)S(1)}, u32[]{:S(2)}, u32[]{:S(2)}) collective-permute-start(bf16[64,2048]{1,0:T(8,128)(2,1)S(1)} %get-tuple-element.33), channel_id=1, source_target_pairs={{0,1},{1,0},{2,3},{3,2},{4,5},{5,4},{6,7},{7,6},{8,9},{9,8},{10,11... | collective-permute-start | bytes 786440 | tf_op jit(solution)/shard_map/ppermute | solution.py:73
  71.7 8.9 %copy-start.13 = (bf16[1,2048,1024]{2,1,0:T(8,128)(2,1)S(1)}, bf16[1,2048,1024]{2,1,0:T(8,128)(2,1)}, u32[]{:S(2)}) copy-start(bf16[1,2048,1024]{2,1,0:T(8,128)(2,1)} %param.13) | copy-start | bytes 12582916
  79.0 12.7 %collective-permute-start.24 = (bf16[512,2048]{1,0:T(8,128)(2,1)}, bf16[512,2048]{1,0:T(8,128)(2,1)S(1)}, u32[]{:S(2)}, u32[]{:S(2)}) collective-permute-start(bf16[512,2048]{1,0:T(8,128)(2,1)} %get-tuple-element.97), channel_id=1, source_target_pairs={{0,2},{2,0},{4,6},{6,4},{8,10},{10,8},{12,14},{14,12},{1,3},{3,1},... | collective-permute-start | bytes 6291464 | tf_op jit(solution)/shard_map/ppermute | solution.py:75
  80.6 6.5 %copy-start.6 = (bf16[1024,2048]{1,0:T(8,128)(2,1)S(1)}, bf16[1024,2048]{1,0:T(8,128)(2,1)}, u32[]{:S(2)}) copy-start(bf16[1024,2048]{1,0:T(8,128)(2,1)} %constant_dynamic-update-slice_fusion.7) | copy-start | bytes 12582916
  80.6 6.5 %copy-start.15 = (bf16[1,2048,1024]{2,1,0:T(8,128)(2,1)S(1)}, bf16[1,2048,1024]{2,1,0:T(8,128)(2,1)}, u32[]{:S(2)}) copy-start(bf16[1,2048,1024]{2,1,0:T(8,128)(2,1)} %param.12) | copy-start | bytes 12582916
  87.1 4.9 %copy-start = (f32[1024,1024]{0,1:T(8,128)}, f32[1024,1024]{0,1:T(8,128)S(1)}, u32[]{:S(2)}) copy-start(f32[1024,1024]{0,1:T(8,128)S(1)} %fusion.6) | copy-start | bytes 12582916
  87.1 4.6 %copy-start.3 = (bf16[1024,2048]{1,0:T(8,128)(2,1)S(1)}, bf16[1024,2048]{1,0:T(8,128)(2,1)}, u32[]{:S(2)}) copy-start(bf16[1024,2048]{1,0:T(8,128)(2,1)} %get-tuple-element.98) | copy-start | bytes 12582916
  91.7 10.2 %copy-start.1 = (f32[1024,1024]{0,1:T(8,128)}, f32[1024,1024]{0,1:T(8,128)S(1)}, u32[]{:S(2)}) copy-start(f32[1024,1024]{0,1:T(8,128)S(1)} %fusion.10) | copy-start | bytes 12582916
  95.4 6.5 %copy-start.4 = (bf16[1024,2048]{1,0:T(8,128)(2,1)}, bf16[1024,2048]{1,0:T(8,128)(2,1)S(1)}, u32[]{:S(2)}) copy-start(bf16[1024,2048]{1,0:T(8,128)(2,1)S(1)} %constant_dynamic-update-slice_fusion.22) | copy-start | bytes 12582916
  95.4 39.5 %copy-start.10 = (s32[128,4]{0,1:T(4,128)S(1)}, s32[128,4]{0,1:T(4,128)}, u32[]{:S(2)}) copy-start(s32[128,4]{0,1:T(4,128)} %param.9) | copy-start | bytes 6148
  149.9 6.2 %copy-start.5 = (bf16[1024,2048]{1,0:T(8,128)(2,1)S(1)}, bf16[1024,2048]{1,0:T(8,128)(2,1)}, u32[]{:S(2)}) copy-start(bf16[1024,2048]{1,0:T(8,128)(2,1)} %copy-done.4) | copy-start | bytes 12582916
  156.0 6.1 %copy-start.12 = (bf16[1,1024,2048]{2,1,0:T(8,128)(2,1)S(1)}, bf16[1,1024,2048]{2,1,0:T(8,128)(2,1)}, u32[]{:S(2)}) copy-start(bf16[1,1024,2048]{2,1,0:T(8,128)(2,1)} %param.14) | copy-start | bytes 12582916
  167.6 30.3 %collective-permute-start.8 = (bf16[512,2048]{1,0:T(8,128)(2,1)S(1)}, bf16[512,2048]{1,0:T(8,128)(2,1)S(1)}, u32[]{:S(2)}, u32[]{:S(2)}) collective-permute-start(bf16[512,2048]{1,0:T(8,128)(2,1)S(1)} %get-tuple-element.44), channel_id=1, source_target_pairs={{0,2},{2,0},{4,6},{6,4},{8,10},{10,8},{12,14},{14,12},{1,3},{3,1},... | collective-permute-start | bytes 6291464 | tf_op jit(solution)/shard_map/ppermute | solution.py:94
  169.3 6.8 %copy-start.16 = (bf16[1,2048,1024]{2,1,0:T(8,128)(2,1)S(1)}, bf16[1,2048,1024]{2,1,0:T(8,128)(2,1)}, u32[]{:S(2)}) copy-start(bf16[1,2048,1024]{2,1,0:T(8,128)(2,1)} %param.12) | copy-start | bytes 12582916
  183.7 19.3 %collective-permute-start.25 = (bf16[512,2048]{1,0:T(8,128)(2,1)S(1)}, bf16[512,2048]{1,0:T(8,128)(2,1)S(1)}, u32[]{:S(2)}, u32[]{:S(2)}) collective-permute-start(bf16[512,2048]{1,0:T(8,128)(2,1)S(1)} %get-tuple-element.40), channel_id=1, source_target_pairs={{0,2},{2,0},{4,6},{6,4},{8,10},{10,8},{12,14},{14,12},{1,3},{3,1},... | collective-permute-start | bytes 6291464 | tf_op jit(solution)/shard_map/ppermute | solution.py:94
  198.9 37.0 %collective-permute-start.9 = (bf16[128,1024]{1,0:T(8,128)(2,1)S(1)}, bf16[128,1024]{1,0:T(8,128)(2,1)S(1)}, u32[]{:S(2)}, u32[]{:S(2)}) collective-permute-start(bf16[128,1024]{1,0:T(8,128)(2,1)S(1)} %get-tuple-element.53), channel_id=1, source_target_pairs={{0,1},{1,0},{2,3},{3,2},{4,5},{5,4},{6,7},{7,6},{8,9},{9,8},{10,11... | collective-permute-start | bytes 786440 | tf_op jit(solution)/shard_map/ppermute | solution.py:108
  199.0 38.8 %collective-permute-start.14 = (bf16[128,1024]{1,0:T(8,128)(2,1)S(1)}, bf16[128,1024]{1,0:T(8,128)(2,1)S(1)}, u32[]{:S(2)}, u32[]{:S(2)}) collective-permute-start(bf16[128,1024]{1,0:T(8,128)(2,1)S(1)} %get-tuple-element.54), channel_id=1, source_target_pairs={{0,1},{1,0},{2,3},{3,2},{4,5},{5,4},{6,7},{7,6},{8,9},{9,8},{10,11... | collective-permute-start | bytes 786440 | tf_op jit(solution)/shard_map/ppermute | solution.py:108
  201.0 18.3 %collective-permute-start.11 = (bf16[128,1024]{1,0:T(8,128)(2,1)S(1)}, bf16[128,1024]{1,0:T(8,128)(2,1)S(1)}, u32[]{:S(2)}, u32[]{:S(2)}) collective-permute-start(bf16[128,1024]{1,0:T(8,128)(2,1)S(1)} %get-tuple-element.55), channel_id=1, source_target_pairs={{0,1},{1,0},{2,3},{3,2},{4,5},{5,4},{6,7},{7,6},{8,9},{9,8},{10,11... | collective-permute-start | bytes 786440 | tf_op jit(solution)/shard_map/ppermute | solution.py:108
  201.1 37.4 %collective-permute-start.10 = (bf16[128,1024]{1,0:T(8,128)(2,1)S(1)}, bf16[128,1024]{1,0:T(8,128)(2,1)S(1)}, u32[]{:S(2)}, u32[]{:S(2)}) collective-permute-start(bf16[128,1024]{1,0:T(8,128)(2,1)S(1)} %get-tuple-element.56), channel_id=1, source_target_pairs={{0,1},{1,0},{2,3},{3,2},{4,5},{5,4},{6,7},{7,6},{8,9},{9,8},{10,11... | collective-permute-start | bytes 786440 | tf_op jit(solution)/shard_map/ppermute | solution.py:108
  204.1 38.8 %collective-permute-start.26 = (bf16[128,1024]{1,0:T(8,128)(2,1)S(1)}, bf16[128,1024]{1,0:T(8,128)(2,1)S(1)}, u32[]{:S(2)}, u32[]{:S(2)}) collective-permute-start(bf16[128,1024]{1,0:T(8,128)(2,1)S(1)} %get-tuple-element.49), channel_id=1, source_target_pairs={{0,1},{1,0},{2,3},{3,2},{4,5},{5,4},{6,7},{7,6},{8,9},{9,8},{10,11... | collective-permute-start | bytes 786440 | tf_op jit(solution)/shard_map/ppermute | solution.py:108
  219.4 16.2 %collective-permute-start.28 = (bf16[128,1024]{1,0:T(8,128)(2,1)S(1)}, bf16[128,1024]{1,0:T(8,128)(2,1)S(1)}, u32[]{:S(2)}, u32[]{:S(2)}) collective-permute-start(bf16[128,1024]{1,0:T(8,128)(2,1)S(1)} %get-tuple-element.51), channel_id=1, source_target_pairs={{0,1},{1,0},{2,3},{3,2},{4,5},{5,4},{6,7},{7,6},{8,9},{9,8},{10,11... | collective-permute-start | bytes 786440 | tf_op jit(solution)/shard_map/ppermute | solution.py:108
  235.6 9.2 %collective-permute-start.31 = (bf16[128,1024]{1,0:T(8,128)(2,1)S(1)}, bf16[128,1024]{1,0:T(8,128)(2,1)S(1)}, u32[]{:S(2)}, u32[]{:S(2)}) collective-permute-start(bf16[128,1024]{1,0:T(8,128)(2,1)S(1)} %get-tuple-element.50), channel_id=1, source_target_pairs={{0,1},{1,0},{2,3},{3,2},{4,5},{5,4},{6,7},{7,6},{8,9},{9,8},{10,11... | collective-permute-start | bytes 786440 | tf_op jit(solution)/shard_map/ppermute | solution.py:108
  236.0 14.5 %collective-permute-start.27 = (bf16[128,1024]{1,0:T(8,128)(2,1)S(1)}, bf16[128,1024]{1,0:T(8,128)(2,1)S(1)}, u32[]{:S(2)}, u32[]{:S(2)}) collective-permute-start(bf16[128,1024]{1,0:T(8,128)(2,1)S(1)} %get-tuple-element.52), channel_id=1, source_target_pairs={{0,1},{1,0},{2,3},{3,2},{4,5},{5,4},{6,7},{7,6},{8,9},{9,8},{10,11... | collective-permute-start | bytes 786440 | tf_op jit(solution)/shard_map/ppermute | solution.py:108
  237.8 19.3 %collective-permute-start.16 = (bf16[128,1024]{1,0:T(8,128)(2,1)S(1)}, bf16[128,1024]{1,0:T(8,128)(2,1)S(1)}, u32[]{:S(2)}, u32[]{:S(2)}) collective-permute-start(bf16[128,1024]{1,0:T(8,128)(2,1)S(1)} %fusion.26), channel_id=1, source_target_pairs={{4,8},{6,10},{8,4},{10,6},{5,9},{7,11},{9,5},{11,7},{20,24},{22,26... | collective-permute-start | bytes 786440 | tf_op jit(solution)/shard_map/ppermute | solution.py:115
  238.5 11.0 %collective-permute-start.12 = (bf16[128,1024]{1,0:T(8,128)(2,1)S(1)}, bf16[128,1024]{1,0:T(8,128)(2,1)S(1)}, u32[]{:S(2)}, u32[]{:S(2)}) collective-permute-start(bf16[128,1024]{1,0:T(8,128)(2,1)S(1)} %fusion.26), channel_id=1, source_target_pairs={{0,4},{2,6},{12,8},{14,10},{1,5},{3,7},{13,9},{15,11},{16,20},{18,... | collective-permute-start | bytes 786440 | tf_op jit(solution)/shard_map/ppermute | solution.py:110
  242.9 23.8 %collective-permute-start.33 = (bf16[128,1024]{1,0:T(8,128)(2,1)S(1)}, bf16[128,1024]{1,0:T(8,128)(2,1)S(1)}, u32[]{:S(2)}, u32[]{:S(2)}) collective-permute-start(bf16[128,1024]{1,0:T(8,128)(2,1)S(1)} %fusion.19), channel_id=1, source_target_pairs={{4,8},{6,10},{8,4},{10,6},{5,9},{7,11},{9,5},{11,7},{20,24},{22,26... | collective-permute-start | bytes 786440 | tf_op jit(solution)/shard_map/ppermute | solution.py:115
  244.8 10.3 %collective-permute-start.29 = (bf16[128,1024]{1,0:T(8,128)(2,1)S(1)}, bf16[128,1024]{1,0:T(8,128)(2,1)S(1)}, u32[]{:S(2)}, u32[]{:S(2)}) collective-permute-start(bf16[128,1024]{1,0:T(8,128)(2,1)S(1)} %fusion.19), channel_id=1, source_target_pairs={{0,4},{2,6},{12,8},{14,10},{1,5},{3,7},{13,9},{15,11},{16,20},{18,... | collective-permute-start | bytes 786440 | tf_op jit(solution)/shard_map/ppermute | solution.py:110
  249.7 15.9 %collective-permute-start.13 = (bf16[128,1024]{1,0:T(8,128)(2,1)S(1)}, bf16[128,1024]{1,0:T(8,128)(2,1)S(1)}, u32[]{:S(2)}, u32[]{:S(2)}) collective-permute-start(bf16[128,1024]{1,0:T(8,128)(2,1)S(1)} %get-tuple-element.47), channel_id=1, source_target_pairs={{0,8},{2,10},{4,12},{6,14},{8,0},{10,2},{12,4},{14,6},{1,9},{3,11}... | collective-permute-start | bytes 786440 | tf_op jit(solution)/shard_map/ppermute | solution.py:111
  250.5 15.9 %collective-permute-start.15 = (bf16[128,1024]{1,0:T(8,128)(2,1)S(1)}, bf16[128,1024]{1,0:T(8,128)(2,1)S(1)}, u32[]{:S(2)}, u32[]{:S(2)}) collective-permute-start(bf16[128,1024]{1,0:T(8,128)(2,1)S(1)} %get-tuple-element.48), channel_id=1, source_target_pairs={{0,4},{2,6},{4,0},{6,2},{8,12},{10,14},{12,8},{14,10},{1,5},{3,7},... | collective-permute-start | bytes 786440 | tf_op jit(solution)/shard_map/ppermute | solution.py:114
  255.3 18.5 %collective-permute-start.30 = (bf16[128,1024]{1,0:T(8,128)(2,1)S(1)}, bf16[128,1024]{1,0:T(8,128)(2,1)S(1)}, u32[]{:S(2)}, u32[]{:S(2)}) collective-permute-start(bf16[128,1024]{1,0:T(8,128)(2,1)S(1)} %get-tuple-element.45), channel_id=1, source_target_pairs={{0,8},{2,10},{4,12},{6,14},{8,0},{10,2},{12,4},{14,6},{1,9},{3,11}... | collective-permute-start | bytes 786440 | tf_op jit(solution)/shard_map/ppermute | solution.py:111
  257.1 18.3 %collective-permute-start.32 = (bf16[128,1024]{1,0:T(8,128)(2,1)S(1)}, bf16[128,1024]{1,0:T(8,128)(2,1)S(1)}, u32[]{:S(2)}, u32[]{:S(2)}) collective-permute-start(bf16[128,1024]{1,0:T(8,128)(2,1)S(1)} %get-tuple-element.46), channel_id=1, source_target_pairs={{0,4},{2,6},{4,0},{6,2},{8,12},{10,14},{12,8},{14,10},{1,5},{3,7},... | collective-permute-start | bytes 786440 | tf_op jit(solution)/shard_map/ppermute | solution.py:114
  (3 other events, 8.1 us)
where the time goes:
time: 278 us; the launch traced here: 277 us
  waiting for transfers between devices  89.8 us (32%)
  matrix products  55 us (20%)
  blocking collectives  46.4 us (17%)
  starting transfers between devices  45.5 us (16%)
  local copies, waits for them, and re-layouts  22.2 us (8%)
  other arithmetic  17 us (6%)
    ppermute x8, waiting for transfers between devices, combine(): arrived = swap_halves(lax.ppermute(sent[s], 'helper', self.sides))  32.5 us
    all_gather x1, blocking collectives, on_device(): lax.all_gather(plan.unorder(gate_part), ('expert', 'helper'), tiled=False)  32.2 us
    dot_general x3, matrix products, right_transposed(): lax.dot_general(first_mat, second_mat, (((1,), (1,)), ((), ())), preferre...  20.3 us
    dot_general x3, matrix products, transposed_product(): lax.dot_general(first_mat, second_mat, (((0,), (0,)), ((), ())), preferre...  18.6 us
    ppermute x6, waiting for transfers between devices, dispatch(): pieces = pieces + [piece, lax.ppermute(piece, 'helper', self.sides)]  17.6 us
    dot_general x3, matrix products, product(): return jnp.dot(first_mat, second_mat, preferred_element_type=jnp.float32)  16 us
    ppermute x2, waiting for transfers between devices, combine(): lax.ppermute((slots[2] + relay.astype(jnp.float32)).astype(jnp.bfloat16),...  14.8 us
    all_gather x1, blocking collectives, on_device(): tables = lax.all_gather(gate_table.T, 'expert', tiled=False)  14.2 us
  transfers between devices with their start and end apart: 34, of which 17 were waited for; matrix products, arithmetic and copies ran while one was open for 22% of the time, Pallas kernels for 0%

commit v1 on v0

v1 whole, which is shorter than its diff:
```python
import functools

import jax
import jax.numpy as jnp
from jax import lax
from jax.experimental import pallas as pl
from jax.experimental.pallas import tpu as pltpu
from jax.sharding import PartitionSpec as P

LANES = 128
VMEM_BYTES = 56 * 2**20
ANY = pl.BlockSpec(memory_space=pl.ANY)
SCALARS = pl.BlockSpec(memory_space=pltpu.SMEM)


def product(first_mat, second_mat):
    return jnp.dot(first_mat, second_mat, preferred_element_type=jnp.float32)


def transposed_product(first_mat, second_mat):
    return lax.dot_general(
        first_mat, second_mat, (((0,), (0,)), ((), ())), preferred_element_type=jnp.float32
    )


def right_transposed(first_mat, second_mat):
    return lax.dot_general(
        first_mat, second_mat, (((1,), (1,)), ((), ())), preferred_element_type=jnp.float32
    )


def silu_parts(argument):
    sigmoid_part = jax.nn.sigmoid(argument)
    return argument * sigmoid_part, sigmoid_part * (1.0 + argument * (1.0 - sigmoid_part))


def params(steps=1):
    return pltpu.CompilerParams(
        dimension_semantics=("arbitrary",) * steps, vmem_limit_bytes=VMEM_BYTES
    )


def cost(flops, moved):
    return pl.CostEstimate(flops=flops, bytes_accessed=moved, transcendentals=0)


def lanes_of(rows):
    return lax.broadcasted_iota(jnp.int32, (rows, LANES), 1)


def hi_lo(values, is_high):
    high = values.astype(jnp.bfloat16).astype(jnp.float32)
    return jnp.where(is_high, high, values - high).astype(jnp.bfloat16)


def gate_columns(counts, scores):
    used = [(counts > k).astype(jnp.float32) for k in range(scores.shape[1])]
    weighted = [scores[:, k : k + 1] * used[k] for k in range(scores.shape[1])]
    score_sum = functools.reduce(jnp.add, weighted)
    return [w / score_sum for w in weighted], used, score_sum


def prepare_rows_kernel(experts, place, ids, counts, scores, rows, own, other):
    total, width = rows.shape
    half = total // 2
    lane = lanes_of(total)
    gates, _, _ = gate_columns(counts[...], scores[...])
    table = jnp.zeros((total, LANES), jnp.float32)
    for k, gate in enumerate(gates):
        named = ids[:, k : k + 1]
        table = table + jnp.where((lane == named) | (lane == named + experts), gate, 0.0)
    table = hi_lo(table, lane < experts)
    first = place[0] == 0

    @pl.when(first)
    def _():
        own[:, :width], other[:, :width] = rows[:half, :], rows[half:, :]
        own[:, width:], other[:, width:] = table[:half], table[half:]

    @pl.when(jnp.logical_not(first))
    def _():
        own[:, :width], other[:, :width] = rows[half:, :], rows[:half, :]
        own[:, width:], other[:, width:] = table[half:], table[:half]


def prepare_rows(place, ids, counts, scores, rows, experts):
    total, width = rows.shape
    piece = jax.ShapeDtypeStruct((total // 2, width + LANES), jnp.bfloat16)
    vmem = pl.BlockSpec(memory_space=pltpu.VMEM)
    return pl.pallas_call(
        functools.partial(prepare_rows_kernel, experts),
        out_shape=(piece, piece),
        in_specs=[SCALARS] + [vmem] * 4,
        out_specs=(vmem, vmem),
        compiler_params=pltpu.CompilerParams(vmem_limit_bytes=VMEM_BYTES),
        name="prepare_rows",
    )(place, ids, counts, scores, rows)


def prepare_grads_kernel(place, rows, after, own, other):
    half = rows.shape[0] // 2
    first = place[0] == 0

    @pl.when(first)
    def _():
        own[...], other[...] = rows[:half, :], rows[half:, :]

    @pl.when(jnp.logical_not(first))
    def _():
        own[...], other[...] = rows[half:, :], rows[:half, :]


def prepare_grads(place, rows, after):
    total, width = rows.shape
    piece = jax.ShapeDtypeStruct((total // 2, width), jnp.bfloat16)
    vmem = pl.BlockSpec(memory_space=pltpu.VMEM)
    return pl.pallas_call(
        prepare_grads_kernel,
        out_shape=(piece, piece),
        in_specs=[SCALARS, vmem, ANY],
        out_specs=(vmem, vmem),
        compiler_params=pltpu.CompilerParams(vmem_limit_bytes=VMEM_BYTES),
        name="prepare_grads",
    )(place, rows, after)


def bring_pieces(pieces, columns, target, sems):
    rows = pieces[0].shape[0]
    return [
        pltpu.make_async_copy(
            piece.at[:, columns], target.at[pl.ds(i * rows, rows), :], sems.at[i]
        )
        for i, piece in enumerate(pieces)
    ]


def forward_kernel(tiles, experts, place, *refs):
    pieces, refs = refs[:8], refs[8:]
    gate_mat, up_mat, down_mat, pre_gate, pre_up, gated, own, other = refs[:8]
    rows, gates, down, row_sems, gate_sems, down_sems = refs[8:]
    step = pl.program_id(0)
    width = rows.shape[1]
    half = width // 2
    tile = gate_mat.shape[1]
    kept = gated.shape[0] // 2

    def down_copy(i):
        side = place[0] if i == 1 else 1 - place[0]
        start = pl.multiple_of(side * half, half)
        return pltpu.make_async_copy(
            down_mat.at[:, pl.ds(start, half)], down.at[i], down_sems.at[i]
        )

    @pl.when(step == 0)
    def _():
        copies = bring_pieces(pieces, pl.ds(0, width), rows, row_sems)
        copies = copies + bring_pieces(pieces, pl.ds(width, LANES), gates, gate_sems)
        for copy in copies:
            copy.start()
        for i in range(2):
            down_copy(i).start()
        for copy in copies:
            copy.wait()

    @pl.when(step < tiles)
    def _():
        gate_part = product(rows[...], gate_mat[...])
        up_part = product(rows[...], up_mat[...])
        lane = lanes_of(gates.shape[0])
        mine = (lane == place[1]) | (lane == place[1] + experts)
        gate = jnp.sum(jnp.where(mine, gates[...].astype(jnp.float32), 0.0), axis=1, keepdims=True)
        silu_value, _ = silu_parts(gate_part)
        pre_gate[...] = gate_part
        pre_up[...] = up_part
        columns = pl.ds(pl.multiple_of(step * tile, tile), tile)
        gated[:, columns] = (gate * silu_value * up_part).astype(jnp.bfloat16)

    for i in range(2):

        @pl.when(step == tiles + i)
        def _(i=i):
            down_copy(i).wait()
            out = product(gated[...], down[i]).astype(jnp.bfloat16)
            own[0] = out[:kept]
            other[0] = out[kept:]


def forward(place, pieces, gate_mat, up_mat, down_mat, experts):
    width, hidden = gate_mat.shape
    total = 8 * pieces[0].shape[0]
    tile = 256
    tiles = hidden // tile
    early = lambda s: (0, jnp.minimum(s, tiles - 1))
    late = lambda s: (jnp.maximum(s - tiles, 0), 0, 0)
    pre = jax.ShapeDtypeStruct((total, hidden), jnp.float32)
    act = jax.ShapeDtypeStruct((total, hidden), jnp.bfloat16)
    sums = jax.ShapeDtypeStruct((2, total // 2, width // 2), jnp.bfloat16)
    return pl.pallas_call(
        functools.partial(forward_kernel, tiles, experts),
        grid=(tiles + 2,),
        out_shape=(pre, pre, act, sums, sums),
        in_specs=[SCALARS]
        + [ANY] * 8
        + [pl.BlockSpec((width, tile), early), pl.BlockSpec((width, tile), early), ANY],
        out_specs=(
            pl.BlockSpec((total, tile), early),
            pl.BlockSpec((total, tile), early),
            pl.BlockSpec((total, hidden), lambda s: (0, 0)),
            pl.BlockSpec((1, total // 2, width // 2), late),
            pl.BlockSpec((1, total // 2, width // 2), late),
        ),
        scratch_shapes=[
            pltpu.VMEM((total, width), jnp.bfloat16),
            pltpu.VMEM((total, LANES), jnp.bfloat16),
            pltpu.VMEM((2, hidden, width // 2), jnp.bfloat16),
            pltpu.SemaphoreType.DMA((8,)),
            pltpu.SemaphoreType.DMA((8,)),
            pltpu.SemaphoreType.DMA((2,)),
        ],
        compiler_params=params(),
        cost_estimate=cost(6 * total * width * hidden, 16 * 2**20),
        name="forward",
    )(place, *pieces, gate_mat, up_mat, down_mat)


def backward_kernel(tiles, experts, place, *refs):
    pieces, gate_pieces, refs = refs[:8], refs[8:16], refs[16:]
    down_mat, pre_gate, pre_up, gate_mat, up_mat, after = refs[:6]
    d_gate, d_up, own, other = refs[6:10]
    grads, gates, gate_half, up_half, parts, row_sems, gate_sems, mat_sems = refs[10:]
    step = pl.program_id(0)
    width = grads.shape[1]
    half = width // 2
    tile = down_mat.shape[0]
    total = grads.shape[0]
    kept = total // 2

    def mat_copy(i, which):
        side = place[0] if i == 1 else 1 - place[0]
        start = pl.multiple_of(side * half, half)
        source, target = ((gate_mat, gate_half), (up_mat, up_half))[which]
        return pltpu.make_async_copy(
            source.at[pl.ds(start, half), :], target.at[i], mat_sems.at[i, which]
        )

    @pl.when(step == 0)
    def _():
        copies = bring_pieces(pieces, pl.ds(0, width), grads, row_sems)
        copies = copies + bring_pieces(gate_pieces, pl.ds(width, LANES), gates, gate_sems)
        for copy in copies:
            copy.start()
        for i in range(2):
            for which in range(2):
                mat_copy(i, which).start()
        for copy in copies:
            copy.wait()
        parts[...] = jnp.zeros_like(parts)

    @pl.when(step < tiles)
    def _():
        raw = right_transposed(grads[...], down_mat[...])
        lane = lanes_of(total)
        mine = (lane == place[1]) | (lane == place[1] + experts)
        gate = jnp.sum(jnp.where(mine, gates[...].astype(jnp.float32), 0.0), axis=1, keepdims=True)
        up_part = pre_up[...]
        silu_value, silu_slope = silu_parts(pre_gate[...])
        shares = raw * silu_value * up_part
        parts[...] += functools.reduce(
            jnp.add, [shares[:, c : c + LANES] for c in range(0, tile, LANES)]
        )
        d_act = gate * raw
        columns = pl.ds(pl.multiple_of(step * tile, tile), tile)
        d_gate[:, columns] = (d_act * up_part * silu_slope).astype(jnp.bfloat16)
        d_up[:, columns] = (d_act * silu_value).astype(jnp.bfloat16)

    for i in range(2):

        @pl.when(step == tiles + i)
        def _(i=i):
            for which in range(2):
                mat_copy(i, which).wait()
            back = right_transposed(d_gate[...], gate_half[i]) + right_transposed(
                d_up[...], up_half[i]
            )
            back = back.astype(jnp.bfloat16)
            own[0, :, :half] = back[:kept]
            other[0, :, :half] = back[kept:]
            lane = lanes_of(total)
            high = 2 * place[1] + place[0]
            value = jnp.sum(parts[...], axis=1, keepdims=True)
            value = jnp.where((lane == high) | (lane == high + 2 * experts), value, 0.0)
            value = hi_lo(value, lane < 2 * experts)
            own[0, :, half:] = value[:kept]
            other[0, :, half:] = value[kept:]


def backward(place, pieces, gate_pieces, pre_gate, pre_up, gate_mat, up_mat, down_mat, after, experts):
    width, hidden = gate_mat.shape
    total = pre_gate.shape[0]
    tile = 256
    tiles = hidden // tile
    early = lambda s: (0, jnp.minimum(s, tiles - 1))
    late = lambda s: (jnp.maximum(s - tiles, 0), 0, 0)
    act = jax.ShapeDtypeStruct((total, hidden), jnp.bfloat16)
    sums = jax.ShapeDtypeStruct((2, total // 2, width // 2 + LANES), jnp.bfloat16)
    return pl.pallas_call(
        functools.partial(backward_kernel, tiles, experts),
        grid=(tiles + 2,),
        out_shape=(act, act, sums, sums),
        in_specs=[SCALARS]
        + [ANY] * 16
        + [
            pl.BlockSpec((tile, width), lambda s: (jnp.minimum(s, tiles - 1), 0)),
            pl.BlockSpec((total, tile), early),
            pl.BlockSpec((total, tile), early),
            ANY,
            ANY,
            ANY,
        ],
        out_specs=(
            pl.BlockSpec((total, hidden), lambda s: (0, 0)),
            pl.BlockSpec((total, hidden), lambda s: (0, 0)),
            pl.BlockSpec((1, total // 2, width // 2 + LANES), late),
            pl.BlockSpec((1, total // 2, width // 2 + LANES), late),
        ),
        scratch_shapes=[
            pltpu.VMEM((total, width), jnp.bfloat16),
            pltpu.VMEM((total, LANES), jnp.bfloat16),
            pltpu.VMEM((2, width // 2, hidden), jnp.bfloat16),
            pltpu.VMEM((2, width // 2, hidden), jnp.bfloat16),
            pltpu.VMEM((total, LANES), jnp.float32),
            pltpu.SemaphoreType.DMA((8,)),
            pltpu.SemaphoreType.DMA((8,)),
            pltpu.SemaphoreType.DMA((2, 2)),
        ],
        compiler_params=params(),
        cost_estimate=cost(6 * total * width * hidden, 20 * 2**20),
        name="backward",
    )(place, *pieces, *gate_pieces, down_mat, pre_gate, pre_up, gate_mat, up_mat, after)


def input_weights_kernel(*refs):
    pieces, refs = refs[:16], refs[16:]
    gates, ups, refs = refs[:2], refs[2:4], refs[4:]
    after, grad_gate, grad_up, gate_all, up_all = refs
    rows = gates[0].shape[0]

    @pl.when(pl.program_id(0) == 0)
    def _():
        for i in range(2):
            gate_all[pl.ds(i * rows, rows), :] = gates[i][...]
            up_all[pl.ds(i * rows, rows), :] = ups[i][...]

    tokens = jnp.concatenate([piece[...] for piece in pieces], axis=0)
    grad_gate[...] = transposed_product(tokens, gate_all[...]).astype(jnp.bfloat16)
    grad_up[...] = transposed_product(tokens, up_all[...]).astype(jnp.bfloat16)


def input_weights(pieces, gates, ups, after, width):
    rows, hidden = gates[0].shape
    tile = 256
    whole = pl.BlockSpec((rows, hidden), lambda s: (0, 0))
    grad = jax.ShapeDtypeStruct((width, hidden), jnp.bfloat16)
    return pl.pallas_call(
        input_weights_kernel,
        grid=(width // tile,),
        out_shape=(grad, grad),
        in_specs=[pl.BlockSpec((pieces[0].shape[0], tile), lambda s: (0, s))] * 16
        + [whole] * 4
        + [ANY],
        out_specs=(pl.BlockSpec((tile, hidden), lambda s: (s, 0)),) * 2,
        scratch_shapes=[pltpu.VMEM((2 * rows, hidden), jnp.bfloat16)] * 2,
        compiler_params=params(),
        cost_estimate=cost(8 * rows * width * hidden, 16 * 2**20),
        name="input_weights",
    )(*pieces, *gates, *ups, after)


def output_weights_kernel(*refs):
    pieces, refs = refs[:16], refs[16:]
    first, second, after, grad_down, grads, sems = refs

    @pl.when(pl.program_id(0) == 0)
    def _():
        copies = bring_pieces(pieces, pl.ds(0, grads.shape[1]), grads, sems)
        for copy in copies:
            copy.start()
        for copy in copies:
            copy.wait()

    acts = jnp.concatenate([first[...], second[...]], axis=0)
    grad_down[...] = transposed_product(acts, grads[...]).astype(jnp.bfloat16)


def output_weights(pieces, acts, after):
    rows, hidden = acts[0].shape
    width = pieces[0].shape[1]
    tile = 256
    column = pl.BlockSpec((rows, tile), lambda s: (0, s))
    return pl.pallas_call(
        output_weights_kernel,
        grid=(hidden // tile,),
        out_shape=jax.ShapeDtypeStruct((hidden, width), jnp.bfloat16),
        in_specs=[ANY] * 16 + [column, column, ANY],
        out_specs=pl.BlockSpec((tile, width), lambda s: (s, 0)),
        scratch_shapes=[
            pltpu.VMEM((2 * rows, width), jnp.bfloat16),
            pltpu.SemaphoreType.DMA((16,)),
        ],
        compiler_params=params(),
        cost_estimate=cost(4 * rows * width * hidden, 12 * 2**20),
        name="output_weights",
    )(*pieces, *acts, after)


def finish_kernel(experts, place, ids, counts, scores, own, far, near, middle, columns, d_scores):
    total = own.shape[0]
    half = total // 2
    width = columns.shape[1]
    total_sum = functools.reduce(
        jnp.add, [ref[...].astype(jnp.float32) for ref in (own, far, near, middle)]
    )
    swapped = jnp.concatenate([total_sum[half:], total_sum[:half]], axis=0)
    total_sum = jnp.where(place[0] == 0, total_sum, swapped)
    columns[...] = total_sum[:, :width].astype(jnp.bfloat16)
    table = total_sum[:, width:]
    lane = lanes_of(total)
    named_by = (lane % (2 * experts)) // 2
    gates, used, score_sum = gate_columns(counts[...], scores[...])
    d_gates = []
    for k in range(len(gates)):
        hit = (named_by == ids[:, k : k + 1]) & (lane < 4 * experts)
        d_gates.append(jnp.sum(jnp.where(hit, table, 0.0), axis=1, keepdims=True))
    mean = functools.reduce(jnp.add, [g * d for g, d in zip(gates, d_gates)])
    pick = lax.broadcasted_iota(jnp.int32, d_scores.shape, 1)
    result = jnp.zeros(d_scores.shape, jnp.float32)
    for k in range(len(gates)):
        result = jnp.where(pick == k, used[k] * (d_gates[k] - mean) / score_sum, result)
    d_scores[...] = result


def finish(place, ids, counts, scores, own, far, near, middle, experts):
    total, width = own.shape
    vmem = pl.BlockSpec(memory_space=pltpu.VMEM)
    return pl.pallas_call(
        functools.partial(finish_kernel, experts),
        out_shape=(
            jax.ShapeDtypeStruct((total, width - LANES), jnp.bfloat16),
            jax.ShapeDtypeStruct(scores.shape, jnp.float32),
        ),
        in_specs=[SCALARS] + [vmem] * 7,
        out_specs=(vmem, vmem),
        compiler_params=pltpu.CompilerParams(vmem_limit_bytes=VMEM_BYTES),
        name="finish",
    )(place, ids, counts, scores, own, far, near, middle)


class FourChips:
    def __init__(self):
        both = lambda pairs: [(2 * a + c, 2 * b + c) for a, b in pairs for c in (0, 1)]
        self.near = both([(z, z ^ 1) for z in range(4)])
        self.far = both([(z, z ^ 2) for z in range(4)])
        self.middle = both([(1, 2), (2, 1)])
        self.outward = both([(1, 0), (2, 3)])
        self.inward = both([(0, 1), (3, 2)])
        self.cores = [(i, i ^ 1) for i in range(8)]
        self.sides = [(0, 1), (1, 0)]

    def line(self, array, pairs):
        return lax.ppermute(array, "expert", pairs)

    def across(self, array):
        return lax.ppermute(array, "helper", self.sides)

    def dispatch(self, own, other):
        far = self.line(own, self.far)
        near = self.line(own, self.near)
        middle = self.line(own, self.middle)
        last = middle + self.line(far, self.outward)
        near_pieces = [own, other, near, self.across(near)]
        far_pieces = [far, self.across(far), last, self.across(last)]
        near_pieces = near_pieces + [self.line(p, self.cores) for p in near_pieces]
        far_pieces = far_pieces + [self.line(p, self.cores) for p in far_pieces]
        return near_pieces, far_pieces, far

    def two_slots(self, own, other):
        received = self.line(other, self.cores)
        sent = own[0] + received[0]
        arrived = self.across(sent)
        rows = sent.shape[0] // 4
        arrived = arrived.reshape(2, 2, rows, -1)[:, ::-1].reshape(4 * rows, -1)
        total = (
            own[1].astype(jnp.float32)
            + received[1].astype(jnp.float32)
            + arrived.astype(jnp.float32)
        ).astype(jnp.bfloat16)
        return total[: 2 * rows], total[2 * rows :], sent

    def combine(self, near_chunk, far_chunk):
        far_slot, last_slot, far_sent = self.two_slots(*far_chunk)
        own_slot, near_slot, near_sent = self.two_slots(*near_chunk)
        far_slot = far_slot + self.line(last_slot, self.inward)
        middle = self.line(last_slot, self.middle)
        far = self.line(far_slot, self.far)
        near = self.line(near_slot, self.near)
        return (own_slot, far, near, middle), near_sent


def lined_up(tokens, expert_ids, pick_counts, gate_scores, gate_local, up_local, down_local, grad_out):
    experts = lax.axis_size("expert")
    width = tokens.shape[1]
    plan = FourChips()
    side = lax.axis_index("helper")
    place = jnp.stack([side, lax.axis_index("expert")]).astype(jnp.int32)
    counts = pick_counts[:, None]
    own, other = prepare_rows(place, expert_ids, counts, gate_scores, tokens, experts)
    near_rows, far_rows, far_token = plan.dispatch(own, other)
    own, other = prepare_grads(place, grad_out, far_token)
    near_grads, far_grads, _ = plan.dispatch(own, other)

    near_gate, near_up, near_act, *near_out = forward(
        place, near_rows, gate_local, up_local, down_local, experts
    )
    far_gate, far_up, far_act, *far_out = forward(
        place, far_rows, gate_local, up_local, down_local, experts
    )
    out_sums, _ = plan.combine(near_out, far_out)

    far_d_gate, far_d_up, *far_in = backward(
        place, far_grads, far_rows, far_gate, far_up, gate_local, up_local, down_local, place, experts
    )
    near_d_gate, near_d_up, *near_in = backward(
        place, near_grads, near_rows, near_gate, near_up, gate_local, up_local, down_local, far_d_gate, experts
    )
    in_sums, sent = plan.combine(near_in, far_in)
    grad_down = output_weights(near_grads + far_grads, (near_act, far_act), near_d_gate)
    grad_gate, grad_up = input_weights(
        near_rows + far_rows, (near_d_gate, far_d_gate), (near_d_up, far_d_up), sent, width
    )

    total = functools.reduce(jnp.add, [s.astype(jnp.float32) for s in out_sums])
    half = total.shape[0] // 2
    swapped = jnp.concatenate([total[half:], total[:half]], axis=0)
    output_cols = jnp.where(side == 0, total, swapped).astype(jnp.bfloat16)
    input_cols, d_scores = finish(
        place, expert_ids, counts, gate_scores, *in_sums, experts
    )
    return output_cols, input_cols, d_scores, grad_gate[None], grad_up[None], grad_down[None]


def any_mesh(tokens, expert_ids, pick_counts, gate_scores, gate_local, up_local, down_local, grad_out):
    tok_rows = tokens.shape[0]
    pick_width = expert_ids.shape[1]
    experts = lax.axis_size("expert")
    active_mask = lax.broadcasted_iota(jnp.int32, (tok_rows, pick_width), 1) < pick_counts[:, None]
    active_float = active_mask.astype(jnp.float32)
    weighted = gate_scores * active_float
    score_sum = jnp.sum(weighted, axis=1, keepdims=True)
    gate_weights = weighted / score_sum
    picked = (expert_ids[:, :, None] == lax.broadcasted_iota(jnp.int32, (1, 1, experts), 2)).astype(
        jnp.float32
    )
    gate_table = jnp.sum(gate_weights[:, :, None] * picked, axis=1)

    def combine(partial):
        summed = lax.psum_scatter(partial, "expert", scatter_dimension=0, tiled=True)
        return lax.psum_scatter(summed, "helper", scatter_dimension=1, tiled=True)

    rows = lax.all_gather(tokens, "expert", tiled=True)
    tables = lax.all_gather(gate_table.T, "expert", tiled=False)
    gates = jnp.take(tables, lax.axis_index("expert"), axis=1).reshape(-1, 1)
    grads = lax.all_gather(grad_out, "expert", tiled=True)

    pre_gate = product(rows, gate_local)
    pre_up = product(rows, up_local)
    silu_value, silu_slope = silu_parts(pre_gate)
    hidden_act = silu_value * pre_up
    gated_act = (gates * hidden_act).astype(jnp.bfloat16)
    output_cols = combine(product(gated_act, down_local).astype(jnp.bfloat16))

    raw_act = right_transposed(grads, down_local)
    gate_part = jnp.sum(raw_act * hidden_act, axis=1)
    d_act = gates * raw_act
    d_pre_gate = (d_act * pre_up * silu_slope).astype(jnp.bfloat16)
    d_pre_up = (d_act * silu_value).astype(jnp.bfloat16)
    input_cols = combine(
        (right_transposed(d_pre_gate, gate_local) + right_transposed(d_pre_up, up_local)).astype(
            jnp.bfloat16
        )
    )

    gate_parts = lax.all_gather(
        gate_part.reshape(-1, tok_rows), ("expert", "helper"), tiled=False
    )
    own_parts = jnp.take(gate_parts, lax.axis_index("expert"), axis=1)
    by_expert = jnp.sum(own_parts.reshape(experts, -1, tok_rows), axis=1).T
    d_gates = jnp.sum(by_expert[:, None, :] * picked, axis=2)
    d_scores = (
        active_float
        * (d_gates - jnp.sum(gate_weights * d_gates, axis=1, keepdims=True))
        / score_sum
    )

    def over_dp(whole, dimension):
        return lax.psum_scatter(
            whole.astype(jnp.bfloat16), "dp", scatter_dimension=dimension, tiled=True
        )[None]

    grad_w_gate = over_dp(transposed_product(rows, d_pre_gate), 0)
    grad_w_up = over_dp(transposed_product(rows, d_pre_up), 0)
    grad_w_down = over_dp(transposed_product(gated_act, grads), 1)
    return output_cols, input_cols, d_scores, grad_w_gate, grad_w_up, grad_w_down


def on_device(tokens, expert_ids, pick_counts, gate_scores, w_gate, w_up, w_down, grad_out):
    sizes = tuple(lax.axis_size(axis) for axis in ("expert", "helper", "dp"))
    layer = lined_up if sizes == (8, 2, 1) else any_mesh
    return layer(
        tokens, expert_ids, pick_counts, gate_scores, w_gate[0], w_up[0], w_down[0], grad_out
    )


def solution(mesh):
    in_specs = (
        P(("groups", "expert", "dp"), None),
        P(("groups", "expert", "dp"), None),
        P(("groups", "expert", "dp")),
        P(("groups", "expert", "dp"), None),
        P("expert", None, "helper"),
        P("expert", None, "helper"),
        P("expert", "helper", None),
        P(("groups", "expert", "dp"), None),
    )
    out_specs = (
        P(("groups", "expert", "dp"), "helper"),
        P(("groups", "expert", "dp"), "helper"),
        P(("groups", "expert", "dp"), None),
        P(("groups", "expert"), "dp", "helper"),
        P(("groups", "expert"), "dp", "helper"),
        P(("groups", "expert"), "helper", "dp"),
    )
    return jax.shard_map(
        on_device, mesh=mesh, in_specs=in_specs, out_specs=out_specs, check_vma=False
    )
```

time: 278 us -> 226 us (0.81)
  Pallas kernels: 0 us -> 93.9 us
  matrix products: 55 us -> 0 us
  blocking collectives: 46.4 us -> 0 us
  waiting for transfers between devices: 89.8 us -> 56.2 us
  local copies, waits for them, and re-layouts: 22.2 us -> 15.4 us
  other arithmetic: 17 us -> 13.8 us
    pallas_call x0 -> x9, Pallas kernels: none -> 93.9 us  [the longest x2 32.7 us: backward(): pl.pallas_call(functools.partial(backward_kernel, tiles, experts), grid=(...]
    dot_general x9 -> x0, matrix products: 55 us -> none  [the longest x3 20.3 us: right_transposed(): lax.dot_general(first_mat, second_mat, (((1,), (1,)), ((), ())), preferre...]
    all_gather x2 -> x0, blocking collectives: 46.4 us -> none  [the longest x1 32.2 us: on_device(): lax.all_gather(plan.unorder(gate_part), ('expert', 'helper'), tiled=False)]
    ppermute x34 -> x46, waiting for transfers between devices: 89.8 us -> 56.2 us  [the longest x36 47.3 us: line(): return lax.ppermute(array, 'expert', pairs)]
    add x2 -> x9, other arithmetic: 0.4 us -> 7.1 us  [the longest x4 4.93 us: two_slots(): sent = own[0] + received[0]]
    unnamed x44 -> x79, local copies, waits for them, and re-layouts: 13.6 us -> 7.75 us
    unnamed x4 -> x0, other arithmetic: 4.91 us -> none
    convert_element_type x9 -> x5, other arithmetic: 10.1 us -> 6.06 us  [the longest x4 5.28 us: two_slots(): total = (own[1].astype(jnp.float32) + received[1].astype(jnp.float32) + a...]
  transfers between devices with their start and end apart: 34 -> 46, of which waited for: 17 -> 11; matrix products, arithmetic and copies ran while one was open for 22% -> 9% of each run, Pallas kernels for 0% -> 39%
where the time goes in v1:
time: 226 us; the launch traced here: 224 us
  Pallas kernels  93.9 us (42%)
  waiting for transfers between devices  56.2 us (25%)
  starting transfers between devices  43.9 us (19%)
  local copies, waits for them, and re-layouts  15.4 us (7%)
  other arithmetic  13.8 us (6%)
    ppermute x36, waiting for transfers between devices, line(): return lax.ppermute(array, 'expert', pairs)  47.3 us
    ppermute x36, starting transfers between devices, line(): return lax.ppermute(array, 'expert', pairs)  33.4 us
    pallas_call x2, Pallas kernels, backward(): pl.pallas_call(functools.partial(backward_kernel, tiles, experts), grid=(...  32.7 us
    pallas_call x2, Pallas kernels, forward(): pl.pallas_call(functools.partial(forward_kernel, tiles, experts), grid=(t...  28.9 us
    pallas_call x1, Pallas kernels, input_weights(): pl.pallas_call(input_weights_kernel, grid=(width // tile,), out_shape=(gr...  15 us
    ppermute x10, starting transfers between devices, across(): return lax.ppermute(array, 'helper', self.sides)  10.5 us
    pallas_call x1, Pallas kernels, output_weights(): pl.pallas_call(output_weights_kernel, grid=(hidden // tile,), out_shape=j...  9.74 us
    ppermute x10, waiting for transfers between devices, across(): return lax.ppermute(array, 'helper', self.sides)  8.93 us
  transfers between devices with their start and end apart: 46, of which 11 were waited for; matrix products, arithmetic and copies ran while one was open for 9% of the time, Pallas kernels for 39%

profile of v1, /device:TPU:0, one launch (start us, length us, event | category | flops | bytes accessed | tf_op | source)
XLA Modules:
  0.0 224.5 jit_solution(1485066947050025569)
XLA Ops:
  0.6 1.4 copy.14.ids
  2.0 1.4 copy.15.counts
  3.4 1.4 copy.16.scores
  5.5 2.5 %prepare_rows.1 = (bf16[64,2176]{1,0:T(8,128)(2,1)}, bf16[64,2176]{1,0:T(8,128)(2,1)}) custom-call(s32[2]{0:T(128)} %pad_add_fusion.place.refs_21_, s32[128,4]{1,0:T(8,128)} %copy.14.ids, s32[128,1]{1,0:T(8,128)} %copy.15.counts, f32[128,4]{1,0:T(8,128)} %copy.16.scores, bf16[128,2048]{1,0:T(8,128)(2,1)} %rows.2), custom_call_target="tpu_custom_call" | custom-call | tf_op jit(solution)/shard_map/prepare_rows/pallas_call | solution.py:90
  8.0 4.0 %collective-permute-start.8 = (bf16[64,2176]{1,0:T(8,128)(2,1)}, bf16[64,2176]{1,0:T(8,128)(2,1)S(1)}, u32[]{:S(2)}, u32[]{:S(2)}) collective-permute-start(bf16[64,2176]{1,0:T(8,128)(2,1)} %get-tuple-element.32.refs_0_.refs_8_), channel_id=1, source_target_pairs={{0,8},{2,10},{4,12},{6,14},{8,0},{10,2},{12,4},{14,6},{1,9},{3,11}... | collective-permute-start | bytes 835592 | tf_op jit(solution)/shard_map/ppermute | solution.py:470
  12.7 2.9 %collective-permute-start = (bf16[64,2176]{1,0:T(8,128)(2,1)}, bf16[64,2176]{1,0:T(8,128)(2,1)S(1)}, u32[]{:S(2)}, u32[]{:S(2)}) collective-permute-start(bf16[64,2176]{1,0:T(8,128)(2,1)} %get-tuple-element.32.refs_0_.refs_8_), channel_id=1, source_target_pairs={{0,4},{2,6},{4,0},{6,2},{8,12},{10,14},{12,8},{14,10},{1,5},{3,7},... | collective-permute-start | bytes 835592 | tf_op jit(solution)/shard_map/ppermute | solution.py:470
  15.6 10.1 %collective-permute-done.8.refs_0_.after.refs_8_ = bf16[64,2176]{1,0:T(8,128)(2,1)S(1)} collective-permute-done((bf16[64,2176]{1,0:T(8,128)(2,1)}, bf16[64,2176]{1,0:T(8,128)(2,1)S(1)}, u32[]{:S(2)}, u32[]{:S(2)}) %collective-permute-start.8) | collective-permute-done | bytes 278560 | tf_op jit(solution)/shard_map/ppermute | solution.py:470
  25.8 1.3 collective-permute-start.11
  27.1 1.9 prepare_grads.1
  29.0 4.0 %collective-permute-start.29 = (bf16[64,2048]{1,0:T(8,128)(2,1)}, bf16[64,2048]{1,0:T(8,128)(2,1)}, u32[]{:S(2)}, u32[]{:S(2)}) collective-permute-start(bf16[64,2048]{1,0:T(8,128)(2,1)} %get-tuple-element.38.refs_0_), channel_id=1, source_target_pairs={{0,8},{2,10},{4,12},{6,14},{8,0},{10,2},{12,4},{14,6},{1,9},{3,11}... | collective-permute-start | bytes 786440 | tf_op jit(solution)/shard_map/ppermute | solution.py:470
  33.0 1.6 collective-permute-start.1
  34.6 9.8 %collective-permute-done.29.refs_0_.refs_8_ = bf16[64,2048]{1,0:T(8,128)(2,1)} collective-permute-done((bf16[64,2048]{1,0:T(8,128)(2,1)}, bf16[64,2048]{1,0:T(8,128)(2,1)}, u32[]{:S(2)}, u32[]{:S(2)}) %collective-permute-start.29) | collective-permute-done | bytes 262176 | tf_op jit(solution)/shard_map/ppermute | solution.py:470
  45.1 1.3 collective-permute-start.32
  46.5 1.3 collective-permute-start.9
  49.4 5.9 %collective-permute-done.32 = bf16[64,2048]{1,0:T(8,128)(2,1)S(1)} collective-permute-done((bf16[64,2048]{1,0:T(8,128)(2,1)}, bf16[64,2048]{1,0:T(8,128)(2,1)S(1)}, u32[]{:S(2)}, u32[]{:S(2)}) %collective-permute-start.32) | collective-permute-done | bytes 262176 | tf_op jit(solution)/shard_map/ppermute | solution.py:470
  56.4 1.3 collective-permute-start.30
  58.2 4.2 %collective-permute-done.12.refs_3_.refs_11_ = bf16[64,2176]{1,0:T(8,128)(2,1)} collective-permute-done((bf16[64,2176]{1,0:T(8,128)(2,1)S(1)}, bf16[64,2176]{1,0:T(8,128)(2,1)}, u32[]{:S(2)}, u32[]{:S(2)}) %collective-permute-start.12) | collective-permute-done | bytes 278560 | tf_op jit(solution)/shard_map/ppermute | solution.py:473
  62.4 1.3 collective-permute-start.33
  64.3 14.4 %forward.2 = (f32[512,1024]{1,0:T(8,128)}, f32[512,1024]{1,0:T(8,128)}, bf16[512,1024]{1,0:T(8,128)(2,1)}, bf16[2,256,1024]{2,1,0:T(8,128)(2,1)}, bf16[2,256,1024]{2,1,0:T(8,128)(2,1)}) custom-call(s32[2]{0:T(128)} %pad_add_fusion.place.refs_21_, bf16[64,2176]{1,0:T(8,128)(2,1)} %get-tuple-element.32.refs_0_.refs_8_, ...), custom_call_target="tpu_custom_call" | custom-call | flops 6442450944 | bytes 16777216 | tf_op jit(solution)/shard_map/forward/pallas_call | solution.py:198
  81.0 14.4 %forward.3 = (f32[512,1024]{1,0:T(8,128)}, f32[512,1024]{1,0:T(8,128)}, bf16[512,1024]{1,0:T(8,128)(2,1)}, bf16[2,256,1024]{2,1,0:T(8,128)(2,1)}, bf16[2,256,1024]{2,1,0:T(8,128)(2,1)}) custom-call(s32[2]{0:T(128)} %pad_add_fusion.place.refs_21_, bf16[64,2176]{1,0:T(8,128)(2,1)} %copy-done.10, bf16[64,2176]{1,0:T(8,128)(2,1)} %collective-permute-done.9.refs_1_.refs_9_, ...), custom_call_target="tpu_custom_call" | custom-call | flops 6442450944 | bytes 16777216 | tf_op jit(solution)/shard_map/forward/pallas_call | solution.py:198
  97.4 16.3 %backward.2 = (bf16[512,1024]{1,0:T(8,128)(2,1)}, bf16[512,1024]{1,0:T(8,128)(2,1)}, bf16[2,256,1152]{2,1,0:T(8,128)(2,1)}, bf16[2,256,1152]{2,1,0:T(8,128)(2,1)}) custom-call(s32[2]{0:T(128)} %pad_add_fusion.place.refs_21_, bf16[64,2048]{1,0:T(8,128)(2,1)} %collective-permute-done.29.refs_0_.refs_8_, bf16[64,2048]{1,0:T(8,128)(2,1)} %copy-done.27, ...), custom_call_target="tpu_custom_call" | custom-call | flops 6442450944 | bytes 20971520 | tf_op jit(solution)/shard_map/backward/pallas_call | solution.py:306
  114.9 16.5 %backward.3 = (bf16[512,1024]{1,0:T(8,128)(2,1)}, bf16[512,1024]{1,0:T(8,128)(2,1)}, bf16[2,256,1152]{2,1,0:T(8,128)(2,1)}, bf16[2,256,1152]{2,1,0:T(8,128)(2,1)}) custom-call(s32[2]{0:T(128)} %pad_add_fusion.place.refs_21_, bf16[64,2048]{1,0:T(8,128)(2,1)} %get-tuple-element.38.refs_0_, bf16[64,2048]{1,0:T(8,128)(2,1)} %get-tuple-element.39.refs_1_, ...), custom_call_target="tpu_custom_call" | custom-call | flops 6442450944 | bytes 20971520 | tf_op jit(solution)/shard_map/backward/pallas_call | solution.py:306
  132.0 1.3 collective-permute-start.7
  133.4 9.7 %output_weights.1 = bf16[1024,2048]{1,0:T(8,128)(2,1)} custom-call(bf16[64,2048]{1,0:T(8,128)(2,1)} %get-tuple-element.38.refs_0_, bf16[64,2048]{1,0:T(8,128)(2,1)} %get-tuple-element.39.refs_1_, bf16[64,2048]{1,0:T(8,128)(2,1)} %collective-permute-done.23.refs_2_, bf16[64,2048]{1,0:T(8,128)(2,1)} %copy-done.30, bf16[64,2048]{1,0:T(8,128)(2,1)} %copy-done.34, ...), custom_call_target="tpu_custom_call" | custom-call | flops 4294967296 | bytes 12582912 | tf_op jit(solution)/shard_map/output_weights/pallas_call | solution.py:400
  144.9 1.4 collective-permute-done.7
  146.3 1.4 fusion.3
  148.5 2.4 %collective-permute-start.21 = (bf16[128,1024]{1,0:T(8,128)(2,1)}, bf16[128,1024]{1,0:T(8,128)(2,1)}, u32[]{:S(2)}, u32[]{:S(2)}) collective-permute-start(bf16[128,1024]{1,0:T(8,128)(2,1)} %slice.111), channel_id=1, source_target_pairs={{0,4},{2,6},{4,0},{6,2},{8,12},{10,14},{12,8},{14,10},{1,5},{3,7},... | collective-permute-start | bytes 786440 | tf_op jit(solution)/shard_map/ppermute | solution.py:470
  150.9 2.0 fusion.5.refs_20_
  153.9 2.0 fusion.4
  156.8 2.4 %collective-permute-done.18 = bf16[256,1024]{1,0:T(8,128)(2,1)} collective-permute-done((bf16[256,1024]{1,0:T(8,128)(2,1)}, bf16[256,1024]{1,0:T(8,128)(2,1)}, u32[]{:S(2)}, u32[]{:S(2)}) %collective-permute-start.18) | collective-permute-done | bytes 524320 | tf_op jit(solution)/shard_map/ppermute | solution.py:473
  159.2 1.1 rev.13
  160.3 1.3 fusion.2
  162.3 4.1 %collective-permute-start.19 = (bf16[128,1024]{1,0:T(8,128)(2,1)}, bf16[128,1024]{1,0:T(8,128)(2,1)S(1)}, u32[]{:S(2)}, u32[]{:S(2)}) collective-permute-start(bf16[128,1024]{1,0:T(8,128)(2,1)} %slice.110), channel_id=1, source_target_pairs={{0,4},{2,6},{12,8},{14,10},{1,5},{3,7},{13,9},{15,11},{16,20},{18,... | collective-permute-start | bytes 786440 | tf_op jit(solution)/shard_map/ppermute | solution.py:470
  166.4 15.0 %input_weights.1 = (bf16[2048,1024]{1,0:T(8,128)(2,1)}, bf16[2048,1024]{1,0:T(8,128)(2,1)}) custom-call(bf16[64,2176]{1,0:T(8,128)(2,1)} %get-tuple-element.32.refs_0_.refs_8_, bf16[64,2176]{1,0:T(8,128)(2,1)} %get-tuple-element.33.refs_1_.refs_9_, bf16[64,2176]{1,0:T(8,128)(2,1)} %copy-done.15, bf16[64,2176]{1,0:T(8,128)(2,1)} %copy-done.18, ...), custom_call_target="tpu_custom_call" | custom-call | flops 8589934592 | bytes 16777216 | tf_op jit(solution)/shard_map/input_weights/pallas_call | solution.py:364
  181.5 1.4 collective-permute-start.22
  183.6 1.4 collective-permute-start.20
  185.0 1.1 rev.15
  186.1 1.3 fusion
  188.1 2.7 %collective-permute-start.42 = (bf16[128,1152]{1,0:T(8,128)(2,1)}, bf16[128,1152]{1,0:T(8,128)(2,1)S(1)}, u32[]{:S(2)}, u32[]{:S(2)}) collective-permute-start(bf16[128,1152]{1,0:T(8,128)(2,1)} %slice.120), channel_id=1, source_target_pairs={{0,4},{2,6},{12,8},{14,10},{1,5},{3,7},{13,9},{15,11},{16,20},{18,... | collective-permute-start | bytes 884744 | tf_op jit(solution)/shard_map/ppermute | solution.py:470
  191.6 1.1 rev.14
  192.7 1.3 fusion.1
  194.7 1.9 collective-permute-start.44
  196.6 6.0 %collective-permute-done.20 = bf16[128,1024]{1,0:T(8,128)(2,1)} collective-permute-done((bf16[128,1024]{1,0:T(8,128)(2,1)}, bf16[128,1024]{1,0:T(8,128)(2,1)}, u32[]{:S(2)}, u32[]{:S(2)}) %collective-permute-start.20) | collective-permute-done | bytes 262176 | tf_op jit(solution)/shard_map/ppermute | solution.py:470
  202.6 1.3 convert_add_fusion.4
  204.8 1.8 collective-permute-done.44.near
  206.7 12.5 %collective-permute-done.43.far = bf16[128,1152]{1,0:T(8,128)(2,1)S(1)} collective-permute-done((bf16[128,1152]{1,0:T(8,128)(2,1)S(1)}, bf16[128,1152]{1,0:T(8,128)(2,1)S(1)}, u32[]{:S(2)}, u32[]{:S(2)}) %collective-permute-start.43) | collective-permute-done | bytes 294944 | tf_op jit(solution)/shard_map/ppermute | solution.py:470
  219.9 3.1 %finish.1 = (bf16[128,1024]{1,0:T(8,128)(2,1)}, f32[128,4]{1,0:T(8,128)}) custom-call(s32[2]{0:T(128)} %pad_add_fusion.place.refs_21_, s32[128,4]{1,0:T(8,128)} %copy.14.ids, s32[128,1]{1,0:T(8,128)} %copy.15.counts, f32[128,4]{1,0:T(8,128)} %copy.16.scores, bf16[128,1152]{1,0:T(8,128)(2,1)} %get-tuple-element.65.own, bf16[128,1152]{1,0:T(8,128)(2,1)} %copy-done.9, ...), custom_call_target="tpu_custom_call" | custom-call | tf_op jit(solution)/shard_map/finish/pallas_call | solution.py:445
  223.0 1.5 copy.20
  (157 shorter events, 21.6 us)
Async XLA Ops:
  8.0 17.7 %collective-permute-start.8 = (bf16[64,2176]{1,0:T(8,128)(2,1)}, bf16[64,2176]{1,0:T(8,128)(2,1)S(1)}, u32[]{:S(2)}, u32[]{:S(2)}) collective-permute-start(bf16[64,2176]{1,0:T(8,128)(2,1)} %get-tuple-element.32.refs_0_.refs_8_), channel_id=1, source_target_pairs={{0,8},{2,10},{4,12},{6,14},{8,0},{10,2},{12,4},{14,6},{1,9},{3,11}... | collective-permute-start | bytes 835592 | tf_op jit(solution)/shard_map/ppermute | solution.py:470
  12.1 20.9 %collective-permute-start.10 = (bf16[64,2176]{1,0:T(8,128)(2,1)}, bf16[64,2176]{1,0:T(8,128)(2,1)S(1)}, u32[]{:S(2)}, u32[]{:S(2)}) collective-permute-start(bf16[64,2176]{1,0:T(8,128)(2,1)} %get-tuple-element.32.refs_0_.refs_8_), channel_id=1, source_target_pairs={{4,8},{6,10},{8,4},{10,6},{5,9},{7,11},{9,5},{11,7},{20,24},{22,26... | collective-permute-start | bytes 835592 | tf_op jit(solution)/shard_map/ppermute | solution.py:470
  12.7 20.2 %collective-permute-start = (bf16[64,2176]{1,0:T(8,128)(2,1)}, bf16[64,2176]{1,0:T(8,128)(2,1)S(1)}, u32[]{:S(2)}, u32[]{:S(2)}) collective-permute-start(bf16[64,2176]{1,0:T(8,128)(2,1)} %get-tuple-element.32.refs_0_.refs_8_), channel_id=1, source_target_pairs={{0,4},{2,6},{4,0},{6,2},{8,12},{10,14},{12,8},{14,10},{1,5},{3,7},... | collective-permute-start | bytes 835592 | tf_op jit(solution)/shard_map/ppermute | solution.py:470
  15.6 18.9 %collective-permute-start.2 = (bf16[64,2176]{1,0:T(8,128)(2,1)}, bf16[64,2176]{1,0:T(8,128)(2,1)S(1)}, u32[]{:S(2)}, u32[]{:S(2)}) collective-permute-start(bf16[64,2176]{1,0:T(8,128)(2,1)} %get-tuple-element.32.refs_0_.refs_8_), channel_id=1, source_target_pairs={{0,2},{2,0},{4,6},{6,4},{8,10},{10,8},{12,14},{14,12},{1,3},{3,1},... | collective-permute-start | bytes 835592 | tf_op jit(solution)/shard_map/ppermute | solution.py:470
  25.8 19.3 %collective-permute-start.11 = (bf16[64,2176]{1,0:T(8,128)(2,1)S(1)}, bf16[64,2176]{1,0:T(8,128)(2,1)S(1)}, u32[]{:S(2)}, u32[]{:S(2)}) collective-permute-start(bf16[64,2176]{1,0:T(8,128)(2,1)S(1)} %collective-permute-done.8.refs_0_.after.refs_8_), channel_id=1, source_target_pairs={{4,0},{6,2},{8,12},{10,14},{5,1},{7,3},{9,13},{11,15},{20,16},{22,... | collective-permute-start | bytes 835592 | tf_op jit(solution)/shard_map/ppermute | solution.py:470
  29.0 15.4 %collective-permute-start.29 = (bf16[64,2048]{1,0:T(8,128)(2,1)}, bf16[64,2048]{1,0:T(8,128)(2,1)}, u32[]{:S(2)}, u32[]{:S(2)}) collective-permute-start(bf16[64,2048]{1,0:T(8,128)(2,1)} %get-tuple-element.38.refs_0_), channel_id=1, source_target_pairs={{0,8},{2,10},{4,12},{6,14},{8,0},{10,2},{12,4},{14,6},{1,9},{3,11}... | collective-permute-start | bytes 786440 | tf_op jit(solution)/shard_map/ppermute | solution.py:470
  33.0 13.5 %collective-permute-start.3 = (bf16[64,2176]{1,0:T(8,128)(2,1)}, bf16[64,2176]{1,0:T(8,128)(2,1)S(1)}, u32[]{:S(2)}, u32[]{:S(2)}) collective-permute-start(bf16[64,2176]{1,0:T(8,128)(2,1)} %get-tuple-element.33.refs_1_.refs_9_), channel_id=1, source_target_pairs={{0,2},{2,0},{4,6},{6,4},{8,10},{10,8},{12,14},{14,12},{1,3},{3,1},... | collective-permute-start | bytes 835592 | tf_op jit(solution)/shard_map/ppermute | solution.py:470
  33.0 30.7 %copy-start.15 = (bf16[64,2176]{1,0:T(8,128)(2,1)}, bf16[64,2176]{1,0:T(8,128)(2,1)S(1)}, u32[]{:S(2)}) copy-start(bf16[64,2176]{1,0:T(8,128)(2,1)S(1)} %collective-permute-done.refs_2_.refs_10_) | copy-start | bytes 835588
  33.0 16.3 %collective-permute-start.1 = (bf16[64,2176]{1,0:T(8,128)(2,1)S(1)}, bf16[64,2176]{1,0:T(8,128)(2,1)S(1)}, u32[]{:S(2)}, u32[]{:S(2)}) collective-permute-start(bf16[64,2176]{1,0:T(8,128)(2,1)S(1)} %collective-permute-done.refs_2_.refs_10_), channel_id=1, source_target_pairs={{0,1},{1,0},{2,3},{3,2},{4,5},{5,4},{6,7},{7,6},{8,9},{9,8},{10,11... | collective-permute-start | bytes 835592 | tf_op jit(solution)/shard_map/ppermute | solution.py:473
  34.6 14.2 %collective-permute-start.23 = (bf16[64,2048]{1,0:T(8,128)(2,1)}, bf16[64,2048]{1,0:T(8,128)(2,1)}, u32[]{:S(2)}, u32[]{:S(2)}) collective-permute-start(bf16[64,2048]{1,0:T(8,128)(2,1)} %get-tuple-element.38.refs_0_), channel_id=1, source_target_pairs={{0,4},{2,6},{4,0},{6,2},{8,12},{10,14},{12,8},{14,10},{1,5},{3,7},... | collective-permute-start | bytes 786440 | tf_op jit(solution)/shard_map/ppermute | solution.py:470
  44.4 4.4 %collective-permute-start.31 = (bf16[64,2048]{1,0:T(8,128)(2,1)}, bf16[64,2048]{1,0:T(8,128)(2,1)S(1)}, u32[]{:S(2)}, u32[]{:S(2)}) collective-permute-start(bf16[64,2048]{1,0:T(8,128)(2,1)} %get-tuple-element.38.refs_0_), channel_id=1, source_target_pairs={{4,8},{6,10},{8,4},{10,6},{5,9},{7,11},{9,5},{11,7},{20,24},{22,26... | collective-permute-start | bytes 786440 | tf_op jit(solution)/shard_map/ppermute | solution.py:470
  45.1 10.3 %collective-permute-start.32 = (bf16[64,2048]{1,0:T(8,128)(2,1)}, bf16[64,2048]{1,0:T(8,128)(2,1)S(1)}, u32[]{:S(2)}, u32[]{:S(2)}) collective-permute-start(bf16[64,2048]{1,0:T(8,128)(2,1)} %collective-permute-done.29.refs_0_.refs_8_), channel_id=1, source_target_pairs={{4,0},{6,2},{8,12},{10,14},{5,1},{7,3},{9,13},{11,15},{20,16},{22,... | collective-permute-start | bytes 786440 | tf_op jit(solution)/shard_map/ppermute | solution.py:470
  46.4 32.3 %copy-start.11 = (bf16[64,2176]{1,0:T(8,128)(2,1)}, bf16[64,2176]{1,0:T(8,128)(2,1)S(1)}, u32[]{:S(2)}) copy-start(bf16[64,2176]{1,0:T(8,128)(2,1)S(1)} %add.85.refs_2_.refs_10_) | copy-start | bytes 835588
  46.5 9.9 %collective-permute-start.9 = (bf16[64,2176]{1,0:T(8,128)(2,1)}, bf16[64,2176]{1,0:T(8,128)(2,1)}, u32[]{:S(2)}, u32[]{:S(2)}) collective-permute-start(bf16[64,2176]{1,0:T(8,128)(2,1)} %copy-done.10), channel_id=1, source_target_pairs={{0,1},{1,0},{2,3},{3,2},{4,5},{5,4},{6,7},{7,6},{8,9},{9,8},{10,11... | collective-permute-start | bytes 835592 | tf_op jit(solution)/shard_map/ppermute | solution.py:473
  48.8 8.9 %collective-permute-start.13 = (bf16[64,2176]{1,0:T(8,128)(2,1)}, bf16[64,2176]{1,0:T(8,128)(2,1)S(1)}, u32[]{:S(2)}, u32[]{:S(2)}) collective-permute-start(bf16[64,2176]{1,0:T(8,128)(2,1)} %copy-done.10), channel_id=1, source_target_pairs={{0,2},{2,0},{4,6},{6,4},{8,10},{10,8},{12,14},{14,12},{1,3},{3,1},... | collective-permute-start | bytes 835592 | tf_op jit(solution)/shard_map/ppermute | solution.py:470
  48.8 8.9 %collective-permute-start.4 = (bf16[64,2176]{1,0:T(8,128)(2,1)S(1)}, bf16[64,2176]{1,0:T(8,128)(2,1)S(1)}, u32[]{:S(2)}, u32[]{:S(2)}) collective-permute-start(bf16[64,2176]{1,0:T(8,128)(2,1)S(1)} %collective-permute-done.refs_2_.refs_10_), channel_id=1, source_target_pairs={{0,2},{2,0},{4,6},{6,4},{8,10},{10,8},{12,14},{14,12},{1,3},{3,1},... | collective-permute-start | bytes 835592 | tf_op jit(solution)/shard_map/ppermute | solution.py:470
  49.3 13.1 %collective-permute-start.12 = (bf16[64,2176]{1,0:T(8,128)(2,1)S(1)}, bf16[64,2176]{1,0:T(8,128)(2,1)}, u32[]{:S(2)}, u32[]{:S(2)}) collective-permute-start(bf16[64,2176]{1,0:T(8,128)(2,1)S(1)} %add.85.refs_2_.refs_10_), channel_id=1, source_target_pairs={{0,1},{1,0},{2,3},{3,2},{4,5},{5,4},{6,7},{7,6},{8,9},{9,8},{10,11... | collective-permute-start | bytes 835592 | tf_op jit(solution)/shard_map/ppermute | solution.py:473
  55.3 8.3 %collective-permute-start.5 = (bf16[64,2176]{1,0:T(8,128)(2,1)S(1)}, bf16[64,2176]{1,0:T(8,128)(2,1)S(1)}, u32[]{:S(2)}, u32[]{:S(2)}) collective-permute-start(bf16[64,2176]{1,0:T(8,128)(2,1)S(1)} %collective-permute-done.1.refs_3_.refs_11_), channel_id=1, source_target_pairs={{0,2},{2,0},{4,6},{6,4},{8,10},{10,8},{12,14},{14,12},{1,3},{3,1},... | collective-permute-start | bytes 835592 | tf_op jit(solution)/shard_map/ppermute | solution.py:470
  56.4 22.4 %collective-permute-start.30 = (bf16[64,2048]{1,0:T(8,128)(2,1)}, bf16[64,2048]{1,0:T(8,128)(2,1)S(1)}, u32[]{:S(2)}, u32[]{:S(2)}) collective-permute-start(bf16[64,2048]{1,0:T(8,128)(2,1)} %collective-permute-done.29.refs_0_.refs_8_), channel_id=1, source_target_pairs={{0,1},{1,0},{2,3},{3,2},{4,5},{5,4},{6,7},{7,6},{8,9},{9,8},{10,11... | collective-permute-start | bytes 786440 | tf_op jit(solution)/shard_map/ppermute | solution.py:473
  57.7 22.1 %collective-permute-start.15 = (bf16[64,2176]{1,0:T(8,128)(2,1)S(1)}, bf16[64,2176]{1,0:T(8,128)(2,1)S(1)}, u32[]{:S(2)}, u32[]{:S(2)}) collective-permute-start(bf16[64,2176]{1,0:T(8,128)(2,1)S(1)} %add.85.refs_2_.refs_10_), channel_id=1, source_target_pairs={{0,2},{2,0},{4,6},{6,4},{8,10},{10,8},{12,14},{14,12},{1,3},{3,1},... | collective-permute-start | bytes 835592 | tf_op jit(solution)/shard_map/ppermute | solution.py:470
  57.7 21.2 %collective-permute-start.14 = (bf16[64,2176]{1,0:T(8,128)(2,1)}, bf16[64,2176]{1,0:T(8,128)(2,1)S(1)}, u32[]{:S(2)}, u32[]{:S(2)}) collective-permute-start(bf16[64,2176]{1,0:T(8,128)(2,1)} %collective-permute-done.9.refs_1_.refs_9_), channel_id=1, source_target_pairs={{0,2},{2,0},{4,6},{6,4},{8,10},{10,8},{12,14},{14,12},{1,3},{3,1},... | collective-permute-start | bytes 835592 | tf_op jit(solution)/shard_map/ppermute | solution.py:470
  62.4 17.6 %collective-permute-start.33 = (bf16[64,2048]{1,0:T(8,128)(2,1)S(1)}, bf16[64,2048]{1,0:T(8,128)(2,1)S(1)}, u32[]{:S(2)}, u32[]{:S(2)}) collective-permute-start(bf16[64,2048]{1,0:T(8,128)(2,1)S(1)} %add.95.refs_2_.refs_10_), channel_id=1, source_target_pairs={{0,1},{1,0},{2,3},{3,2},{4,5},{5,4},{6,7},{7,6},{8,9},{9,8},{10,11... | collective-permute-start | bytes 786440 | tf_op jit(solution)/shard_map/ppermute | solution.py:473
  63.6 16.7 %collective-permute-start.16 = (bf16[64,2176]{1,0:T(8,128)(2,1)}, bf16[64,2176]{1,0:T(8,128)(2,1)S(1)}, u32[]{:S(2)}, u32[]{:S(2)}) collective-permute-start(bf16[64,2176]{1,0:T(8,128)(2,1)} %collective-permute-done.12.refs_3_.refs_11_), channel_id=1, source_target_pairs={{0,2},{2,0},{4,6},{6,4},{8,10},{10,8},{12,14},{14,12},{1,3},{3,1},... | collective-permute-start | bytes 835592 | tf_op jit(solution)/shard_map/ppermute | solution.py:470
  78.8 16.9 %collective-permute-start.34 = (bf16[64,2048]{1,0:T(8,128)(2,1)}, bf16[64,2048]{1,0:T(8,128)(2,1)S(1)}, u32[]{:S(2)}, u32[]{:S(2)}) collective-permute-start(bf16[64,2048]{1,0:T(8,128)(2,1)} %collective-permute-done.29.refs_0_.refs_8_), channel_id=1, source_target_pairs={{0,2},{2,0},{4,6},{6,4},{8,10},{10,8},{12,14},{14,12},{1,3},{3,1},... | collective-permute-start | bytes 786440 | tf_op jit(solution)/shard_map/ppermute | solution.py:470
  78.9 16.6 %collective-permute-start.24 = (bf16[64,2048]{1,0:T(8,128)(2,1)}, bf16[64,2048]{1,0:T(8,128)(2,1)S(1)}, u32[]{:S(2)}, u32[]{:S(2)}) collective-permute-start(bf16[64,2048]{1,0:T(8,128)(2,1)} %collective-permute-done.23.refs_2_), channel_id=1, source_target_pairs={{0,1},{1,0},{2,3},{3,2},{4,5},{5,4},{6,7},{7,6},{8,9},{9,8},{10,11... | collective-permute-start | bytes 786440 | tf_op jit(solution)/shard_map/ppermute | solution.py:473
  79.8 16.6 %collective-permute-start.36 = (bf16[64,2048]{1,0:T(8,128)(2,1)S(1)}, bf16[64,2048]{1,0:T(8,128)(2,1)S(1)}, u32[]{:S(2)}, u32[]{:S(2)}) collective-permute-start(bf16[64,2048]{1,0:T(8,128)(2,1)S(1)} %add.95.refs_2_.refs_10_), channel_id=1, source_target_pairs={{0,2},{2,0},{4,6},{6,4},{8,10},{10,8},{12,14},{14,12},{1,3},{3,1},... | collective-permute-start | bytes 786440 | tf_op jit(solution)/shard_map/ppermute | solution.py:470
  80.0 16.2 %collective-permute-start.35 = (bf16[64,2048]{1,0:T(8,128)(2,1)S(1)}, bf16[64,2048]{1,0:T(8,128)(2,1)S(1)}, u32[]{:S(2)}, u32[]{:S(2)}) collective-permute-start(bf16[64,2048]{1,0:T(8,128)(2,1)S(1)} %collective-permute-done.30.refs_1_.refs_9_), channel_id=1, source_target_pairs={{0,2},{2,0},{4,6},{6,4},{8,10},{10,8},{12,14},{14,12},{1,3},{3,1},... | collective-permute-start | bytes 786440 | tf_op jit(solution)/shard_map/ppermute | solution.py:470
  80.3 16.4 %collective-permute-start.37 = (bf16[64,2048]{1,0:T(8,128)(2,1)S(1)}, bf16[64,2048]{1,0:T(8,128)(2,1)S(1)}, u32[]{:S(2)}, u32[]{:S(2)}) collective-permute-start(bf16[64,2048]{1,0:T(8,128)(2,1)S(1)} %collective-permute-done.33.refs_3_.refs_11_), channel_id=1, source_target_pairs={{0,2},{2,0},{4,6},{6,4},{8,10},{10,8},{12,14},{14,12},{1,3},{3,1},... | collective-permute-start | bytes 786440 | tf_op jit(solution)/shard_map/ppermute | solution.py:470
  95.5 18.2 %collective-permute-start.25 = (bf16[64,2048]{1,0:T(8,128)(2,1)S(1)}, bf16[64,2048]{1,0:T(8,128)(2,1)S(1)}, u32[]{:S(2)}, u32[]{:S(2)}) collective-permute-start(bf16[64,2048]{1,0:T(8,128)(2,1)S(1)} %copy-done.25), channel_id=1, source_target_pairs={{0,2},{2,0},{4,6},{6,4},{8,10},{10,8},{12,14},{14,12},{1,3},{3,1},... | collective-permute-start | bytes 786440 | tf_op jit(solution)/shard_map/ppermute | solution.py:470
  95.8 18.2 %collective-permute-start.26 = (bf16[64,2048]{1,0:T(8,128)(2,1)S(1)}, bf16[64,2048]{1,0:T(8,128)(2,1)S(1)}, u32[]{:S(2)}, u32[]{:S(2)}) collective-permute-start(bf16[64,2048]{1,0:T(8,128)(2,1)S(1)} %copy-done.26), channel_id=1, source_target_pairs={{0,2},{2,0},{4,6},{6,4},{8,10},{10,8},{12,14},{14,12},{1,3},{3,1},... | collective-permute-start | bytes 786440 | tf_op jit(solution)/shard_map/ppermute | solution.py:470
  96.2 17.8 %collective-permute-start.27 = (bf16[64,2048]{1,0:T(8,128)(2,1)}, bf16[64,2048]{1,0:T(8,128)(2,1)S(1)}, u32[]{:S(2)}, u32[]{:S(2)}) collective-permute-start(bf16[64,2048]{1,0:T(8,128)(2,1)} %collective-permute-done.23.refs_2_), channel_id=1, source_target_pairs={{0,2},{2,0},{4,6},{6,4},{8,10},{10,8},{12,14},{14,12},{1,3},{3,1},... | collective-permute-start | bytes 786440 | tf_op jit(solution)/shard_map/ppermute | solution.py:470
  96.4 17.6 %collective-permute-start.28 = (bf16[64,2048]{1,0:T(8,128)(2,1)S(1)}, bf16[64,2048]{1,0:T(8,128)(2,1)S(1)}, u32[]{:S(2)}, u32[]{:S(2)}) collective-permute-start(bf16[64,2048]{1,0:T(8,128)(2,1)S(1)} %collective-permute-done.24.refs_3_), channel_id=1, source_target_pairs={{0,2},{2,0},{4,6},{6,4},{8,10},{10,8},{12,14},{14,12},{1,3},{3,1},... | collective-permute-start | bytes 786440 | tf_op jit(solution)/shard_map/ppermute | solution.py:470
  96.7 35.2 %collective-permute-start.6 = (bf16[2,256,1024]{2,1,0:T(8,128)(2,1)S(1)}, bf16[2,256,1024]{2,1,0:T(8,128)(2,1)S(1)}, u32[]{:S(2)}, u32[]{:S(2)}) collective-permute-start(bf16[2,256,1024]{2,1,0:T(8,128)(2,1)S(1)} %copy-done.13), channel_id=1, source_target_pairs={{0,2},{2,0},{4,6},{6,4},{8,10},{10,8},{12,14},{14,12},{1,3},{3,1},... | collective-permute-start | bytes 3145736 | tf_op jit(solution)/shard_map/ppermute | solution.py:470
  113.7 29.4 %collective-permute-start.17 = (bf16[2,256,1024]{2,1,0:T(8,128)(2,1)S(1)}, bf16[2,256,1024]{2,1,0:T(8,128)(2,1)S(1)}, u32[]{:S(2)}, u32[]{:S(2)}) collective-permute-start(bf16[2,256,1024]{2,1,0:T(8,128)(2,1)S(1)} %copy-done.14), channel_id=1, source_target_pairs={{0,2},{2,0},{4,6},{6,4},{8,10},{10,8},{12,14},{14,12},{1,3},{3,1},... | collective-permute-start | bytes 3145736 | tf_op jit(solution)/shard_map/ppermute | solution.py:470
  131.4 19.5 %collective-permute-start.38 = (bf16[2,256,1152]{2,1,0:T(8,128)(2,1)}, bf16[2,256,1152]{2,1,0:T(8,128)(2,1)}, u32[]{:S(2)}, u32[]{:S(2)}) collective-permute-start(bf16[2,256,1152]{2,1,0:T(8,128)(2,1)} %get-tuple-element.46), channel_id=1, source_target_pairs={{0,2},{2,0},{4,6},{6,4},{8,10},{10,8},{12,14},{14,12},{1,3},{3,1},... | collective-permute-start | bytes 3538952 | tf_op jit(solution)/shard_map/ppermute | solution.py:470
  131.8 22.1 %collective-permute-start.40 = (bf16[2,256,1152]{2,1,0:T(8,128)(2,1)}, bf16[2,256,1152]{2,1,0:T(8,128)(2,1)}, u32[]{:S(2)}, u32[]{:S(2)}) collective-permute-start(bf16[2,256,1152]{2,1,0:T(8,128)(2,1)} %get-tuple-element.48), channel_id=1, source_target_pairs={{0,2},{2,0},{4,6},{6,4},{8,10},{10,8},{12,14},{14,12},{1,3},{3,1},... | collective-permute-start | bytes 3538952 | tf_op jit(solution)/shard_map/ppermute | solution.py:470
  132.0 14.2 %collective-permute-start.7 = (bf16[256,1024]{1,0:T(8,128)(2,1)S(1)}, bf16[256,1024]{1,0:T(8,128)(2,1)S(1)}, u32[]{:S(2)}, u32[]{:S(2)}) collective-permute-start(bf16[256,1024]{1,0:T(8,128)(2,1)S(1)} %fusion.7), channel_id=1, source_target_pairs={{0,1},{1,0},{2,3},{3,2},{4,5},{5,4},{6,7},{7,6},{8,9},{9,8},{10,11... | collective-permute-start | bytes 1572872 | tf_op jit(solution)/shard_map/ppermute | solution.py:473
  144.1 15.1 %collective-permute-start.18 = (bf16[256,1024]{1,0:T(8,128)(2,1)}, bf16[256,1024]{1,0:T(8,128)(2,1)}, u32[]{:S(2)}, u32[]{:S(2)}) collective-permute-start(bf16[256,1024]{1,0:T(8,128)(2,1)} %fusion.6), channel_id=1, source_target_pairs={{0,1},{1,0},{2,3},{3,2},{4,5},{5,4},{6,7},{7,6},{8,9},{9,8},{10,11... | collective-permute-start | bytes 1572872 | tf_op jit(solution)/shard_map/ppermute | solution.py:473
  148.5 46.3 %collective-permute-start.21 = (bf16[128,1024]{1,0:T(8,128)(2,1)}, bf16[128,1024]{1,0:T(8,128)(2,1)}, u32[]{:S(2)}, u32[]{:S(2)}) collective-permute-start(bf16[128,1024]{1,0:T(8,128)(2,1)} %slice.111), channel_id=1, source_target_pairs={{0,4},{2,6},{4,0},{6,2},{8,12},{10,14},{12,8},{14,10},{1,5},{3,7},... | collective-permute-start | bytes 786440 | tf_op jit(solution)/shard_map/ppermute | solution.py:470
  152.8 38.0 %collective-permute-start.39 = (bf16[256,1152]{1,0:T(8,128)(2,1)}, bf16[256,1152]{1,0:T(8,128)(2,1)}, u32[]{:S(2)}, u32[]{:S(2)}) collective-permute-start(bf16[256,1152]{1,0:T(8,128)(2,1)} %fusion.5.refs_20_), channel_id=1, source_target_pairs={{0,1},{1,0},{2,3},{3,2},{4,5},{5,4},{6,7},{7,6},{8,9},{9,8},{10,11... | collective-permute-start | bytes 1769480 | tf_op jit(solution)/shard_map/ppermute | solution.py:473
  155.8 29.1 %collective-permute-start.41 = (bf16[256,1152]{1,0:T(8,128)(2,1)}, bf16[256,1152]{1,0:T(8,128)(2,1)}, u32[]{:S(2)}, u32[]{:S(2)}) collective-permute-start(bf16[256,1152]{1,0:T(8,128)(2,1)} %fusion.4), channel_id=1, source_target_pairs={{0,1},{1,0},{2,3},{3,2},{4,5},{5,4},{6,7},{7,6},{8,9},{9,8},{10,11... | collective-permute-start | bytes 1769480 | tf_op jit(solution)/shard_map/ppermute | solution.py:473
  162.3 20.5 %collective-permute-start.19 = (bf16[128,1024]{1,0:T(8,128)(2,1)}, bf16[128,1024]{1,0:T(8,128)(2,1)S(1)}, u32[]{:S(2)}, u32[]{:S(2)}) collective-permute-start(bf16[128,1024]{1,0:T(8,128)(2,1)} %slice.110), channel_id=1, source_target_pairs={{0,4},{2,6},{12,8},{14,10},{1,5},{3,7},{13,9},{15,11},{16,20},{18,... | collective-permute-start | bytes 786440 | tf_op jit(solution)/shard_map/ppermute | solution.py:470
  181.5 15.2 %collective-permute-start.22 = (bf16[128,1024]{1,0:T(8,128)(2,1)}, bf16[128,1024]{1,0:T(8,128)(2,1)}, u32[]{:S(2)}, u32[]{:S(2)}) collective-permute-start(bf16[128,1024]{1,0:T(8,128)(2,1)} %slice.110), channel_id=1, source_target_pairs={{4,8},{6,10},{8,4},{10,6},{5,9},{7,11},{9,5},{11,7},{20,24},{22,26... | collective-permute-start | bytes 786440 | tf_op jit(solution)/shard_map/ppermute | solution.py:470
  183.6 19.0 %collective-permute-start.20 = (bf16[128,1024]{1,0:T(8,128)(2,1)}, bf16[128,1024]{1,0:T(8,128)(2,1)}, u32[]{:S(2)}, u32[]{:S(2)}) collective-permute-start(bf16[128,1024]{1,0:T(8,128)(2,1)} %slice_add_fusion.5), channel_id=1, source_target_pairs={{0,8},{2,10},{4,12},{6,14},{8,0},{10,2},{12,4},{14,6},{1,9},{3,11}... | collective-permute-start | bytes 786440 | tf_op jit(solution)/shard_map/ppermute | solution.py:470
  188.1 15.8 %collective-permute-start.42 = (bf16[128,1152]{1,0:T(8,128)(2,1)}, bf16[128,1152]{1,0:T(8,128)(2,1)S(1)}, u32[]{:S(2)}, u32[]{:S(2)}) collective-permute-start(bf16[128,1152]{1,0:T(8,128)(2,1)} %slice.120), channel_id=1, source_target_pairs={{0,4},{2,6},{12,8},{14,10},{1,5},{3,7},{13,9},{15,11},{16,20},{18,... | collective-permute-start | bytes 884744 | tf_op jit(solution)/shard_map/ppermute | solution.py:470
  190.9 15.8 %collective-permute-start.45 = (bf16[128,1152]{1,0:T(8,128)(2,1)}, bf16[128,1152]{1,0:T(8,128)(2,1)S(1)}, u32[]{:S(2)}, u32[]{:S(2)}) collective-permute-start(bf16[128,1152]{1,0:T(8,128)(2,1)} %slice.120), channel_id=1, source_target_pairs={{4,8},{6,10},{8,4},{10,6},{5,9},{7,11},{9,5},{11,7},{20,24},{22,26... | collective-permute-start | bytes 884744 | tf_op jit(solution)/shard_map/ppermute | solution.py:470
  194.7 11.9 %collective-permute-start.44 = (bf16[128,1152]{1,0:T(8,128)(2,1)S(1)}, bf16[128,1152]{1,0:T(8,128)(2,1)S(1)}, u32[]{:S(2)}, u32[]{:S(2)}) collective-permute-start(bf16[128,1152]{1,0:T(8,128)(2,1)S(1)} %get-tuple-element.64), channel_id=1, source_target_pairs={{0,4},{2,6},{4,0},{6,2},{8,12},{10,14},{12,8},{14,10},{1,5},{3,7},... | collective-permute-start | bytes 884744 | tf_op jit(solution)/shard_map/ppermute | solution.py:470
  203.9 15.2 %collective-permute-start.43 = (bf16[128,1152]{1,0:T(8,128)(2,1)S(1)}, bf16[128,1152]{1,0:T(8,128)(2,1)S(1)}, u32[]{:S(2)}, u32[]{:S(2)}) collective-permute-start(bf16[128,1152]{1,0:T(8,128)(2,1)S(1)} %slice_add_fusion.4), channel_id=1, source_target_pairs={{0,8},{2,10},{4,12},{6,14},{8,0},{10,2},{12,4},{14,6},{1,9},{3,11}... | collective-permute-start | bytes 884744 | tf_op jit(solution)/shard_map/ppermute | solution.py:470
  (36 other events, 309.9 us)

commit v2 on v0

v2 whole, which is shorter than its diff:
```python
import functools

import jax
import jax.numpy as jnp
from jax import lax
from jax.experimental import pallas as pl
from jax.experimental.pallas import tpu as pltpu
from jax.sharding import PartitionSpec as P

LANES = 128
VMEM = pl.BlockSpec(memory_space=pltpu.VMEM)


def product(first_mat, second_mat):
    return jnp.dot(first_mat, second_mat, preferred_element_type=jnp.float32)


def transposed_product(first_mat, second_mat):
    return lax.dot_general(
        first_mat, second_mat, (((0,), (0,)), ((), ())), preferred_element_type=jnp.float32
    )


def right_transposed(first_mat, second_mat):
    return lax.dot_general(
        first_mat, second_mat, (((1,), (1,)), ((), ())), preferred_element_type=jnp.float32
    )


def silu_parts(argument):
    sigmoid_part = jax.nn.sigmoid(argument)
    return argument * sigmoid_part, sigmoid_part * (1.0 + argument * (1.0 - sigmoid_part))


def total_of(terms):
    return functools.reduce(jnp.add, terms)


def call(kernel, name, operands, out_shape, scratch=(), flops=0, moved=0, mebibytes=16):
    return pl.pallas_call(
        kernel,
        out_shape=out_shape,
        in_specs=[VMEM] * len(operands),
        out_specs=jax.tree.map(lambda _: VMEM, out_shape),
        scratch_shapes=scratch,
        compiler_params=pltpu.CompilerParams(vmem_limit_bytes=mebibytes * 2**20),
        cost_estimate=pl.CostEstimate(
            flops=flops, bytes_accessed=moved, transcendentals=0
        ),
        name=name,
    )(*operands)


def half_at(array, which):
    rows = array.shape[0] // 2
    return array[which * rows : (which + 1) * rows]


def swap_halves(array):
    return jnp.concatenate([half_at(array, 1), half_at(array, 0)], axis=0)


def hi_lo(values, is_high):
    high = values.astype(jnp.bfloat16).astype(jnp.float32)
    return jnp.where(is_high, high, values - high).astype(jnp.bfloat16)


def gate_rows(counts, scores):
    used = [(counts > k).astype(jnp.float32) for k in range(scores.shape[0])]
    weighted = [scores[k : k + 1] * used[k] for k in range(scores.shape[0])]
    score_sum = total_of(weighted)
    return [w / score_sum for w in weighted], used, score_sum


def prepare_rows_kernel(experts, ids, counts, scores, rows, own, other, clock):
    total, width = rows.shape
    clock[...] = jnp.zeros_like(clock)
    lane = lax.broadcasted_iota(jnp.int32, (LANES, total), 0)
    gates, _, _ = gate_rows(counts[...], scores[...])
    table = jnp.zeros((LANES, total), jnp.float32)
    for k, gate in enumerate(gates):
        named = ids[k : k + 1, :]
        table = table + jnp.where((lane == named) | (lane == named + experts), gate, 0.0)
    table = table.T
    table = hi_lo(table, lax.broadcasted_iota(jnp.int32, table.shape, 1) < experts)
    for side in range(2):

        @pl.when(lax.axis_index("helper") == side)
        def _(side=side):
            for target, which in ((own, side), (other, 1 - side)):
                target[:, :width] = half_at(rows, which)
                target[:, width:] = half_at(table, which)


def prepare_rows(ids, counts, scores, rows, experts):
    total, width = rows.shape
    piece = jax.ShapeDtypeStruct((total // 2, width + LANES), jnp.bfloat16)
    return call(
        functools.partial(prepare_rows_kernel, experts),
        "prepare_rows",
        (ids, counts, scores, rows),
        (piece, piece, jax.ShapeDtypeStruct((8, LANES), jnp.float32)),
    )


def prepare_grads_kernel(rows, own, other):
    for side in range(2):

        @pl.when(lax.axis_index("helper") == side)
        def _(side=side):
            own[...] = half_at(rows, side)
            other[...] = half_at(rows, 1 - side)


def prepare_grads(rows):
    total, width = rows.shape
    piece = jax.ShapeDtypeStruct((total // 2, width), jnp.bfloat16)
    return call(prepare_grads_kernel, "prepare_grads", (rows,), (piece, piece))


def lay_out(pieces, target, columns):
    rows = pieces[0].shape[0]
    for i, piece in enumerate(pieces):
        target[i * rows : (i + 1) * rows, :] = piece[:, columns]


def gate_column(experts, pieces, width):
    table = jnp.concatenate([piece[:, width:] for piece in pieces], axis=0)
    lane = lax.broadcasted_iota(jnp.int32, table.shape, 1)
    expert = lax.axis_index("expert")
    mine = (lane == expert) | (lane == expert + experts)
    return jnp.sum(jnp.where(mine, table.astype(jnp.float32), 0.0), axis=1, keepdims=True)


def forward_kernel(experts, tile, *refs):
    pieces, refs = refs[:8], refs[8:]
    gate_mat, up_mat, down_mat, pre_gate, pre_up, gated, own, other, rows = refs
    width = rows.shape[1]
    half = width // 2
    lay_out(pieces, rows, slice(0, width))
    gate = gate_column(experts, pieces, width)
    for start in range(0, gated.shape[1], tile):
        columns = slice(start, start + tile)
        gate_part = product(rows[...], gate_mat[:, columns])
        up_part = product(rows[...], up_mat[:, columns])
        silu_value, _ = silu_parts(gate_part)
        pre_gate[:, columns] = gate_part
        pre_up[:, columns] = up_part
        gated[:, columns] = (gate * silu_value * up_part).astype(jnp.bfloat16)
    for which in range(2):
        stays = (lax.axis_index("helper") == which).astype(jnp.int32)
        for start in range(0, half, tile):
            columns = slice(start, start + tile)
            first = which * half + start
            out = product(gated[...], down_mat[:, first : first + tile]).astype(jnp.bfloat16)
            own[stays, :, columns] = half_at(out, 0)
            other[stays, :, columns] = half_at(out, 1)


def forward(pieces, gate_mat, up_mat, down_mat, experts):
    width, hidden = gate_mat.shape
    total = 8 * pieces[0].shape[0]
    pre = jax.ShapeDtypeStruct((total, hidden), jnp.float32)
    act = jax.ShapeDtypeStruct((total, hidden), jnp.bfloat16)
    sums = jax.ShapeDtypeStruct((2, total // 2, width // 2), jnp.bfloat16)
    return call(
        functools.partial(forward_kernel, experts, 256),
        "forward",
        (*pieces, gate_mat, up_mat, down_mat),
        (pre, pre, act, sums, sums),
        [pltpu.VMEM((total, width), jnp.bfloat16)],
        flops=6 * total * width * hidden,
    )


def backward_kernel(experts, tile, *refs):
    pieces, gate_pieces, refs = refs[:8], refs[8:16], refs[16:]
    down_mat, pre_gate, pre_up, gate_mat, up_mat = refs[:5]
    d_gate, d_up, own, other, grads = refs[5:]
    total, width = grads.shape
    half = width // 2
    lay_out(pieces, grads, slice(0, width))
    gate = gate_column(experts, gate_pieces, width)
    shares = []
    for start in range(0, d_gate.shape[1], tile):
        columns = slice(start, start + tile)
        raw = right_transposed(grads[...], down_mat[columns, :])
        up_part = pre_up[:, columns]
        silu_value, silu_slope = silu_parts(pre_gate[:, columns])
        share = raw * silu_value * up_part
        shares = shares + [share[:, c : c + LANES] for c in range(0, tile, LANES)]
        d_act = gate * raw
        d_gate[:, columns] = (d_act * up_part * silu_slope).astype(jnp.bfloat16)
        d_up[:, columns] = (d_act * silu_value).astype(jnp.bfloat16)
    value = jnp.sum(total_of(shares), axis=1, keepdims=True)
    lane = lax.broadcasted_iota(jnp.int32, (total, LANES), 1)
    high = 2 * lax.axis_index("expert") + lax.axis_index("helper")
    value = jnp.where((lane == high) | (lane == high + 2 * experts), value, 0.0)
    value = hi_lo(value, lane < 2 * experts)
    for which in range(2):
        own[which, :, half:] = half_at(value, 0)
        other[which, :, half:] = half_at(value, 1)
    for which in range(2):
        stays = (lax.axis_index("helper") == which).astype(jnp.int32)
        for start in range(0, half, tile):
            columns = slice(start, start + tile)
            first = which * half + start
            back = right_transposed(d_gate[...], gate_mat[first : first + tile, :])
            back = back + right_transposed(d_up[...], up_mat[first : first + tile, :])
            back = back.astype(jnp.bfloat16)
            own[stays, :, columns] = half_at(back, 0)
            other[stays, :, columns] = half_at(back, 1)


def backward(pieces, gate_pieces, pre_gate, pre_up, gate_mat, up_mat, down_mat, experts):
    width, hidden = gate_mat.shape
    total = pre_gate.shape[0]
    act = jax.ShapeDtypeStruct((total, hidden), jnp.bfloat16)
    sums = jax.ShapeDtypeStruct((2, total // 2, width // 2 + LANES), jnp.bfloat16)
    return call(
        functools.partial(backward_kernel, experts, 256),
        "backward",
        (*pieces, *gate_pieces, down_mat, pre_gate, pre_up, gate_mat, up_mat),
        (act, act, sums, sums),
        [pltpu.VMEM((total, width), jnp.bfloat16)],
        flops=6 * total * width * hidden,
    )


def weights_kernel(width, hidden, tile, *refs):
    pieces, refs = refs[:16], refs[16:]
    first, second, grad, rows, acts = refs
    lay_out(pieces, rows, slice(0, width))
    lay_out((first, second), acts, slice(0, hidden))
    left, right = (acts, rows) if grad.shape[0] == hidden else (rows, acts)
    for start in range(0, grad.shape[0], tile):
        columns = slice(start, start + tile)
        grad[columns, :] = transposed_product(left[:, columns], right[...]).astype(jnp.bfloat16)


def weights(name, pieces, acts, width, by_hidden):
    rows, hidden = acts[0].shape
    shape = (hidden, width) if by_hidden else (width, hidden)
    return call(
        functools.partial(weights_kernel, width, hidden, 256),
        name,
        (*pieces, *acts),
        jax.ShapeDtypeStruct(shape, jnp.bfloat16),
        [
            pltpu.VMEM((2 * rows, width), jnp.bfloat16),
            pltpu.VMEM((2 * rows, hidden), jnp.bfloat16),
        ],
        flops=4 * rows * width * hidden,
    )


def send_kernel(own, received, sent):
    sent[...] = own[0] + received[0]


def slots_kernel(own, received, arrived, first, second):
    rows = first.shape[0]
    half = rows // 2
    for slot, target in enumerate((first, second)):
        for which in range(2):
            here = slice(slot * rows + which * half, slot * rows + (which + 1) * half)
            there = slice(slot * rows + (1 - which) * half, slot * rows + (2 - which) * half)
            terms = (own[1, here, :], received[1, here, :], arrived[there, :])
            target[which * half : (which + 1) * half, :] = total_of(
                [term.astype(jnp.float32) for term in terms]
            ).astype(jnp.bfloat16)


def finish_outputs_kernel(*refs):
    columns = refs[-1]
    whole = total_of([ref[...].astype(jnp.float32) for ref in refs[:-1]])
    whole = jnp.where(lax.axis_index("helper") == 0, whole, swap_halves(whole))
    columns[...] = whole.astype(jnp.bfloat16)


def finish_inputs_kernel(experts, ids, counts, scores, clock, *refs):
    columns, d_scores = refs[-2:]
    width = columns.shape[1]
    whole = total_of([ref[...].astype(jnp.float32) for ref in refs[:-2]])
    whole = jnp.where(lax.axis_index("helper") == 0, whole, swap_halves(whole))
    columns[...] = whole[:, :width].astype(jnp.bfloat16)
    table = whole[:, width:].T
    lane = lax.broadcasted_iota(jnp.int32, table.shape, 0)
    named_by = (lane % (2 * experts)) // 2
    gates, used, score_sum = gate_rows(counts[...], scores[...])
    d_gates = []
    for k in range(len(gates)):
        hit = (named_by == ids[k : k + 1, :]) & (lane < 4 * experts)
        d_gates.append(jnp.sum(jnp.where(hit, table, 0.0), axis=0, keepdims=True))
    mean = total_of([gate * d_gate for gate, d_gate in zip(gates, d_gates)])
    for k, d_gate in enumerate(d_gates):
        d_scores[k : k + 1, :] = used[k] * (d_gate - mean) / score_sum


class FourChips:
    def __init__(self, label):
        self.label = label
        both = lambda pairs: [(2 * a + c, 2 * b + c) for a, b in pairs for c in (0, 1)]
        self.near = both([(z, z ^ 1) for z in range(4)])
        self.far = both([(z, z ^ 2) for z in range(4)])
        self.middle = both([(1, 2), (2, 1)])
        self.outward = both([(1, 0), (2, 3)])
        self.inward = both([(0, 1), (3, 2)])
        self.cores = [(i, i ^ 1) for i in range(8)]
        self.sides = [(0, 1), (1, 0)]

    def line(self, array, pairs):
        with jax.named_scope(self.label + "_line"):
            return lax.ppermute(array, "expert", pairs)

    def sibling(self, array):
        with jax.named_scope(self.label + "_cores"):
            return lax.ppermute(array, "expert", self.cores)

    def across(self, array):
        with jax.named_scope(self.label + "_across"):
            return lax.ppermute(array, "helper", self.sides)

    def first_hops(self, own):
        near = self.line(own, self.near)
        far = self.line(own, self.far)
        middle = self.line(own, self.middle)
        return near, far, middle

    def chunk(self, *pieces):
        return [*pieces, *(self.sibling(p) for p in pieces)]

    def send(self, own, received):
        return call(
            send_kernel,
            self.label + "_send",
            (own, received),
            jax.ShapeDtypeStruct(own.shape[1:], own.dtype),
        )

    def slots(self, own, received, arrived):
        rows, columns = arrived.shape
        slot = jax.ShapeDtypeStruct((rows // 2, columns), arrived.dtype)
        return call(slots_kernel, self.label + "_slots", (own, received, arrived), (slot, slot))


def load_kernel(*refs):
    sources, targets, sems = refs[:3], refs[3:6], refs[6]
    copies = [
        pltpu.make_async_copy(source, target, sems.at[i])
        for i, (source, target) in enumerate(zip(sources, targets))
    ]
    for copy in copies:
        copy.start()
    for copy in copies:
        copy.wait()


def load(*mats):
    return pl.pallas_call(
        load_kernel,
        out_shape=tuple(jax.ShapeDtypeStruct(mat.shape, mat.dtype) for mat in mats),
        in_specs=[pl.BlockSpec(memory_space=pltpu.HBM)] * len(mats),
        out_specs=(VMEM,) * len(mats),
        scratch_shapes=[pltpu.SemaphoreType.DMA((len(mats),))],
        compiler_params=pltpu.CompilerParams(vmem_limit_bytes=2**20),
        name="load",
    )(*mats)


def space(clock):
    return pl.pallas_call(
        lambda old, new: None,
        out_shape=jax.ShapeDtypeStruct(clock.shape, clock.dtype),
        in_specs=[pl.BlockSpec(memory_space=pl.ANY)],
        out_specs=pl.BlockSpec(memory_space=pl.ANY),
        input_output_aliases={0: 0},
        compiler_params=pltpu.CompilerParams(vmem_limit_bytes=2**20),
        cost_estimate=pl.CostEstimate(flops=12 * 10**9, bytes_accessed=0, transcendentals=0),
        name="space",
    )(clock)


class Order:
    def __init__(self):
        self.token = None

    def __call__(self, function, *operands, also=()):
        if self.token is not None:
            operands, _ = lax.optimization_barrier((operands, (self.token, also)))
        result = function(*operands)
        self.token = result
        return result


def lined_up(tokens, expert_ids, pick_counts, gate_scores, gate_local, up_local, down_local, grad_out):
    experts = lax.axis_size("expert")
    width = tokens.shape[1]
    picks = (expert_ids.T, pick_counts[None, :], gate_scores.T)
    rows, grads, outs, ins = (FourChips(label) for label in ("rows", "grads", "out", "in"))
    order = Order()

    own, other, clock = order(lambda r: prepare_rows(*picks, r, experts), tokens)
    near, far, middle = rows.first_hops(own)
    mats = order(load, gate_local, up_local, down_local)
    near_across = rows.across(near)
    near_rows = rows.chunk(own, other, near, near_across)
    relay = rows.line(far, rows.outward)
    far_across = rows.across(far)
    own, other = order(prepare_grads, grad_out, also=(far, middle, near))
    near, far_grad, middle_grad = grads.first_hops(own)
    near_grads = grads.chunk(own, other, near, grads.across(near))
    last = order(jnp.add, middle, relay)
    far_rows = rows.chunk(far, far_across, last, rows.across(last))

    near_gate, near_up, near_act, near_out, sent = order(
        lambda *r: forward(r, *mats, experts), *near_rows, also=far_across
    )
    near_received = outs.sibling(sent)
    relay = grads.line(far_grad, grads.outward)
    far_gate, far_up, far_act, far_out, sent = order(
        lambda *r: forward(r, *mats, experts), *far_rows, also=(near, far_grad, middle_grad)
    )
    far_received = outs.sibling(sent)
    far_across = grads.across(far_grad)
    last = order(jnp.add, middle_grad, relay)
    far_grads = grads.chunk(far_grad, far_across, last, grads.across(last))
    clock = order(space, clock, also=(far_across, near_grads))
    sent = order(outs.send, far_out, far_received)
    far_arrived = outs.across(sent)
    step = lambda g, r, *pre: backward(g, r, *pre, *mats, experts)
    near_d_gate, near_d_up, near_in, sent = order(
        step, near_grads, near_rows, near_gate, near_up
    )
    near_in_received = ins.sibling(sent)
    clock = order(space, clock, also=far_grads)
    sent = order(outs.send, near_out, near_received)
    near_arrived = outs.across(sent)
    far_d_gate, far_d_up, far_in, sent = order(step, far_grads, far_rows, far_gate, far_up)
    far_in_received = ins.sibling(sent)
    far_slot, last_slot = order(outs.slots, far_out, far_received, far_arrived)
    relay = outs.line(last_slot, outs.inward)
    middle = outs.line(last_slot, outs.middle)
    clock = order(space, clock)
    sent = order(ins.send, far_in, far_in_received)
    far_in_arrived = ins.across(sent)
    sent = order(ins.send, near_in, near_in_received)
    near_in_arrived = ins.across(sent)
    product_of = lambda name, by_hidden: lambda r, *acts: weights(name, r, acts, width, by_hidden)
    grad_down = order(
        product_of("grad_down", True), near_grads + far_grads, near_act, far_act
    )
    own_slot, near_slot = order(outs.slots, near_out, near_received, near_arrived)
    near = outs.line(near_slot, outs.near)
    far = outs.line(order(jnp.add, far_slot, relay), outs.far)
    out_sums = (own_slot, far, near, middle)
    all_rows = near_rows + far_rows
    grad_gate = order(product_of("grad_gate", False), all_rows, near_d_gate, far_d_gate)
    far_slot, last_slot = order(ins.slots, far_in, far_in_received, far_in_arrived)
    relay = ins.line(last_slot, ins.inward)
    middle = ins.line(last_slot, ins.middle)
    grad_up = order(product_of("grad_up", False), all_rows, near_d_up, far_d_up)
    far = ins.line(order(jnp.add, far_slot, relay), ins.far)
    own_slot, near_slot = order(ins.slots, near_in, near_in_received, near_in_arrived)
    near = ins.line(near_slot, ins.near)
    in_sums = (own_slot, far, near, middle)

    columns = jax.ShapeDtypeStruct((tokens.shape[0], width // 2), jnp.bfloat16)
    output_cols = order(
        lambda *sums: call(finish_outputs_kernel, "finish_outputs", sums, columns), *out_sums
    )
    input_cols, d_scores = order(
        lambda *sums: call(
            functools.partial(finish_inputs_kernel, experts),
            "finish_inputs",
            (*picks, clock, *sums),
            (columns, jax.ShapeDtypeStruct(picks[2].shape, jnp.float32)),
        ),
        *in_sums,
    )
    return output_cols, input_cols, d_scores.T, grad_gate[None], grad_up[None], grad_down[None]


def any_mesh(tokens, expert_ids, pick_counts, gate_scores, gate_local, up_local, down_local, grad_out):
    tok_rows = tokens.shape[0]
    pick_width = expert_ids.shape[1]
    experts = lax.axis_size("expert")
    active_mask = lax.broadcasted_iota(jnp.int32, (tok_rows, pick_width), 1) < pick_counts[:, None]
    active_float = active_mask.astype(jnp.float32)
    weighted = gate_scores * active_float
    score_sum = jnp.sum(weighted, axis=1, keepdims=True)
    gate_weights = weighted / score_sum
    picked = (expert_ids[:, :, None] == lax.broadcasted_iota(jnp.int32, (1, 1, experts), 2)).astype(
        jnp.float32
    )
    gate_table = jnp.sum(gate_weights[:, :, None] * picked, axis=1)

    def combine(partial):
        summed = lax.psum_scatter(partial, "expert", scatter_dimension=0, tiled=True)
        return lax.psum_scatter(summed, "helper", scatter_dimension=1, tiled=True)

    rows = lax.all_gather(tokens, "expert", tiled=True)
    tables = lax.all_gather(gate_table.T, "expert", tiled=False)
    gates = jnp.take(tables, lax.axis_index("expert"), axis=1).reshape(-1, 1)
    grads = lax.all_gather(grad_out, "expert", tiled=True)

    pre_gate = product(rows, gate_local)
    pre_up = product(rows, up_local)
    silu_value, silu_slope = silu_parts(pre_gate)
    hidden_act = silu_value * pre_up
    gated_act = (gates * hidden_act).astype(jnp.bfloat16)
    output_cols = combine(product(gated_act, down_local).astype(jnp.bfloat16))

    raw_act = right_transposed(grads, down_local)
    gate_part = jnp.sum(raw_act * hidden_act, axis=1)
    d_act = gates * raw_act
    d_pre_gate = (d_act * pre_up * silu_slope).astype(jnp.bfloat16)
    d_pre_up = (d_act * silu_value).astype(jnp.bfloat16)
    input_cols = combine(
        (right_transposed(d_pre_gate, gate_local) + right_transposed(d_pre_up, up_local)).astype(
            jnp.bfloat16
        )
    )

    gate_parts = lax.all_gather(
        gate_part.reshape(-1, tok_rows), ("expert", "helper"), tiled=False
    )
    own_parts = jnp.take(gate_parts, lax.axis_index("expert"), axis=1)
    by_expert = jnp.sum(own_parts.reshape(experts, -1, tok_rows), axis=1).T
    d_gates = jnp.sum(by_expert[:, None, :] * picked, axis=2)
    d_scores = (
        active_float
        * (d_gates - jnp.sum(gate_weights * d_gates, axis=1, keepdims=True))
        / score_sum
    )

    def over_dp(whole, dimension):
        return lax.psum_scatter(
            whole.astype(jnp.bfloat16), "dp", scatter_dimension=dimension, tiled=True
        )[None]

    grad_w_gate = over_dp(transposed_product(rows, d_pre_gate), 0)
    grad_w_up = over_dp(transposed_product(rows, d_pre_up), 0)
    grad_w_down = over_dp(transposed_product(gated_act, grads), 1)
    return output_cols, input_cols, d_scores, grad_w_gate, grad_w_up, grad_w_down


def on_device(tokens, expert_ids, pick_counts, gate_scores, w_gate, w_up, w_down, grad_out):
    sizes = tuple(lax.axis_size(axis) for axis in ("expert", "helper", "dp"))
    layer = lined_up if sizes == (8, 2, 1) else any_mesh
    return layer(
        tokens, expert_ids, pick_counts, gate_scores, w_gate[0], w_up[0], w_down[0], grad_out
    )


def solution(mesh):
    in_specs = (
        P(("groups", "expert", "dp"), None),
        P(("groups", "expert", "dp"), None),
        P(("groups", "expert", "dp")),
        P(("groups", "expert", "dp"), None),
        P("expert", None, "helper"),
        P("expert", None, "helper"),
        P("expert", "helper", None),
        P(("groups", "expert", "dp"), None),
    )
    out_specs = (
        P(("groups", "expert", "dp"), "helper"),
        P(("groups", "expert", "dp"), "helper"),
        P(("groups", "expert", "dp"), None),
        P(("groups", "expert"), "dp", "helper"),
        P(("groups", "expert"), "dp", "helper"),
        P(("groups", "expert"), "helper", "dp"),
    )
    return jax.shard_map(
        on_device, mesh=mesh, in_specs=in_specs, out_specs=out_specs, check_vma=False
    )
```

time: 278 us -> 175 us (0.63)
  matrix products: 55 us -> 0 us
  Pallas kernels: 0 us -> 51.9 us
  blocking collectives: 46.4 us -> 0 us
  waiting for transfers between devices: 89.8 us -> 65.4 us
  other arithmetic: 17 us -> 0.27 us
  local copies, waits for them, and re-layouts: 22.2 us -> 10.8 us
    dot_general x9 -> x0, matrix products: 55 us -> none  [the longest x3 20.3 us: right_transposed(): lax.dot_general(first_mat, second_mat, (((1,), (1,)), ((), ())), preferre...]
    pallas_call x0 -> x23, Pallas kernels: none -> 51.9 us  [the longest x19 51.1 us: call(): pl.pallas_call(kernel, out_shape=out_shape, in_specs=[VMEM] * len(operand...]
    all_gather x2 -> x0, blocking collectives: 46.4 us -> none  [the longest x1 32.2 us: on_device(): lax.all_gather(plan.unorder(gate_part), ('expert', 'helper'), tiled=False)]
    ppermute x34 -> x46, waiting for transfers between devices: 89.8 us -> 65.4 us  [the longest x16 45.2 us: line(): return lax.ppermute(array, 'expert', pairs)]
    convert_element_type x9 -> x0, other arithmetic: 10.1 us -> none  [the longest x1 6.16 us: on_device(): d_pre_gate = (d_act * pre_up * silu_slope).astype(jnp.bfloat16)]
    unnamed x4 -> x0, other arithmetic: 4.91 us -> none
    concatenate x5 -> x0, local copies, waits for them, and re-layouts: 3.57 us -> none  [the longest x2 1.81 us: dispatch(): return jnp.concatenate([own_core, other_core], axis=0)]
    unnamed x44 -> x26, local copies, waits for them, and re-layouts: 13.6 us -> 10.8 us
  transfers between devices with their start and end apart: 34 -> 46, of which waited for: 17 -> 8; matrix products, arithmetic and copies ran while one was open for 22% -> 0% of each run, Pallas kernels for 0% -> 29%
where the time goes in v2:
time: 175 us; the launch traced here: 174 us
  waiting for transfers between devices  65.4 us (37%)
  Pallas kernels  51.9 us (30%)
  starting transfers between devices  44.8 us (26%)
  local copies, waits for them, and re-layouts  10.8 us (6%)
    pallas_call x19, Pallas kernels, call(): pl.pallas_call(kernel, out_shape=out_shape, in_specs=[VMEM] * len(operand...  51.1 us
    ppermute x16, waiting for transfers between devices, line(): return lax.ppermute(array, 'expert', pairs)  45.2 us
    ppermute x16, starting transfers between devices, line(): return lax.ppermute(array, 'expert', pairs)  29.7 us
    ppermute x10, waiting for transfers between devices, across(): return lax.ppermute(array, 'helper', self.sides)  20.2 us
    unnamed x26, local copies, waits for them, and re-layouts  10.8 us
    ppermute x10, starting transfers between devices, across(): return lax.ppermute(array, 'helper', self.sides)  10.5 us
    ppermute x20, starting transfers between devices, sibling(): return lax.ppermute(array, 'expert', self.cores)  4.55 us
  transfers between devices with their start and end apart: 46, of which 8 were waited for; matrix products, arithmetic and copies ran while one was open for 0% of the time, Pallas kernels for 29%

profile of v2, /device:TPU:0, one launch (start us, length us, event | category | flops | bytes accessed | tf_op | source)
XLA Modules:
  0.0 174.3 jit_solution(5650503056309602595)
XLA Ops:
  0.6 1.0 copy-done.3
  1.7 0.7 copy-done.5
  2.4 0.7 copy-done.7
  3.0 0.7 copy-done.9
  3.8 4.1 %collective-permute-start.7 = (bf16[64,2176]{1,0:T(8,128)(2,1)S(1)}, bf16[64,2176]{1,0:T(8,128)(2,1)S(1)}, u32[]{:S(2)}, u32[]{:S(2)}) collective-permute-start(bf16[64,2176]{1,0:T(8,128)(2,1)S(1)} %get-tuple-element.341.refs_0_.refs_8_), channel_id=1, source_target_pairs={{0,8},{2,10},{4,12},{6,14},{8,0},{10,2},{12,4},{14,6},{1,9},{3,11}... | collective-permute-start | bytes 835592 | tf_op jit(solution)/shard_map/rows_line/ppermute | solution.py:314
  8.0 1.6 collective-permute-start
  9.5 0.7 collective-permute-start.6
  10.3 11.2 %collective-permute-done.7.refs_0_.refs_8_ = bf16[64,2176]{1,0:T(8,128)(2,1)S(1)} collective-permute-done((bf16[64,2176]{1,0:T(8,128)(2,1)S(1)}, bf16[64,2176]{1,0:T(8,128)(2,1)S(1)}, u32[]{:S(2)}, u32[]{:S(2)}) %collective-permute-start.7) | collective-permute-done | bytes 278560 | tf_op jit(solution)/shard_map/rows_line/ppermute | solution.py:314
  21.4 1.3 collective-permute-start.8
  22.8 1.9 %collective-permute-start.1 = (bf16[64,2176]{1,0:T(8,128)(2,1)S(1)}, bf16[64,2176]{1,0:T(8,128)(2,1)S(1)}, u32[]{:S(2)}, u32[]{:S(2)}) collective-permute-start(bf16[64,2176]{1,0:T(8,128)(2,1)S(1)} %collective-permute-done.refs_2_.refs_10_), channel_id=1, source_target_pairs={{0,1},{1,0},{2,3},{3,2},{4,5},{5,4},{6,7},{7,6},{8,9},{9,8},{10,11... | collective-permute-start | bytes 835592 | tf_op jit(solution)/shard_map/rows_across/ppermute | solution.py:322
  24.8 2.2 %copy-done = bf16[1,2048,1024]{2,1,0:T(8,128)(2,1)S(1)} copy-done((bf16[1,2048,1024]{2,1,0:T(8,128)(2,1)S(1)}, bf16[1,2048,1024]{2,1,0:T(8,128)(2,1)}, u32[]{:S(2)}) %copy-start) | copy-done | bytes 4194328
  26.9 2.2 %copy-done.1 = bf16[1,2048,1024]{2,1,0:T(8,128)(2,1)S(1)} copy-done((bf16[1,2048,1024]{2,1,0:T(8,128)(2,1)S(1)}, bf16[1,2048,1024]{2,1,0:T(8,128)(2,1)}, u32[]{:S(2)}) %copy-start.1) | copy-done | bytes 4194328
  29.1 2.2 %copy-done.2 = bf16[1,1024,2048]{2,1,0:T(8,128)(2,1)S(1)} copy-done((bf16[1,1024,2048]{2,1,0:T(8,128)(2,1)S(1)}, bf16[1,1024,2048]{2,1,0:T(8,128)(2,1)}, u32[]{:S(2)}) %copy-start.2) | copy-done | bytes 4194328
  31.3 0.9 load.1
  32.6 2.7 %collective-permute-start.19 = (bf16[64,2048]{1,0:T(8,128)(2,1)S(1)}, bf16[64,2048]{1,0:T(8,128)(2,1)S(1)}, u32[]{:S(2)}, u32[]{:S(2)}) collective-permute-start(bf16[64,2048]{1,0:T(8,128)(2,1)S(1)} %get-tuple-element.293.refs_0_), channel_id=1, source_target_pairs={{0,4},{2,6},{4,0},{6,2},{8,12},{10,14},{12,8},{14,10},{1,5},{3,7},... | collective-permute-start | bytes 786440 | tf_op jit(solution)/shard_map/grads_line/ppermute | solution.py:314
  35.3 1.4 collective-permute-start.12
  37.2 10.2 %collective-permute-done.19.refs_2_ = bf16[64,2048]{1,0:T(8,128)(2,1)S(1)} collective-permute-done((bf16[64,2048]{1,0:T(8,128)(2,1)S(1)}, bf16[64,2048]{1,0:T(8,128)(2,1)S(1)}, u32[]{:S(2)}, u32[]{:S(2)}) %collective-permute-start.19) | collective-permute-done | bytes 262176 | tf_op jit(solution)/shard_map/grads_line/ppermute | solution.py:314
  47.4 2.4 %collective-permute-done.12.refs_0_.refs_8_ = bf16[64,2048]{1,0:T(8,128)(2,1)S(1)} collective-permute-done((bf16[64,2048]{1,0:T(8,128)(2,1)S(1)}, bf16[64,2048]{1,0:T(8,128)(2,1)S(1)}, u32[]{:S(2)}, u32[]{:S(2)}) %collective-permute-start.12) | collective-permute-done | bytes 262176 | tf_op jit(solution)/shard_map/grads_line/ppermute | solution.py:314
  49.9 1.7 collective-permute-start.14
  51.5 0.7 collective-permute-start.11
  52.7 1.3 collective-permute-start.13
  54.5 4.8 %collective-permute-done.14.refs_3_.refs_11_ = bf16[64,2176]{1,0:T(8,128)(2,1)S(1)} collective-permute-done((bf16[64,2176]{1,0:T(8,128)(2,1)S(1)}, bf16[64,2176]{1,0:T(8,128)(2,1)S(1)}, u32[]{:S(2)}, u32[]{:S(2)}) %collective-permute-start.14) | collective-permute-done | bytes 278560 | tf_op jit(solution)/shard_map/rows_across/ppermute | solution.py:322
  59.3 6.8 %forward.2 = (f32[512,1024]{1,0:T(8,128)S(1)}, f32[512,1024]{1,0:T(8,128)S(1)}, bf16[512,1024]{1,0:T(8,128)(2,1)S(1)}, bf16[2,256,1024]{2,1,0:T(8,128)(2,1)S(1)}, bf16[2,256,1024]{2,1,0:T(8,128)(2,1)S(1)}) custom-call(bf16[64,2176]{1,0:T(8,128)(2,1)S(1)} %get-tuple-element.341.refs_0_.refs_8_, bf16[64,2176]{1,0:T(8,128)(2,1)S(1)} %get-tuple-element.342.refs_1_.refs_9_, ...), custom_call_target="tpu_custom_call" | custom-call | flops 6442450944 | tf_op jit(solution)/shard_map/forward/pallas_call | solution.py:40
  66.1 0.6 collective-permute-start.23
  67.2 1.5 collective-permute-start.20
  68.7 6.7 %forward.3 = (f32[512,1024]{1,0:T(8,128)S(1)}, f32[512,1024]{1,0:T(8,128)S(1)}, bf16[512,1024]{1,0:T(8,128)(2,1)S(1)}, bf16[2,256,1024]{2,1,0:T(8,128)(2,1)S(1)}, bf16[2,256,1024]{2,1,0:T(8,128)(2,1)S(1)}) custom-call(bf16[64,2176]{1,0:T(8,128)(2,1)S(1)} %collective-permute-done.7.refs_0_.refs_8_, ...), custom_call_target="tpu_custom_call" | custom-call | flops 6442450944 | tf_op jit(solution)/shard_map/forward/pallas_call | solution.py:40
  75.5 1.0 copy-done.11
  76.5 0.6 collective-permute-start.28
  78.2 8.1 %collective-permute-done.27.refs_3_.refs_11_ = bf16[64,2048]{1,0:T(8,128)(2,1)S(1)} collective-permute-done((bf16[64,2048]{1,0:T(8,128)(2,1)S(1)}, bf16[64,2048]{1,0:T(8,128)(2,1)S(1)}, u32[]{:S(2)}, u32[]{:S(2)}) %collective-permute-start.27) | collective-permute-done | bytes 262176 | tf_op jit(solution)/shard_map/grads_across/ppermute | solution.py:322
  86.9 7.5 %backward.2 = (bf16[512,1024]{1,0:T(8,128)(2,1)S(1)}, bf16[512,1024]{1,0:T(8,128)(2,1)S(1)}, bf16[2,256,1152]{2,1,0:T(8,128)(2,1)S(1)}, bf16[2,256,1152]{2,1,0:T(8,128)(2,1)S(1)}) custom-call(bf16[64,2048]{1,0:T(8,128)(2,1)S(1)} %get-tuple-element.293.refs_0_, bf16[64,2048]{1,0:T(8,128)(2,1)S(1)} %get-tuple-element.294.refs_1_, ...), custom_call_target="tpu_custom_call" | custom-call | flops 6442450944 | tf_op jit(solution)/shard_map/backward/pallas_call | solution.py:40
  95.2 7.2 %backward.3 = (bf16[512,1024]{1,0:T(8,128)(2,1)S(1)}, bf16[512,1024]{1,0:T(8,128)(2,1)S(1)}, bf16[2,256,1152]{2,1,0:T(8,128)(2,1)S(1)}, bf16[2,256,1152]{2,1,0:T(8,128)(2,1)S(1)}) custom-call(bf16[64,2048]{1,0:T(8,128)(2,1)S(1)} %collective-permute-done.12.refs_0_.refs_8_, bf16[64,2048]{1,0:T(8,128)(2,1)S(1)} %collective-permute-done.20.refs_1_.refs_9_, ...), custom_call_target="tpu_custom_call" | custom-call | flops 6442450944 | tf_op jit(solution)/shard_map/backward/pallas_call | solution.py:40
  102.9 1.5 collective-permute-start.32
  104.4 4.9 %collective-permute-done.35.arrived = bf16[256,1024]{1,0:T(8,128)(2,1)S(1)} collective-permute-done((bf16[256,1024]{1,0:T(8,128)(2,1)S(1)}, bf16[256,1024]{1,0:T(8,128)(2,1)S(1)}, u32[]{:S(2)}, u32[]{:S(2)}) %collective-permute-start.35) | collective-permute-done | bytes 524320 | tf_op jit(solution)/shard_map/out_across/ppermute | solution.py:322
  109.5 0.7 collective-permute-start.39
  110.2 4.9 %collective-permute-start.36 = (bf16[128,1024]{1,0:T(8,128)(2,1)S(1)}, bf16[128,1024]{1,0:T(8,128)(2,1)S(1)}, u32[]{:S(2)}, u32[]{:S(2)}) collective-permute-start(bf16[128,1024]{1,0:T(8,128)(2,1)S(1)} %get-tuple-element.287), channel_id=1, source_target_pairs={{0,4},{2,6},{12,8},{14,10},{1,5},{3,7},{13,9},{15,11},{16,20},{18,... | collective-permute-start | bytes 786440 | tf_op jit(solution)/shard_map/out_line/ppermute | solution.py:314
  115.2 1.5 collective-permute-start.41
  116.8 0.7 collective-permute-start.40
  117.4 6.6 %grad_down.1 = bf16[1024,2048]{1,0:T(8,128)(2,1)} custom-call(bf16[64,2048]{1,0:T(8,128)(2,1)S(1)} %get-tuple-element.293.refs_0_, bf16[64,2048]{1,0:T(8,128)(2,1)S(1)} %get-tuple-element.294.refs_1_, bf16[64,2048]{1,0:T(8,128)(2,1)S(1)} %collective-permute-done.19.refs_2_, bf16[64,2048]{1,0:T(8,128)(2,1)S(1)} %collective-permute-done.21.refs_3_, ...), custom_call_target="tpu_custom_call" | custom-call | flops 4294967296 | tf_op jit(solution)/shard_map/grad_down/pallas_call | solution.py:40
  124.3 6.6 %grad_gate.1 = bf16[2048,1024]{1,0:T(8,128)(2,1)} custom-call(bf16[64,2176]{1,0:T(8,128)(2,1)S(1)} %get-tuple-element.341.refs_0_.refs_8_, bf16[64,2176]{1,0:T(8,128)(2,1)S(1)} %get-tuple-element.342.refs_1_.refs_9_, bf16[64,2176]{1,0:T(8,128)(2,1)S(1)} %collective-permute-done.refs_2_.refs_10_, ...), custom_call_target="tpu_custom_call" | custom-call | flops 4294967296 | tf_op jit(solution)/shard_map/grad_gate/pallas_call | solution.py:40
  130.9 2.3 %collective-permute-done.41.arrived = bf16[256,1152]{1,0:T(8,128)(2,1)S(1)} collective-permute-done((bf16[256,1152]{1,0:T(8,128)(2,1)S(1)}, bf16[256,1152]{1,0:T(8,128)(2,1)S(1)}, u32[]{:S(2)}, u32[]{:S(2)}) %collective-permute-start.41) | collective-permute-done | bytes 589856 | tf_op jit(solution)/shard_map/in_across/ppermute | solution.py:322
  133.4 0.7 collective-permute-start.45
  134.1 4.9 %collective-permute-start.42 = (bf16[128,1152]{1,0:T(8,128)(2,1)S(1)}, bf16[128,1152]{1,0:T(8,128)(2,1)S(1)}, u32[]{:S(2)}, u32[]{:S(2)}) collective-permute-start(bf16[128,1152]{1,0:T(8,128)(2,1)S(1)} %get-tuple-element.340), channel_id=1, source_target_pairs={{0,4},{2,6},{12,8},{14,10},{1,5},{3,7},{13,9},{15,11},{16,20},{18,... | collective-permute-start | bytes 884744 | tf_op jit(solution)/shard_map/in_line/ppermute | solution.py:314
  139.0 6.6 %grad_up.1 = bf16[2048,1024]{1,0:T(8,128)(2,1)} custom-call(bf16[64,2176]{1,0:T(8,128)(2,1)S(1)} %get-tuple-element.341.refs_0_.refs_8_, bf16[64,2176]{1,0:T(8,128)(2,1)S(1)} %get-tuple-element.342.refs_1_.refs_9_, bf16[64,2176]{1,0:T(8,128)(2,1)S(1)} %collective-permute-done.refs_2_.refs_10_, bf16[64,2176]{1,0:T(8,128)(2,1)S(1)} %collective-permute-done.1.refs_3_.refs_11_, ...), custom_call_target="tpu_custom_call" | custom-call | flops 4294967296 | tf_op jit(solution)/shard_map/grad_up/pallas_call | solution.py:40
  146.1 2.8 %collective-permute-start.43 = (bf16[128,1152]{1,0:T(8,128)(2,1)S(1)}, bf16[128,1152]{1,0:T(8,128)(2,1)S(1)}, u32[]{:S(2)}, u32[]{:S(2)}) collective-permute-start(bf16[128,1152]{1,0:T(8,128)(2,1)S(1)} %add.15), channel_id=1, source_target_pairs={{0,8},{2,10},{4,12},{6,14},{8,0},{10,2},{12,4},{14,6},{1,9},{3,11}... | collective-permute-start | bytes 884744 | tf_op jit(solution)/shard_map/in_line/ppermute | solution.py:314
  149.0 1.9 %collective-permute-start.38 = (bf16[128,1024]{1,0:T(8,128)(2,1)S(1)}, bf16[128,1024]{1,0:T(8,128)(2,1)S(1)}, u32[]{:S(2)}, u32[]{:S(2)}) collective-permute-start(bf16[128,1024]{1,0:T(8,128)(2,1)S(1)} %get-tuple-element.315), channel_id=1, source_target_pairs={{0,4},{2,6},{4,0},{6,2},{8,12},{10,14},{12,8},{14,10},{1,5},{3,7},... | collective-permute-start | bytes 786440 | tf_op jit(solution)/shard_map/out_line/ppermute | solution.py:314
  151.0 21.4 %collective-permute-done.37.refs_1_ = bf16[128,1024]{1,0:T(8,128)(2,1)S(1)} collective-permute-done((bf16[128,1024]{1,0:T(8,128)(2,1)S(1)}, bf16[128,1024]{1,0:T(8,128)(2,1)S(1)}, u32[]{:S(2)}, u32[]{:S(2)}) %collective-permute-start.37) | collective-permute-done | bytes 262176 | tf_op jit(solution)/shard_map/out_line/ppermute | solution.py:314
  172.4 0.9 finish_outputs.1
  173.3 1.0 finish_inputs.1
  (97 shorter events, 7.2 us)
Async XLA Ops:
  3.8 17.6 %collective-permute-start.7 = (bf16[64,2176]{1,0:T(8,128)(2,1)S(1)}, bf16[64,2176]{1,0:T(8,128)(2,1)S(1)}, u32[]{:S(2)}, u32[]{:S(2)}) collective-permute-start(bf16[64,2176]{1,0:T(8,128)(2,1)S(1)} %get-tuple-element.341.refs_0_.refs_8_), channel_id=1, source_target_pairs={{0,8},{2,10},{4,12},{6,14},{8,0},{10,2},{12,4},{14,6},{1,9},{3,11}... | collective-permute-start | bytes 835592 | tf_op jit(solution)/shard_map/rows_line/ppermute | solution.py:314
  8.0 14.9 %collective-permute-start = (bf16[64,2176]{1,0:T(8,128)(2,1)S(1)}, bf16[64,2176]{1,0:T(8,128)(2,1)S(1)}, u32[]{:S(2)}, u32[]{:S(2)}) collective-permute-start(bf16[64,2176]{1,0:T(8,128)(2,1)S(1)} %get-tuple-element.341.refs_0_.refs_8_), channel_id=1, source_target_pairs={{0,4},{2,6},{4,0},{6,2},{8,12},{10,14},{12,8},{14,10},{1,5},{3,7},... | collective-permute-start | bytes 835592 | tf_op jit(solution)/shard_map/rows_line/ppermute | solution.py:314
  9.5 22.7 %collective-permute-start.6 = (bf16[64,2176]{1,0:T(8,128)(2,1)S(1)}, bf16[64,2176]{1,0:T(8,128)(2,1)S(1)}, u32[]{:S(2)}, u32[]{:S(2)}) collective-permute-start(bf16[64,2176]{1,0:T(8,128)(2,1)S(1)} %get-tuple-element.341.refs_0_.refs_8_), channel_id=1, source_target_pairs={{4,8},{6,10},{8,4},{10,6},{5,9},{7,11},{9,5},{11,7},{20,24},{22,26... | collective-permute-start | bytes 835592 | tf_op jit(solution)/shard_map/rows_line/ppermute | solution.py:314
  10.2 22.4 %collective-permute-start.3 = (bf16[64,2176]{1,0:T(8,128)(2,1)S(1)}, bf16[64,2176]{1,0:T(8,128)(2,1)S(1)}, u32[]{:S(2)}, u32[]{:S(2)}) collective-permute-start(bf16[64,2176]{1,0:T(8,128)(2,1)S(1)} %get-tuple-element.342.refs_1_.refs_9_), channel_id=1, source_target_pairs={{0,2},{2,0},{4,6},{6,4},{8,10},{10,8},{12,14},{14,12},{1,3},{3,1},... | collective-permute-start | bytes 835592 | tf_op jit(solution)/shard_map/rows_cores/ppermute | solution.py:318
  21.4 13.8 %collective-permute-start.8 = (bf16[64,2176]{1,0:T(8,128)(2,1)S(1)}, bf16[64,2176]{1,0:T(8,128)(2,1)S(1)}, u32[]{:S(2)}, u32[]{:S(2)}) collective-permute-start(bf16[64,2176]{1,0:T(8,128)(2,1)S(1)} %collective-permute-done.7.refs_0_.refs_8_), channel_id=1, source_target_pairs={{4,0},{6,2},{8,12},{10,14},{5,1},{7,3},{9,13},{11,15},{20,16},{22,... | collective-permute-start | bytes 835592 | tf_op jit(solution)/shard_map/rows_line/ppermute | solution.py:314
  22.7 13.9 %collective-permute-start.2 = (bf16[64,2176]{1,0:T(8,128)(2,1)S(1)}, bf16[64,2176]{1,0:T(8,128)(2,1)S(1)}, u32[]{:S(2)}, u32[]{:S(2)}) collective-permute-start(bf16[64,2176]{1,0:T(8,128)(2,1)S(1)} %get-tuple-element.341.refs_0_.refs_8_), channel_id=1, source_target_pairs={{0,2},{2,0},{4,6},{6,4},{8,10},{10,8},{12,14},{14,12},{1,3},{3,1},... | collective-permute-start | bytes 835592 | tf_op jit(solution)/shard_map/rows_cores/ppermute | solution.py:318
  22.8 13.8 %collective-permute-start.1 = (bf16[64,2176]{1,0:T(8,128)(2,1)S(1)}, bf16[64,2176]{1,0:T(8,128)(2,1)S(1)}, u32[]{:S(2)}, u32[]{:S(2)}) collective-permute-start(bf16[64,2176]{1,0:T(8,128)(2,1)S(1)} %collective-permute-done.refs_2_.refs_10_), channel_id=1, source_target_pairs={{0,1},{1,0},{2,3},{3,2},{4,5},{5,4},{6,7},{7,6},{8,9},{9,8},{10,11... | collective-permute-start | bytes 835592 | tf_op jit(solution)/shard_map/rows_across/ppermute | solution.py:322
  32.4 19.1 %collective-permute-start.9 = (bf16[64,2176]{1,0:T(8,128)(2,1)S(1)}, bf16[64,2176]{1,0:T(8,128)(2,1)S(1)}, u32[]{:S(2)}, u32[]{:S(2)}) collective-permute-start(bf16[64,2176]{1,0:T(8,128)(2,1)S(1)} %collective-permute-done.7.refs_0_.refs_8_), channel_id=1, source_target_pairs={{0,1},{1,0},{2,3},{3,2},{4,5},{5,4},{6,7},{7,6},{8,9},{9,8},{10,11... | collective-permute-start | bytes 835592 | tf_op jit(solution)/shard_map/rows_across/ppermute | solution.py:322
  32.6 14.8 %collective-permute-start.19 = (bf16[64,2048]{1,0:T(8,128)(2,1)S(1)}, bf16[64,2048]{1,0:T(8,128)(2,1)S(1)}, u32[]{:S(2)}, u32[]{:S(2)}) collective-permute-start(bf16[64,2048]{1,0:T(8,128)(2,1)S(1)} %get-tuple-element.293.refs_0_), channel_id=1, source_target_pairs={{0,4},{2,6},{4,0},{6,2},{8,12},{10,14},{12,8},{14,10},{1,5},{3,7},... | collective-permute-start | bytes 786440 | tf_op jit(solution)/shard_map/grads_line/ppermute | solution.py:314
  35.3 14.6 %collective-permute-start.12 = (bf16[64,2048]{1,0:T(8,128)(2,1)S(1)}, bf16[64,2048]{1,0:T(8,128)(2,1)S(1)}, u32[]{:S(2)}, u32[]{:S(2)}) collective-permute-start(bf16[64,2048]{1,0:T(8,128)(2,1)S(1)} %get-tuple-element.293.refs_0_), channel_id=1, source_target_pairs={{0,8},{2,10},{4,12},{6,14},{8,0},{10,2},{12,4},{14,6},{1,9},{3,11}... | collective-permute-start | bytes 786440 | tf_op jit(solution)/shard_map/grads_line/ppermute | solution.py:314
  36.7 15.5 %collective-permute-start.4 = (bf16[64,2176]{1,0:T(8,128)(2,1)S(1)}, bf16[64,2176]{1,0:T(8,128)(2,1)S(1)}, u32[]{:S(2)}, u32[]{:S(2)}) collective-permute-start(bf16[64,2176]{1,0:T(8,128)(2,1)S(1)} %collective-permute-done.refs_2_.refs_10_), channel_id=1, source_target_pairs={{0,2},{2,0},{4,6},{6,4},{8,10},{10,8},{12,14},{14,12},{1,3},{3,1},... | collective-permute-start | bytes 835592 | tf_op jit(solution)/shard_map/rows_cores/ppermute | solution.py:318
  36.7 16.0 %collective-permute-start.5 = (bf16[64,2176]{1,0:T(8,128)(2,1)S(1)}, bf16[64,2176]{1,0:T(8,128)(2,1)S(1)}, u32[]{:S(2)}, u32[]{:S(2)}) collective-permute-start(bf16[64,2176]{1,0:T(8,128)(2,1)S(1)} %collective-permute-done.1.refs_3_.refs_11_), channel_id=1, source_target_pairs={{0,2},{2,0},{4,6},{6,4},{8,10},{10,8},{12,14},{14,12},{1,3},{3,1},... | collective-permute-start | bytes 835592 | tf_op jit(solution)/shard_map/rows_cores/ppermute | solution.py:318
  47.4 6.6 %collective-permute-start.15 = (bf16[64,2176]{1,0:T(8,128)(2,1)S(1)}, bf16[64,2176]{1,0:T(8,128)(2,1)S(1)}, u32[]{:S(2)}, u32[]{:S(2)}) collective-permute-start(bf16[64,2176]{1,0:T(8,128)(2,1)S(1)} %collective-permute-done.7.refs_0_.refs_8_), channel_id=1, source_target_pairs={{0,2},{2,0},{4,6},{6,4},{8,10},{10,8},{12,14},{14,12},{1,3},{3,1},... | collective-permute-start | bytes 835592 | tf_op jit(solution)/shard_map/rows_cores/ppermute | solution.py:318
  49.9 9.4 %collective-permute-start.14 = (bf16[64,2176]{1,0:T(8,128)(2,1)S(1)}, bf16[64,2176]{1,0:T(8,128)(2,1)S(1)}, u32[]{:S(2)}, u32[]{:S(2)}) collective-permute-start(bf16[64,2176]{1,0:T(8,128)(2,1)S(1)} %add.12.refs_2_.refs_10_), channel_id=1, source_target_pairs={{0,1},{1,0},{2,3},{3,2},{4,5},{5,4},{6,7},{7,6},{8,9},{9,8},{10,11... | collective-permute-start | bytes 835592 | tf_op jit(solution)/shard_map/rows_across/ppermute | solution.py:322
  51.5 2.4 %collective-permute-start.11 = (bf16[64,2048]{1,0:T(8,128)(2,1)S(1)}, bf16[64,2048]{1,0:T(8,128)(2,1)S(1)}, u32[]{:S(2)}, u32[]{:S(2)}) collective-permute-start(bf16[64,2048]{1,0:T(8,128)(2,1)S(1)} %get-tuple-element.293.refs_0_), channel_id=1, source_target_pairs={{4,8},{6,10},{8,4},{10,6},{5,9},{7,11},{9,5},{11,7},{20,24},{22,26... | collective-permute-start | bytes 786440 | tf_op jit(solution)/shard_map/grads_line/ppermute | solution.py:314
  52.2 15.0 %collective-permute-start.21 = (bf16[64,2048]{1,0:T(8,128)(2,1)S(1)}, bf16[64,2048]{1,0:T(8,128)(2,1)S(1)}, u32[]{:S(2)}, u32[]{:S(2)}) collective-permute-start(bf16[64,2048]{1,0:T(8,128)(2,1)S(1)} %collective-permute-done.19.refs_2_), channel_id=1, source_target_pairs={{0,1},{1,0},{2,3},{3,2},{4,5},{5,4},{6,7},{7,6},{8,9},{9,8},{10,11... | collective-permute-start | bytes 786440 | tf_op jit(solution)/shard_map/grads_across/ppermute | solution.py:322
  52.7 16.1 %collective-permute-start.13 = (bf16[64,2048]{1,0:T(8,128)(2,1)S(1)}, bf16[64,2048]{1,0:T(8,128)(2,1)S(1)}, u32[]{:S(2)}, u32[]{:S(2)}) collective-permute-start(bf16[64,2048]{1,0:T(8,128)(2,1)S(1)} %collective-permute-done.12.refs_0_.refs_8_), channel_id=1, source_target_pairs={{4,0},{6,2},{8,12},{10,14},{5,1},{7,3},{9,13},{11,15},{20,16},{22,... | collective-permute-start | bytes 786440 | tf_op jit(solution)/shard_map/grads_line/ppermute | solution.py:314
  54.0 12.7 %collective-permute-start.17 = (bf16[64,2176]{1,0:T(8,128)(2,1)S(1)}, bf16[64,2176]{1,0:T(8,128)(2,1)S(1)}, u32[]{:S(2)}, u32[]{:S(2)}) collective-permute-start(bf16[64,2176]{1,0:T(8,128)(2,1)S(1)} %add.12.refs_2_.refs_10_), channel_id=1, source_target_pairs={{0,2},{2,0},{4,6},{6,4},{8,10},{10,8},{12,14},{14,12},{1,3},{3,1},... | collective-permute-start | bytes 835592 | tf_op jit(solution)/shard_map/rows_cores/ppermute | solution.py:318
  54.0 12.1 %collective-permute-start.16 = (bf16[64,2176]{1,0:T(8,128)(2,1)S(1)}, bf16[64,2176]{1,0:T(8,128)(2,1)S(1)}, u32[]{:S(2)}, u32[]{:S(2)}) collective-permute-start(bf16[64,2176]{1,0:T(8,128)(2,1)S(1)} %collective-permute-done.9.refs_1_.refs_9_), channel_id=1, source_target_pairs={{0,2},{2,0},{4,6},{6,4},{8,10},{10,8},{12,14},{14,12},{1,3},{3,1},... | collective-permute-start | bytes 835592 | tf_op jit(solution)/shard_map/rows_cores/ppermute | solution.py:318
  59.3 7.5 %collective-permute-start.18 = (bf16[64,2176]{1,0:T(8,128)(2,1)S(1)}, bf16[64,2176]{1,0:T(8,128)(2,1)S(1)}, u32[]{:S(2)}, u32[]{:S(2)}) collective-permute-start(bf16[64,2176]{1,0:T(8,128)(2,1)S(1)} %collective-permute-done.14.refs_3_.refs_11_), channel_id=1, source_target_pairs={{0,2},{2,0},{4,6},{6,4},{8,10},{10,8},{12,14},{14,12},{1,3},{3,1},... | collective-permute-start | bytes 835592 | tf_op jit(solution)/shard_map/rows_cores/ppermute | solution.py:318
  66.1 10.4 %collective-permute-start.23 = (bf16[64,2048]{1,0:T(8,128)(2,1)S(1)}, bf16[64,2048]{1,0:T(8,128)(2,1)S(1)}, u32[]{:S(2)}, u32[]{:S(2)}) collective-permute-start(bf16[64,2048]{1,0:T(8,128)(2,1)S(1)} %get-tuple-element.294.refs_1_), channel_id=1, source_target_pairs={{0,2},{2,0},{4,6},{6,4},{8,10},{10,8},{12,14},{14,12},{1,3},{3,1},... | collective-permute-start | bytes 786440 | tf_op jit(solution)/shard_map/grads_cores/ppermute | solution.py:318
  66.7 10.5 %collective-permute-start.22 = (bf16[64,2048]{1,0:T(8,128)(2,1)S(1)}, bf16[64,2048]{1,0:T(8,128)(2,1)S(1)}, u32[]{:S(2)}, u32[]{:S(2)}) collective-permute-start(bf16[64,2048]{1,0:T(8,128)(2,1)S(1)} %get-tuple-element.293.refs_0_), channel_id=1, source_target_pairs={{0,2},{2,0},{4,6},{6,4},{8,10},{10,8},{12,14},{14,12},{1,3},{3,1},... | collective-permute-start | bytes 786440 | tf_op jit(solution)/shard_map/grads_cores/ppermute | solution.py:318
  66.8 10.8 %collective-permute-start.24 = (bf16[64,2048]{1,0:T(8,128)(2,1)S(1)}, bf16[64,2048]{1,0:T(8,128)(2,1)S(1)}, u32[]{:S(2)}, u32[]{:S(2)}) collective-permute-start(bf16[64,2048]{1,0:T(8,128)(2,1)S(1)} %collective-permute-done.19.refs_2_), channel_id=1, source_target_pairs={{0,2},{2,0},{4,6},{6,4},{8,10},{10,8},{12,14},{14,12},{1,3},{3,1},... | collective-permute-start | bytes 786440 | tf_op jit(solution)/shard_map/grads_cores/ppermute | solution.py:318
  67.2 9.9 %collective-permute-start.20 = (bf16[64,2048]{1,0:T(8,128)(2,1)S(1)}, bf16[64,2048]{1,0:T(8,128)(2,1)S(1)}, u32[]{:S(2)}, u32[]{:S(2)}) collective-permute-start(bf16[64,2048]{1,0:T(8,128)(2,1)S(1)} %collective-permute-done.12.refs_0_.refs_8_), channel_id=1, source_target_pairs={{0,1},{1,0},{2,3},{3,2},{4,5},{5,4},{6,7},{7,6},{8,9},{9,8},{10,11... | collective-permute-start | bytes 786440 | tf_op jit(solution)/shard_map/grads_across/ppermute | solution.py:322
  68.7 9.0 %collective-permute-start.25 = (bf16[64,2048]{1,0:T(8,128)(2,1)S(1)}, bf16[64,2048]{1,0:T(8,128)(2,1)S(1)}, u32[]{:S(2)}, u32[]{:S(2)}) collective-permute-start(bf16[64,2048]{1,0:T(8,128)(2,1)S(1)} %collective-permute-done.21.refs_3_), channel_id=1, source_target_pairs={{0,2},{2,0},{4,6},{6,4},{8,10},{10,8},{12,14},{14,12},{1,3},{3,1},... | collective-permute-start | bytes 786440 | tf_op jit(solution)/shard_map/grads_cores/ppermute | solution.py:318
  76.5 18.0 %collective-permute-start.28 = (bf16[64,2048]{1,0:T(8,128)(2,1)S(1)}, bf16[64,2048]{1,0:T(8,128)(2,1)S(1)}, u32[]{:S(2)}, u32[]{:S(2)}) collective-permute-start(bf16[64,2048]{1,0:T(8,128)(2,1)S(1)} %collective-permute-done.12.refs_0_.refs_8_), channel_id=1, source_target_pairs={{0,2},{2,0},{4,6},{6,4},{8,10},{10,8},{12,14},{14,12},{1,3},{3,1},... | collective-permute-start | bytes 786440 | tf_op jit(solution)/shard_map/grads_cores/ppermute | solution.py:318
  77.1 18.0 %collective-permute-start.29 = (bf16[64,2048]{1,0:T(8,128)(2,1)S(1)}, bf16[64,2048]{1,0:T(8,128)(2,1)S(1)}, u32[]{:S(2)}, u32[]{:S(2)}) collective-permute-start(bf16[64,2048]{1,0:T(8,128)(2,1)S(1)} %collective-permute-done.20.refs_1_.refs_9_), channel_id=1, source_target_pairs={{0,2},{2,0},{4,6},{6,4},{8,10},{10,8},{12,14},{14,12},{1,3},{3,1},... | collective-permute-start | bytes 786440 | tf_op jit(solution)/shard_map/grads_cores/ppermute | solution.py:318
  77.2 17.9 %collective-permute-start.10 = (bf16[2,256,1024]{2,1,0:T(8,128)(2,1)S(1)}, bf16[2,256,1024]{2,1,0:T(8,128)(2,1)S(1)}, u32[]{:S(2)}, u32[]{:S(2)}) collective-permute-start(bf16[2,256,1024]{2,1,0:T(8,128)(2,1)S(1)} %get-tuple-element.214), channel_id=1, source_target_pairs={{0,2},{2,0},{4,6},{6,4},{8,10},{10,8},{12,14},{14,12},{1,3},{3,1},... | collective-permute-start | bytes 3145736 | tf_op jit(solution)/shard_map/out_cores/ppermute | solution.py:318
  77.6 8.7 %collective-permute-start.26 = (bf16[2,256,1024]{2,1,0:T(8,128)(2,1)S(1)}, bf16[2,256,1024]{2,1,0:T(8,128)(2,1)S(1)}, u32[]{:S(2)}, u32[]{:S(2)}) collective-permute-start(bf16[2,256,1024]{2,1,0:T(8,128)(2,1)S(1)} %get-tuple-element.230), channel_id=1, source_target_pairs={{0,2},{2,0},{4,6},{6,4},{8,10},{10,8},{12,14},{14,12},{1,3},{3,1},... | collective-permute-start | bytes 3145736 | tf_op jit(solution)/shard_map/out_cores/ppermute | solution.py:318
  77.7 8.7 %collective-permute-start.27 = (bf16[64,2048]{1,0:T(8,128)(2,1)S(1)}, bf16[64,2048]{1,0:T(8,128)(2,1)S(1)}, u32[]{:S(2)}, u32[]{:S(2)}) collective-permute-start(bf16[64,2048]{1,0:T(8,128)(2,1)S(1)} %add.13.refs_2_.refs_10_), channel_id=1, source_target_pairs={{0,1},{1,0},{2,3},{3,2},{4,5},{5,4},{6,7},{7,6},{8,9},{9,8},{10,11... | collective-permute-start | bytes 786440 | tf_op jit(solution)/shard_map/grads_across/ppermute | solution.py:322
  86.4 8.7 %collective-permute-start.30 = (bf16[64,2048]{1,0:T(8,128)(2,1)S(1)}, bf16[64,2048]{1,0:T(8,128)(2,1)S(1)}, u32[]{:S(2)}, u32[]{:S(2)}) collective-permute-start(bf16[64,2048]{1,0:T(8,128)(2,1)S(1)} %add.13.refs_2_.refs_10_), channel_id=1, source_target_pairs={{0,2},{2,0},{4,6},{6,4},{8,10},{10,8},{12,14},{14,12},{1,3},{3,1},... | collective-permute-start | bytes 786440 | tf_op jit(solution)/shard_map/grads_cores/ppermute | solution.py:318
  86.4 8.7 %collective-permute-start.31 = (bf16[64,2048]{1,0:T(8,128)(2,1)S(1)}, bf16[64,2048]{1,0:T(8,128)(2,1)S(1)}, u32[]{:S(2)}, u32[]{:S(2)}) collective-permute-start(bf16[64,2048]{1,0:T(8,128)(2,1)S(1)} %collective-permute-done.27.refs_3_.refs_11_), channel_id=1, source_target_pairs={{0,2},{2,0},{4,6},{6,4},{8,10},{10,8},{12,14},{14,12},{1,3},{3,1},... | collective-permute-start | bytes 786440 | tf_op jit(solution)/shard_map/grads_cores/ppermute | solution.py:318
  94.5 14.9 %collective-permute-start.35 = (bf16[256,1024]{1,0:T(8,128)(2,1)S(1)}, bf16[256,1024]{1,0:T(8,128)(2,1)S(1)}, u32[]{:S(2)}, u32[]{:S(2)}) collective-permute-start(bf16[256,1024]{1,0:T(8,128)(2,1)S(1)} %out_send.2), channel_id=1, source_target_pairs={{0,1},{1,0},{2,3},{3,2},{4,5},{5,4},{6,7},{7,6},{8,9},{9,8},{10,11... | collective-permute-start | bytes 1572872 | tf_op jit(solution)/shard_map/out_across/ppermute | solution.py:322
  102.3 12.8 %collective-permute-start.34 = (bf16[2,256,1152]{2,1,0:T(8,128)(2,1)S(1)}, bf16[2,256,1152]{2,1,0:T(8,128)(2,1)S(1)}, u32[]{:S(2)}, u32[]{:S(2)}) collective-permute-start(bf16[2,256,1152]{2,1,0:T(8,128)(2,1)S(1)} %get-tuple-element.280), channel_id=1, source_target_pairs={{0,2},{2,0},{4,6},{6,4},{8,10},{10,8},{12,14},{14,12},{1,3},{3,1},... | collective-permute-start | bytes 3538952 | tf_op jit(solution)/shard_map/in_cores/ppermute | solution.py:318
  102.4 14.3 %collective-permute-start.33 = (bf16[2,256,1152]{2,1,0:T(8,128)(2,1)S(1)}, bf16[2,256,1152]{2,1,0:T(8,128)(2,1)S(1)}, u32[]{:S(2)}, u32[]{:S(2)}) collective-permute-start(bf16[2,256,1152]{2,1,0:T(8,128)(2,1)S(1)} %get-tuple-element.257), channel_id=1, source_target_pairs={{0,2},{2,0},{4,6},{6,4},{8,10},{10,8},{12,14},{14,12},{1,3},{3,1},... | collective-permute-start | bytes 3538952 | tf_op jit(solution)/shard_map/in_cores/ppermute | solution.py:318
  102.9 21.1 %collective-permute-start.32 = (bf16[256,1024]{1,0:T(8,128)(2,1)S(1)}, bf16[256,1024]{1,0:T(8,128)(2,1)S(1)}, u32[]{:S(2)}, u32[]{:S(2)}) collective-permute-start(bf16[256,1024]{1,0:T(8,128)(2,1)S(1)} %out_send.3), channel_id=1, source_target_pairs={{0,1},{1,0},{2,3},{3,2},{4,5},{5,4},{6,7},{7,6},{8,9},{9,8},{10,11... | collective-permute-start | bytes 1572872 | tf_op jit(solution)/shard_map/out_across/ppermute | solution.py:322
  109.5 39.5 %collective-permute-start.39 = (bf16[128,1024]{1,0:T(8,128)(2,1)S(1)}, bf16[128,1024]{1,0:T(8,128)(2,1)S(1)}, u32[]{:S(2)}, u32[]{:S(2)}) collective-permute-start(bf16[128,1024]{1,0:T(8,128)(2,1)S(1)} %get-tuple-element.287), channel_id=1, source_target_pairs={{4,8},{6,10},{8,4},{10,6},{5,9},{7,11},{9,5},{11,7},{20,24},{22,26... | collective-permute-start | bytes 786440 | tf_op jit(solution)/shard_map/out_line/ppermute | solution.py:314
  110.2 14.0 %collective-permute-start.36 = (bf16[128,1024]{1,0:T(8,128)(2,1)S(1)}, bf16[128,1024]{1,0:T(8,128)(2,1)S(1)}, u32[]{:S(2)}, u32[]{:S(2)}) collective-permute-start(bf16[128,1024]{1,0:T(8,128)(2,1)S(1)} %get-tuple-element.287), channel_id=1, source_target_pairs={{0,4},{2,6},{12,8},{14,10},{1,5},{3,7},{13,9},{15,11},{16,20},{18,... | collective-permute-start | bytes 786440 | tf_op jit(solution)/shard_map/out_line/ppermute | solution.py:314
  115.2 18.0 %collective-permute-start.41 = (bf16[256,1152]{1,0:T(8,128)(2,1)S(1)}, bf16[256,1152]{1,0:T(8,128)(2,1)S(1)}, u32[]{:S(2)}, u32[]{:S(2)}) collective-permute-start(bf16[256,1152]{1,0:T(8,128)(2,1)S(1)} %in_send.2), channel_id=1, source_target_pairs={{0,1},{1,0},{2,3},{3,2},{4,5},{5,4},{6,7},{7,6},{8,9},{9,8},{10,11... | collective-permute-start | bytes 1769480 | tf_op jit(solution)/shard_map/in_across/ppermute | solution.py:322
  116.8 28.9 %collective-permute-start.40 = (bf16[256,1152]{1,0:T(8,128)(2,1)S(1)}, bf16[256,1152]{1,0:T(8,128)(2,1)S(1)}, u32[]{:S(2)}, u32[]{:S(2)}) collective-permute-start(bf16[256,1152]{1,0:T(8,128)(2,1)S(1)} %in_send.3), channel_id=1, source_target_pairs={{0,1},{1,0},{2,3},{3,2},{4,5},{5,4},{6,7},{7,6},{8,9},{9,8},{10,11... | collective-permute-start | bytes 1769480 | tf_op jit(solution)/shard_map/in_across/ppermute | solution.py:322
  133.4 39.8 %collective-permute-start.45 = (bf16[128,1152]{1,0:T(8,128)(2,1)S(1)}, bf16[128,1152]{1,0:T(8,128)(2,1)S(1)}, u32[]{:S(2)}, u32[]{:S(2)}) collective-permute-start(bf16[128,1152]{1,0:T(8,128)(2,1)S(1)} %get-tuple-element.340), channel_id=1, source_target_pairs={{4,8},{6,10},{8,4},{10,6},{5,9},{7,11},{9,5},{11,7},{20,24},{22,26... | collective-permute-start | bytes 884744 | tf_op jit(solution)/shard_map/in_line/ppermute | solution.py:314
  134.1 11.5 %collective-permute-start.42 = (bf16[128,1152]{1,0:T(8,128)(2,1)S(1)}, bf16[128,1152]{1,0:T(8,128)(2,1)S(1)}, u32[]{:S(2)}, u32[]{:S(2)}) collective-permute-start(bf16[128,1152]{1,0:T(8,128)(2,1)S(1)} %get-tuple-element.340), channel_id=1, source_target_pairs={{0,4},{2,6},{12,8},{14,10},{1,5},{3,7},{13,9},{15,11},{16,20},{18,... | collective-permute-start | bytes 884744 | tf_op jit(solution)/shard_map/in_line/ppermute | solution.py:314
  145.7 27.6 %copy-start.6 = (s32[128,4]{0,1:T(4,128)S(1)}, s32[128,4]{0,1:T(4,128)}, u32[]{:S(2)}) copy-start(s32[128,4]{0,1:T(4,128)} %param.9) | copy-start | bytes 6148
  145.7 27.6 %copy-start.8 = (f32[128,4]{0,1:T(4,128)S(1)}, f32[128,4]{0,1:T(4,128)}, u32[]{:S(2)}) copy-start(f32[128,4]{0,1:T(4,128)} %param.11) | copy-start | bytes 6148
  146.0 27.3 %collective-permute-start.44 = (bf16[128,1152]{1,0:T(8,128)(2,1)S(1)}, bf16[128,1152]{1,0:T(8,128)(2,1)S(1)}, u32[]{:S(2)}, u32[]{:S(2)}) collective-permute-start(bf16[128,1152]{1,0:T(8,128)(2,1)S(1)} %get-tuple-element.365), channel_id=1, source_target_pairs={{0,4},{2,6},{4,0},{6,2},{8,12},{10,14},{12,8},{14,10},{1,5},{3,7},... | collective-permute-start | bytes 884744 | tf_op jit(solution)/shard_map/in_line/ppermute | solution.py:314
  146.1 27.2 %collective-permute-start.43 = (bf16[128,1152]{1,0:T(8,128)(2,1)S(1)}, bf16[128,1152]{1,0:T(8,128)(2,1)S(1)}, u32[]{:S(2)}, u32[]{:S(2)}) collective-permute-start(bf16[128,1152]{1,0:T(8,128)(2,1)S(1)} %add.15), channel_id=1, source_target_pairs={{0,8},{2,10},{4,12},{6,14},{8,0},{10,2},{12,4},{14,6},{1,9},{3,11}... | collective-permute-start | bytes 884744 | tf_op jit(solution)/shard_map/in_line/ppermute | solution.py:314
  148.9 23.5 %collective-permute-start.37 = (bf16[128,1024]{1,0:T(8,128)(2,1)S(1)}, bf16[128,1024]{1,0:T(8,128)(2,1)S(1)}, u32[]{:S(2)}, u32[]{:S(2)}) collective-permute-start(bf16[128,1024]{1,0:T(8,128)(2,1)S(1)} %add.14), channel_id=1, source_target_pairs={{0,8},{2,10},{4,12},{6,14},{8,0},{10,2},{12,4},{14,6},{1,9},{3,11}... | collective-permute-start | bytes 786440 | tf_op jit(solution)/shard_map/out_line/ppermute | solution.py:314
  149.0 23.3 %collective-permute-start.38 = (bf16[128,1024]{1,0:T(8,128)(2,1)S(1)}, bf16[128,1024]{1,0:T(8,128)(2,1)S(1)}, u32[]{:S(2)}, u32[]{:S(2)}) collective-permute-start(bf16[128,1024]{1,0:T(8,128)(2,1)S(1)} %get-tuple-element.315), channel_id=1, source_target_pairs={{0,4},{2,6},{4,0},{6,2},{8,12},{10,14},{12,8},{14,10},{1,5},{3,7},... | collective-permute-start | bytes 786440 | tf_op jit(solution)/shard_map/out_line/ppermute | solution.py:314
  (11 other events, 41.4 us)

commit v3 on v2

--- a/solution.py
+++ b/solution.py
@@ -72,7 +72,17 @@
     return [w / score_sum for w in weighted], used, score_sum
 
 
-def prepare_rows_kernel(experts, ids, counts, scores, rows, own, other, clock):
+def prepare_rows_kernel(experts, *refs):
+    sources, (own, other, clock), targets, sems = refs[:4], refs[4:7], refs[7:11], refs[11]
+    ids, counts, scores, rows = targets
+    copies = [
+        pltpu.make_async_copy(source, target, sems.at[i])
+        for i, (source, target) in enumerate(zip(sources, targets))
+    ]
+    for copy in copies:
+        copy.start()
+    for copy in copies:
+        copy.wait()
     total, width = rows.shape
     clock[...] = jnp.zeros_like(clock)
     lane = lax.broadcasted_iota(jnp.int32, (LANES, total), 0)
@@ -95,12 +105,19 @@
 def prepare_rows(ids, counts, scores, rows, experts):
     total, width = rows.shape
     piece = jax.ShapeDtypeStruct((total // 2, width + LANES), jnp.bfloat16)
-    return call(
+    operands = (ids, counts, scores, rows)
+    return pl.pallas_call(
         functools.partial(prepare_rows_kernel, experts),
-        "prepare_rows",
-        (ids, counts, scores, rows),
-        (piece, piece, jax.ShapeDtypeStruct((8, LANES), jnp.float32)),
-    )
+        out_shape=(piece, piece, jax.ShapeDtypeStruct((8, LANES), jnp.float32)),
+        in_specs=[pl.BlockSpec(memory_space=pltpu.HBM)] * len(operands),
+        out_specs=(VMEM,) * 3,
+        scratch_shapes=[
+            *(pltpu.VMEM(operand.shape, operand.dtype) for operand in operands),
+            pltpu.SemaphoreType.DMA((len(operands),)),
+        ],
+        compiler_params=pltpu.CompilerParams(vmem_limit_bytes=8 * 2**20),
+        name="prepare_rows",
+    )(*(pltpu.with_memory_space_constraint(operand, pltpu.HBM) for operand in operands))
 
 
 def prepare_grads_kernel(rows, own, other):
@@ -157,7 +174,7 @@
             other[stays, :, columns] = half_at(out, 1)
 
 
-def forward(pieces, gate_mat, up_mat, down_mat, experts):
+def forward(pieces, gate_mat, up_mat, down_mat, experts, estimate):
     width, hidden = gate_mat.shape
     total = 8 * pieces[0].shape[0]
     pre = jax.ShapeDtypeStruct((total, hidden), jnp.float32)
@@ -169,7 +186,7 @@
         (*pieces, gate_mat, up_mat, down_mat),
         (pre, pre, act, sums, sums),
         [pltpu.VMEM((total, width), jnp.bfloat16)],
-        flops=6 * total * width * hidden,
+        flops=estimate,
     )
 
 
@@ -254,21 +271,32 @@
     )
 
 
-def send_kernel(own, received, sent):
-    sent[...] = own[0] + received[0]
+def send_kernel(own, received, *sent):
+    rows = sent[0].shape[0]
+    for i, target in enumerate(sent):
+        here = slice(i * rows, (i + 1) * rows)
+        target[...] = own[0, here, :] + received[0, here, :]
+
+
+def slot_sum(own, received, arrived, slot, offset):
+    rows = LANES
+    half = rows // 2
+    here = slice(slot * rows, (slot + 1) * rows)
+    other = arrived[offset : offset + rows, :].astype(jnp.float32)
+    kept = own[1, here, :].astype(jnp.float32) + received[1, here, :].astype(jnp.float32)
+    return kept + jnp.concatenate([other[half:], other[:half]], axis=0)
 
 
 def slots_kernel(own, received, arrived, first, second):
-    rows = first.shape[0]
-    half = rows // 2
     for slot, target in enumerate((first, second)):
-        for which in range(2):
-            here = slice(slot * rows + which * half, slot * rows + (which + 1) * half)
-            there = slice(slot * rows + (1 - which) * half, slot * rows + (2 - which) * half)
-            terms = (own[1, here, :], received[1, here, :], arrived[there, :])
-            target[which * half : (which + 1) * half, :] = total_of(
-                [term.astype(jnp.float32) for term in terms]
-            ).astype(jnp.bfloat16)
+        target[...] = slot_sum(own, received, arrived, slot, slot * LANES).astype(target.dtype)
+
+
+def slot_kernel(slot, own, received, arrived, *refs):
+    whole = slot_sum(own, received, arrived, slot, 0)
+    if len(refs) > 1:
+        whole = whole + refs[0][...].astype(jnp.float32)
+    refs[-1][...] = whole.astype(refs[-1].dtype)
 
 
 def finish_outputs_kernel(*refs):
@@ -278,10 +306,11 @@
     columns[...] = whole.astype(jnp.bfloat16)
 
 
-def finish_inputs_kernel(experts, ids, counts, scores, clock, *refs):
+def finish_inputs_kernel(experts, ids, counts, scores, clock, own, received, arrived, *refs):
     columns, d_scores = refs[-2:]
     width = columns.shape[1]
-    whole = total_of([ref[...].astype(jnp.float32) for ref in refs[:-2]])
+    whole = slot_sum(own, received, arrived, 0, 0)
+    whole = total_of([whole] + [ref[...].astype(jnp.float32) for ref in refs[:-2]])
     whole = jnp.where(lax.axis_index("helper") == 0, whole, swap_halves(whole))
     columns[...] = whole[:, :width].astype(jnp.bfloat16)
     table = whole[:, width:].T
@@ -303,6 +332,7 @@
         both = lambda pairs: [(2 * a + c, 2 * b + c) for a, b in pairs for c in (0, 1)]
         self.near = both([(z, z ^ 1) for z in range(4)])
         self.far = both([(z, z ^ 2) for z in range(4)])
+        self.last = both([(z, z ^ 3) for z in range(4)])
         self.middle = both([(1, 2), (2, 1)])
         self.outward = both([(1, 0), (2, 3)])
         self.inward = both([(0, 1), (3, 2)])
@@ -321,27 +351,26 @@
         with jax.named_scope(self.label + "_across"):
             return lax.ppermute(array, "helper", self.sides)
 
-    def first_hops(self, own):
-        near = self.line(own, self.near)
-        far = self.line(own, self.far)
-        middle = self.line(own, self.middle)
-        return near, far, middle
-
     def chunk(self, *pieces):
         return [*pieces, *(self.sibling(p) for p in pieces)]
 
-    def send(self, own, received):
-        return call(
-            send_kernel,
-            self.label + "_send",
-            (own, received),
-            jax.ShapeDtypeStruct(own.shape[1:], own.dtype),
-        )
+    def send(self, own, received, parts=1):
+        _, rows, columns = own.shape
+        part = jax.ShapeDtypeStruct((rows // parts, columns), own.dtype)
+        return call(send_kernel, self.label + "_send", (own, received), (part,) * parts)
 
     def slots(self, own, received, arrived):
         rows, columns = arrived.shape
         slot = jax.ShapeDtypeStruct((rows // 2, columns), arrived.dtype)
         return call(slots_kernel, self.label + "_slots", (own, received, arrived), (slot, slot))
+
+    def slot(self, which, own, received, arrived, *others):
+        return call(
+            functools.partial(slot_kernel, which),
+            self.label + "_slot",
+            (own, received, arrived, *others),
+            jax.ShapeDtypeStruct(arrived.shape, arrived.dtype),
+        )
 
 
 def load_kernel(*refs):
@@ -365,10 +394,10 @@
         scratch_shapes=[pltpu.SemaphoreType.DMA((len(mats),))],
         compiler_params=pltpu.CompilerParams(vmem_limit_bytes=2**20),
         name="load",
-    )(*mats)
-
-
-def space(clock):
+    )(*(pltpu.with_memory_space_constraint(mat, pltpu.HBM) for mat in mats))
+
+
+def space(clock, flops=12 * 10**9):
     return pl.pallas_call(
         lambda old, new: None,
         out_shape=jax.ShapeDtypeStruct(clock.shape, clock.dtype),
@@ -376,9 +405,13 @@
         out_specs=pl.BlockSpec(memory_space=pl.ANY),
         input_output_aliases={0: 0},
         compiler_params=pltpu.CompilerParams(vmem_limit_bytes=2**20),
-        cost_estimate=pl.CostEstimate(flops=12 * 10**9, bytes_accessed=0, transcendentals=0),
+        cost_estimate=pl.CostEstimate(flops=flops, bytes_accessed=0, transcendentals=0),
         name="space",
     )(clock)
+
+
+def tick(clock):
+    return space(clock, 2 * 10**9)
 
 
 class Order:
@@ -399,76 +432,108 @@
     picks = (expert_ids.T, pick_counts[None, :], gate_scores.T)
     rows, grads, outs, ins = (FourChips(label) for label in ("rows", "grads", "out", "in"))
     order = Order()
+    hold = lambda value, *tokens: lax.optimization_barrier((value, tokens))[0]
 
     own, other, clock = order(lambda r: prepare_rows(*picks, r, experts), tokens)
-    near, far, middle = rows.first_hops(own)
+    near = rows.line(own, rows.near)
+    middle = rows.line(own, rows.middle)
     mats = order(load, gate_local, up_local, down_local)
+    clock = order(space, clock)
+    near, middle = hold((near, middle), clock)
+    far = rows.line(hold(own, near), rows.far)
     near_across = rows.across(near)
-    near_rows = rows.chunk(own, other, near, near_across)
+    clock = order(space, clock, also=(near, middle))
+    near_rows = rows.chunk(own, other, near, hold(near_across, clock))
+    near_gate, near_up, near_act, near_out, sent = order(
+        lambda *r: forward(r, *mats, experts, 0), *near_rows
+    )
+    near_received = outs.sibling(sent)
+    far = hold(far, near_act)
+    far_across = rows.across(far)
     relay = rows.line(far, rows.outward)
-    far_across = rows.across(far)
-    own, other = order(prepare_grads, grad_out, also=(far, middle, near))
-    near, far_grad, middle_grad = grads.first_hops(own)
-    near_grads = grads.chunk(own, other, near, grads.across(near))
-    last = order(jnp.add, middle, relay)
-    far_rows = rows.chunk(far, far_across, last, rows.across(last))
-
-    near_gate, near_up, near_act, near_out, sent = order(
-        lambda *r: forward(r, *mats, experts), *near_rows, also=far_across
-    )
-    near_received = outs.sibling(sent)
+    own, other = order(prepare_grads, grad_out, also=far)
+    far_grad = grads.line(own, grads.far)
+    clock = order(space, clock)
+    far_across, relay = hold((far_across, relay), clock)
+    last = order(jnp.add, middle, relay, also=far_across)
+    last_across = rows.across(last)
+    near = grads.line(hold(own, last), grads.near)
+    middle_grad = grads.line(hold(own, last), grads.middle)
+    clock = order(tick, clock, also=far_grad)
+    last_across, near, middle_grad = hold((last_across, near, middle_grad), clock)
+    far_rows = rows.chunk(far, far_across, last, last_across)
+    far_across = grads.across(far_grad)
+    near_across = grads.across(near)
     relay = grads.line(far_grad, grads.outward)
+    clock = order(space, clock, also=(last_across, near, middle_grad, far_grad))
+
     far_gate, far_up, far_act, far_out, sent = order(
-        lambda *r: forward(r, *mats, experts), *far_rows, also=(near, far_grad, middle_grad)
+        lambda *r: forward(r, *mats, experts, 6 * far.size * 8 * gate_local.shape[1]), *far_rows
     )
     far_received = outs.sibling(sent)
-    far_across = grads.across(far_grad)
+    relay, far_across, near_across = hold((relay, far_across, near_across), far_act)
+    near_grads = grads.chunk(own, other, near, near_across)
     last = order(jnp.add, middle_grad, relay)
-    far_grads = grads.chunk(far_grad, far_across, last, grads.across(last))
+    last_across = grads.across(last)
+    far_grads = grads.chunk(far_grad, far_across, last, last_across)
     clock = order(space, clock, also=(far_across, near_grads))
-    sent = order(outs.send, far_out, far_received)
+    (sent,) = order(outs.send, far_out, far_received)
     far_arrived = outs.across(sent)
+    clock = order(space, clock)
     step = lambda g, r, *pre: backward(g, r, *pre, *mats, experts)
     near_d_gate, near_d_up, near_in, sent = order(
         step, near_grads, near_rows, near_gate, near_up
     )
     near_in_received = ins.sibling(sent)
+    (sent,) = order(outs.send, near_out, near_received, also=last_across)
+    near_arrived = outs.across(sent)
     clock = order(space, clock, also=far_grads)
-    sent = order(outs.send, near_out, near_received)
-    near_arrived = outs.across(sent)
     far_d_gate, far_d_up, far_in, sent = order(step, far_grads, far_rows, far_gate, far_up)
     far_in_received = ins.sibling(sent)
     far_slot, last_slot = order(outs.slots, far_out, far_received, far_arrived)
-    relay = outs.line(last_slot, outs.inward)
-    middle = outs.line(last_slot, outs.middle)
-    clock = order(space, clock)
-    sent = order(ins.send, far_in, far_in_received)
-    far_in_arrived = ins.across(sent)
-    sent = order(ins.send, near_in, near_in_received)
-    near_in_arrived = ins.across(sent)
+    far_sum = outs.line(far_slot, outs.far)
+    last_sum = outs.line(last_slot, outs.last)
+    clock = order(space, clock)
+    far_sent, last_sent = order(lambda *s: ins.send(*s, parts=2), far_in, far_in_received)
+    last_arrived = ins.across(last_sent)
+    far_in_arrived = ins.across(far_sent)
+    own_sent, near_sent = order(lambda *s: ins.send(*s, parts=2), near_in, near_in_received)
+    near_in_arrived = ins.across(near_sent)
+    clock = order(space, clock)
     product_of = lambda name, by_hidden: lambda r, *acts: weights(name, r, acts, width, by_hidden)
     grad_down = order(
         product_of("grad_down", True), near_grads + far_grads, near_act, far_act
     )
     own_slot, near_slot = order(outs.slots, near_out, near_received, near_arrived)
-    near = outs.line(near_slot, outs.near)
-    far = outs.line(order(jnp.add, far_slot, relay), outs.far)
-    out_sums = (own_slot, far, near, middle)
+    near_sum = outs.line(near_slot, outs.near)
     all_rows = near_rows + far_rows
     grad_gate = order(product_of("grad_gate", False), all_rows, near_d_gate, far_d_gate)
-    far_slot, last_slot = order(ins.slots, far_in, far_in_received, far_in_arrived)
-    relay = ins.line(last_slot, ins.inward)
-    middle = ins.line(last_slot, ins.middle)
-    grad_up = order(product_of("grad_up", False), all_rows, near_d_up, far_d_up)
-    far = ins.line(order(jnp.add, far_slot, relay), ins.far)
-    own_slot, near_slot = order(ins.slots, near_in, near_in_received, near_in_arrived)
-    near = ins.line(near_slot, ins.near)
-    in_sums = (own_slot, far, near, middle)
-
+    slot = order(lambda *s: ins.slot(1, *s), far_in, far_in_received, last_arrived)
+    relay = ins.line(slot, ins.inward)
+    middle = ins.line(slot, ins.middle)
+    clock = order(space, clock)
+    grad_up = order(
+        product_of("grad_up", False), all_rows, near_d_up, far_d_up
+    )
+    slot = order(lambda *s: ins.slot(0, *s), far_in, far_in_received, far_in_arrived, relay)
+    far = ins.line(slot, ins.far)
+    own_in_arrived = ins.across(hold(own_sent, slot))
+    clock = order(space, clock)
+
+    slot = order(
+        lambda *s: ins.slot(1, *s), near_in, near_in_received, near_in_arrived, also=middle
+    )
+    near = ins.line(slot, ins.near)
+    clock = order(space, clock)
     columns = jax.ShapeDtypeStruct((tokens.shape[0], width // 2), jnp.bfloat16)
     output_cols = order(
-        lambda *sums: call(finish_outputs_kernel, "finish_outputs", sums, columns), *out_sums
-    )
+        lambda *sums: call(finish_outputs_kernel, "finish_outputs", sums, columns),
+        own_slot,
+        near_sum,
+        far_sum,
+        last_sum,
+    )
+    near, far, own_in_arrived = hold((near, far, own_in_arrived), output_cols)
     input_cols, d_scores = order(
         lambda *sums: call(
             functools.partial(finish_inputs_kernel, experts),
@@ -476,7 +541,12 @@
             (*picks, clock, *sums),
             (columns, jax.ShapeDtypeStruct(picks[2].shape, jnp.float32)),
         ),
-        *in_sums,
+        near_in,
+        near_in_received,
+        own_in_arrived,
+        far,
+        near,
+        middle,
     )
     return output_cols, input_cols, d_scores.T, grad_gate[None], grad_up[None], grad_down[None]
 

time: 175 us -> 168 us (0.960)
  local copies, waits for them, and re-layouts: 10.8 us -> 0.02 us
  Pallas kernels: 51.9 us -> 56.6 us
  waiting for transfers between devices: 65.4 us -> 67.4 us
  starting transfers between devices: 44.8 us -> 43 us
    ppermute x10 -> x12, waiting for transfers between devices: 20.2 us -> 33 us  [across(): return lax.ppermute(array, 'helper', self.sides)]
    ppermute x16 -> x15, waiting for transfers between devices: 45.2 us -> 34 us  [line(): return lax.ppermute(array, 'expert', pairs)]
    unnamed x26 -> x8, local copies, waits for them, and re-layouts: 10.8 us -> 0.02 us
    pallas_call x1, Pallas kernels: 0.87 us -> 4.68 us  [load(): pl.pallas_call(load_kernel, out_shape=tuple((jax.ShapeDtypeStruct(mat.sha...]
    ppermute x16 -> x15, starting transfers between devices: 29.7 us -> 26.8 us  [line(): return lax.ppermute(array, 'expert', pairs)]
    ppermute x10 -> x12, starting transfers between devices: 10.5 us -> 12.3 us  [across(): return lax.ppermute(array, 'helper', self.sides)]
  transfers between devices with their start and end apart: 46 -> 47, of which waited for: 8 -> 15; matrix products, arithmetic and copies ran while one was open for 0% -> 0% of each run, Pallas kernels for 29% -> 32%
where the time goes in v3:
time: 168 us
  waiting for transfers between devices  67.4 us (40%)
  Pallas kernels  56.6 us (34%)
  starting transfers between devices  43 us (26%)
    pallas_call x19, Pallas kernels, call(): pl.pallas_call(kernel, out_shape=out_shape, in_specs=[VMEM] * len(operand...  50.6 us
    ppermute x15, waiting for transfers between devices, line(): return lax.ppermute(array, 'expert', pairs)  34 us
    ppermute x12, waiting for transfers between devices, across(): return lax.ppermute(array, 'helper', self.sides)  33 us
    ppermute x15, starting transfers between devices, line(): return lax.ppermute(array, 'expert', pairs)  26.8 us
    ppermute x12, starting transfers between devices, across(): return lax.ppermute(array, 'helper', self.sides)  12.3 us
    pallas_call x1, Pallas kernels, load(): pl.pallas_call(load_kernel, out_shape=tuple((jax.ShapeDtypeStruct(mat.sha...  4.68 us
    ppermute x20, starting transfers between devices, sibling(): return lax.ppermute(array, 'expert', self.cores)  3.84 us
  transfers between devices with their start and end apart: 47, of which 15 were waited for; matrix products, arithmetic and copies ran while one was open for 0% of the time, Pallas kernels for 32%

profile of v3, /device:TPU:0, one launch (start us, length us, event | category | flops | bytes accessed | tf_op | source)
XLA Modules:
  0.0 168.2 jit_solution(17918169671789632676)
XLA Ops:
  0.6 1.3 prepare_rows.1
  2.4 0.7 collective-permute-start.1
  3.1 5.5 %collective-permute-start = (bf16[64,2176]{1,0:T(8,128)(2,1)S(1)}, bf16[64,2176]{1,0:T(8,128)(2,1)S(1)}, u32[]{:S(2)}, u32[]{:S(2)}) collective-permute-start(bf16[64,2176]{1,0:T(8,128)(2,1)S(1)} %get-tuple-element.393.refs_0_.refs_8_), channel_id=1, source_target_pairs={{0,4},{2,6},{4,0},{6,2},{8,12},{10,14},{12,8},{14,10},{1,5},{3,7},... | collective-permute-start | bytes 835592 | tf_op jit(solution)/shard_map/rows_line/ppermute | solution.py:344
  8.6 4.7 %load.1 = (bf16[2048,1024]{1,0:T(8,128)(2,1)S(1)}, bf16[2048,1024]{1,0:T(8,128)(2,1)S(1)}, bf16[1024,2048]{1,0:T(8,128)(2,1)S(1)}) custom-call(bf16[2048,1024]{1,0:T(8,128)(2,1)} %bitcast.16, bf16[2048,1024]{1,0:T(8,128)(2,1)} %bitcast.17, bf16[1024,2048]{1,0:T(8,128)(2,1)} %bitcast.18), custom_call_target="tpu_custom_call" | custom-call | tf_op jit(solution)/shard_map/load/pallas_call | solution.py:389
  13.3 2.3 %collective-permute-done.refs_2_.refs_10_ = bf16[64,2176]{1,0:T(8,128)(2,1)S(1)} collective-permute-done((bf16[64,2176]{1,0:T(8,128)(2,1)S(1)}, bf16[64,2176]{1,0:T(8,128)(2,1)S(1)}, u32[]{:S(2)}, u32[]{:S(2)}) %collective-permute-start) | collective-permute-done | bytes 278560 | tf_op jit(solution)/shard_map/rows_line/ppermute | solution.py:344
  15.6 1.5 collective-permute-start.2
  17.1 7.5 %collective-permute-done.2.refs_3_.refs_11_ = bf16[64,2176]{1,0:T(8,128)(2,1)S(1)} collective-permute-done((bf16[64,2176]{1,0:T(8,128)(2,1)S(1)}, bf16[64,2176]{1,0:T(8,128)(2,1)S(1)}, u32[]{:S(2)}, u32[]{:S(2)}) %collective-permute-start.2) | collective-permute-done | bytes 278560 | tf_op jit(solution)/shard_map/rows_across/ppermute | solution.py:352
  24.7 1.6 collective-permute-start.8
  26.3 6.7 %forward.2 = (f32[512,1024]{1,0:T(8,128)S(1)}, f32[512,1024]{1,0:T(8,128)S(1)}, bf16[512,1024]{1,0:T(8,128)(2,1)S(1)}, bf16[2,256,1024]{2,1,0:T(8,128)(2,1)S(1)}, bf16[2,256,1024]{2,1,0:T(8,128)(2,1)S(1)}) custom-call(bf16[64,2176]{1,0:T(8,128)(2,1)S(1)} %get-tuple-element.393.refs_0_.refs_8_, bf16[64,2176]{1,0:T(8,128)(2,1)S(1)} %get-tuple-element.394.refs_1_.refs_9_, ...), custom_call_target="tpu_custom_call" | custom-call | tf_op jit(solution)/shard_map/forward/pallas_call | solution.py:40
  33.0 7.6 %collective-permute-done.8.refs_0_.refs_8_ = bf16[64,2176]{1,0:T(8,128)(2,1)S(1)} collective-permute-done((bf16[64,2176]{1,0:T(8,128)(2,1)S(1)}, bf16[64,2176]{1,0:T(8,128)(2,1)S(1)}, u32[]{:S(2)}, u32[]{:S(2)}) %collective-permute-start.8) | collective-permute-done | bytes 278560 | tf_op jit(solution)/shard_map/rows_line/ppermute | solution.py:344
  40.6 1.3 collective-permute-start.10
  41.9 1.6 collective-permute-start.9
  43.5 2.7 %collective-permute-start.14 = (bf16[64,2048]{1,0:T(8,128)(2,1)S(1)}, bf16[64,2048]{1,0:T(8,128)(2,1)S(1)}, u32[]{:S(2)}, u32[]{:S(2)}) collective-permute-start(bf16[64,2048]{1,0:T(8,128)(2,1)S(1)} %get-tuple-element.348.refs_0_), channel_id=1, source_target_pairs={{0,8},{2,10},{4,12},{6,14},{8,0},{10,2},{12,4},{14,6},{1,9},{3,11}... | collective-permute-start | bytes 786440 | tf_op jit(solution)/shard_map/grads_line/ppermute | solution.py:344
  46.3 6.4 %collective-permute-done.10 = bf16[64,2176]{1,0:T(8,128)(2,1)S(1)} collective-permute-done((bf16[64,2176]{1,0:T(8,128)(2,1)S(1)}, bf16[64,2176]{1,0:T(8,128)(2,1)S(1)}, u32[]{:S(2)}, u32[]{:S(2)}) %collective-permute-start.10) | collective-permute-done | bytes 278560 | tf_op jit(solution)/shard_map/rows_line/ppermute | solution.py:344
  52.7 1.6 collective-permute-start.11
  54.3 0.7 collective-permute-start.13
  55.0 2.0 %collective-permute-start.12 = (bf16[64,2048]{1,0:T(8,128)(2,1)S(1)}, bf16[64,2048]{1,0:T(8,128)(2,1)S(1)}, u32[]{:S(2)}, u32[]{:S(2)}) collective-permute-start(bf16[64,2048]{1,0:T(8,128)(2,1)S(1)} %get-tuple-element.348.refs_0_), channel_id=1, source_target_pairs={{0,4},{2,6},{4,0},{6,2},{8,12},{10,14},{12,8},{14,10},{1,5},{3,7},... | collective-permute-start | bytes 786440 | tf_op jit(solution)/shard_map/grads_line/ppermute | solution.py:344
  56.9 1.9 %collective-permute-done.14.refs_0_.refs_8_ = bf16[64,2048]{1,0:T(8,128)(2,1)S(1)} collective-permute-done((bf16[64,2048]{1,0:T(8,128)(2,1)S(1)}, bf16[64,2048]{1,0:T(8,128)(2,1)S(1)}, u32[]{:S(2)}, u32[]{:S(2)}) %collective-permute-start.14) | collective-permute-done | bytes 262176 | tf_op jit(solution)/shard_map/grads_line/ppermute | solution.py:344
  59.3 4.1 %collective-permute-done.12.refs_2_ = bf16[64,2048]{1,0:T(8,128)(2,1)S(1)} collective-permute-done((bf16[64,2048]{1,0:T(8,128)(2,1)S(1)}, bf16[64,2048]{1,0:T(8,128)(2,1)S(1)}, u32[]{:S(2)}, u32[]{:S(2)}) %collective-permute-start.12) | collective-permute-done | bytes 262176 | tf_op jit(solution)/shard_map/grads_line/ppermute | solution.py:344
  65.0 1.5 collective-permute-start.15
  66.5 1.1 collective-permute-start.17
  67.6 6.7 %forward.3 = (f32[512,1024]{1,0:T(8,128)S(1)}, f32[512,1024]{1,0:T(8,128)S(1)}, bf16[512,1024]{1,0:T(8,128)(2,1)S(1)}, bf16[2,256,1024]{2,1,0:T(8,128)(2,1)S(1)}, bf16[2,256,1024]{2,1,0:T(8,128)(2,1)S(1)}) custom-call(bf16[64,2176]{1,0:T(8,128)(2,1)S(1)} %collective-permute-done.8.refs_0_.refs_8_, ...), custom_call_target="tpu_custom_call" | custom-call | flops 6845104128 | tf_op jit(solution)/shard_map/forward/pallas_call | solution.py:40
  74.4 0.8 collective-permute-done.15
  75.2 3.1 %collective-permute-done.17.refs_3_ = bf16[64,2048]{1,0:T(8,128)(2,1)S(1)} collective-permute-done((bf16[64,2048]{1,0:T(8,128)(2,1)S(1)}, bf16[64,2048]{1,0:T(8,128)(2,1)S(1)}, u32[]{:S(2)}, u32[]{:S(2)}) %collective-permute-start.17) | collective-permute-done | bytes 262176 | tf_op jit(solution)/shard_map/grads_across/ppermute | solution.py:352
  80.0 7.8 %collective-permute-done.27.refs_3_.refs_11_ = bf16[64,2048]{1,0:T(8,128)(2,1)S(1)} collective-permute-done((bf16[64,2048]{1,0:T(8,128)(2,1)S(1)}, bf16[64,2048]{1,0:T(8,128)(2,1)S(1)}, u32[]{:S(2)}, u32[]{:S(2)}) %collective-permute-start.27) | collective-permute-done | bytes 262176 | tf_op jit(solution)/shard_map/grads_across/ppermute | solution.py:352
  88.4 7.1 %backward.2 = (bf16[512,1024]{1,0:T(8,128)(2,1)S(1)}, bf16[512,1024]{1,0:T(8,128)(2,1)S(1)}, bf16[2,256,1152]{2,1,0:T(8,128)(2,1)S(1)}, bf16[2,256,1152]{2,1,0:T(8,128)(2,1)S(1)}) custom-call(bf16[64,2048]{1,0:T(8,128)(2,1)S(1)} %get-tuple-element.348.refs_0_, bf16[64,2048]{1,0:T(8,128)(2,1)S(1)} %get-tuple-element.349.refs_1_, ...), custom_call_target="tpu_custom_call" | custom-call | flops 6442450944 | tf_op jit(solution)/shard_map/backward/pallas_call | solution.py:40
  95.5 0.6 collective-permute-start.33
  96.2 7.4 %backward.3 = (bf16[512,1024]{1,0:T(8,128)(2,1)S(1)}, bf16[512,1024]{1,0:T(8,128)(2,1)S(1)}, bf16[2,256,1152]{2,1,0:T(8,128)(2,1)S(1)}, bf16[2,256,1152]{2,1,0:T(8,128)(2,1)S(1)}) custom-call(bf16[64,2048]{1,0:T(8,128)(2,1)S(1)} %collective-permute-done.14.refs_0_.refs_8_, bf16[64,2048]{1,0:T(8,128)(2,1)S(1)} %collective-permute-done.16.refs_1_.refs_9_, ...), custom_call_target="tpu_custom_call" | custom-call | flops 6442450944 | tf_op jit(solution)/shard_map/backward/pallas_call | solution.py:40
  104.1 1.5 collective-permute-start.28
  105.7 4.7 %collective-permute-done.33.arrived = bf16[256,1024]{1,0:T(8,128)(2,1)S(1)} collective-permute-done((bf16[256,1024]{1,0:T(8,128)(2,1)S(1)}, bf16[256,1024]{1,0:T(8,128)(2,1)S(1)}, u32[]{:S(2)}, u32[]{:S(2)}) %collective-permute-start.33) | collective-permute-done | bytes 524320 | tf_op jit(solution)/shard_map/out_across/ppermute | solution.py:352
  110.5 1.9 %collective-permute-start.37 = (bf16[128,1024]{1,0:T(8,128)(2,1)S(1)}, bf16[128,1024]{1,0:T(8,128)(2,1)S(1)}, u32[]{:S(2)}, u32[]{:S(2)}) collective-permute-start(bf16[128,1024]{1,0:T(8,128)(2,1)S(1)} %get-tuple-element.336), channel_id=1, source_target_pairs={{0,8},{2,10},{4,12},{6,14},{8,0},{10,2},{12,4},{14,6},{1,9},{3,11}... | collective-permute-start | bytes 786440 | tf_op jit(solution)/shard_map/out_line/ppermute | solution.py:344
  112.5 1.7 %collective-permute-start.38 = (bf16[128,1024]{1,0:T(8,128)(2,1)S(1)}, bf16[128,1024]{1,0:T(8,128)(2,1)S(1)}, u32[]{:S(2)}, u32[]{:S(2)}) collective-permute-start(bf16[128,1024]{1,0:T(8,128)(2,1)S(1)} %get-tuple-element.337), channel_id=1, source_target_pairs={{0,12},{2,14},{4,8},{6,10},{8,4},{10,6},{12,0},{14,2},{1,13},{3,15... | collective-permute-start | bytes 786440 | tf_op jit(solution)/shard_map/out_line/ppermute | solution.py:344
  114.3 0.6 collective-permute-start.40
  114.8 1.5 collective-permute-start.39
  116.5 6.6 %grad_down.1 = bf16[1024,2048]{1,0:T(8,128)(2,1)} custom-call(bf16[64,2048]{1,0:T(8,128)(2,1)S(1)} %get-tuple-element.348.refs_0_, bf16[64,2048]{1,0:T(8,128)(2,1)S(1)} %get-tuple-element.349.refs_1_, bf16[64,2048]{1,0:T(8,128)(2,1)S(1)} %collective-permute-done.12.refs_2_, bf16[64,2048]{1,0:T(8,128)(2,1)S(1)} %collective-permute-done.17.refs_3_, ...), custom_call_target="tpu_custom_call" | custom-call | flops 4294967296 | tf_op jit(solution)/shard_map/grad_down/pallas_call | solution.py:40
  123.3 6.6 %grad_gate.1 = bf16[2048,1024]{1,0:T(8,128)(2,1)} custom-call(bf16[64,2176]{1,0:T(8,128)(2,1)S(1)} %get-tuple-element.393.refs_0_.refs_8_, bf16[64,2176]{1,0:T(8,128)(2,1)S(1)} %get-tuple-element.394.refs_1_.refs_9_, bf16[64,2176]{1,0:T(8,128)(2,1)S(1)} %collective-permute-done.refs_2_.refs_10_, ...), custom_call_target="tpu_custom_call" | custom-call | flops 4294967296 | tf_op jit(solution)/shard_map/grad_gate/pallas_call | solution.py:40
  129.9 3.4 %collective-permute-done.39.arrived = bf16[128,1152]{1,0:T(8,128)(2,1)S(1)} collective-permute-done((bf16[128,1152]{1,0:T(8,128)(2,1)S(1)}, bf16[128,1152]{1,0:T(8,128)(2,1)S(1)}, u32[]{:S(2)}, u32[]{:S(2)}) %collective-permute-start.39) | collective-permute-done | bytes 294944 | tf_op jit(solution)/shard_map/in_across/ppermute | solution.py:352
  133.4 3.4 %collective-permute-start.41 = (bf16[128,1152]{1,0:T(8,128)(2,1)S(1)}, bf16[128,1152]{1,0:T(8,128)(2,1)S(1)}, u32[]{:S(2)}, u32[]{:S(2)}) collective-permute-start(bf16[128,1152]{1,0:T(8,128)(2,1)S(1)} %in_slot.3), channel_id=1, source_target_pairs={{0,4},{2,6},{12,8},{14,10},{1,5},{3,7},{13,9},{15,11},{16,20},{18,... | collective-permute-start | bytes 884744 | tf_op jit(solution)/shard_map/in_line/ppermute | solution.py:344
  136.8 6.6 %grad_up.1 = bf16[2048,1024]{1,0:T(8,128)(2,1)} custom-call(bf16[64,2176]{1,0:T(8,128)(2,1)S(1)} %get-tuple-element.393.refs_0_.refs_8_, bf16[64,2176]{1,0:T(8,128)(2,1)S(1)} %get-tuple-element.394.refs_1_.refs_9_, bf16[64,2176]{1,0:T(8,128)(2,1)S(1)} %collective-permute-done.refs_2_.refs_10_, bf16[64,2176]{1,0:T(8,128)(2,1)S(1)} %collective-permute-done.2.refs_3_.refs_11_, ...), custom_call_target="tpu_custom_call" | custom-call | flops 4294967296 | tf_op jit(solution)/shard_map/grad_up/pallas_call | solution.py:40
  143.9 0.7 collective-permute-start.43
  144.7 6.5 %collective-permute-done.42.arrived = bf16[128,1152]{1,0:T(8,128)(2,1)S(1)} collective-permute-done((bf16[128,1152]{1,0:T(8,128)(2,1)S(1)}, bf16[128,1152]{1,0:T(8,128)(2,1)S(1)}, u32[]{:S(2)}, u32[]{:S(2)}) %collective-permute-start.42) | collective-permute-done | bytes 294944 | tf_op jit(solution)/shard_map/in_across/ppermute | solution.py:352
  151.3 2.5 %collective-permute-start.44 = (bf16[128,1152]{1,0:T(8,128)(2,1)S(1)}, bf16[128,1152]{1,0:T(8,128)(2,1)S(1)}, u32[]{:S(2)}, u32[]{:S(2)}) collective-permute-start(bf16[128,1152]{1,0:T(8,128)(2,1)S(1)} %in_slot.5), channel_id=1, source_target_pairs={{0,4},{2,6},{4,0},{6,2},{8,12},{10,14},{12,8},{14,10},{1,5},{3,7},... | collective-permute-start | bytes 884744 | tf_op jit(solution)/shard_map/in_line/ppermute | solution.py:344
  153.8 0.7 collective-permute-start.45
  154.5 0.8 collective-permute-start.46
  155.4 0.9 finish_outputs.1
  156.2 7.9 %collective-permute-done.44.refs_1_ = bf16[128,1152]{1,0:T(8,128)(2,1)S(1)} collective-permute-done((bf16[128,1152]{1,0:T(8,128)(2,1)S(1)}, bf16[128,1152]{1,0:T(8,128)(2,1)S(1)}, u32[]{:S(2)}, u32[]{:S(2)}) %collective-permute-start.44) | collective-permute-done | bytes 294944 | tf_op jit(solution)/shard_map/in_line/ppermute | solution.py:344
  164.1 2.9 %collective-permute-done.45.refs_0_ = bf16[128,1152]{1,0:T(8,128)(2,1)S(1)} collective-permute-done((bf16[128,1152]{1,0:T(8,128)(2,1)S(1)}, bf16[128,1152]{1,0:T(8,128)(2,1)S(1)}, u32[]{:S(2)}, u32[]{:S(2)}) %collective-permute-start.45) | collective-permute-done | bytes 294944 | tf_op jit(solution)/shard_map/in_line/ppermute | solution.py:344
  167.0 1.1 finish_inputs.1
  (90 shorter events, 7.2 us)
Async XLA Ops:
  1.9 24.4 %collective-permute-start.3 = (bf16[64,2176]{1,0:T(8,128)(2,1)S(1)}, bf16[64,2176]{1,0:T(8,128)(2,1)S(1)}, u32[]{:S(2)}, u32[]{:S(2)}) collective-permute-start(bf16[64,2176]{1,0:T(8,128)(2,1)S(1)} %get-tuple-element.393.refs_0_.refs_8_), channel_id=1, source_target_pairs={{0,2},{2,0},{4,6},{6,4},{8,10},{10,8},{12,14},{14,12},{1,3},{3,1},... | collective-permute-start | bytes 835592 | tf_op jit(solution)/shard_map/rows_cores/ppermute | solution.py:348
  2.4 10.9 %collective-permute-start.1 = (bf16[64,2176]{1,0:T(8,128)(2,1)S(1)}, bf16[64,2176]{1,0:T(8,128)(2,1)S(1)}, u32[]{:S(2)}, u32[]{:S(2)}) collective-permute-start(bf16[64,2176]{1,0:T(8,128)(2,1)S(1)} %get-tuple-element.393.refs_0_.refs_8_), channel_id=1, source_target_pairs={{4,8},{6,10},{8,4},{10,6},{5,9},{7,11},{9,5},{11,7},{20,24},{22,26... | collective-permute-start | bytes 835592 | tf_op jit(solution)/shard_map/rows_line/ppermute | solution.py:344
  3.1 12.5 %collective-permute-start = (bf16[64,2176]{1,0:T(8,128)(2,1)S(1)}, bf16[64,2176]{1,0:T(8,128)(2,1)S(1)}, u32[]{:S(2)}, u32[]{:S(2)}) collective-permute-start(bf16[64,2176]{1,0:T(8,128)(2,1)S(1)} %get-tuple-element.393.refs_0_.refs_8_), channel_id=1, source_target_pairs={{0,4},{2,6},{4,0},{6,2},{8,12},{10,14},{12,8},{14,10},{1,5},{3,7},... | collective-permute-start | bytes 835592 | tf_op jit(solution)/shard_map/rows_line/ppermute | solution.py:344
  8.6 17.7 %collective-permute-start.4 = (bf16[64,2176]{1,0:T(8,128)(2,1)S(1)}, bf16[64,2176]{1,0:T(8,128)(2,1)S(1)}, u32[]{:S(2)}, u32[]{:S(2)}) collective-permute-start(bf16[64,2176]{1,0:T(8,128)(2,1)S(1)} %get-tuple-element.394.refs_1_.refs_9_), channel_id=1, source_target_pairs={{0,2},{2,0},{4,6},{6,4},{8,10},{10,8},{12,14},{14,12},{1,3},{3,1},... | collective-permute-start | bytes 835592 | tf_op jit(solution)/shard_map/rows_cores/ppermute | solution.py:348
  15.6 10.7 %collective-permute-start.5 = (bf16[64,2176]{1,0:T(8,128)(2,1)S(1)}, bf16[64,2176]{1,0:T(8,128)(2,1)S(1)}, u32[]{:S(2)}, u32[]{:S(2)}) collective-permute-start(bf16[64,2176]{1,0:T(8,128)(2,1)S(1)} %collective-permute-done.refs_2_.refs_10_), channel_id=1, source_target_pairs={{0,2},{2,0},{4,6},{6,4},{8,10},{10,8},{12,14},{14,12},{1,3},{3,1},... | collective-permute-start | bytes 835592 | tf_op jit(solution)/shard_map/rows_cores/ppermute | solution.py:348
  15.6 9.1 %collective-permute-start.2 = (bf16[64,2176]{1,0:T(8,128)(2,1)S(1)}, bf16[64,2176]{1,0:T(8,128)(2,1)S(1)}, u32[]{:S(2)}, u32[]{:S(2)}) collective-permute-start(bf16[64,2176]{1,0:T(8,128)(2,1)S(1)} %collective-permute-done.refs_2_.refs_10_), channel_id=1, source_target_pairs={{0,1},{1,0},{2,3},{3,2},{4,5},{5,4},{6,7},{7,6},{8,9},{9,8},{10,11... | collective-permute-start | bytes 835592 | tf_op jit(solution)/shard_map/rows_across/ppermute | solution.py:352
  17.1 26.4 %copy-start = (bf16[128,2048]{1,0:T(8,128)(2,1)S(1)}, bf16[128,2048]{1,0:T(8,128)(2,1)}, u32[]{:S(2)}) copy-start(bf16[128,2048]{1,0:T(8,128)(2,1)} %rows) | copy-start | bytes 1572868
  24.7 1.6 collective-permute-start.6
  24.7 15.9 %collective-permute-start.8 = (bf16[64,2176]{1,0:T(8,128)(2,1)S(1)}, bf16[64,2176]{1,0:T(8,128)(2,1)S(1)}, u32[]{:S(2)}, u32[]{:S(2)}) collective-permute-start(bf16[64,2176]{1,0:T(8,128)(2,1)S(1)} %get-tuple-element.393.refs_0_.refs_8_), channel_id=1, source_target_pairs={{0,8},{2,10},{4,12},{6,14},{8,0},{10,2},{12,4},{14,6},{1,9},{3,11}... | collective-permute-start | bytes 835592 | tf_op jit(solution)/shard_map/rows_line/ppermute | solution.py:344
  40.6 12.0 %collective-permute-start.10 = (bf16[64,2176]{1,0:T(8,128)(2,1)S(1)}, bf16[64,2176]{1,0:T(8,128)(2,1)S(1)}, u32[]{:S(2)}, u32[]{:S(2)}) collective-permute-start(bf16[64,2176]{1,0:T(8,128)(2,1)S(1)} %collective-permute-done.8.refs_0_.refs_8_), channel_id=1, source_target_pairs={{4,0},{6,2},{8,12},{10,14},{5,1},{7,3},{9,13},{11,15},{20,16},{22,... | collective-permute-start | bytes 835592 | tf_op jit(solution)/shard_map/rows_line/ppermute | solution.py:344
  41.9 10.8 %collective-permute-start.9 = (bf16[64,2176]{1,0:T(8,128)(2,1)S(1)}, bf16[64,2176]{1,0:T(8,128)(2,1)S(1)}, u32[]{:S(2)}, u32[]{:S(2)}) collective-permute-start(bf16[64,2176]{1,0:T(8,128)(2,1)S(1)} %collective-permute-done.8.refs_0_.refs_8_), channel_id=1, source_target_pairs={{0,1},{1,0},{2,3},{3,2},{4,5},{5,4},{6,7},{7,6},{8,9},{9,8},{10,11... | collective-permute-start | bytes 835592 | tf_op jit(solution)/shard_map/rows_across/ppermute | solution.py:352
  43.5 15.3 %collective-permute-start.14 = (bf16[64,2048]{1,0:T(8,128)(2,1)S(1)}, bf16[64,2048]{1,0:T(8,128)(2,1)S(1)}, u32[]{:S(2)}, u32[]{:S(2)}) collective-permute-start(bf16[64,2048]{1,0:T(8,128)(2,1)S(1)} %get-tuple-element.348.refs_0_), channel_id=1, source_target_pairs={{0,8},{2,10},{4,12},{6,14},{8,0},{10,2},{12,4},{14,6},{1,9},{3,11}... | collective-permute-start | bytes 786440 | tf_op jit(solution)/shard_map/grads_line/ppermute | solution.py:344
  52.7 10.7 %collective-permute-start.11 = (bf16[64,2176]{1,0:T(8,128)(2,1)S(1)}, bf16[64,2176]{1,0:T(8,128)(2,1)S(1)}, u32[]{:S(2)}, u32[]{:S(2)}) collective-permute-start(bf16[64,2176]{1,0:T(8,128)(2,1)S(1)} %add.6.refs_2_.refs_10_), channel_id=1, source_target_pairs={{0,1},{1,0},{2,3},{3,2},{4,5},{5,4},{6,7},{7,6},{8,9},{9,8},{10,11... | collective-permute-start | bytes 835592 | tf_op jit(solution)/shard_map/rows_across/ppermute | solution.py:352
  54.3 4.5 %collective-permute-start.13 = (bf16[64,2048]{1,0:T(8,128)(2,1)S(1)}, bf16[64,2048]{1,0:T(8,128)(2,1)S(1)}, u32[]{:S(2)}, u32[]{:S(2)}) collective-permute-start(bf16[64,2048]{1,0:T(8,128)(2,1)S(1)} %get-tuple-element.348.refs_0_), channel_id=1, source_target_pairs={{4,8},{6,10},{8,4},{10,6},{5,9},{7,11},{9,5},{11,7},{20,24},{22,26... | collective-permute-start | bytes 786440 | tf_op jit(solution)/shard_map/grads_line/ppermute | solution.py:344
  55.0 8.4 %collective-permute-start.12 = (bf16[64,2048]{1,0:T(8,128)(2,1)S(1)}, bf16[64,2048]{1,0:T(8,128)(2,1)S(1)}, u32[]{:S(2)}, u32[]{:S(2)}) collective-permute-start(bf16[64,2048]{1,0:T(8,128)(2,1)S(1)} %get-tuple-element.348.refs_0_), channel_id=1, source_target_pairs={{0,4},{2,6},{4,0},{6,2},{8,12},{10,14},{12,8},{14,10},{1,5},{3,7},... | collective-permute-start | bytes 786440 | tf_op jit(solution)/shard_map/grads_line/ppermute | solution.py:344
  56.9 7.0 %collective-permute-start.18 = (bf16[64,2176]{1,0:T(8,128)(2,1)S(1)}, bf16[64,2176]{1,0:T(8,128)(2,1)S(1)}, u32[]{:S(2)}, u32[]{:S(2)}) collective-permute-start(bf16[64,2176]{1,0:T(8,128)(2,1)S(1)} %collective-permute-done.8.refs_0_.refs_8_), channel_id=1, source_target_pairs={{0,2},{2,0},{4,6},{6,4},{8,10},{10,8},{12,14},{14,12},{1,3},{3,1},... | collective-permute-start | bytes 835592 | tf_op jit(solution)/shard_map/rows_cores/ppermute | solution.py:348
  58.8 20.1 %collective-permute-start.23 = (bf16[64,2048]{1,0:T(8,128)(2,1)S(1)}, bf16[64,2048]{1,0:T(8,128)(2,1)S(1)}, u32[]{:S(2)}, u32[]{:S(2)}) collective-permute-start(bf16[64,2048]{1,0:T(8,128)(2,1)S(1)} %get-tuple-element.349.refs_1_), channel_id=1, source_target_pairs={{0,2},{2,0},{4,6},{6,4},{8,10},{10,8},{12,14},{14,12},{1,3},{3,1},... | collective-permute-start | bytes 786440 | tf_op jit(solution)/shard_map/grads_cores/ppermute | solution.py:348
  58.8 5.2 %collective-permute-start.20 = (bf16[64,2176]{1,0:T(8,128)(2,1)S(1)}, bf16[64,2176]{1,0:T(8,128)(2,1)S(1)}, u32[]{:S(2)}, u32[]{:S(2)}) collective-permute-start(bf16[64,2176]{1,0:T(8,128)(2,1)S(1)} %add.6.refs_2_.refs_10_), channel_id=1, source_target_pairs={{0,2},{2,0},{4,6},{6,4},{8,10},{10,8},{12,14},{14,12},{1,3},{3,1},... | collective-permute-start | bytes 835592 | tf_op jit(solution)/shard_map/rows_cores/ppermute | solution.py:348
  63.4 1.6 collective-permute-start.19
  63.4 3.0 %collective-permute-start.21 = (bf16[64,2176]{1,0:T(8,128)(2,1)S(1)}, bf16[64,2176]{1,0:T(8,128)(2,1)S(1)}, u32[]{:S(2)}, u32[]{:S(2)}) collective-permute-start(bf16[64,2176]{1,0:T(8,128)(2,1)S(1)} %collective-permute-done.11.refs_3_.refs_11_), channel_id=1, source_target_pairs={{0,2},{2,0},{4,6},{6,4},{8,10},{10,8},{12,14},{14,12},{1,3},{3,1},... | collective-permute-start | bytes 835592 | tf_op jit(solution)/shard_map/rows_cores/ppermute | solution.py:348
  64.0 15.0 %collective-permute-start.22 = (bf16[64,2048]{1,0:T(8,128)(2,1)S(1)}, bf16[64,2048]{1,0:T(8,128)(2,1)S(1)}, u32[]{:S(2)}, u32[]{:S(2)}) collective-permute-start(bf16[64,2048]{1,0:T(8,128)(2,1)S(1)} %get-tuple-element.348.refs_0_), channel_id=1, source_target_pairs={{0,2},{2,0},{4,6},{6,4},{8,10},{10,8},{12,14},{14,12},{1,3},{3,1},... | collective-permute-start | bytes 786440 | tf_op jit(solution)/shard_map/grads_cores/ppermute | solution.py:348
  64.0 10.3 %collective-permute-start.16 = (bf16[64,2048]{1,0:T(8,128)(2,1)S(1)}, bf16[64,2048]{1,0:T(8,128)(2,1)S(1)}, u32[]{:S(2)}, u32[]{:S(2)}) collective-permute-start(bf16[64,2048]{1,0:T(8,128)(2,1)S(1)} %collective-permute-done.14.refs_0_.refs_8_), channel_id=1, source_target_pairs={{0,1},{1,0},{2,3},{3,2},{4,5},{5,4},{6,7},{7,6},{8,9},{9,8},{10,11... | collective-permute-start | bytes 786440 | tf_op jit(solution)/shard_map/grads_across/ppermute | solution.py:352
  65.0 10.2 %collective-permute-start.15 = (bf16[64,2048]{1,0:T(8,128)(2,1)S(1)}, bf16[64,2048]{1,0:T(8,128)(2,1)S(1)}, u32[]{:S(2)}, u32[]{:S(2)}) collective-permute-start(bf16[64,2048]{1,0:T(8,128)(2,1)S(1)} %collective-permute-done.14.refs_0_.refs_8_), channel_id=1, source_target_pairs={{4,0},{6,2},{8,12},{10,14},{5,1},{7,3},{9,13},{11,15},{20,16},{22,... | collective-permute-start | bytes 786440 | tf_op jit(solution)/shard_map/grads_line/ppermute | solution.py:344
  66.5 11.8 %collective-permute-start.17 = (bf16[64,2048]{1,0:T(8,128)(2,1)S(1)}, bf16[64,2048]{1,0:T(8,128)(2,1)S(1)}, u32[]{:S(2)}, u32[]{:S(2)}) collective-permute-start(bf16[64,2048]{1,0:T(8,128)(2,1)S(1)} %collective-permute-done.12.refs_2_), channel_id=1, source_target_pairs={{0,1},{1,0},{2,3},{3,2},{4,5},{5,4},{6,7},{7,6},{8,9},{9,8},{10,11... | collective-permute-start | bytes 786440 | tf_op jit(solution)/shard_map/grads_across/ppermute | solution.py:352
  74.3 5.2 %collective-permute-start.24 = (bf16[64,2048]{1,0:T(8,128)(2,1)S(1)}, bf16[64,2048]{1,0:T(8,128)(2,1)S(1)}, u32[]{:S(2)}, u32[]{:S(2)}) collective-permute-start(bf16[64,2048]{1,0:T(8,128)(2,1)S(1)} %collective-permute-done.12.refs_2_), channel_id=1, source_target_pairs={{0,2},{2,0},{4,6},{6,4},{8,10},{10,8},{12,14},{14,12},{1,3},{3,1},... | collective-permute-start | bytes 786440 | tf_op jit(solution)/shard_map/grads_cores/ppermute | solution.py:348
  78.3 1.7 collective-permute-start.25
  78.3 17.2 %collective-permute-start.7 = (bf16[2,256,1024]{2,1,0:T(8,128)(2,1)S(1)}, bf16[2,256,1024]{2,1,0:T(8,128)(2,1)S(1)}, u32[]{:S(2)}, u32[]{:S(2)}) collective-permute-start(bf16[2,256,1024]{2,1,0:T(8,128)(2,1)S(1)} %get-tuple-element.244), channel_id=1, source_target_pairs={{0,2},{2,0},{4,6},{6,4},{8,10},{10,8},{12,14},{14,12},{1,3},{3,1},... | collective-permute-start | bytes 3145736 | tf_op jit(solution)/shard_map/out_cores/ppermute | solution.py:348
  78.9 17.2 %collective-permute-start.29 = (bf16[64,2048]{1,0:T(8,128)(2,1)S(1)}, bf16[64,2048]{1,0:T(8,128)(2,1)S(1)}, u32[]{:S(2)}, u32[]{:S(2)}) collective-permute-start(bf16[64,2048]{1,0:T(8,128)(2,1)S(1)} %collective-permute-done.14.refs_0_.refs_8_), channel_id=1, source_target_pairs={{0,2},{2,0},{4,6},{6,4},{8,10},{10,8},{12,14},{14,12},{1,3},{3,1},... | collective-permute-start | bytes 786440 | tf_op jit(solution)/shard_map/grads_cores/ppermute | solution.py:348
  79.0 17.2 %collective-permute-start.31 = (bf16[64,2048]{1,0:T(8,128)(2,1)S(1)}, bf16[64,2048]{1,0:T(8,128)(2,1)S(1)}, u32[]{:S(2)}, u32[]{:S(2)}) collective-permute-start(bf16[64,2048]{1,0:T(8,128)(2,1)S(1)} %add.7.refs_2_.refs_10_), channel_id=1, source_target_pairs={{0,2},{2,0},{4,6},{6,4},{8,10},{10,8},{12,14},{14,12},{1,3},{3,1},... | collective-permute-start | bytes 786440 | tf_op jit(solution)/shard_map/grads_cores/ppermute | solution.py:348
  79.5 8.3 %collective-permute-start.27 = (bf16[64,2048]{1,0:T(8,128)(2,1)S(1)}, bf16[64,2048]{1,0:T(8,128)(2,1)S(1)}, u32[]{:S(2)}, u32[]{:S(2)}) collective-permute-start(bf16[64,2048]{1,0:T(8,128)(2,1)S(1)} %add.7.refs_2_.refs_10_), channel_id=1, source_target_pairs={{0,1},{1,0},{2,3},{3,2},{4,5},{5,4},{6,7},{7,6},{8,9},{9,8},{10,11... | collective-permute-start | bytes 786440 | tf_op jit(solution)/shard_map/grads_across/ppermute | solution.py:352
  80.0 7.8 %collective-permute-start.26 = (bf16[2,256,1024]{2,1,0:T(8,128)(2,1)S(1)}, bf16[2,256,1024]{2,1,0:T(8,128)(2,1)S(1)}, u32[]{:S(2)}, u32[]{:S(2)}) collective-permute-start(bf16[2,256,1024]{2,1,0:T(8,128)(2,1)S(1)} %get-tuple-element.278), channel_id=1, source_target_pairs={{0,2},{2,0},{4,6},{6,4},{8,10},{10,8},{12,14},{14,12},{1,3},{3,1},... | collective-permute-start | bytes 3145736 | tf_op jit(solution)/shard_map/out_cores/ppermute | solution.py:348
  87.8 8.4 %collective-permute-start.30 = (bf16[64,2048]{1,0:T(8,128)(2,1)S(1)}, bf16[64,2048]{1,0:T(8,128)(2,1)S(1)}, u32[]{:S(2)}, u32[]{:S(2)}) collective-permute-start(bf16[64,2048]{1,0:T(8,128)(2,1)S(1)} %collective-permute-done.16.refs_1_.refs_9_), channel_id=1, source_target_pairs={{0,2},{2,0},{4,6},{6,4},{8,10},{10,8},{12,14},{14,12},{1,3},{3,1},... | collective-permute-start | bytes 786440 | tf_op jit(solution)/shard_map/grads_cores/ppermute | solution.py:348
  87.8 8.4 %collective-permute-start.32 = (bf16[64,2048]{1,0:T(8,128)(2,1)S(1)}, bf16[64,2048]{1,0:T(8,128)(2,1)S(1)}, u32[]{:S(2)}, u32[]{:S(2)}) collective-permute-start(bf16[64,2048]{1,0:T(8,128)(2,1)S(1)} %collective-permute-done.27.refs_3_.refs_11_), channel_id=1, source_target_pairs={{0,2},{2,0},{4,6},{6,4},{8,10},{10,8},{12,14},{14,12},{1,3},{3,1},... | collective-permute-start | bytes 786440 | tf_op jit(solution)/shard_map/grads_cores/ppermute | solution.py:348
  95.5 14.9 %collective-permute-start.33 = (bf16[256,1024]{1,0:T(8,128)(2,1)S(1)}, bf16[256,1024]{1,0:T(8,128)(2,1)S(1)}, u32[]{:S(2)}, u32[]{:S(2)}) collective-permute-start(bf16[256,1024]{1,0:T(8,128)(2,1)S(1)} %out_send.2), channel_id=1, source_target_pairs={{0,1},{1,0},{2,3},{3,2},{4,5},{5,4},{6,7},{7,6},{8,9},{9,8},{10,11... | collective-permute-start | bytes 1572872 | tf_op jit(solution)/shard_map/out_across/ppermute | solution.py:352
  103.6 10.6 %collective-permute-start.35 = (bf16[2,256,1152]{2,1,0:T(8,128)(2,1)S(1)}, bf16[2,256,1152]{2,1,0:T(8,128)(2,1)S(1)}, u32[]{:S(2)}, u32[]{:S(2)}) collective-permute-start(bf16[2,256,1152]{2,1,0:T(8,128)(2,1)S(1)} %get-tuple-element.332), channel_id=1, source_target_pairs={{0,2},{2,0},{4,6},{6,4},{8,10},{10,8},{12,14},{14,12},{1,3},{3,1},... | collective-permute-start | bytes 3538952 | tf_op jit(solution)/shard_map/in_cores/ppermute | solution.py:348
  103.6 11.2 %collective-permute-start.34 = (bf16[2,256,1152]{2,1,0:T(8,128)(2,1)S(1)}, bf16[2,256,1152]{2,1,0:T(8,128)(2,1)S(1)}, u32[]{:S(2)}, u32[]{:S(2)}) collective-permute-start(bf16[2,256,1152]{2,1,0:T(8,128)(2,1)S(1)} %get-tuple-element.307), channel_id=1, source_target_pairs={{0,2},{2,0},{4,6},{6,4},{8,10},{10,8},{12,14},{14,12},{1,3},{3,1},... | collective-permute-start | bytes 3538952 | tf_op jit(solution)/shard_map/in_cores/ppermute | solution.py:348
  104.1 18.9 %collective-permute-start.28 = (bf16[256,1024]{1,0:T(8,128)(2,1)S(1)}, bf16[256,1024]{1,0:T(8,128)(2,1)S(1)}, u32[]{:S(2)}, u32[]{:S(2)}) collective-permute-start(bf16[256,1024]{1,0:T(8,128)(2,1)S(1)} %out_send.3), channel_id=1, source_target_pairs={{0,1},{1,0},{2,3},{3,2},{4,5},{5,4},{6,7},{7,6},{8,9},{9,8},{10,11... | collective-permute-start | bytes 1572872 | tf_op jit(solution)/shard_map/out_across/ppermute | solution.py:352
  110.5 44.0 %collective-permute-start.37 = (bf16[128,1024]{1,0:T(8,128)(2,1)S(1)}, bf16[128,1024]{1,0:T(8,128)(2,1)S(1)}, u32[]{:S(2)}, u32[]{:S(2)}) collective-permute-start(bf16[128,1024]{1,0:T(8,128)(2,1)S(1)} %get-tuple-element.336), channel_id=1, source_target_pairs={{0,8},{2,10},{4,12},{6,14},{8,0},{10,2},{12,4},{14,6},{1,9},{3,11}... | collective-permute-start | bytes 786440 | tf_op jit(solution)/shard_map/out_line/ppermute | solution.py:344
  112.5 42.9 %collective-permute-start.38 = (bf16[128,1024]{1,0:T(8,128)(2,1)S(1)}, bf16[128,1024]{1,0:T(8,128)(2,1)S(1)}, u32[]{:S(2)}, u32[]{:S(2)}) collective-permute-start(bf16[128,1024]{1,0:T(8,128)(2,1)S(1)} %get-tuple-element.337), channel_id=1, source_target_pairs={{0,12},{2,14},{4,8},{6,10},{8,4},{10,6},{12,0},{14,2},{1,13},{3,15... | collective-permute-start | bytes 786440 | tf_op jit(solution)/shard_map/out_line/ppermute | solution.py:344
  114.3 29.1 %collective-permute-start.40 = (bf16[128,1152]{1,0:T(8,128)(2,1)S(1)}, bf16[128,1152]{1,0:T(8,128)(2,1)S(1)}, u32[]{:S(2)}, u32[]{:S(2)}) collective-permute-start(bf16[128,1152]{1,0:T(8,128)(2,1)S(1)} %get-tuple-element.341), channel_id=1, source_target_pairs={{0,1},{1,0},{2,3},{3,2},{4,5},{5,4},{6,7},{7,6},{8,9},{9,8},{10,11... | collective-permute-start | bytes 884744 | tf_op jit(solution)/shard_map/in_across/ppermute | solution.py:352
  114.8 18.4 %collective-permute-start.39 = (bf16[128,1152]{1,0:T(8,128)(2,1)S(1)}, bf16[128,1152]{1,0:T(8,128)(2,1)S(1)}, u32[]{:S(2)}, u32[]{:S(2)}) collective-permute-start(bf16[128,1152]{1,0:T(8,128)(2,1)S(1)} %get-tuple-element.342), channel_id=1, source_target_pairs={{0,1},{1,0},{2,3},{3,2},{4,5},{5,4},{6,7},{7,6},{8,9},{9,8},{10,11... | collective-permute-start | bytes 884744 | tf_op jit(solution)/shard_map/in_across/ppermute | solution.py:352
  123.2 32.2 %collective-permute-start.36 = (bf16[128,1024]{1,0:T(8,128)(2,1)S(1)}, bf16[128,1024]{1,0:T(8,128)(2,1)S(1)}, u32[]{:S(2)}, u32[]{:S(2)}) collective-permute-start(bf16[128,1024]{1,0:T(8,128)(2,1)S(1)} %get-tuple-element.370), channel_id=1, source_target_pairs={{0,4},{2,6},{4,0},{6,2},{8,12},{10,14},{12,8},{14,10},{1,5},{3,7},... | collective-permute-start | bytes 786440 | tf_op jit(solution)/shard_map/out_line/ppermute | solution.py:344
  133.4 10.5 %collective-permute-start.41 = (bf16[128,1152]{1,0:T(8,128)(2,1)S(1)}, bf16[128,1152]{1,0:T(8,128)(2,1)S(1)}, u32[]{:S(2)}, u32[]{:S(2)}) collective-permute-start(bf16[128,1152]{1,0:T(8,128)(2,1)S(1)} %in_slot.3), channel_id=1, source_target_pairs={{0,4},{2,6},{12,8},{14,10},{1,5},{3,7},{13,9},{15,11},{16,20},{18,... | collective-permute-start | bytes 884744 | tf_op jit(solution)/shard_map/in_line/ppermute | solution.py:344
  143.4 7.8 %collective-permute-start.42 = (bf16[128,1152]{1,0:T(8,128)(2,1)S(1)}, bf16[128,1152]{1,0:T(8,128)(2,1)S(1)}, u32[]{:S(2)}, u32[]{:S(2)}) collective-permute-start(bf16[128,1152]{1,0:T(8,128)(2,1)S(1)} %get-tuple-element.346), channel_id=1, source_target_pairs={{0,1},{1,0},{2,3},{3,2},{4,5},{5,4},{6,7},{7,6},{8,9},{9,8},{10,11... | collective-permute-start | bytes 884744 | tf_op jit(solution)/shard_map/in_across/ppermute | solution.py:352
  143.9 7.3 %collective-permute-start.43 = (bf16[128,1152]{1,0:T(8,128)(2,1)S(1)}, bf16[128,1152]{1,0:T(8,128)(2,1)S(1)}, u32[]{:S(2)}, u32[]{:S(2)}) collective-permute-start(bf16[128,1152]{1,0:T(8,128)(2,1)S(1)} %in_slot.3), channel_id=1, source_target_pairs={{4,8},{6,10},{8,4},{10,6},{5,9},{7,11},{9,5},{11,7},{20,24},{22,26... | collective-permute-start | bytes 884744 | tf_op jit(solution)/shard_map/in_line/ppermute | solution.py:344
  151.3 12.8 %collective-permute-start.44 = (bf16[128,1152]{1,0:T(8,128)(2,1)S(1)}, bf16[128,1152]{1,0:T(8,128)(2,1)S(1)}, u32[]{:S(2)}, u32[]{:S(2)}) collective-permute-start(bf16[128,1152]{1,0:T(8,128)(2,1)S(1)} %in_slot.5), channel_id=1, source_target_pairs={{0,4},{2,6},{4,0},{6,2},{8,12},{10,14},{12,8},{14,10},{1,5},{3,7},... | collective-permute-start | bytes 884744 | tf_op jit(solution)/shard_map/in_line/ppermute | solution.py:344
  153.8 13.2 %collective-permute-start.45 = (bf16[128,1152]{1,0:T(8,128)(2,1)S(1)}, bf16[128,1152]{1,0:T(8,128)(2,1)S(1)}, u32[]{:S(2)}, u32[]{:S(2)}) collective-permute-start(bf16[128,1152]{1,0:T(8,128)(2,1)S(1)} %in_slot.4), channel_id=1, source_target_pairs={{0,8},{2,10},{4,12},{6,14},{8,0},{10,2},{12,4},{14,6},{1,9},{3,11}... | collective-permute-start | bytes 884744 | tf_op jit(solution)/shard_map/in_line/ppermute | solution.py:344
  154.5 9.6 %collective-permute-start.46 = (bf16[128,1152]{1,0:T(8,128)(2,1)S(1)}, bf16[128,1152]{1,0:T(8,128)(2,1)S(1)}, u32[]{:S(2)}, u32[]{:S(2)}) collective-permute-start(bf16[128,1152]{1,0:T(8,128)(2,1)S(1)} %get-tuple-element.424), channel_id=1, source_target_pairs={{0,1},{1,0},{2,3},{3,2},{4,5},{5,4},{6,7},{7,6},{8,9},{9,8},{10,11... | collective-permute-start | bytes 884744 | tf_op jit(solution)/shard_map/in_across/ppermute | solution.py:352
  (3 other events, 47.2 us)

commit v4 on v3

--- a/solution.py
+++ b/solution.py
@@ -73,7 +73,7 @@
 
 
 def prepare_rows_kernel(experts, *refs):
-    sources, (own, other, clock), targets, sems = refs[:4], refs[4:7], refs[7:11], refs[11]
+    sources, (own, pair, clock), targets, sems = refs[:4], refs[4:7], refs[7:11], refs[11]
     ids, counts, scores, rows = targets
     copies = [
         pltpu.make_async_copy(source, target, sems.at[i])
@@ -97,9 +97,12 @@
 
         @pl.when(lax.axis_index("helper") == side)
         def _(side=side):
-            for target, which in ((own, side), (other, 1 - side)):
-                target[:, :width] = half_at(rows, which)
-                target[:, width:] = half_at(table, which)
+            own[:, :width] = half_at(rows, side)
+            own[:, width:] = half_at(table, side)
+            for i, which in enumerate((side, 1 - side)):
+                here = slice(i * total // 2, (i + 1) * total // 2)
+                pair[here, :width] = half_at(rows, which)
+                pair[here, width:] = half_at(table, which)
 
 
 def prepare_rows(ids, counts, scores, rows, experts):
@@ -108,7 +111,11 @@
     operands = (ids, counts, scores, rows)
     return pl.pallas_call(
         functools.partial(prepare_rows_kernel, experts),
-        out_shape=(piece, piece, jax.ShapeDtypeStruct((8, LANES), jnp.float32)),
+        out_shape=(
+            piece,
+            jax.ShapeDtypeStruct((total, width + LANES), jnp.bfloat16),
+            jax.ShapeDtypeStruct((8, LANES), jnp.float32),
+        ),
         in_specs=[pl.BlockSpec(memory_space=pltpu.HBM)] * len(operands),
         out_specs=(VMEM,) * 3,
         scratch_shapes=[
@@ -120,19 +127,38 @@
     )(*(pltpu.with_memory_space_constraint(operand, pltpu.HBM) for operand in operands))
 
 
-def prepare_grads_kernel(rows, own, other):
+def prepare_grads_kernel(rows, own, pair):
+    half = rows.shape[0] // 2
     for side in range(2):
 
         @pl.when(lax.axis_index("helper") == side)
         def _(side=side):
             own[...] = half_at(rows, side)
-            other[...] = half_at(rows, 1 - side)
+            pair[:half, :] = half_at(rows, side)
+            pair[half:, :] = half_at(rows, 1 - side)
 
 
 def prepare_grads(rows):
     total, width = rows.shape
     piece = jax.ShapeDtypeStruct((total // 2, width), jnp.bfloat16)
-    return call(prepare_grads_kernel, "prepare_grads", (rows,), (piece, piece))
+    return call(
+        prepare_grads_kernel,
+        "prepare_grads",
+        (rows,),
+        (piece, jax.ShapeDtypeStruct(rows.shape, jnp.bfloat16)),
+    )
+
+
+def pair_kernel(first, second, pair):
+    half = first.shape[0]
+    pair[:half, :] = first[...]
+    pair[half:, :] = second[...]
+
+
+def pair_up(first, second):
+    rows, width = first.shape
+    shape = jax.ShapeDtypeStruct((2 * rows, width), first.dtype)
+    return call(pair_kernel, "pair", (first, second), shape)
 
 
 def lay_out(pieces, target, columns):
@@ -150,7 +176,7 @@
 
 
 def forward_kernel(experts, tile, *refs):
-    pieces, refs = refs[:8], refs[8:]
+    pieces, refs = refs[:4], refs[4:]
     gate_mat, up_mat, down_mat, pre_gate, pre_up, gated, own, other, rows = refs
     width = rows.shape[1]
     half = width // 2
@@ -176,7 +202,7 @@
 
 def forward(pieces, gate_mat, up_mat, down_mat, experts, estimate):
     width, hidden = gate_mat.shape
-    total = 8 * pieces[0].shape[0]
+    total = 4 * pieces[0].shape[0]
     pre = jax.ShapeDtypeStruct((total, hidden), jnp.float32)
     act = jax.ShapeDtypeStruct((total, hidden), jnp.bfloat16)
     sums = jax.ShapeDtypeStruct((2, total // 2, width // 2), jnp.bfloat16)
@@ -191,7 +217,7 @@
 
 
 def backward_kernel(experts, tile, *refs):
-    pieces, gate_pieces, refs = refs[:8], refs[8:16], refs[16:]
+    pieces, gate_pieces, refs = refs[:4], refs[4:8], refs[8:]
     down_mat, pre_gate, pre_up, gate_mat, up_mat = refs[:5]
     d_gate, d_up, own, other, grads = refs[5:]
     total, width = grads.shape
@@ -245,7 +271,7 @@
 
 
 def weights_kernel(width, hidden, tile, *refs):
-    pieces, refs = refs[:16], refs[16:]
+    pieces, refs = refs[:8], refs[8:]
     first, second, grad, rows, acts = refs
     lay_out(pieces, rows, slice(0, width))
     lay_out((first, second), acts, slice(0, hidden))
@@ -351,9 +377,6 @@
         with jax.named_scope(self.label + "_across"):
             return lax.ppermute(array, "helper", self.sides)
 
-    def chunk(self, *pieces):
-        return [*pieces, *(self.sibling(p) for p in pieces)]
-
     def send(self, own, received, parts=1):
         _, rows, columns = own.shape
         part = jax.ShapeDtypeStruct((rows // parts, columns), own.dtype)
@@ -397,7 +420,7 @@
     )(*(pltpu.with_memory_space_constraint(mat, pltpu.HBM) for mat in mats))
 
 
-def space(clock, flops=12 * 10**9):
+def space(clock):
     return pl.pallas_call(
         lambda old, new: None,
         out_shape=jax.ShapeDtypeStruct(clock.shape, clock.dtype),
@@ -405,13 +428,9 @@
         out_specs=pl.BlockSpec(memory_space=pl.ANY),
         input_output_aliases={0: 0},
         compiler_params=pltpu.CompilerParams(vmem_limit_bytes=2**20),
-        cost_estimate=pl.CostEstimate(flops=flops, bytes_accessed=0, transcendentals=0),
+        cost_estimate=pl.CostEstimate(flops=12 * 10**9, bytes_accessed=0, transcendentals=0),
         name="space",
     )(clock)
-
-
-def tick(clock):
-    return space(clock, 2 * 10**9)
 
 
 class Order:
@@ -428,103 +447,100 @@
 
 def lined_up(tokens, expert_ids, pick_counts, gate_scores, gate_local, up_local, down_local, grad_out):
     experts = lax.axis_size("expert")
-    width = tokens.shape[1]
+    width, hidden = gate_local.shape
     picks = (expert_ids.T, pick_counts[None, :], gate_scores.T)
     rows, grads, outs, ins = (FourChips(label) for label in ("rows", "grads", "out", "in"))
     order = Order()
     hold = lambda value, *tokens: lax.optimization_barrier((value, tokens))[0]
-
-    own, other, clock = order(lambda r: prepare_rows(*picks, r, experts), tokens)
+    ahead = lambda *pieces: forward(pieces, *mats, experts, 24 * tokens.size * hidden)
+    back = lambda g, r, *pre: backward(g, r, *pre, *mats, experts)
+    product_of = lambda name, by_hidden: lambda r, *acts: weights(name, r, acts, width, by_hidden)
+
+    own, pair, clock = order(lambda r: prepare_rows(*picks, r, experts), tokens)
     near = rows.line(own, rows.near)
     middle = rows.line(own, rows.middle)
+    sibling_pair = rows.sibling(pair)
     mats = order(load, gate_local, up_local, down_local)
-    clock = order(space, clock)
-    near, middle = hold((near, middle), clock)
+    near, sibling_pair = hold((near, sibling_pair), mats)
+    near_across = rows.across(near)
     far = rows.line(hold(own, near), rows.far)
-    near_across = rows.across(near)
-    clock = order(space, clock, also=(near, middle))
-    near_rows = rows.chunk(own, other, near, hold(near_across, clock))
-    near_gate, near_up, near_act, near_out, sent = order(
-        lambda *r: forward(r, *mats, experts, 0), *near_rows
-    )
-    near_received = outs.sibling(sent)
-    far = hold(far, near_act)
+    near_first = pair
+    near_sibling = sibling_pair
+
+    own, pair = order(prepare_grads, grad_out, also=(far, middle))
     far_across = rows.across(far)
     relay = rows.line(far, rows.outward)
-    own, other = order(prepare_grads, grad_out, also=far)
     far_grad = grads.line(own, grads.far)
-    clock = order(space, clock)
-    far_across, relay = hold((far_across, relay), clock)
-    last = order(jnp.add, middle, relay, also=far_across)
+    sibling_pair = grads.sibling(pair)
+    near_pair = order(pair_up, near, near_across)
+    near_rows = [near_first, near_pair, near_sibling, rows.sibling(near_pair)]
+    near_gate, near_up, near_act, near_out, sent = order(ahead, *near_rows)
+    near_received = outs.sibling(sent)
+
+    relay, far_across = hold((relay, far_across), near_act)
+    last = order(jnp.add, middle, relay)
     last_across = rows.across(last)
     near = grads.line(hold(own, last), grads.near)
     middle_grad = grads.line(hold(own, last), grads.middle)
-    clock = order(tick, clock, also=far_grad)
-    last_across, near, middle_grad = hold((last_across, near, middle_grad), clock)
-    far_rows = rows.chunk(far, far_across, last, last_across)
+    far_pair = order(pair_up, far, far_across, also=sibling_pair)
+    far_sibling = rows.sibling(far_pair)
+    clock = order(space, clock, also=far_grad)
+    last_across, near, middle_grad, far_sibling = hold(
+        (last_across, near, middle_grad, far_sibling), clock
+    )
     far_across = grads.across(far_grad)
+    relay = grads.line(far_grad, grads.outward)
+    last_pair = order(pair_up, last, last_across, also=(far_grad, far_sibling))
+    far_rows = [far_pair, last_pair, far_sibling, rows.sibling(last_pair)]
     near_across = grads.across(near)
-    relay = grads.line(far_grad, grads.outward)
-    clock = order(space, clock, also=(last_across, near, middle_grad, far_grad))
-
-    far_gate, far_up, far_act, far_out, sent = order(
-        lambda *r: forward(r, *mats, experts, 6 * far.size * 8 * gate_local.shape[1]), *far_rows
-    )
+    far_gate, far_up, far_act, far_out, sent = order(ahead, *far_rows, also=(near, middle_grad))
     far_received = outs.sibling(sent)
+
     relay, far_across, near_across = hold((relay, far_across, near_across), far_act)
-    near_grads = grads.chunk(own, other, near, near_across)
     last = order(jnp.add, middle_grad, relay)
     last_across = grads.across(last)
-    far_grads = grads.chunk(far_grad, far_across, last, last_across)
-    clock = order(space, clock, also=(far_across, near_grads))
-    (sent,) = order(outs.send, far_out, far_received)
+    near_pair = order(pair_up, near, near_across)
+    near_grads = [pair, near_pair, sibling_pair, grads.sibling(near_pair)]
+    far_pair = order(pair_up, far_grad, far_across)
+    far_sibling = grads.sibling(far_pair)
+    clock = order(space, clock)
+    far_received, near_received = hold((far_received, near_received), clock)
+    (sent,) = order(outs.send, far_out, far_received, also=(far_sibling, near_grads))
     far_arrived = outs.across(sent)
-    clock = order(space, clock)
-    step = lambda g, r, *pre: backward(g, r, *pre, *mats, experts)
+    (near_sent,) = order(outs.send, near_out, near_received)
     near_d_gate, near_d_up, near_in, sent = order(
-        step, near_grads, near_rows, near_gate, near_up
+        back, near_grads, near_rows, near_gate, near_up
     )
     near_in_received = ins.sibling(sent)
-    (sent,) = order(outs.send, near_out, near_received, also=last_across)
-    near_arrived = outs.across(sent)
-    clock = order(space, clock, also=far_grads)
-    far_d_gate, far_d_up, far_in, sent = order(step, far_grads, far_rows, far_gate, far_up)
-    far_in_received = ins.sibling(sent)
+    near_arrived = outs.across(hold(near_sent, near_d_gate))
     far_slot, last_slot = order(outs.slots, far_out, far_received, far_arrived)
     far_sum = outs.line(far_slot, outs.far)
     last_sum = outs.line(last_slot, outs.last)
+    last_across = hold(last_across, near_d_gate)
+    last_pair = order(pair_up, last, last_across)
+    far_grads = [far_pair, last_pair, far_sibling, grads.sibling(last_pair)]
+    far_d_gate, far_d_up, far_in, sent = order(
+        back, far_grads, far_rows, far_gate, far_up
+    )
+    far_in_received = ins.sibling(sent)
+    near_arrived = hold(near_arrived, far_d_gate)
+    own_slot, near_slot = order(outs.slots, near_out, near_received, near_arrived)
+    near_sum = outs.line(near_slot, outs.near)
     clock = order(space, clock)
+    far_in_received = hold(far_in_received, clock)
     far_sent, last_sent = order(lambda *s: ins.send(*s, parts=2), far_in, far_in_received)
     last_arrived = ins.across(last_sent)
     far_in_arrived = ins.across(far_sent)
     own_sent, near_sent = order(lambda *s: ins.send(*s, parts=2), near_in, near_in_received)
-    near_in_arrived = ins.across(near_sent)
-    clock = order(space, clock)
-    product_of = lambda name, by_hidden: lambda r, *acts: weights(name, r, acts, width, by_hidden)
     grad_down = order(
         product_of("grad_down", True), near_grads + far_grads, near_act, far_act
     )
-    own_slot, near_slot = order(outs.slots, near_out, near_received, near_arrived)
-    near_sum = outs.line(near_slot, outs.near)
     all_rows = near_rows + far_rows
-    grad_gate = order(product_of("grad_gate", False), all_rows, near_d_gate, far_d_gate)
     slot = order(lambda *s: ins.slot(1, *s), far_in, far_in_received, last_arrived)
+    near_in_arrived = ins.across(hold(near_sent, slot))
     relay = ins.line(slot, ins.inward)
     middle = ins.line(slot, ins.middle)
-    clock = order(space, clock)
-    grad_up = order(
-        product_of("grad_up", False), all_rows, near_d_up, far_d_up
-    )
-    slot = order(lambda *s: ins.slot(0, *s), far_in, far_in_received, far_in_arrived, relay)
-    far = ins.line(slot, ins.far)
-    own_in_arrived = ins.across(hold(own_sent, slot))
-    clock = order(space, clock)
-
-    slot = order(
-        lambda *s: ins.slot(1, *s), near_in, near_in_received, near_in_arrived, also=middle
-    )
-    near = ins.line(slot, ins.near)
-    clock = order(space, clock)
+    grad_gate = order(product_of("grad_gate", False), all_rows, near_d_gate, far_d_gate)
     columns = jax.ShapeDtypeStruct((tokens.shape[0], width // 2), jnp.bfloat16)
     output_cols = order(
         lambda *sums: call(finish_outputs_kernel, "finish_outputs", sums, columns),
@@ -533,7 +549,14 @@
         far_sum,
         last_sum,
     )
-    near, far, own_in_arrived = hold((near, far, own_in_arrived), output_cols)
+    slot = order(lambda *s: ins.slot(0, *s), far_in, far_in_received, far_in_arrived, relay)
+    far = ins.line(slot, ins.far)
+    own_in_arrived = ins.across(hold(own_sent, slot))
+    grad_up = order(product_of("grad_up", False), all_rows, near_d_up, far_d_up)
+    slot = order(
+        lambda *s: ins.slot(1, *s), near_in, near_in_received, near_in_arrived, also=middle
+    )
+    near = ins.line(slot, ins.near)
     input_cols, d_scores = order(
         lambda *sums: call(
             functools.partial(finish_inputs_kernel, experts),

time: 168 us -> 156 us (0.929)
  waiting for transfers between devices: 67.4 us -> 55.2 us
    ppermute x12, waiting for transfers between devices: 33 us -> 13.6 us  [across(): return lax.ppermute(array, 'helper', self.sides)]
    ppermute x15, waiting for transfers between devices: 34 us -> 39.3 us  [line(): return lax.ppermute(array, 'expert', pairs)]
    ppermute x15, starting transfers between devices: 26.8 us -> 23.2 us  [line(): return lax.ppermute(array, 'expert', pairs)]
    ppermute x12, starting transfers between devices: 12.3 us -> 15.6 us  [across(): return lax.ppermute(array, 'helper', self.sides)]
    ppermute x20 -> x12, waiting for transfers between devices: 0.51 us -> 2.3 us  [sibling(): return lax.ppermute(array, 'expert', self.cores)]
    ppermute x20 -> x12, starting transfers between devices: 3.84 us -> 2.78 us  [sibling(): return lax.ppermute(array, 'expert', self.cores)]
    pallas_call x19 -> x25, Pallas kernels: 50.6 us -> 51.2 us  [call(): pl.pallas_call(kernel, out_shape=out_shape, in_specs=[VMEM] * len(operand...]
  transfers between devices with their start and end apart: 47 -> 39, of which waited for: 15 -> 13; matrix products, arithmetic and copies ran while one was open for 0% -> 0% of each run, Pallas kernels for 32% -> 35%
where the time goes in v4:
time: 156 us
  Pallas kernels  57.2 us (37%)
  waiting for transfers between devices  55.2 us (35%)
  starting transfers between devices  41.6 us (27%)
    pallas_call x25, Pallas kernels, call(): pl.pallas_call(kernel, out_shape=out_shape, in_specs=[VMEM] * len(operand...  51.2 us
    ppermute x15, waiting for transfers between devices, line(): return lax.ppermute(array, 'expert', pairs)  39.3 us
    ppermute x15, starting transfers between devices, line(): return lax.ppermute(array, 'expert', pairs)  23.2 us
    ppermute x12, starting transfers between devices, across(): return lax.ppermute(array, 'helper', self.sides)  15.6 us
    ppermute x12, waiting for transfers between devices, across(): return lax.ppermute(array, 'helper', self.sides)  13.6 us
    pallas_call x1, Pallas kernels, load(): pl.pallas_call(load_kernel, out_shape=tuple((jax.ShapeDtypeStruct(mat.sha...  4.73 us
  transfers between devices with their start and end apart: 39, of which 13 were waited for; matrix products, arithmetic and copies ran while one was open for 0% of the time, Pallas kernels for 35%

profile of v4, /device:TPU:0, one launch (start us, length us, event | category | flops | bytes accessed | tf_op | source)
XLA Modules:
  0.0 156.1 jit_solution(10369968915574232214)
XLA Ops:
  0.6 1.3 prepare_rows.1
  2.5 2.6 %collective-permute-start = (bf16[64,2176]{1,0:T(8,128)(2,1)S(1)}, bf16[64,2176]{1,0:T(8,128)(2,1)S(1)}, u32[]{:S(2)}, u32[]{:S(2)}) collective-permute-start(bf16[64,2176]{1,0:T(8,128)(2,1)S(1)} %get-tuple-element.188), channel_id=1, source_target_pairs={{0,4},{2,6},{4,0},{6,2},{8,12},{10,14},{12,8},{14,10},{1,5},{3,7},... | collective-permute-start | bytes 835592 | tf_op jit(solution)/shard_map/rows_line/ppermute | solution.py:370
  5.1 0.7 collective-permute-start.4
  5.8 4.7 %load.1 = (bf16[2048,1024]{1,0:T(8,128)(2,1)S(1)}, bf16[2048,1024]{1,0:T(8,128)(2,1)S(1)}, bf16[1024,2048]{1,0:T(8,128)(2,1)S(1)}) custom-call(bf16[2048,1024]{1,0:T(8,128)(2,1)} %bitcast.16, bf16[2048,1024]{1,0:T(8,128)(2,1)} %bitcast.17, bf16[1024,2048]{1,0:T(8,128)(2,1)} %bitcast.18), custom_call_target="tpu_custom_call" | custom-call | tf_op jit(solution)/shard_map/load/pallas_call | solution.py:412
  10.5 1.8 %collective-permute-done.first = bf16[64,2176]{1,0:T(8,128)(2,1)S(1)} collective-permute-done((bf16[64,2176]{1,0:T(8,128)(2,1)S(1)}, bf16[64,2176]{1,0:T(8,128)(2,1)S(1)}, u32[]{:S(2)}, u32[]{:S(2)}) %collective-permute-start) | collective-permute-done | bytes 278560 | tf_op jit(solution)/shard_map/rows_line/ppermute | solution.py:370
  12.4 2.8 %collective-permute-start.3 = (bf16[64,2176]{1,0:T(8,128)(2,1)S(1)}, bf16[64,2176]{1,0:T(8,128)(2,1)S(1)}, u32[]{:S(2)}, u32[]{:S(2)}) collective-permute-start(bf16[64,2176]{1,0:T(8,128)(2,1)S(1)} %get-tuple-element.188), channel_id=1, source_target_pairs={{0,8},{2,10},{4,12},{6,14},{8,0},{10,2},{12,4},{14,6},{1,9},{3,11}... | collective-permute-start | bytes 835592 | tf_op jit(solution)/shard_map/rows_line/ppermute | solution.py:370
  15.1 1.5 collective-permute-start.2
  16.6 11.9 %collective-permute-done.3.first = bf16[64,2176]{1,0:T(8,128)(2,1)S(1)} collective-permute-done((bf16[64,2176]{1,0:T(8,128)(2,1)S(1)}, bf16[64,2176]{1,0:T(8,128)(2,1)S(1)}, u32[]{:S(2)}, u32[]{:S(2)}) %collective-permute-start.3) | collective-permute-done | bytes 278560 | tf_op jit(solution)/shard_map/rows_line/ppermute | solution.py:370
  29.2 1.3 collective-permute-start.6
  30.5 1.6 %collective-permute-start.7 = (bf16[64,2176]{1,0:T(8,128)(2,1)S(1)}, bf16[64,2176]{1,0:T(8,128)(2,1)S(1)}, u32[]{:S(2)}, u32[]{:S(2)}) collective-permute-start(bf16[64,2176]{1,0:T(8,128)(2,1)S(1)} %collective-permute-done.3.first), channel_id=1, source_target_pairs={{0,1},{1,0},{2,3},{3,2},{4,5},{5,4},{6,7},{7,6},{8,9},{9,8},{10,11... | collective-permute-start | bytes 835592 | tf_op jit(solution)/shard_map/rows_across/ppermute | solution.py:378
  32.1 6.8 %forward.2 = (f32[512,1024]{1,0:T(8,128)S(1)}, f32[512,1024]{1,0:T(8,128)S(1)}, bf16[512,1024]{1,0:T(8,128)(2,1)S(1)}, bf16[2,256,1024]{2,1,0:T(8,128)(2,1)S(1)}, bf16[2,256,1024]{2,1,0:T(8,128)(2,1)S(1)}) custom-call(bf16[128,2176]{1,0:T(8,128)(2,1)S(1)} %get-tuple-element.329.refs_0_.refs_4_, bf16[128,2176]{1,0:T(8,128)(2,1)S(1)} %pair.6.refs_1_.refs_5_, ...), custom_call_target="tpu_custom_call" | custom-call | flops 6442450944 | tf_op jit(solution)/shard_map/forward/pallas_call | solution.py:40
  38.9 6.9 %collective-permute-done.6 = bf16[64,2176]{1,0:T(8,128)(2,1)S(1)} collective-permute-done((bf16[64,2176]{1,0:T(8,128)(2,1)S(1)}, bf16[64,2176]{1,0:T(8,128)(2,1)S(1)}, u32[]{:S(2)}, u32[]{:S(2)}) %collective-permute-start.6) | collective-permute-done | bytes 278560 | tf_op jit(solution)/shard_map/rows_line/ppermute | solution.py:370
  46.0 0.7 collective-permute-start.11
  46.6 1.6 %collective-permute-start.9 = (bf16[64,2176]{1,0:T(8,128)(2,1)S(1)}, bf16[64,2176]{1,0:T(8,128)(2,1)S(1)}, u32[]{:S(2)}, u32[]{:S(2)}) collective-permute-start(bf16[64,2176]{1,0:T(8,128)(2,1)S(1)} %add.6.first), channel_id=1, source_target_pairs={{0,1},{1,0},{2,3},{3,2},{4,5},{5,4},{6,7},{7,6},{8,9},{9,8},{10,11... | collective-permute-start | bytes 835592 | tf_op jit(solution)/shard_map/rows_across/ppermute | solution.py:378
  48.4 5.0 %collective-permute-done.10.first = bf16[64,2048]{1,0:T(8,128)(2,1)S(1)} collective-permute-done((bf16[64,2048]{1,0:T(8,128)(2,1)S(1)}, bf16[64,2048]{1,0:T(8,128)(2,1)S(1)}, u32[]{:S(2)}, u32[]{:S(2)}) %collective-permute-start.10) | collective-permute-done | bytes 262176 | tf_op jit(solution)/shard_map/grads_line/ppermute | solution.py:370
  53.4 1.1 collective-permute-done.9.second
  54.6 1.5 collective-permute-start.17
  56.1 1.6 %collective-permute-start.18 = (bf16[64,2048]{1,0:T(8,128)(2,1)S(1)}, bf16[64,2048]{1,0:T(8,128)(2,1)S(1)}, u32[]{:S(2)}, u32[]{:S(2)}) collective-permute-start(bf16[64,2048]{1,0:T(8,128)(2,1)S(1)} %collective-permute-done.13.first), channel_id=1, source_target_pairs={{0,1},{1,0},{2,3},{3,2},{4,5},{5,4},{6,7},{7,6},{8,9},{9,8},{10,11... | collective-permute-start | bytes 786440 | tf_op jit(solution)/shard_map/grads_across/ppermute | solution.py:378
  58.4 6.7 %forward.3 = (f32[512,1024]{1,0:T(8,128)S(1)}, f32[512,1024]{1,0:T(8,128)S(1)}, bf16[512,1024]{1,0:T(8,128)(2,1)S(1)}, bf16[2,256,1024]{2,1,0:T(8,128)(2,1)S(1)}, bf16[2,256,1024]{2,1,0:T(8,128)(2,1)S(1)}) custom-call(bf16[128,2176]{1,0:T(8,128)(2,1)S(1)} %pair.7.refs_0_.refs_4_, bf16[128,2176]{1,0:T(8,128)(2,1)S(1)} %pair.8.refs_1_.refs_5_, ...), custom_call_target="tpu_custom_call" | custom-call | flops 6442450944 | tf_op jit(solution)/shard_map/forward/pallas_call | solution.py:40
  65.2 1.0 copy-done.4
  66.1 0.6 collective-permute-done.17
  66.7 3.8 %collective-permute-done.19.second = bf16[64,2048]{1,0:T(8,128)(2,1)S(1)} collective-permute-done((bf16[64,2048]{1,0:T(8,128)(2,1)S(1)}, bf16[64,2048]{1,0:T(8,128)(2,1)S(1)}, u32[]{:S(2)}, u32[]{:S(2)}) %collective-permute-start.19) | collective-permute-done | bytes 262176 | tf_op jit(solution)/shard_map/grads_across/ppermute | solution.py:378
  70.7 0.6 collective-permute-start.20
  71.4 1.5 collective-permute-start.23
  72.9 1.9 %collective-permute-done.15.received = bf16[2,256,1024]{2,1,0:T(8,128)(2,1)S(1)} collective-permute-done((bf16[2,256,1024]{2,1,0:T(8,128)(2,1)S(1)}, bf16[2,256,1024]{2,1,0:T(8,128)(2,1)S(1)}, u32[]{:S(2)}, u32[]{:S(2)}) %collective-permute-start.15) | collective-permute-done | bytes 1048608 | tf_op jit(solution)/shard_map/out_cores/ppermute | solution.py:374
  74.9 1.6 %collective-permute-start.24 = (bf16[256,1024]{1,0:T(8,128)(2,1)S(1)}, bf16[256,1024]{1,0:T(8,128)(2,1)S(1)}, u32[]{:S(2)}, u32[]{:S(2)}) collective-permute-start(bf16[256,1024]{1,0:T(8,128)(2,1)S(1)} %out_send.2), channel_id=1, source_target_pairs={{0,1},{1,0},{2,3},{3,2},{4,5},{5,4},{6,7},{7,6},{8,9},{9,8},{10,11... | collective-permute-start | bytes 1572872 | tf_op jit(solution)/shard_map/out_across/ppermute | solution.py:378
  76.5 7.3 %backward.2 = (bf16[512,1024]{1,0:T(8,128)(2,1)S(1)}, bf16[512,1024]{1,0:T(8,128)(2,1)S(1)}, bf16[2,256,1152]{2,1,0:T(8,128)(2,1)S(1)}, bf16[2,256,1152]{2,1,0:T(8,128)(2,1)S(1)}) custom-call(bf16[128,2048]{1,0:T(8,128)(2,1)S(1)} %get-tuple-element.296.refs_0_, bf16[128,2048]{1,0:T(8,128)(2,1)S(1)} %pair.9.refs_1_, ...), custom_call_target="tpu_custom_call" | custom-call | flops 6442450944 | tf_op jit(solution)/shard_map/backward/pallas_call | solution.py:40
  83.8 7.4 %collective-permute-done.24.arrived = bf16[256,1024]{1,0:T(8,128)(2,1)S(1)} collective-permute-done((bf16[256,1024]{1,0:T(8,128)(2,1)S(1)}, bf16[256,1024]{1,0:T(8,128)(2,1)S(1)}, u32[]{:S(2)}, u32[]{:S(2)}) %collective-permute-start.24) | collective-permute-done | bytes 524320 | tf_op jit(solution)/shard_map/out_across/ppermute | solution.py:378
  91.6 1.6 %collective-permute-start.22 = (bf16[256,1024]{1,0:T(8,128)(2,1)S(1)}, bf16[256,1024]{1,0:T(8,128)(2,1)S(1)}, u32[]{:S(2)}, u32[]{:S(2)}) collective-permute-start(bf16[256,1024]{1,0:T(8,128)(2,1)S(1)} %out_send.3), channel_id=1, source_target_pairs={{0,1},{1,0},{2,3},{3,2},{4,5},{5,4},{6,7},{7,6},{8,9},{9,8},{10,11... | collective-permute-start | bytes 1572872 | tf_op jit(solution)/shard_map/out_across/ppermute | solution.py:378
  93.5 7.4 %backward.3 = (bf16[512,1024]{1,0:T(8,128)(2,1)S(1)}, bf16[512,1024]{1,0:T(8,128)(2,1)S(1)}, bf16[2,256,1152]{2,1,0:T(8,128)(2,1)S(1)}, bf16[2,256,1152]{2,1,0:T(8,128)(2,1)S(1)}) custom-call(bf16[128,2048]{1,0:T(8,128)(2,1)S(1)} %pair.10.refs_0_.refs_4_, bf16[128,2048]{1,0:T(8,128)(2,1)S(1)} %pair.11.refs_1_.refs_5_, ...), custom_call_target="tpu_custom_call" | custom-call | flops 6442450944 | tf_op jit(solution)/shard_map/backward/pallas_call | solution.py:40
  101.5 4.1 %collective-permute-start.27 = (bf16[128,1024]{1,0:T(8,128)(2,1)S(1)}, bf16[128,1024]{1,0:T(8,128)(2,1)S(1)}, u32[]{:S(2)}, u32[]{:S(2)}) collective-permute-start(bf16[128,1024]{1,0:T(8,128)(2,1)S(1)} %get-tuple-element.262), channel_id=1, source_target_pairs={{0,8},{2,10},{4,12},{6,14},{8,0},{10,2},{12,4},{14,6},{1,9},{3,11}... | collective-permute-start | bytes 786440 | tf_op jit(solution)/shard_map/out_line/ppermute | solution.py:370
  105.6 2.1 %collective-permute-start.28 = (bf16[128,1024]{1,0:T(8,128)(2,1)S(1)}, bf16[128,1024]{1,0:T(8,128)(2,1)S(1)}, u32[]{:S(2)}, u32[]{:S(2)}) collective-permute-start(bf16[128,1024]{1,0:T(8,128)(2,1)S(1)} %get-tuple-element.263), channel_id=1, source_target_pairs={{0,12},{2,14},{4,8},{6,10},{8,4},{10,6},{12,0},{14,2},{1,13},{3,15... | collective-permute-start | bytes 786440 | tf_op jit(solution)/shard_map/out_line/ppermute | solution.py:370
  107.9 2.2 %collective-permute-start.26 = (bf16[128,1024]{1,0:T(8,128)(2,1)S(1)}, bf16[128,1024]{1,0:T(8,128)(2,1)S(1)}, u32[]{:S(2)}, u32[]{:S(2)}) collective-permute-start(bf16[128,1024]{1,0:T(8,128)(2,1)S(1)} %get-tuple-element.285), channel_id=1, source_target_pairs={{0,4},{2,6},{4,0},{6,2},{8,12},{10,14},{12,8},{14,10},{1,5},{3,7},... | collective-permute-start | bytes 786440 | tf_op jit(solution)/shard_map/out_line/ppermute | solution.py:370
  110.1 1.6 %collective-permute-start.30 = (bf16[128,1152]{1,0:T(8,128)(2,1)S(1)}, bf16[128,1152]{1,0:T(8,128)(2,1)S(1)}, u32[]{:S(2)}, u32[]{:S(2)}) collective-permute-start(bf16[128,1152]{1,0:T(8,128)(2,1)S(1)} %get-tuple-element.290), channel_id=1, source_target_pairs={{0,1},{1,0},{2,3},{3,2},{4,5},{5,4},{6,7},{7,6},{8,9},{9,8},{10,11... | collective-permute-start | bytes 884744 | tf_op jit(solution)/shard_map/in_across/ppermute | solution.py:378
  112.3 6.6 %grad_down.1 = bf16[1024,2048]{1,0:T(8,128)(2,1)} custom-call(bf16[128,2048]{1,0:T(8,128)(2,1)S(1)} %get-tuple-element.296.refs_0_, bf16[128,2048]{1,0:T(8,128)(2,1)S(1)} %pair.9.refs_1_, bf16[128,2048]{1,0:T(8,128)(2,1)S(1)} %collective-permute-done.8.refs_2_, bf16[128,2048]{1,0:T(8,128)(2,1)S(1)} %collective-permute-done.21.refs_3_, ...), custom_call_target="tpu_custom_call" | custom-call | flops 4294967296 | tf_op jit(solution)/shard_map/grad_down/pallas_call | solution.py:40
  118.9 1.3 collective-permute-done.30.arrived
  120.2 1.9 %collective-permute-start.33 = (bf16[128,1152]{1,0:T(8,128)(2,1)S(1)}, bf16[128,1152]{1,0:T(8,128)(2,1)S(1)}, u32[]{:S(2)}, u32[]{:S(2)}) collective-permute-start(bf16[128,1152]{1,0:T(8,128)(2,1)S(1)} %in_slot.3), channel_id=1, source_target_pairs={{0,4},{2,6},{12,8},{14,10},{1,5},{3,7},{13,9},{15,11},{16,20},{18,... | collective-permute-start | bytes 884744 | tf_op jit(solution)/shard_map/in_line/ppermute | solution.py:370
  122.2 6.6 %grad_gate.1 = bf16[2048,1024]{1,0:T(8,128)(2,1)} custom-call(bf16[128,2176]{1,0:T(8,128)(2,1)S(1)} %get-tuple-element.329.refs_0_.refs_4_, bf16[128,2176]{1,0:T(8,128)(2,1)S(1)} %pair.6.refs_1_.refs_5_, bf16[128,2176]{1,0:T(8,128)(2,1)S(1)} %collective-permute-done.1.refs_2_.refs_6_, bf16[128,2176]{1,0:T(8,128)(2,1)S(1)} %collective-permute-done.5.refs_3_.refs_7_, ...), custom_call_target="tpu_custom_call" | custom-call | flops 4294967296 | tf_op jit(solution)/shard_map/grad_gate/pallas_call | solution.py:40
  128.8 0.9 collective-permute-start.37
  129.7 1.6 %collective-permute-start.36 = (bf16[128,1152]{1,0:T(8,128)(2,1)S(1)}, bf16[128,1152]{1,0:T(8,128)(2,1)S(1)}, u32[]{:S(2)}, u32[]{:S(2)}) collective-permute-start(bf16[128,1152]{1,0:T(8,128)(2,1)S(1)} %get-tuple-element.328), channel_id=1, source_target_pairs={{0,1},{1,0},{2,3},{3,2},{4,5},{5,4},{6,7},{7,6},{8,9},{9,8},{10,11... | collective-permute-start | bytes 884744 | tf_op jit(solution)/shard_map/in_across/ppermute | solution.py:378
  131.3 0.8 finish_outputs.1
  132.3 6.6 %grad_up.1 = bf16[2048,1024]{1,0:T(8,128)(2,1)} custom-call(bf16[128,2176]{1,0:T(8,128)(2,1)S(1)} %get-tuple-element.329.refs_0_.refs_4_, bf16[128,2176]{1,0:T(8,128)(2,1)S(1)} %pair.6.refs_1_.refs_5_, bf16[128,2176]{1,0:T(8,128)(2,1)S(1)} %collective-permute-done.1.refs_2_.refs_6_, bf16[128,2176]{1,0:T(8,128)(2,1)S(1)} %collective-permute-done.5.refs_3_.refs_7_, ...), custom_call_target="tpu_custom_call" | custom-call | flops 4294967296 | tf_op jit(solution)/shard_map/grad_up/pallas_call | solution.py:40
  139.0 1.5 collective-permute-start.38
  140.5 0.5 collective-permute-start.34
  141.0 0.9 collective-permute-start.35
  141.9 8.5 %collective-permute-done.38.refs_1_ = bf16[128,1152]{1,0:T(8,128)(2,1)S(1)} collective-permute-done((bf16[128,1152]{1,0:T(8,128)(2,1)S(1)}, bf16[128,1152]{1,0:T(8,128)(2,1)S(1)}, u32[]{:S(2)}, u32[]{:S(2)}) %collective-permute-start.38) | collective-permute-done | bytes 294944 | tf_op jit(solution)/shard_map/in_line/ppermute | solution.py:370
  150.4 4.6 %collective-permute-done.35.refs_0_ = bf16[128,1152]{1,0:T(8,128)(2,1)S(1)} collective-permute-done((bf16[128,1152]{1,0:T(8,128)(2,1)S(1)}, bf16[128,1152]{1,0:T(8,128)(2,1)S(1)}, u32[]{:S(2)}, u32[]{:S(2)}) %collective-permute-start.35) | collective-permute-done | bytes 294944 | tf_op jit(solution)/shard_map/in_line/ppermute | solution.py:370
  155.0 1.1 finish_inputs.1
  (74 shorter events, 5.1 us)
Async XLA Ops:
  1.9 10.4 %collective-permute-start.1 = (bf16[128,2176]{1,0:T(8,128)(2,1)S(1)}, bf16[128,2176]{1,0:T(8,128)(2,1)S(1)}, u32[]{:S(2)}, u32[]{:S(2)}) collective-permute-start(bf16[128,2176]{1,0:T(8,128)(2,1)S(1)} %get-tuple-element.329.refs_0_.refs_4_), channel_id=1, source_target_pairs={{0,2},{2,0},{4,6},{6,4},{8,10},{10,8},{12,14},{14,12},{1,3},{3,1},... | collective-permute-start | bytes 1671176 | tf_op jit(solution)/shard_map/rows_cores/ppermute | solution.py:374
  2.5 9.9 %collective-permute-start = (bf16[64,2176]{1,0:T(8,128)(2,1)S(1)}, bf16[64,2176]{1,0:T(8,128)(2,1)S(1)}, u32[]{:S(2)}, u32[]{:S(2)}) collective-permute-start(bf16[64,2176]{1,0:T(8,128)(2,1)S(1)} %get-tuple-element.188), channel_id=1, source_target_pairs={{0,4},{2,6},{4,0},{6,2},{8,12},{10,14},{12,8},{14,10},{1,5},{3,7},... | collective-permute-start | bytes 835592 | tf_op jit(solution)/shard_map/rows_line/ppermute | solution.py:370
  5.1 11.5 %collective-permute-start.4 = (bf16[64,2176]{1,0:T(8,128)(2,1)S(1)}, bf16[64,2176]{1,0:T(8,128)(2,1)S(1)}, u32[]{:S(2)}, u32[]{:S(2)}) collective-permute-start(bf16[64,2176]{1,0:T(8,128)(2,1)S(1)} %get-tuple-element.188), channel_id=1, source_target_pairs={{4,8},{6,10},{8,4},{10,6},{5,9},{7,11},{9,5},{11,7},{20,24},{22,26... | collective-permute-start | bytes 835592 | tf_op jit(solution)/shard_map/rows_line/ppermute | solution.py:370
  5.8 22.7 %copy-start = (bf16[128,2048]{1,0:T(8,128)(2,1)S(1)}, bf16[128,2048]{1,0:T(8,128)(2,1)}, u32[]{:S(2)}) copy-start(bf16[128,2048]{1,0:T(8,128)(2,1)} %rows) | copy-start | bytes 1572868
  12.4 16.1 %collective-permute-start.3 = (bf16[64,2176]{1,0:T(8,128)(2,1)S(1)}, bf16[64,2176]{1,0:T(8,128)(2,1)S(1)}, u32[]{:S(2)}, u32[]{:S(2)}) collective-permute-start(bf16[64,2176]{1,0:T(8,128)(2,1)S(1)} %get-tuple-element.188), channel_id=1, source_target_pairs={{0,8},{2,10},{4,12},{6,14},{8,0},{10,2},{12,4},{14,6},{1,9},{3,11}... | collective-permute-start | bytes 835592 | tf_op jit(solution)/shard_map/rows_line/ppermute | solution.py:370
  15.1 13.4 %collective-permute-start.2 = (bf16[64,2176]{1,0:T(8,128)(2,1)S(1)}, bf16[64,2176]{1,0:T(8,128)(2,1)S(1)}, u32[]{:S(2)}, u32[]{:S(2)}) collective-permute-start(bf16[64,2176]{1,0:T(8,128)(2,1)S(1)} %collective-permute-done.first), channel_id=1, source_target_pairs={{0,1},{1,0},{2,3},{3,2},{4,5},{5,4},{6,7},{7,6},{8,9},{9,8},{10,11... | collective-permute-start | bytes 835592 | tf_op jit(solution)/shard_map/rows_across/ppermute | solution.py:378
  28.6 3.4 %collective-permute-start.5 = (bf16[128,2176]{1,0:T(8,128)(2,1)S(1)}, bf16[128,2176]{1,0:T(8,128)(2,1)S(1)}, u32[]{:S(2)}, u32[]{:S(2)}) collective-permute-start(bf16[128,2176]{1,0:T(8,128)(2,1)S(1)} %pair.6.refs_1_.refs_5_), channel_id=1, source_target_pairs={{0,2},{2,0},{4,6},{6,4},{8,10},{10,8},{12,14},{14,12},{1,3},{3,1},... | collective-permute-start | bytes 1671176 | tf_op jit(solution)/shard_map/rows_cores/ppermute | solution.py:374
  28.7 19.5 %collective-permute-start.8 = (bf16[128,2048]{1,0:T(8,128)(2,1)S(1)}, bf16[128,2048]{1,0:T(8,128)(2,1)S(1)}, u32[]{:S(2)}, u32[]{:S(2)}) collective-permute-start(bf16[128,2048]{1,0:T(8,128)(2,1)S(1)} %get-tuple-element.296.refs_0_), channel_id=1, source_target_pairs={{0,2},{2,0},{4,6},{6,4},{8,10},{10,8},{12,14},{14,12},{1,3},{3,1},... | collective-permute-start | bytes 1572872 | tf_op jit(solution)/shard_map/grads_cores/ppermute | solution.py:374
  29.2 19.1 %collective-permute-start.13 = (bf16[64,2048]{1,0:T(8,128)(2,1)S(1)}, bf16[64,2048]{1,0:T(8,128)(2,1)S(1)}, u32[]{:S(2)}, u32[]{:S(2)}) collective-permute-start(bf16[64,2048]{1,0:T(8,128)(2,1)S(1)} %get-tuple-element.210), channel_id=1, source_target_pairs={{0,8},{2,10},{4,12},{6,14},{8,0},{10,2},{12,4},{14,6},{1,9},{3,11}... | collective-permute-start | bytes 786440 | tf_op jit(solution)/shard_map/grads_line/ppermute | solution.py:370
  29.2 16.6 %collective-permute-start.6 = (bf16[64,2176]{1,0:T(8,128)(2,1)S(1)}, bf16[64,2176]{1,0:T(8,128)(2,1)S(1)}, u32[]{:S(2)}, u32[]{:S(2)}) collective-permute-start(bf16[64,2176]{1,0:T(8,128)(2,1)S(1)} %collective-permute-done.3.first), channel_id=1, source_target_pairs={{4,0},{6,2},{8,12},{10,14},{5,1},{7,3},{9,13},{11,15},{20,16},{22,... | collective-permute-start | bytes 835592 | tf_op jit(solution)/shard_map/rows_line/ppermute | solution.py:370
  30.5 15.3 %collective-permute-start.7 = (bf16[64,2176]{1,0:T(8,128)(2,1)S(1)}, bf16[64,2176]{1,0:T(8,128)(2,1)S(1)}, u32[]{:S(2)}, u32[]{:S(2)}) collective-permute-start(bf16[64,2176]{1,0:T(8,128)(2,1)S(1)} %collective-permute-done.3.first), channel_id=1, source_target_pairs={{0,1},{1,0},{2,3},{3,2},{4,5},{5,4},{6,7},{7,6},{8,9},{9,8},{10,11... | collective-permute-start | bytes 835592 | tf_op jit(solution)/shard_map/rows_across/ppermute | solution.py:378
  45.9 7.5 %collective-permute-start.10 = (bf16[64,2048]{1,0:T(8,128)(2,1)S(1)}, bf16[64,2048]{1,0:T(8,128)(2,1)S(1)}, u32[]{:S(2)}, u32[]{:S(2)}) collective-permute-start(bf16[64,2048]{1,0:T(8,128)(2,1)S(1)} %get-tuple-element.210), channel_id=1, source_target_pairs={{0,4},{2,6},{4,0},{6,2},{8,12},{10,14},{12,8},{14,10},{1,5},{3,7},... | collective-permute-start | bytes 786440 | tf_op jit(solution)/shard_map/grads_line/ppermute | solution.py:370
  46.0 7.4 %collective-permute-start.11 = (bf16[64,2048]{1,0:T(8,128)(2,1)S(1)}, bf16[64,2048]{1,0:T(8,128)(2,1)S(1)}, u32[]{:S(2)}, u32[]{:S(2)}) collective-permute-start(bf16[64,2048]{1,0:T(8,128)(2,1)S(1)} %get-tuple-element.210), channel_id=1, source_target_pairs={{4,8},{6,10},{8,4},{10,6},{5,9},{7,11},{9,5},{11,7},{20,24},{22,26... | collective-permute-start | bytes 786440 | tf_op jit(solution)/shard_map/grads_line/ppermute | solution.py:370
  46.6 7.9 %collective-permute-start.9 = (bf16[64,2176]{1,0:T(8,128)(2,1)S(1)}, bf16[64,2176]{1,0:T(8,128)(2,1)S(1)}, u32[]{:S(2)}, u32[]{:S(2)}) collective-permute-start(bf16[64,2176]{1,0:T(8,128)(2,1)S(1)} %add.6.first), channel_id=1, source_target_pairs={{0,1},{1,0},{2,3},{3,2},{4,5},{5,4},{6,7},{7,6},{8,9},{9,8},{10,11... | collective-permute-start | bytes 835592 | tf_op jit(solution)/shard_map/rows_across/ppermute | solution.py:378
  48.3 6.2 %collective-permute-start.12 = (bf16[128,2176]{1,0:T(8,128)(2,1)S(1)}, bf16[128,2176]{1,0:T(8,128)(2,1)S(1)}, u32[]{:S(2)}, u32[]{:S(2)}) collective-permute-start(bf16[128,2176]{1,0:T(8,128)(2,1)S(1)} %pair.7.refs_0_.refs_4_), channel_id=1, source_target_pairs={{0,2},{2,0},{4,6},{6,4},{8,10},{10,8},{12,14},{14,12},{1,3},{3,1},... | collective-permute-start | bytes 1671176 | tf_op jit(solution)/shard_map/rows_cores/ppermute | solution.py:374
  54.6 3.9 %collective-permute-start.14 = (bf16[128,2176]{1,0:T(8,128)(2,1)S(1)}, bf16[128,2176]{1,0:T(8,128)(2,1)S(1)}, u32[]{:S(2)}, u32[]{:S(2)}) collective-permute-start(bf16[128,2176]{1,0:T(8,128)(2,1)S(1)} %pair.8.refs_1_.refs_5_), channel_id=1, source_target_pairs={{0,2},{2,0},{4,6},{6,4},{8,10},{10,8},{12,14},{14,12},{1,3},{3,1},... | collective-permute-start | bytes 1671176 | tf_op jit(solution)/shard_map/rows_cores/ppermute | solution.py:374
  54.6 12.1 %collective-permute-start.17 = (bf16[64,2048]{1,0:T(8,128)(2,1)S(1)}, bf16[64,2048]{1,0:T(8,128)(2,1)S(1)}, u32[]{:S(2)}, u32[]{:S(2)}) collective-permute-start(bf16[64,2048]{1,0:T(8,128)(2,1)S(1)} %collective-permute-done.13.first), channel_id=1, source_target_pairs={{4,0},{6,2},{8,12},{10,14},{5,1},{7,3},{9,13},{11,15},{20,16},{22,... | collective-permute-start | bytes 786440 | tf_op jit(solution)/shard_map/grads_line/ppermute | solution.py:370
  56.1 10.6 %collective-permute-start.18 = (bf16[64,2048]{1,0:T(8,128)(2,1)S(1)}, bf16[64,2048]{1,0:T(8,128)(2,1)S(1)}, u32[]{:S(2)}, u32[]{:S(2)}) collective-permute-start(bf16[64,2048]{1,0:T(8,128)(2,1)S(1)} %collective-permute-done.13.first), channel_id=1, source_target_pairs={{0,1},{1,0},{2,3},{3,2},{4,5},{5,4},{6,7},{7,6},{8,9},{9,8},{10,11... | collective-permute-start | bytes 786440 | tf_op jit(solution)/shard_map/grads_across/ppermute | solution.py:378
  57.7 15.2 %collective-permute-start.16 = (bf16[2,256,1024]{2,1,0:T(8,128)(2,1)S(1)}, bf16[2,256,1024]{2,1,0:T(8,128)(2,1)S(1)}, u32[]{:S(2)}, u32[]{:S(2)}) collective-permute-start(bf16[2,256,1024]{2,1,0:T(8,128)(2,1)S(1)} %get-tuple-element.205), channel_id=1, source_target_pairs={{0,2},{2,0},{4,6},{6,4},{8,10},{10,8},{12,14},{14,12},{1,3},{3,1},... | collective-permute-start | bytes 3145736 | tf_op jit(solution)/shard_map/out_cores/ppermute | solution.py:374
  57.9 12.6 %collective-permute-start.19 = (bf16[64,2048]{1,0:T(8,128)(2,1)S(1)}, bf16[64,2048]{1,0:T(8,128)(2,1)S(1)}, u32[]{:S(2)}, u32[]{:S(2)}) collective-permute-start(bf16[64,2048]{1,0:T(8,128)(2,1)S(1)} %collective-permute-done.10.first), channel_id=1, source_target_pairs={{0,1},{1,0},{2,3},{3,2},{4,5},{5,4},{6,7},{7,6},{8,9},{9,8},{10,11... | collective-permute-start | bytes 786440 | tf_op jit(solution)/shard_map/grads_across/ppermute | solution.py:378
  65.2 1.0 copy-start.4
  70.6 4.2 %collective-permute-start.21 = (bf16[128,2048]{1,0:T(8,128)(2,1)S(1)}, bf16[128,2048]{1,0:T(8,128)(2,1)S(1)}, u32[]{:S(2)}, u32[]{:S(2)}) collective-permute-start(bf16[128,2048]{1,0:T(8,128)(2,1)S(1)} %pair.9.refs_1_), channel_id=1, source_target_pairs={{0,2},{2,0},{4,6},{6,4},{8,10},{10,8},{12,14},{14,12},{1,3},{3,1},... | collective-permute-start | bytes 1572872 | tf_op jit(solution)/shard_map/grads_cores/ppermute | solution.py:374
  70.7 4.1 %collective-permute-start.20 = (bf16[128,2048]{1,0:T(8,128)(2,1)S(1)}, bf16[128,2048]{1,0:T(8,128)(2,1)S(1)}, u32[]{:S(2)}, u32[]{:S(2)}) collective-permute-start(bf16[128,2048]{1,0:T(8,128)(2,1)S(1)} %pair.10.refs_0_.refs_4_), channel_id=1, source_target_pairs={{0,2},{2,0},{4,6},{6,4},{8,10},{10,8},{12,14},{14,12},{1,3},{3,1},... | collective-permute-start | bytes 1572872 | tf_op jit(solution)/shard_map/grads_cores/ppermute | solution.py:374
  71.3 3.5 %collective-permute-start.15 = (bf16[2,256,1024]{2,1,0:T(8,128)(2,1)S(1)}, bf16[2,256,1024]{2,1,0:T(8,128)(2,1)S(1)}, u32[]{:S(2)}, u32[]{:S(2)}) collective-permute-start(bf16[2,256,1024]{2,1,0:T(8,128)(2,1)S(1)} %get-tuple-element.222), channel_id=1, source_target_pairs={{0,2},{2,0},{4,6},{6,4},{8,10},{10,8},{12,14},{14,12},{1,3},{3,1},... | collective-permute-start | bytes 3145736 | tf_op jit(solution)/shard_map/out_cores/ppermute | solution.py:374
  71.4 12.5 %collective-permute-start.23 = (bf16[64,2048]{1,0:T(8,128)(2,1)S(1)}, bf16[64,2048]{1,0:T(8,128)(2,1)S(1)}, u32[]{:S(2)}, u32[]{:S(2)}) collective-permute-start(bf16[64,2048]{1,0:T(8,128)(2,1)S(1)} %add.7.first), channel_id=1, source_target_pairs={{0,1},{1,0},{2,3},{3,2},{4,5},{5,4},{6,7},{7,6},{8,9},{9,8},{10,11... | collective-permute-start | bytes 786440 | tf_op jit(solution)/shard_map/grads_across/ppermute | solution.py:378
  74.9 16.4 %collective-permute-start.24 = (bf16[256,1024]{1,0:T(8,128)(2,1)S(1)}, bf16[256,1024]{1,0:T(8,128)(2,1)S(1)}, u32[]{:S(2)}, u32[]{:S(2)}) collective-permute-start(bf16[256,1024]{1,0:T(8,128)(2,1)S(1)} %out_send.2), channel_id=1, source_target_pairs={{0,1},{1,0},{2,3},{3,2},{4,5},{5,4},{6,7},{7,6},{8,9},{9,8},{10,11... | collective-permute-start | bytes 1572872 | tf_op jit(solution)/shard_map/out_across/ppermute | solution.py:378
  91.5 2.0 %collective-permute-start.25 = (bf16[128,2048]{1,0:T(8,128)(2,1)S(1)}, bf16[128,2048]{1,0:T(8,128)(2,1)S(1)}, u32[]{:S(2)}, u32[]{:S(2)}) collective-permute-start(bf16[128,2048]{1,0:T(8,128)(2,1)S(1)} %pair.11.refs_1_.refs_5_), channel_id=1, source_target_pairs={{0,2},{2,0},{4,6},{6,4},{8,10},{10,8},{12,14},{14,12},{1,3},{3,1},... | collective-permute-start | bytes 1572872 | tf_op jit(solution)/shard_map/grads_cores/ppermute | solution.py:374
  91.6 16.1 %collective-permute-start.22 = (bf16[256,1024]{1,0:T(8,128)(2,1)S(1)}, bf16[256,1024]{1,0:T(8,128)(2,1)S(1)}, u32[]{:S(2)}, u32[]{:S(2)}) collective-permute-start(bf16[256,1024]{1,0:T(8,128)(2,1)S(1)} %out_send.3), channel_id=1, source_target_pairs={{0,1},{1,0},{2,3},{3,2},{4,5},{5,4},{6,7},{7,6},{8,9},{9,8},{10,11... | collective-permute-start | bytes 1572872 | tf_op jit(solution)/shard_map/out_across/ppermute | solution.py:378
  100.9 9.2 %collective-permute-start.29 = (bf16[2,256,1152]{2,1,0:T(8,128)(2,1)S(1)}, bf16[2,256,1152]{2,1,0:T(8,128)(2,1)S(1)}, u32[]{:S(2)}, u32[]{:S(2)}) collective-permute-start(bf16[2,256,1152]{2,1,0:T(8,128)(2,1)S(1)} %get-tuple-element.280), channel_id=1, source_target_pairs={{0,2},{2,0},{4,6},{6,4},{8,10},{10,8},{12,14},{14,12},{1,3},{3,1},... | collective-permute-start | bytes 3538952 | tf_op jit(solution)/shard_map/in_cores/ppermute | solution.py:374
  101.1 10.6 %collective-permute-start.31 = (bf16[2,256,1152]{2,1,0:T(8,128)(2,1)S(1)}, bf16[2,256,1152]{2,1,0:T(8,128)(2,1)S(1)}, u32[]{:S(2)}, u32[]{:S(2)}) collective-permute-start(bf16[2,256,1152]{2,1,0:T(8,128)(2,1)S(1)} %get-tuple-element.258), channel_id=1, source_target_pairs={{0,2},{2,0},{4,6},{6,4},{8,10},{10,8},{12,14},{14,12},{1,3},{3,1},... | collective-permute-start | bytes 3538952 | tf_op jit(solution)/shard_map/in_cores/ppermute | solution.py:374
  101.5 27.3 %collective-permute-start.27 = (bf16[128,1024]{1,0:T(8,128)(2,1)S(1)}, bf16[128,1024]{1,0:T(8,128)(2,1)S(1)}, u32[]{:S(2)}, u32[]{:S(2)}) collective-permute-start(bf16[128,1024]{1,0:T(8,128)(2,1)S(1)} %get-tuple-element.262), channel_id=1, source_target_pairs={{0,8},{2,10},{4,12},{6,14},{8,0},{10,2},{12,4},{14,6},{1,9},{3,11}... | collective-permute-start | bytes 786440 | tf_op jit(solution)/shard_map/out_line/ppermute | solution.py:370
  105.6 24.1 %collective-permute-start.28 = (bf16[128,1024]{1,0:T(8,128)(2,1)S(1)}, bf16[128,1024]{1,0:T(8,128)(2,1)S(1)}, u32[]{:S(2)}, u32[]{:S(2)}) collective-permute-start(bf16[128,1024]{1,0:T(8,128)(2,1)S(1)} %get-tuple-element.263), channel_id=1, source_target_pairs={{0,12},{2,14},{4,8},{6,10},{8,4},{10,6},{12,0},{14,2},{1,13},{3,15... | collective-permute-start | bytes 786440 | tf_op jit(solution)/shard_map/out_line/ppermute | solution.py:370
  107.9 21.8 %collective-permute-start.26 = (bf16[128,1024]{1,0:T(8,128)(2,1)S(1)}, bf16[128,1024]{1,0:T(8,128)(2,1)S(1)}, u32[]{:S(2)}, u32[]{:S(2)}) collective-permute-start(bf16[128,1024]{1,0:T(8,128)(2,1)S(1)} %get-tuple-element.285), channel_id=1, source_target_pairs={{0,4},{2,6},{4,0},{6,2},{8,12},{10,14},{12,8},{14,10},{1,5},{3,7},... | collective-permute-start | bytes 786440 | tf_op jit(solution)/shard_map/out_line/ppermute | solution.py:370
  110.0 2.2 %copy-start.5 = (bf16[512,1024]{1,0:T(8,128)(2,1)S(1)}, bf16[512,1024]{1,0:T(8,128)(2,1)}, u32[]{:S(2)}) copy-start(bf16[512,1024]{1,0:T(8,128)(2,1)} %copy-done.4) | copy-start | bytes 3145732
  110.1 10.0 %collective-permute-start.30 = (bf16[128,1152]{1,0:T(8,128)(2,1)S(1)}, bf16[128,1152]{1,0:T(8,128)(2,1)S(1)}, u32[]{:S(2)}, u32[]{:S(2)}) collective-permute-start(bf16[128,1152]{1,0:T(8,128)(2,1)S(1)} %get-tuple-element.290), channel_id=1, source_target_pairs={{0,1},{1,0},{2,3},{3,2},{4,5},{5,4},{6,7},{7,6},{8,9},{9,8},{10,11... | collective-permute-start | bytes 884744 | tf_op jit(solution)/shard_map/in_across/ppermute | solution.py:378
  111.7 20.4 %collective-permute-start.32 = (bf16[128,1152]{1,0:T(8,128)(2,1)S(1)}, bf16[128,1152]{1,0:T(8,128)(2,1)S(1)}, u32[]{:S(2)}, u32[]{:S(2)}) collective-permute-start(bf16[128,1152]{1,0:T(8,128)(2,1)S(1)} %get-tuple-element.291), channel_id=1, source_target_pairs={{0,1},{1,0},{2,3},{3,2},{4,5},{5,4},{6,7},{7,6},{8,9},{9,8},{10,11... | collective-permute-start | bytes 884744 | tf_op jit(solution)/shard_map/in_across/ppermute | solution.py:378
  120.2 11.9 %collective-permute-start.33 = (bf16[128,1152]{1,0:T(8,128)(2,1)S(1)}, bf16[128,1152]{1,0:T(8,128)(2,1)S(1)}, u32[]{:S(2)}, u32[]{:S(2)}) collective-permute-start(bf16[128,1152]{1,0:T(8,128)(2,1)S(1)} %in_slot.3), channel_id=1, source_target_pairs={{0,4},{2,6},{12,8},{14,10},{1,5},{3,7},{13,9},{15,11},{16,20},{18,... | collective-permute-start | bytes 884744 | tf_op jit(solution)/shard_map/in_line/ppermute | solution.py:370
  128.8 10.1 %collective-permute-start.37 = (bf16[128,1152]{1,0:T(8,128)(2,1)S(1)}, bf16[128,1152]{1,0:T(8,128)(2,1)S(1)}, u32[]{:S(2)}, u32[]{:S(2)}) collective-permute-start(bf16[128,1152]{1,0:T(8,128)(2,1)S(1)} %in_slot.3), channel_id=1, source_target_pairs={{4,8},{6,10},{8,4},{10,6},{5,9},{7,11},{9,5},{11,7},{20,24},{22,26... | collective-permute-start | bytes 884744 | tf_op jit(solution)/shard_map/in_line/ppermute | solution.py:370
  129.7 9.2 %collective-permute-start.36 = (bf16[128,1152]{1,0:T(8,128)(2,1)S(1)}, bf16[128,1152]{1,0:T(8,128)(2,1)S(1)}, u32[]{:S(2)}, u32[]{:S(2)}) collective-permute-start(bf16[128,1152]{1,0:T(8,128)(2,1)S(1)} %get-tuple-element.328), channel_id=1, source_target_pairs={{0,1},{1,0},{2,3},{3,2},{4,5},{5,4},{6,7},{7,6},{8,9},{9,8},{10,11... | collective-permute-start | bytes 884744 | tf_op jit(solution)/shard_map/in_across/ppermute | solution.py:378
  138.9 16.1 %copy-start.1 = (s32[128,4]{0,1:T(4,128)S(1)}, s32[128,4]{0,1:T(4,128)}, u32[]{:S(2)}) copy-start(s32[128,4]{0,1:T(4,128)} %param.9) | copy-start | bytes 6148
  138.9 16.1 %copy-start.2 = (f32[128,4]{0,1:T(4,128)S(1)}, f32[128,4]{0,1:T(4,128)}, u32[]{:S(2)}) copy-start(f32[128,4]{0,1:T(4,128)} %param.11) | copy-start | bytes 6148
  138.9 16.1 %copy-start.3 = (s32[128]{0:T(128)S(1)}, s32[128]{0:T(128)}, u32[]{:S(2)}) copy-start(s32[128]{0:T(128)} %param.10) | copy-start | bytes 1540
  139.0 11.4 %collective-permute-start.38 = (bf16[128,1152]{1,0:T(8,128)(2,1)S(1)}, bf16[128,1152]{1,0:T(8,128)(2,1)S(1)}, u32[]{:S(2)}, u32[]{:S(2)}) collective-permute-start(bf16[128,1152]{1,0:T(8,128)(2,1)S(1)} %in_slot.5), channel_id=1, source_target_pairs={{0,4},{2,6},{4,0},{6,2},{8,12},{10,14},{12,8},{14,10},{1,5},{3,7},... | collective-permute-start | bytes 884744 | tf_op jit(solution)/shard_map/in_line/ppermute | solution.py:370
  140.5 9.9 %collective-permute-start.34 = (bf16[128,1152]{1,0:T(8,128)(2,1)S(1)}, bf16[128,1152]{1,0:T(8,128)(2,1)S(1)}, u32[]{:S(2)}, u32[]{:S(2)}) collective-permute-start(bf16[128,1152]{1,0:T(8,128)(2,1)S(1)} %get-tuple-element.327), channel_id=1, source_target_pairs={{0,1},{1,0},{2,3},{3,2},{4,5},{5,4},{6,7},{7,6},{8,9},{9,8},{10,11... | collective-permute-start | bytes 884744 | tf_op jit(solution)/shard_map/in_across/ppermute | solution.py:378
  141.0 13.9 %collective-permute-start.35 = (bf16[128,1152]{1,0:T(8,128)(2,1)S(1)}, bf16[128,1152]{1,0:T(8,128)(2,1)S(1)}, u32[]{:S(2)}, u32[]{:S(2)}) collective-permute-start(bf16[128,1152]{1,0:T(8,128)(2,1)S(1)} %in_slot.4), channel_id=1, source_target_pairs={{0,8},{2,10},{4,12},{6,14},{8,0},{10,2},{12,4},{14,6},{1,9},{3,11}... | collective-permute-start | bytes 884744 | tf_op jit(solution)/shard_map/in_line/ppermute | solution.py:370

commit v5 on v4

--- a/solution.py
+++ b/solution.py
@@ -358,10 +358,6 @@
         both = lambda pairs: [(2 * a + c, 2 * b + c) for a, b in pairs for c in (0, 1)]
         self.near = both([(z, z ^ 1) for z in range(4)])
         self.far = both([(z, z ^ 2) for z in range(4)])
-        self.last = both([(z, z ^ 3) for z in range(4)])
-        self.middle = both([(1, 2), (2, 1)])
-        self.outward = both([(1, 0), (2, 3)])
-        self.inward = both([(0, 1), (3, 2)])
         self.cores = [(i, i ^ 1) for i in range(8)]
         self.sides = [(0, 1), (1, 0)]
 
@@ -420,7 +416,7 @@
     )(*(pltpu.with_memory_space_constraint(mat, pltpu.HBM) for mat in mats))
 
 
-def space(clock):
+def space(clock, flops=12 * 10**9):
     return pl.pallas_call(
         lambda old, new: None,
         out_shape=jax.ShapeDtypeStruct(clock.shape, clock.dtype),
@@ -428,7 +424,7 @@
         out_specs=pl.BlockSpec(memory_space=pl.ANY),
         input_output_aliases={0: 0},
         compiler_params=pltpu.CompilerParams(vmem_limit_bytes=2**20),
-        cost_estimate=pl.CostEstimate(flops=12 * 10**9, bytes_accessed=0, transcendentals=0),
+        cost_estimate=pl.CostEstimate(flops=flops, bytes_accessed=0, transcendentals=0),
         name="space",
     )(clock)
 
@@ -458,46 +454,42 @@
 
     own, pair, clock = order(lambda r: prepare_rows(*picks, r, experts), tokens)
     near = rows.line(own, rows.near)
-    middle = rows.line(own, rows.middle)
+    far = rows.line(own, rows.far)
     sibling_pair = rows.sibling(pair)
     mats = order(load, gate_local, up_local, down_local)
     near, sibling_pair = hold((near, sibling_pair), mats)
     near_across = rows.across(near)
-    far = rows.line(hold(own, near), rows.far)
-    near_first = pair
-    near_sibling = sibling_pair
-
-    own, pair = order(prepare_grads, grad_out, also=(far, middle))
+    far = hold(far, near)
     far_across = rows.across(far)
-    relay = rows.line(far, rows.outward)
-    far_grad = grads.line(own, grads.far)
+    last = rows.line(far, rows.near)
+    near_first, near_sibling = pair, sibling_pair
+    own, pair = order(prepare_grads, grad_out, also=far)
     sibling_pair = grads.sibling(pair)
     near_pair = order(pair_up, near, near_across)
     near_rows = [near_first, near_pair, near_sibling, rows.sibling(near_pair)]
-    near_gate, near_up, near_act, near_out, sent = order(ahead, *near_rows)
-    near_received = outs.sibling(sent)
-
-    relay, far_across = hold((relay, far_across), near_act)
-    last = order(jnp.add, middle, relay)
     last_across = rows.across(last)
     near = grads.line(hold(own, last), grads.near)
-    middle_grad = grads.line(hold(own, last), grads.middle)
-    far_pair = order(pair_up, far, far_across, also=sibling_pair)
+    far_grad = grads.line(hold(own, last), grads.far)
+    near_gate, near_up, near_act, near_out, sent = order(
+        ahead, *near_rows, also=(last, sibling_pair)
+    )
+    near_received = outs.sibling(sent)
+
+    near = hold(near, near_act)
+    far_grad = hold(far_grad, near)
+    far_across, last_across = hold((far_across, last_across), far_grad)
+    far_pair = order(pair_up, far, far_across)
     far_sibling = rows.sibling(far_pair)
-    clock = order(space, clock, also=far_grad)
-    last_across, near, middle_grad, far_sibling = hold(
-        (last_across, near, middle_grad, far_sibling), clock
-    )
-    far_across = grads.across(far_grad)
-    relay = grads.line(far_grad, grads.outward)
-    last_pair = order(pair_up, last, last_across, also=(far_grad, far_sibling))
+    last_pair = order(pair_up, last, last_across, also=far_sibling)
     far_rows = [far_pair, last_pair, far_sibling, rows.sibling(last_pair)]
     near_across = grads.across(near)
-    far_gate, far_up, far_act, far_out, sent = order(ahead, *far_rows, also=(near, middle_grad))
+    far_across = grads.across(far_grad)
+    last = grads.line(far_grad, grads.near)
+    far_gate, far_up, far_act, far_out, sent = order(ahead, *far_rows, also=(near, far_grad))
     far_received = outs.sibling(sent)
 
-    relay, far_across, near_across = hold((relay, far_across, near_across), far_act)
-    last = order(jnp.add, middle_grad, relay)
+    last, near_across = hold((last, near_across), far_act)
+    far_across = hold(far_across, near_across)
     last_across = grads.across(last)
     near_pair = order(pair_up, near, near_across)
     near_grads = [pair, near_pair, sibling_pair, grads.sibling(near_pair)]
@@ -514,8 +506,7 @@
     near_in_received = ins.sibling(sent)
     near_arrived = outs.across(hold(near_sent, near_d_gate))
     far_slot, last_slot = order(outs.slots, far_out, far_received, far_arrived)
-    far_sum = outs.line(far_slot, outs.far)
-    last_sum = outs.line(last_slot, outs.last)
+    last_sum = outs.line(last_slot, outs.near)
     last_across = hold(last_across, near_d_gate)
     last_pair = order(pair_up, last, last_across)
     far_grads = [far_pair, last_pair, far_sibling, grads.sibling(last_pair)]
@@ -524,39 +515,38 @@
     )
     far_in_received = ins.sibling(sent)
     near_arrived = hold(near_arrived, far_d_gate)
-    own_slot, near_slot = order(outs.slots, near_out, near_received, near_arrived)
-    near_sum = outs.line(near_slot, outs.near)
-    clock = order(space, clock)
+    clock = order(space, clock, also=near_arrived)
     far_in_received = hold(far_in_received, clock)
     far_sent, last_sent = order(lambda *s: ins.send(*s, parts=2), far_in, far_in_received)
     last_arrived = ins.across(last_sent)
     far_in_arrived = ins.across(far_sent)
     own_sent, near_sent = order(lambda *s: ins.send(*s, parts=2), near_in, near_in_received)
+    far_sum = outs.line(order(jnp.add, far_slot, last_sum), outs.far)
+    own_slot, near_slot = order(outs.slots, near_out, near_received, near_arrived)
+    near_sum = outs.line(near_slot, outs.near)
+    near_in_arrived = ins.across(hold(near_sent, own_slot))
     grad_down = order(
         product_of("grad_down", True), near_grads + far_grads, near_act, far_act
     )
     all_rows = near_rows + far_rows
     slot = order(lambda *s: ins.slot(1, *s), far_in, far_in_received, last_arrived)
-    near_in_arrived = ins.across(hold(near_sent, slot))
-    relay = ins.line(slot, ins.inward)
-    middle = ins.line(slot, ins.middle)
+    last_sum = ins.line(slot, ins.near)
+    own_in_arrived = ins.across(hold(own_sent, slot))
     grad_gate = order(product_of("grad_gate", False), all_rows, near_d_gate, far_d_gate)
+    slot = order(lambda *s: ins.slot(0, *s), far_in, far_in_received, far_in_arrived, last_sum)
+    far = ins.line(slot, ins.far)
     columns = jax.ShapeDtypeStruct((tokens.shape[0], width // 2), jnp.bfloat16)
     output_cols = order(
         lambda *sums: call(finish_outputs_kernel, "finish_outputs", sums, columns),
         own_slot,
         near_sum,
         far_sum,
-        last_sum,
-    )
-    slot = order(lambda *s: ins.slot(0, *s), far_in, far_in_received, far_in_arrived, relay)
-    far = ins.line(slot, ins.far)
-    own_in_arrived = ins.across(hold(own_sent, slot))
+    )
     grad_up = order(product_of("grad_up", False), all_rows, near_d_up, far_d_up)
-    slot = order(
-        lambda *s: ins.slot(1, *s), near_in, near_in_received, near_in_arrived, also=middle
-    )
+    slot = order(lambda *s: ins.slot(1, *s), near_in, near_in_received, near_in_arrived)
     near = ins.line(slot, ins.near)
+    clock = order(lambda c: space(c, 2 * 10**9), clock, also=far)
+    near, own_in_arrived = hold((near, own_in_arrived), clock)
     input_cols, d_scores = order(
         lambda *sums: call(
             functools.partial(finish_inputs_kernel, experts),
@@ -569,7 +559,6 @@
         own_in_arrived,
         far,
         near,
-        middle,
     )
     return output_cols, input_cols, d_scores.T, grad_gate[None], grad_up[None], grad_down[None]
 

time: 156 us -> 150 us (0.962)
  starting transfers between devices: 41.6 us -> 35.9 us
    ppermute x15 -> x12, waiting for transfers between devices: 39.3 us -> 30.5 us  [line(): return lax.ppermute(array, 'expert', pairs)]
    ppermute x12, waiting for transfers between devices: 13.6 us -> 21.3 us  [across(): return lax.ppermute(array, 'helper', self.sides)]
    ppermute x15 -> x12, starting transfers between devices: 23.2 us -> 17.6 us  [line(): return lax.ppermute(array, 'expert', pairs)]
    ppermute x12, waiting for transfers between devices: 2.3 us -> 4.23 us  [sibling(): return lax.ppermute(array, 'expert', self.cores)]
  transfers between devices with their start and end apart: 39 -> 36, of which waited for: 13 -> 17; matrix products, arithmetic and copies ran while one was open for 0% -> 0% of each run, Pallas kernels for 35% -> 36%
where the time goes in v5:
time: 150 us
  Pallas kernels  57.3 us (38%)
  waiting for transfers between devices  56 us (37%)
  starting transfers between devices  35.9 us (24%)
    pallas_call x25, Pallas kernels, call(): pl.pallas_call(kernel, out_shape=out_shape, in_specs=[VMEM] * len(operand...  51.2 us
    ppermute x12, waiting for transfers between devices, line(): return lax.ppermute(array, 'expert', pairs)  30.5 us
    ppermute x12, waiting for transfers between devices, across(): return lax.ppermute(array, 'helper', self.sides)  21.3 us
    ppermute x12, starting transfers between devices, line(): return lax.ppermute(array, 'expert', pairs)  17.6 us
    ppermute x12, starting transfers between devices, across(): return lax.ppermute(array, 'helper', self.sides)  15.6 us
    pallas_call x1, Pallas kernels, load(): pl.pallas_call(load_kernel, out_shape=tuple((jax.ShapeDtypeStruct(mat.sha...  4.73 us
    ppermute x12, waiting for transfers between devices, sibling(): return lax.ppermute(array, 'expert', self.cores)  4.23 us
  transfers between devices with their start and end apart: 36, of which 17 were waited for; matrix products, arithmetic and copies ran while one was open for 0% of the time, Pallas kernels for 36%

profile of v5, /device:TPU:0, one launch (start us, length us, event | category | flops | bytes accessed | tf_op | source)
XLA Modules:
  0.0 150.1 jit_solution(10635376160064132960)
XLA Ops:
  0.6 1.3 prepare_rows.1
  1.9 0.5 collective-permute-start.1
  2.5 2.6 %collective-permute-start = (bf16[64,2176]{1,0:T(8,128)(2,1)S(1)}, bf16[64,2176]{1,0:T(8,128)(2,1)S(1)}, u32[]{:S(2)}, u32[]{:S(2)}) collective-permute-start(bf16[64,2176]{1,0:T(8,128)(2,1)S(1)} %get-tuple-element.175), channel_id=1, source_target_pairs={{0,4},{2,6},{4,0},{6,2},{8,12},{10,14},{12,8},{14,10},{1,5},{3,7},... | collective-permute-start | bytes 835592 | tf_op jit(solution)/shard_map/rows_line/ppermute | solution.py:366
  5.1 2.6 %collective-permute-start.3 = (bf16[64,2176]{1,0:T(8,128)(2,1)S(1)}, bf16[64,2176]{1,0:T(8,128)(2,1)S(1)}, u32[]{:S(2)}, u32[]{:S(2)}) collective-permute-start(bf16[64,2176]{1,0:T(8,128)(2,1)S(1)} %get-tuple-element.175), channel_id=1, source_target_pairs={{0,8},{2,10},{4,12},{6,14},{8,0},{10,2},{12,4},{14,6},{1,9},{3,11}... | collective-permute-start | bytes 835592 | tf_op jit(solution)/shard_map/rows_line/ppermute | solution.py:366
  7.7 4.7 %load.1 = (bf16[2048,1024]{1,0:T(8,128)(2,1)S(1)}, bf16[2048,1024]{1,0:T(8,128)(2,1)S(1)}, bf16[1024,2048]{1,0:T(8,128)(2,1)S(1)}) custom-call(bf16[2048,1024]{1,0:T(8,128)(2,1)} %bitcast.16, bf16[2048,1024]{1,0:T(8,128)(2,1)} %bitcast.17, bf16[1024,2048]{1,0:T(8,128)(2,1)} %bitcast.18), custom_call_target="tpu_custom_call" | custom-call | tf_op jit(solution)/shard_map/load/pallas_call | solution.py:408
  12.4 5.8 %collective-permute-done.first = bf16[64,2176]{1,0:T(8,128)(2,1)S(1)} collective-permute-done((bf16[64,2176]{1,0:T(8,128)(2,1)S(1)}, bf16[64,2176]{1,0:T(8,128)(2,1)S(1)}, u32[]{:S(2)}, u32[]{:S(2)}) %collective-permute-start) | collective-permute-done | bytes 278560 | tf_op jit(solution)/shard_map/rows_line/ppermute | solution.py:366
  18.2 1.7 %collective-permute-start.2 = (bf16[64,2176]{1,0:T(8,128)(2,1)S(1)}, bf16[64,2176]{1,0:T(8,128)(2,1)S(1)}, u32[]{:S(2)}, u32[]{:S(2)}) collective-permute-start(bf16[64,2176]{1,0:T(8,128)(2,1)S(1)} %collective-permute-done.first), channel_id=1, source_target_pairs={{0,1},{1,0},{2,3},{3,2},{4,5},{5,4},{6,7},{7,6},{8,9},{9,8},{10,11... | collective-permute-start | bytes 835592 | tf_op jit(solution)/shard_map/rows_across/ppermute | solution.py:374
  19.9 0.8 collective-permute-done.3.first
  20.8 5.8 %collective-permute-done.2.second = bf16[64,2176]{1,0:T(8,128)(2,1)S(1)} collective-permute-done((bf16[64,2176]{1,0:T(8,128)(2,1)S(1)}, bf16[64,2176]{1,0:T(8,128)(2,1)S(1)}, u32[]{:S(2)}, u32[]{:S(2)}) %collective-permute-start.2) | collective-permute-done | bytes 278560 | tf_op jit(solution)/shard_map/rows_across/ppermute | solution.py:374
  26.7 0.5 collective-permute-start.6
  27.2 1.5 %collective-permute-start.7 = (bf16[64,2176]{1,0:T(8,128)(2,1)S(1)}, bf16[64,2176]{1,0:T(8,128)(2,1)S(1)}, u32[]{:S(2)}, u32[]{:S(2)}) collective-permute-start(bf16[64,2176]{1,0:T(8,128)(2,1)S(1)} %collective-permute-done.3.first), channel_id=1, source_target_pairs={{0,1},{1,0},{2,3},{3,2},{4,5},{5,4},{6,7},{7,6},{8,9},{9,8},{10,11... | collective-permute-start | bytes 835592 | tf_op jit(solution)/shard_map/rows_across/ppermute | solution.py:374
  28.8 7.1 %collective-permute-done.5.first = bf16[64,2176]{1,0:T(8,128)(2,1)S(1)} collective-permute-done((bf16[64,2176]{1,0:T(8,128)(2,1)S(1)}, bf16[64,2176]{1,0:T(8,128)(2,1)S(1)}, u32[]{:S(2)}, u32[]{:S(2)}) %collective-permute-start.5) | collective-permute-done | bytes 278560 | tf_op jit(solution)/shard_map/rows_line/ppermute | solution.py:366
  36.2 2.7 %collective-permute-start.9 = (bf16[64,2048]{1,0:T(8,128)(2,1)S(1)}, bf16[64,2048]{1,0:T(8,128)(2,1)S(1)}, u32[]{:S(2)}, u32[]{:S(2)}) collective-permute-start(bf16[64,2048]{1,0:T(8,128)(2,1)S(1)} %get-tuple-element.196), channel_id=1, source_target_pairs={{0,8},{2,10},{4,12},{6,14},{8,0},{10,2},{12,4},{14,6},{1,9},{3,11}... | collective-permute-start | bytes 786440 | tf_op jit(solution)/shard_map/grads_line/ppermute | solution.py:366
  38.9 1.5 %collective-permute-start.8 = (bf16[64,2176]{1,0:T(8,128)(2,1)S(1)}, bf16[64,2176]{1,0:T(8,128)(2,1)S(1)}, u32[]{:S(2)}, u32[]{:S(2)}) collective-permute-start(bf16[64,2176]{1,0:T(8,128)(2,1)S(1)} %collective-permute-done.5.first), channel_id=1, source_target_pairs={{0,1},{1,0},{2,3},{3,2},{4,5},{5,4},{6,7},{7,6},{8,9},{9,8},{10,11... | collective-permute-start | bytes 835592 | tf_op jit(solution)/shard_map/rows_across/ppermute | solution.py:374
  40.4 6.8 %forward.2 = (f32[512,1024]{1,0:T(8,128)S(1)}, f32[512,1024]{1,0:T(8,128)S(1)}, bf16[512,1024]{1,0:T(8,128)(2,1)S(1)}, bf16[2,256,1024]{2,1,0:T(8,128)(2,1)S(1)}, bf16[2,256,1024]{2,1,0:T(8,128)(2,1)S(1)}) custom-call(bf16[128,2176]{1,0:T(8,128)(2,1)S(1)} %get-tuple-element.318.refs_0_.refs_4_, bf16[128,2176]{1,0:T(8,128)(2,1)S(1)} %pair.6.refs_1_.refs_5_, ...), custom_call_target="tpu_custom_call" | custom-call | flops 6442450944 | tf_op jit(solution)/shard_map/forward/pallas_call | solution.py:40
  47.2 1.6 %collective-permute-done.10.first = bf16[64,2048]{1,0:T(8,128)(2,1)S(1)} collective-permute-done((bf16[64,2048]{1,0:T(8,128)(2,1)S(1)}, bf16[64,2048]{1,0:T(8,128)(2,1)S(1)}, u32[]{:S(2)}, u32[]{:S(2)}) %collective-permute-start.10) | collective-permute-done | bytes 262176 | tf_op jit(solution)/shard_map/grads_line/ppermute | solution.py:366
  48.8 1.4 collective-permute-done.9.first
  50.3 1.9 %collective-permute-done.11.refs_2_.refs_6_ = bf16[128,2176]{1,0:T(8,128)(2,1)S(1)} collective-permute-done((bf16[128,2176]{1,0:T(8,128)(2,1)S(1)}, bf16[128,2176]{1,0:T(8,128)(2,1)S(1)}, u32[]{:S(2)}, u32[]{:S(2)}) %collective-permute-start.11) | collective-permute-done | bytes 557088 | tf_op jit(solution)/shard_map/rows_cores/ppermute | solution.py:370
  53.0 1.5 %collective-permute-start.17 = (bf16[64,2048]{1,0:T(8,128)(2,1)S(1)}, bf16[64,2048]{1,0:T(8,128)(2,1)S(1)}, u32[]{:S(2)}, u32[]{:S(2)}) collective-permute-start(bf16[64,2048]{1,0:T(8,128)(2,1)S(1)} %collective-permute-done.10.first), channel_id=1, source_target_pairs={{0,1},{1,0},{2,3},{3,2},{4,5},{5,4},{6,7},{7,6},{8,9},{9,8},{10,11... | collective-permute-start | bytes 786440 | tf_op jit(solution)/shard_map/grads_across/ppermute | solution.py:374
  54.5 0.5 collective-permute-start.15
  55.0 6.8 %forward.3 = (f32[512,1024]{1,0:T(8,128)S(1)}, f32[512,1024]{1,0:T(8,128)S(1)}, bf16[512,1024]{1,0:T(8,128)(2,1)S(1)}, bf16[2,256,1024]{2,1,0:T(8,128)(2,1)S(1)}, bf16[2,256,1024]{2,1,0:T(8,128)(2,1)S(1)}) custom-call(bf16[128,2176]{1,0:T(8,128)(2,1)S(1)} %pair.7.refs_0_.refs_4_, bf16[128,2176]{1,0:T(8,128)(2,1)S(1)} %pair.8.refs_1_.refs_5_, ...), custom_call_target="tpu_custom_call" | custom-call | flops 6442450944 | tf_op jit(solution)/shard_map/forward/pallas_call | solution.py:40
  62.2 4.7 %collective-permute-done.15.second = bf16[64,2048]{1,0:T(8,128)(2,1)S(1)} collective-permute-done((bf16[64,2048]{1,0:T(8,128)(2,1)S(1)}, bf16[64,2048]{1,0:T(8,128)(2,1)S(1)}, u32[]{:S(2)}, u32[]{:S(2)}) %collective-permute-start.15) | collective-permute-done | bytes 262176 | tf_op jit(solution)/shard_map/grads_across/ppermute | solution.py:374
  67.1 0.6 collective-permute-start.18
  67.7 1.5 %collective-permute-start.21 = (bf16[64,2048]{1,0:T(8,128)(2,1)S(1)}, bf16[64,2048]{1,0:T(8,128)(2,1)S(1)}, u32[]{:S(2)}, u32[]{:S(2)}) collective-permute-start(bf16[64,2048]{1,0:T(8,128)(2,1)S(1)} %collective-permute-done.16.first), channel_id=1, source_target_pairs={{0,1},{1,0},{2,3},{3,2},{4,5},{5,4},{6,7},{7,6},{8,9},{9,8},{10,11... | collective-permute-start | bytes 786440 | tf_op jit(solution)/shard_map/grads_across/ppermute | solution.py:374
  69.2 1.9 %collective-permute-done.13.received = bf16[2,256,1024]{2,1,0:T(8,128)(2,1)S(1)} collective-permute-done((bf16[2,256,1024]{2,1,0:T(8,128)(2,1)S(1)}, bf16[2,256,1024]{2,1,0:T(8,128)(2,1)S(1)}, u32[]{:S(2)}, u32[]{:S(2)}) %collective-permute-start.13) | collective-permute-done | bytes 1048608 | tf_op jit(solution)/shard_map/out_cores/ppermute | solution.py:370
  71.2 1.6 %collective-permute-start.22 = (bf16[256,1024]{1,0:T(8,128)(2,1)S(1)}, bf16[256,1024]{1,0:T(8,128)(2,1)S(1)}, u32[]{:S(2)}, u32[]{:S(2)}) collective-permute-start(bf16[256,1024]{1,0:T(8,128)(2,1)S(1)} %out_send.2), channel_id=1, source_target_pairs={{0,1},{1,0},{2,3},{3,2},{4,5},{5,4},{6,7},{7,6},{8,9},{9,8},{10,11... | collective-permute-start | bytes 1572872 | tf_op jit(solution)/shard_map/out_across/ppermute | solution.py:374
  72.9 7.5 %backward.2 = (bf16[512,1024]{1,0:T(8,128)(2,1)S(1)}, bf16[512,1024]{1,0:T(8,128)(2,1)S(1)}, bf16[2,256,1152]{2,1,0:T(8,128)(2,1)S(1)}, bf16[2,256,1152]{2,1,0:T(8,128)(2,1)S(1)}) custom-call(bf16[128,2048]{1,0:T(8,128)(2,1)S(1)} %get-tuple-element.287.refs_0_, bf16[128,2048]{1,0:T(8,128)(2,1)S(1)} %pair.9.refs_1_, ...), custom_call_target="tpu_custom_call" | custom-call | flops 6442450944 | tf_op jit(solution)/shard_map/backward/pallas_call | solution.py:40
  80.4 7.2 %collective-permute-done.22.arrived = bf16[256,1024]{1,0:T(8,128)(2,1)S(1)} collective-permute-done((bf16[256,1024]{1,0:T(8,128)(2,1)S(1)}, bf16[256,1024]{1,0:T(8,128)(2,1)S(1)}, u32[]{:S(2)}, u32[]{:S(2)}) %collective-permute-start.22) | collective-permute-done | bytes 524320 | tf_op jit(solution)/shard_map/out_across/ppermute | solution.py:374
  87.9 1.6 %collective-permute-start.20 = (bf16[256,1024]{1,0:T(8,128)(2,1)S(1)}, bf16[256,1024]{1,0:T(8,128)(2,1)S(1)}, u32[]{:S(2)}, u32[]{:S(2)}) collective-permute-start(bf16[256,1024]{1,0:T(8,128)(2,1)S(1)} %out_send.3), channel_id=1, source_target_pairs={{0,1},{1,0},{2,3},{3,2},{4,5},{5,4},{6,7},{7,6},{8,9},{9,8},{10,11... | collective-permute-start | bytes 1572872 | tf_op jit(solution)/shard_map/out_across/ppermute | solution.py:374
  89.8 7.1 %backward.3 = (bf16[512,1024]{1,0:T(8,128)(2,1)S(1)}, bf16[512,1024]{1,0:T(8,128)(2,1)S(1)}, bf16[2,256,1152]{2,1,0:T(8,128)(2,1)S(1)}, bf16[2,256,1152]{2,1,0:T(8,128)(2,1)S(1)}) custom-call(bf16[128,2048]{1,0:T(8,128)(2,1)S(1)} %pair.10.refs_0_.refs_4_, bf16[128,2048]{1,0:T(8,128)(2,1)S(1)} %pair.11.refs_1_.refs_5_, ...), custom_call_target="tpu_custom_call" | custom-call | flops 6442450944 | tf_op jit(solution)/shard_map/backward/pallas_call | solution.py:40
  97.5 1.6 %collective-permute-start.24 = (bf16[128,1024]{1,0:T(8,128)(2,1)S(1)}, bf16[128,1024]{1,0:T(8,128)(2,1)S(1)}, u32[]{:S(2)}, u32[]{:S(2)}) collective-permute-start(bf16[128,1024]{1,0:T(8,128)(2,1)S(1)} %get-tuple-element.252), channel_id=1, source_target_pairs={{0,4},{2,6},{4,0},{6,2},{8,12},{10,14},{12,8},{14,10},{1,5},{3,7},... | collective-permute-start | bytes 786440 | tf_op jit(solution)/shard_map/out_line/ppermute | solution.py:366
  99.1 3.1 %collective-permute-done.20.arrived = bf16[256,1024]{1,0:T(8,128)(2,1)S(1)} collective-permute-done((bf16[256,1024]{1,0:T(8,128)(2,1)S(1)}, bf16[256,1024]{1,0:T(8,128)(2,1)S(1)}, u32[]{:S(2)}, u32[]{:S(2)}) %collective-permute-start.20) | collective-permute-done | bytes 524320 | tf_op jit(solution)/shard_map/out_across/ppermute | solution.py:374
  102.3 1.6 %collective-permute-start.30 = (bf16[128,1152]{1,0:T(8,128)(2,1)S(1)}, bf16[128,1152]{1,0:T(8,128)(2,1)S(1)}, u32[]{:S(2)}, u32[]{:S(2)}) collective-permute-start(bf16[128,1152]{1,0:T(8,128)(2,1)S(1)} %get-tuple-element.275), channel_id=1, source_target_pairs={{0,1},{1,0},{2,3},{3,2},{4,5},{5,4},{6,7},{7,6},{8,9},{9,8},{10,11... | collective-permute-start | bytes 884744 | tf_op jit(solution)/shard_map/in_across/ppermute | solution.py:374
  103.9 0.5 collective-permute-start.29
  104.5 1.4 collective-permute-done.24
  105.9 2.7 %collective-permute-start.28 = (bf16[128,1024]{1,0:T(8,128)(2,1)S(1)}, bf16[128,1024]{1,0:T(8,128)(2,1)S(1)}, u32[]{:S(2)}, u32[]{:S(2)}) collective-permute-start(bf16[128,1024]{1,0:T(8,128)(2,1)S(1)} %add.3), channel_id=1, source_target_pairs={{0,8},{2,10},{4,12},{6,14},{8,0},{10,2},{12,4},{14,6},{1,9},{3,11}... | collective-permute-start | bytes 786440 | tf_op jit(solution)/shard_map/out_line/ppermute | solution.py:366
  109.1 1.5 %collective-permute-start.32 = (bf16[128,1152]{1,0:T(8,128)(2,1)S(1)}, bf16[128,1152]{1,0:T(8,128)(2,1)S(1)}, u32[]{:S(2)}, u32[]{:S(2)}) collective-permute-start(bf16[128,1152]{1,0:T(8,128)(2,1)S(1)} %get-tuple-element.317), channel_id=1, source_target_pairs={{0,1},{1,0},{2,3},{3,2},{4,5},{5,4},{6,7},{7,6},{8,9},{9,8},{10,11... | collective-permute-start | bytes 884744 | tf_op jit(solution)/shard_map/in_across/ppermute | solution.py:374
  110.7 6.8 %grad_down.1 = bf16[1024,2048]{1,0:T(8,128)(2,1)} custom-call(bf16[128,2048]{1,0:T(8,128)(2,1)S(1)} %get-tuple-element.287.refs_0_, bf16[128,2048]{1,0:T(8,128)(2,1)S(1)} %pair.9.refs_1_, bf16[128,2048]{1,0:T(8,128)(2,1)S(1)} %collective-permute-done.6.refs_2_, bf16[128,2048]{1,0:T(8,128)(2,1)S(1)} %collective-permute-done.19.refs_3_, ...), custom_call_target="tpu_custom_call" | custom-call | flops 4294967296 | tf_op jit(solution)/shard_map/grad_down/pallas_call | solution.py:40
  117.6 1.8 %collective-permute-start.31 = (bf16[128,1152]{1,0:T(8,128)(2,1)S(1)}, bf16[128,1152]{1,0:T(8,128)(2,1)S(1)}, u32[]{:S(2)}, u32[]{:S(2)}) collective-permute-start(bf16[128,1152]{1,0:T(8,128)(2,1)S(1)} %in_slot.3), channel_id=1, source_target_pairs={{0,4},{2,6},{4,0},{6,2},{8,12},{10,14},{12,8},{14,10},{1,5},{3,7},... | collective-permute-start | bytes 884744 | tf_op jit(solution)/shard_map/in_line/ppermute | solution.py:366
  119.4 6.5 %grad_gate.1 = bf16[2048,1024]{1,0:T(8,128)(2,1)} custom-call(bf16[128,2176]{1,0:T(8,128)(2,1)S(1)} %get-tuple-element.318.refs_0_.refs_4_, bf16[128,2176]{1,0:T(8,128)(2,1)S(1)} %pair.6.refs_1_.refs_5_, bf16[128,2176]{1,0:T(8,128)(2,1)S(1)} %collective-permute-done.1.refs_2_.refs_6_, bf16[128,2176]{1,0:T(8,128)(2,1)S(1)} %collective-permute-done.4.refs_3_.refs_7_, ...), custom_call_target="tpu_custom_call" | custom-call | flops 4294967296 | tf_op jit(solution)/shard_map/grad_gate/pallas_call | solution.py:40
  126.0 0.5 collective-permute-start.35
  127.1 1.2 collective-permute-start.33
  128.2 0.8 finish_outputs.1
  129.0 6.5 %grad_up.1 = bf16[2048,1024]{1,0:T(8,128)(2,1)} custom-call(bf16[128,2176]{1,0:T(8,128)(2,1)S(1)} %get-tuple-element.318.refs_0_.refs_4_, bf16[128,2176]{1,0:T(8,128)(2,1)S(1)} %pair.6.refs_1_.refs_5_, bf16[128,2176]{1,0:T(8,128)(2,1)S(1)} %collective-permute-done.1.refs_2_.refs_6_, bf16[128,2176]{1,0:T(8,128)(2,1)S(1)} %collective-permute-done.4.refs_3_.refs_7_, ...), custom_call_target="tpu_custom_call" | custom-call | flops 4294967296 | tf_op jit(solution)/shard_map/grad_up/pallas_call | solution.py:40
  135.7 1.3 collective-permute-start.34
  137.0 5.7 %collective-permute-done.33.refs_0_ = bf16[128,1152]{1,0:T(8,128)(2,1)S(1)} collective-permute-done((bf16[128,1152]{1,0:T(8,128)(2,1)S(1)}, bf16[128,1152]{1,0:T(8,128)(2,1)S(1)}, u32[]{:S(2)}, u32[]{:S(2)}) %collective-permute-start.33) | collective-permute-done | bytes 294944 | tf_op jit(solution)/shard_map/in_line/ppermute | solution.py:366
  142.8 6.2 %collective-permute-done.34.refs_1_ = bf16[128,1152]{1,0:T(8,128)(2,1)S(1)} collective-permute-done((bf16[128,1152]{1,0:T(8,128)(2,1)S(1)}, bf16[128,1152]{1,0:T(8,128)(2,1)S(1)}, u32[]{:S(2)}, u32[]{:S(2)}) %collective-permute-start.34) | collective-permute-done | bytes 294944 | tf_op jit(solution)/shard_map/in_line/ppermute | solution.py:366
  149.0 1.1 finish_inputs.1
  (63 shorter events, 4.7 us)
Async XLA Ops:
  1.9 16.3 %collective-permute-start.1 = (bf16[128,2176]{1,0:T(8,128)(2,1)S(1)}, bf16[128,2176]{1,0:T(8,128)(2,1)S(1)}, u32[]{:S(2)}, u32[]{:S(2)}) collective-permute-start(bf16[128,2176]{1,0:T(8,128)(2,1)S(1)} %get-tuple-element.318.refs_0_.refs_4_), channel_id=1, source_target_pairs={{0,2},{2,0},{4,6},{6,4},{8,10},{10,8},{12,14},{14,12},{1,3},{3,1},... | collective-permute-start | bytes 1671176 | tf_op jit(solution)/shard_map/rows_cores/ppermute | solution.py:370
  2.5 15.8 %collective-permute-start = (bf16[64,2176]{1,0:T(8,128)(2,1)S(1)}, bf16[64,2176]{1,0:T(8,128)(2,1)S(1)}, u32[]{:S(2)}, u32[]{:S(2)}) collective-permute-start(bf16[64,2176]{1,0:T(8,128)(2,1)S(1)} %get-tuple-element.175), channel_id=1, source_target_pairs={{0,4},{2,6},{4,0},{6,2},{8,12},{10,14},{12,8},{14,10},{1,5},{3,7},... | collective-permute-start | bytes 835592 | tf_op jit(solution)/shard_map/rows_line/ppermute | solution.py:366
  5.1 15.6 %collective-permute-start.3 = (bf16[64,2176]{1,0:T(8,128)(2,1)S(1)}, bf16[64,2176]{1,0:T(8,128)(2,1)S(1)}, u32[]{:S(2)}, u32[]{:S(2)}) collective-permute-start(bf16[64,2176]{1,0:T(8,128)(2,1)S(1)} %get-tuple-element.175), channel_id=1, source_target_pairs={{0,8},{2,10},{4,12},{6,14},{8,0},{10,2},{12,4},{14,6},{1,9},{3,11}... | collective-permute-start | bytes 835592 | tf_op jit(solution)/shard_map/rows_line/ppermute | solution.py:366
  7.7 13.1 %copy-start = (bf16[128,2048]{1,0:T(8,128)(2,1)S(1)}, bf16[128,2048]{1,0:T(8,128)(2,1)}, u32[]{:S(2)}) copy-start(bf16[128,2048]{1,0:T(8,128)(2,1)} %rows) | copy-start | bytes 1572868
  18.2 8.4 %collective-permute-start.2 = (bf16[64,2176]{1,0:T(8,128)(2,1)S(1)}, bf16[64,2176]{1,0:T(8,128)(2,1)S(1)}, u32[]{:S(2)}, u32[]{:S(2)}) collective-permute-start(bf16[64,2176]{1,0:T(8,128)(2,1)S(1)} %collective-permute-done.first), channel_id=1, source_target_pairs={{0,1},{1,0},{2,3},{3,2},{4,5},{5,4},{6,7},{7,6},{8,9},{9,8},{10,11... | collective-permute-start | bytes 835592 | tf_op jit(solution)/shard_map/rows_across/ppermute | solution.py:374
  26.7 13.8 %collective-permute-start.4 = (bf16[128,2176]{1,0:T(8,128)(2,1)S(1)}, bf16[128,2176]{1,0:T(8,128)(2,1)S(1)}, u32[]{:S(2)}, u32[]{:S(2)}) collective-permute-start(bf16[128,2176]{1,0:T(8,128)(2,1)S(1)} %pair.6.refs_1_.refs_5_), channel_id=1, source_target_pairs={{0,2},{2,0},{4,6},{6,4},{8,10},{10,8},{12,14},{14,12},{1,3},{3,1},... | collective-permute-start | bytes 1671176 | tf_op jit(solution)/shard_map/rows_cores/ppermute | solution.py:370
  26.7 12.2 %collective-permute-start.6 = (bf16[128,2048]{1,0:T(8,128)(2,1)S(1)}, bf16[128,2048]{1,0:T(8,128)(2,1)S(1)}, u32[]{:S(2)}, u32[]{:S(2)}) collective-permute-start(bf16[128,2048]{1,0:T(8,128)(2,1)S(1)} %get-tuple-element.287.refs_0_), channel_id=1, source_target_pairs={{0,2},{2,0},{4,6},{6,4},{8,10},{10,8},{12,14},{14,12},{1,3},{3,1},... | collective-permute-start | bytes 1572872 | tf_op jit(solution)/shard_map/grads_cores/ppermute | solution.py:370
  27.2 8.6 %collective-permute-start.5 = (bf16[64,2176]{1,0:T(8,128)(2,1)S(1)}, bf16[64,2176]{1,0:T(8,128)(2,1)S(1)}, u32[]{:S(2)}, u32[]{:S(2)}) collective-permute-start(bf16[64,2176]{1,0:T(8,128)(2,1)S(1)} %collective-permute-done.3.first), channel_id=1, source_target_pairs={{0,4},{2,6},{4,0},{6,2},{8,12},{10,14},{12,8},{14,10},{1,5},{3,7},... | collective-permute-start | bytes 835592 | tf_op jit(solution)/shard_map/rows_line/ppermute | solution.py:366
  27.2 23.0 %collective-permute-start.7 = (bf16[64,2176]{1,0:T(8,128)(2,1)S(1)}, bf16[64,2176]{1,0:T(8,128)(2,1)S(1)}, u32[]{:S(2)}, u32[]{:S(2)}) collective-permute-start(bf16[64,2176]{1,0:T(8,128)(2,1)S(1)} %collective-permute-done.3.first), channel_id=1, source_target_pairs={{0,1},{1,0},{2,3},{3,2},{4,5},{5,4},{6,7},{7,6},{8,9},{9,8},{10,11... | collective-permute-start | bytes 835592 | tf_op jit(solution)/shard_map/rows_across/ppermute | solution.py:374
  35.9 12.9 %collective-permute-start.10 = (bf16[64,2048]{1,0:T(8,128)(2,1)S(1)}, bf16[64,2048]{1,0:T(8,128)(2,1)S(1)}, u32[]{:S(2)}, u32[]{:S(2)}) collective-permute-start(bf16[64,2048]{1,0:T(8,128)(2,1)S(1)} %get-tuple-element.196), channel_id=1, source_target_pairs={{0,4},{2,6},{4,0},{6,2},{8,12},{10,14},{12,8},{14,10},{1,5},{3,7},... | collective-permute-start | bytes 786440 | tf_op jit(solution)/shard_map/grads_line/ppermute | solution.py:366
  36.2 14.0 %collective-permute-start.9 = (bf16[64,2048]{1,0:T(8,128)(2,1)S(1)}, bf16[64,2048]{1,0:T(8,128)(2,1)S(1)}, u32[]{:S(2)}, u32[]{:S(2)}) collective-permute-start(bf16[64,2048]{1,0:T(8,128)(2,1)S(1)} %get-tuple-element.196), channel_id=1, source_target_pairs={{0,8},{2,10},{4,12},{6,14},{8,0},{10,2},{12,4},{14,6},{1,9},{3,11}... | collective-permute-start | bytes 786440 | tf_op jit(solution)/shard_map/grads_line/ppermute | solution.py:366
  38.9 11.3 %collective-permute-start.8 = (bf16[64,2176]{1,0:T(8,128)(2,1)S(1)}, bf16[64,2176]{1,0:T(8,128)(2,1)S(1)}, u32[]{:S(2)}, u32[]{:S(2)}) collective-permute-start(bf16[64,2176]{1,0:T(8,128)(2,1)S(1)} %collective-permute-done.5.first), channel_id=1, source_target_pairs={{0,1},{1,0},{2,3},{3,2},{4,5},{5,4},{6,7},{7,6},{8,9},{9,8},{10,11... | collective-permute-start | bytes 835592 | tf_op jit(solution)/shard_map/rows_across/ppermute | solution.py:374
  50.3 2.0 %collective-permute-start.11 = (bf16[128,2176]{1,0:T(8,128)(2,1)S(1)}, bf16[128,2176]{1,0:T(8,128)(2,1)S(1)}, u32[]{:S(2)}, u32[]{:S(2)}) collective-permute-start(bf16[128,2176]{1,0:T(8,128)(2,1)S(1)} %pair.7.refs_0_.refs_4_), channel_id=1, source_target_pairs={{0,2},{2,0},{4,6},{6,4},{8,10},{10,8},{12,14},{14,12},{1,3},{3,1},... | collective-permute-start | bytes 1671176 | tf_op jit(solution)/shard_map/rows_cores/ppermute | solution.py:370
  52.3 2.7 %collective-permute-start.12 = (bf16[128,2176]{1,0:T(8,128)(2,1)S(1)}, bf16[128,2176]{1,0:T(8,128)(2,1)S(1)}, u32[]{:S(2)}, u32[]{:S(2)}) collective-permute-start(bf16[128,2176]{1,0:T(8,128)(2,1)S(1)} %pair.8.refs_1_.refs_5_), channel_id=1, source_target_pairs={{0,2},{2,0},{4,6},{6,4},{8,10},{10,8},{12,14},{14,12},{1,3},{3,1},... | collective-permute-start | bytes 1671176 | tf_op jit(solution)/shard_map/rows_cores/ppermute | solution.py:370
  52.5 9.3 %collective-permute-start.16 = (bf16[64,2048]{1,0:T(8,128)(2,1)S(1)}, bf16[64,2048]{1,0:T(8,128)(2,1)S(1)}, u32[]{:S(2)}, u32[]{:S(2)}) collective-permute-start(bf16[64,2048]{1,0:T(8,128)(2,1)S(1)} %collective-permute-done.9.first), channel_id=1, source_target_pairs={{0,4},{2,6},{4,0},{6,2},{8,12},{10,14},{12,8},{14,10},{1,5},{3,7},... | collective-permute-start | bytes 786440 | tf_op jit(solution)/shard_map/grads_line/ppermute | solution.py:366
  53.0 9.2 %collective-permute-start.17 = (bf16[64,2048]{1,0:T(8,128)(2,1)S(1)}, bf16[64,2048]{1,0:T(8,128)(2,1)S(1)}, u32[]{:S(2)}, u32[]{:S(2)}) collective-permute-start(bf16[64,2048]{1,0:T(8,128)(2,1)S(1)} %collective-permute-done.10.first), channel_id=1, source_target_pairs={{0,1},{1,0},{2,3},{3,2},{4,5},{5,4},{6,7},{7,6},{8,9},{9,8},{10,11... | collective-permute-start | bytes 786440 | tf_op jit(solution)/shard_map/grads_across/ppermute | solution.py:374
  54.5 12.4 %collective-permute-start.15 = (bf16[64,2048]{1,0:T(8,128)(2,1)S(1)}, bf16[64,2048]{1,0:T(8,128)(2,1)S(1)}, u32[]{:S(2)}, u32[]{:S(2)}) collective-permute-start(bf16[64,2048]{1,0:T(8,128)(2,1)S(1)} %collective-permute-done.9.first), channel_id=1, source_target_pairs={{0,1},{1,0},{2,3},{3,2},{4,5},{5,4},{6,7},{7,6},{8,9},{9,8},{10,11... | collective-permute-start | bytes 786440 | tf_op jit(solution)/shard_map/grads_across/ppermute | solution.py:374
  55.0 14.2 %collective-permute-start.14 = (bf16[2,256,1024]{2,1,0:T(8,128)(2,1)S(1)}, bf16[2,256,1024]{2,1,0:T(8,128)(2,1)S(1)}, u32[]{:S(2)}, u32[]{:S(2)}) collective-permute-start(bf16[2,256,1024]{2,1,0:T(8,128)(2,1)S(1)} %get-tuple-element.203), channel_id=1, source_target_pairs={{0,2},{2,0},{4,6},{6,4},{8,10},{10,8},{12,14},{14,12},{1,3},{3,1},... | collective-permute-start | bytes 3145736 | tf_op jit(solution)/shard_map/out_cores/ppermute | solution.py:370
  66.9 4.2 %collective-permute-start.19 = (bf16[128,2048]{1,0:T(8,128)(2,1)S(1)}, bf16[128,2048]{1,0:T(8,128)(2,1)S(1)}, u32[]{:S(2)}, u32[]{:S(2)}) collective-permute-start(bf16[128,2048]{1,0:T(8,128)(2,1)S(1)} %pair.9.refs_1_), channel_id=1, source_target_pairs={{0,2},{2,0},{4,6},{6,4},{8,10},{10,8},{12,14},{14,12},{1,3},{3,1},... | collective-permute-start | bytes 1572872 | tf_op jit(solution)/shard_map/grads_cores/ppermute | solution.py:370
  67.1 4.1 %collective-permute-start.18 = (bf16[128,2048]{1,0:T(8,128)(2,1)S(1)}, bf16[128,2048]{1,0:T(8,128)(2,1)S(1)}, u32[]{:S(2)}, u32[]{:S(2)}) collective-permute-start(bf16[128,2048]{1,0:T(8,128)(2,1)S(1)} %pair.10.refs_0_.refs_4_), channel_id=1, source_target_pairs={{0,2},{2,0},{4,6},{6,4},{8,10},{10,8},{12,14},{14,12},{1,3},{3,1},... | collective-permute-start | bytes 1572872 | tf_op jit(solution)/shard_map/grads_cores/ppermute | solution.py:370
  67.6 3.5 %collective-permute-start.13 = (bf16[2,256,1024]{2,1,0:T(8,128)(2,1)S(1)}, bf16[2,256,1024]{2,1,0:T(8,128)(2,1)S(1)}, u32[]{:S(2)}, u32[]{:S(2)}) collective-permute-start(bf16[2,256,1024]{2,1,0:T(8,128)(2,1)S(1)} %get-tuple-element.213), channel_id=1, source_target_pairs={{0,2},{2,0},{4,6},{6,4},{8,10},{10,8},{12,14},{14,12},{1,3},{3,1},... | collective-permute-start | bytes 3145736 | tf_op jit(solution)/shard_map/out_cores/ppermute | solution.py:370
  67.7 12.7 %collective-permute-start.21 = (bf16[64,2048]{1,0:T(8,128)(2,1)S(1)}, bf16[64,2048]{1,0:T(8,128)(2,1)S(1)}, u32[]{:S(2)}, u32[]{:S(2)}) collective-permute-start(bf16[64,2048]{1,0:T(8,128)(2,1)S(1)} %collective-permute-done.16.first), channel_id=1, source_target_pairs={{0,1},{1,0},{2,3},{3,2},{4,5},{5,4},{6,7},{7,6},{8,9},{9,8},{10,11... | collective-permute-start | bytes 786440 | tf_op jit(solution)/shard_map/grads_across/ppermute | solution.py:374
  71.2 16.4 %collective-permute-start.22 = (bf16[256,1024]{1,0:T(8,128)(2,1)S(1)}, bf16[256,1024]{1,0:T(8,128)(2,1)S(1)}, u32[]{:S(2)}, u32[]{:S(2)}) collective-permute-start(bf16[256,1024]{1,0:T(8,128)(2,1)S(1)} %out_send.2), channel_id=1, source_target_pairs={{0,1},{1,0},{2,3},{3,2},{4,5},{5,4},{6,7},{7,6},{8,9},{9,8},{10,11... | collective-permute-start | bytes 1572872 | tf_op jit(solution)/shard_map/out_across/ppermute | solution.py:374
  87.8 2.0 %collective-permute-start.23 = (bf16[128,2048]{1,0:T(8,128)(2,1)S(1)}, bf16[128,2048]{1,0:T(8,128)(2,1)S(1)}, u32[]{:S(2)}, u32[]{:S(2)}) collective-permute-start(bf16[128,2048]{1,0:T(8,128)(2,1)S(1)} %pair.11.refs_1_.refs_5_), channel_id=1, source_target_pairs={{0,2},{2,0},{4,6},{6,4},{8,10},{10,8},{12,14},{14,12},{1,3},{3,1},... | collective-permute-start | bytes 1572872 | tf_op jit(solution)/shard_map/grads_cores/ppermute | solution.py:370
  87.9 14.3 %collective-permute-start.20 = (bf16[256,1024]{1,0:T(8,128)(2,1)S(1)}, bf16[256,1024]{1,0:T(8,128)(2,1)S(1)}, u32[]{:S(2)}, u32[]{:S(2)}) collective-permute-start(bf16[256,1024]{1,0:T(8,128)(2,1)S(1)} %out_send.3), channel_id=1, source_target_pairs={{0,1},{1,0},{2,3},{3,2},{4,5},{5,4},{6,7},{7,6},{8,9},{9,8},{10,11... | collective-permute-start | bytes 1572872 | tf_op jit(solution)/shard_map/out_across/ppermute | solution.py:374
  97.0 5.3 %collective-permute-start.26 = (bf16[2,256,1152]{2,1,0:T(8,128)(2,1)S(1)}, bf16[2,256,1152]{2,1,0:T(8,128)(2,1)S(1)}, u32[]{:S(2)}, u32[]{:S(2)}) collective-permute-start(bf16[2,256,1152]{2,1,0:T(8,128)(2,1)S(1)} %get-tuple-element.268), channel_id=1, source_target_pairs={{0,2},{2,0},{4,6},{6,4},{8,10},{10,8},{12,14},{14,12},{1,3},{3,1},... | collective-permute-start | bytes 3538952 | tf_op jit(solution)/shard_map/in_cores/ppermute | solution.py:370
  97.2 7.3 %collective-permute-start.25 = (bf16[2,256,1152]{2,1,0:T(8,128)(2,1)S(1)}, bf16[2,256,1152]{2,1,0:T(8,128)(2,1)S(1)}, u32[]{:S(2)}, u32[]{:S(2)}) collective-permute-start(bf16[2,256,1152]{2,1,0:T(8,128)(2,1)S(1)} %get-tuple-element.247), channel_id=1, source_target_pairs={{0,2},{2,0},{4,6},{6,4},{8,10},{10,8},{12,14},{14,12},{1,3},{3,1},... | collective-permute-start | bytes 3538952 | tf_op jit(solution)/shard_map/in_cores/ppermute | solution.py:370
  97.5 8.3 %collective-permute-start.24 = (bf16[128,1024]{1,0:T(8,128)(2,1)S(1)}, bf16[128,1024]{1,0:T(8,128)(2,1)S(1)}, u32[]{:S(2)}, u32[]{:S(2)}) collective-permute-start(bf16[128,1024]{1,0:T(8,128)(2,1)S(1)} %get-tuple-element.252), channel_id=1, source_target_pairs={{0,4},{2,6},{4,0},{6,2},{8,12},{10,14},{12,8},{14,10},{1,5},{3,7},... | collective-permute-start | bytes 786440 | tf_op jit(solution)/shard_map/out_line/ppermute | solution.py:366
  102.3 15.2 %collective-permute-start.30 = (bf16[128,1152]{1,0:T(8,128)(2,1)S(1)}, bf16[128,1152]{1,0:T(8,128)(2,1)S(1)}, u32[]{:S(2)}, u32[]{:S(2)}) collective-permute-start(bf16[128,1152]{1,0:T(8,128)(2,1)S(1)} %get-tuple-element.275), channel_id=1, source_target_pairs={{0,1},{1,0},{2,3},{3,2},{4,5},{5,4},{6,7},{7,6},{8,9},{9,8},{10,11... | collective-permute-start | bytes 884744 | tf_op jit(solution)/shard_map/in_across/ppermute | solution.py:374
  103.9 22.0 %collective-permute-start.29 = (bf16[128,1152]{1,0:T(8,128)(2,1)S(1)}, bf16[128,1152]{1,0:T(8,128)(2,1)S(1)}, u32[]{:S(2)}, u32[]{:S(2)}) collective-permute-start(bf16[128,1152]{1,0:T(8,128)(2,1)S(1)} %get-tuple-element.274), channel_id=1, source_target_pairs={{0,1},{1,0},{2,3},{3,2},{4,5},{5,4},{6,7},{7,6},{8,9},{9,8},{10,11... | collective-permute-start | bytes 884744 | tf_op jit(solution)/shard_map/in_across/ppermute | solution.py:374
  105.9 22.3 %collective-permute-start.28 = (bf16[128,1024]{1,0:T(8,128)(2,1)S(1)}, bf16[128,1024]{1,0:T(8,128)(2,1)S(1)}, u32[]{:S(2)}, u32[]{:S(2)}) collective-permute-start(bf16[128,1024]{1,0:T(8,128)(2,1)S(1)} %add.3), channel_id=1, source_target_pairs={{0,8},{2,10},{4,12},{6,14},{8,0},{10,2},{12,4},{14,6},{1,9},{3,11}... | collective-permute-start | bytes 786440 | tf_op jit(solution)/shard_map/out_line/ppermute | solution.py:366
  108.8 19.4 %collective-permute-start.27 = (bf16[128,1024]{1,0:T(8,128)(2,1)S(1)}, bf16[128,1024]{1,0:T(8,128)(2,1)S(1)}, u32[]{:S(2)}, u32[]{:S(2)}) collective-permute-start(bf16[128,1024]{1,0:T(8,128)(2,1)S(1)} %get-tuple-element.286), channel_id=1, source_target_pairs={{0,4},{2,6},{4,0},{6,2},{8,12},{10,14},{12,8},{14,10},{1,5},{3,7},... | collective-permute-start | bytes 786440 | tf_op jit(solution)/shard_map/out_line/ppermute | solution.py:366
  109.1 26.4 %collective-permute-start.32 = (bf16[128,1152]{1,0:T(8,128)(2,1)S(1)}, bf16[128,1152]{1,0:T(8,128)(2,1)S(1)}, u32[]{:S(2)}, u32[]{:S(2)}) collective-permute-start(bf16[128,1152]{1,0:T(8,128)(2,1)S(1)} %get-tuple-element.317), channel_id=1, source_target_pairs={{0,1},{1,0},{2,3},{3,2},{4,5},{5,4},{6,7},{7,6},{8,9},{9,8},{10,11... | collective-permute-start | bytes 884744 | tf_op jit(solution)/shard_map/in_across/ppermute | solution.py:374
  117.6 9.3 %collective-permute-start.31 = (bf16[128,1152]{1,0:T(8,128)(2,1)S(1)}, bf16[128,1152]{1,0:T(8,128)(2,1)S(1)}, u32[]{:S(2)}, u32[]{:S(2)}) collective-permute-start(bf16[128,1152]{1,0:T(8,128)(2,1)S(1)} %in_slot.3), channel_id=1, source_target_pairs={{0,4},{2,6},{4,0},{6,2},{8,12},{10,14},{12,8},{14,10},{1,5},{3,7},... | collective-permute-start | bytes 884744 | tf_op jit(solution)/shard_map/in_line/ppermute | solution.py:366
  126.0 16.8 %collective-permute-start.35 = (bf16[128,1152]{1,0:T(8,128)(2,1)S(1)}, bf16[128,1152]{1,0:T(8,128)(2,1)S(1)}, u32[]{:S(2)}, u32[]{:S(2)}) collective-permute-start(bf16[128,1152]{1,0:T(8,128)(2,1)S(1)} %get-tuple-element.332), channel_id=1, source_target_pairs={{0,1},{1,0},{2,3},{3,2},{4,5},{5,4},{6,7},{7,6},{8,9},{9,8},{10,11... | collective-permute-start | bytes 884744 | tf_op jit(solution)/shard_map/in_across/ppermute | solution.py:374
  127.1 15.7 %collective-permute-start.33 = (bf16[128,1152]{1,0:T(8,128)(2,1)S(1)}, bf16[128,1152]{1,0:T(8,128)(2,1)S(1)}, u32[]{:S(2)}, u32[]{:S(2)}) collective-permute-start(bf16[128,1152]{1,0:T(8,128)(2,1)S(1)} %in_slot.4), channel_id=1, source_target_pairs={{0,8},{2,10},{4,12},{6,14},{8,0},{10,2},{12,4},{14,6},{1,9},{3,11}... | collective-permute-start | bytes 884744 | tf_op jit(solution)/shard_map/in_line/ppermute | solution.py:366
  135.7 13.3 %copy-start.1 = (s32[128,4]{0,1:T(4,128)S(1)}, s32[128,4]{0,1:T(4,128)}, u32[]{:S(2)}) copy-start(s32[128,4]{0,1:T(4,128)} %param.9) | copy-start | bytes 6148
  135.7 13.3 %copy-start.2 = (f32[128,4]{0,1:T(4,128)S(1)}, f32[128,4]{0,1:T(4,128)}, u32[]{:S(2)}) copy-start(f32[128,4]{0,1:T(4,128)} %param.11) | copy-start | bytes 6148
  135.7 13.3 %copy-start.3 = (s32[128]{0:T(128)S(1)}, s32[128]{0:T(128)}, u32[]{:S(2)}) copy-start(s32[128]{0:T(128)} %param.10) | copy-start | bytes 1540
  135.7 13.2 %collective-permute-start.34 = (bf16[128,1152]{1,0:T(8,128)(2,1)S(1)}, bf16[128,1152]{1,0:T(8,128)(2,1)S(1)}, u32[]{:S(2)}, u32[]{:S(2)}) collective-permute-start(bf16[128,1152]{1,0:T(8,128)(2,1)S(1)} %in_slot.5), channel_id=1, source_target_pairs={{0,4},{2,6},{4,0},{6,2},{8,12},{10,14},{12,8},{14,10},{1,5},{3,7},... | collective-permute-start | bytes 884744 | tf_op jit(solution)/shard_map/in_line/ppermute | solution.py:366

commit v6 on v5

--- a/solution.py
+++ b/solution.py
@@ -36,7 +36,7 @@
     return functools.reduce(jnp.add, terms)
 
 
-def call(kernel, name, operands, out_shape, scratch=(), flops=0, moved=0, mebibytes=16):
+def call(kernel, name, operands, out_shape, scratch=(), flops=0, moved=0, mebibytes=12):
     return pl.pallas_call(
         kernel,
         out_shape=out_shape,
@@ -161,25 +161,38 @@
     return call(pair_kernel, "pair", (first, second), shape)
 
 
+def parts_of(pieces):
+    pair, line_pair, across_pair, last_pair = pieces
+    rows = pair.shape[0]
+    half = rows // 2
+    parts = [(pair, 0, rows)]
+    for slot in range(2):
+        parts = parts + [(line_pair, slot * half, half), (across_pair, slot * half, half)]
+    return parts + [(last_pair, 0, rows)]
+
+
 def lay_out(pieces, target, columns):
-    rows = pieces[0].shape[0]
-    for i, piece in enumerate(pieces):
-        target[i * rows : (i + 1) * rows, :] = piece[:, columns]
+    at = 0
+    for piece, start, rows in parts_of(pieces[:4]) + parts_of(pieces[4:]):
+        target[at : at + rows, :] = piece[start : start + rows, columns]
+        at = at + rows
 
 
 def gate_column(experts, pieces, width):
-    table = jnp.concatenate([piece[:, width:] for piece in pieces], axis=0)
+    parts = parts_of(pieces[:4]) + parts_of(pieces[4:])
+    table = jnp.concatenate(
+        [piece[start : start + rows, width:] for piece, start, rows in parts], axis=0
+    )
     lane = lax.broadcasted_iota(jnp.int32, table.shape, 1)
     expert = lax.axis_index("expert")
     mine = (lane == expert) | (lane == expert + experts)
     return jnp.sum(jnp.where(mine, table.astype(jnp.float32), 0.0), axis=1, keepdims=True)
 
 
-def forward_kernel(experts, tile, *refs):
-    pieces, refs = refs[:4], refs[4:]
-    gate_mat, up_mat, down_mat, pre_gate, pre_up, gated, own, other, rows = refs
+def hidden_kernel(experts, tile, *refs):
+    pieces, refs = refs[:8], refs[8:]
+    gate_mat, up_mat, pre_gate, pre_up, gated, rows = refs
     width = rows.shape[1]
-    half = width // 2
     lay_out(pieces, rows, slice(0, width))
     gate = gate_column(experts, pieces, width)
     for start in range(0, gated.shape[1], tile):
@@ -190,6 +203,26 @@
         pre_gate[:, columns] = gate_part
         pre_up[:, columns] = up_part
         gated[:, columns] = (gate * silu_value * up_part).astype(jnp.bfloat16)
+
+
+def hidden_units(pieces, gate_mat, up_mat, experts):
+    width, hidden = gate_mat.shape
+    total = 8 * pieces[0].shape[0]
+    pre = jax.ShapeDtypeStruct((total, hidden), jnp.float32)
+    act = jax.ShapeDtypeStruct((total, hidden), jnp.bfloat16)
+    return call(
+        functools.partial(hidden_kernel, experts, 256),
+        "hidden_units",
+        (*pieces, gate_mat, up_mat),
+        (pre, pre, act),
+        [pltpu.VMEM((total, width), jnp.bfloat16)],
+        flops=4 * total * width * hidden,
+        mebibytes=12,
+    )
+
+
+def outputs_kernel(tile, gated, down_mat, own, other):
+    half = own.shape[2]
     for which in range(2):
         stays = (lax.axis_index("helper") == which).astype(jnp.int32)
         for start in range(0, half, tile):
@@ -200,28 +233,23 @@
             other[stays, :, columns] = half_at(out, 1)
 
 
-def forward(pieces, gate_mat, up_mat, down_mat, experts, estimate):
-    width, hidden = gate_mat.shape
-    total = 4 * pieces[0].shape[0]
-    pre = jax.ShapeDtypeStruct((total, hidden), jnp.float32)
-    act = jax.ShapeDtypeStruct((total, hidden), jnp.bfloat16)
+def outputs_of(gated, down_mat):
+    total, hidden = gated.shape
+    width = down_mat.shape[1]
     sums = jax.ShapeDtypeStruct((2, total // 2, width // 2), jnp.bfloat16)
     return call(
-        functools.partial(forward_kernel, experts, 256),
-        "forward",
-        (*pieces, gate_mat, up_mat, down_mat),
-        (pre, pre, act, sums, sums),
-        [pltpu.VMEM((total, width), jnp.bfloat16)],
-        flops=estimate,
-    )
-
-
-def backward_kernel(experts, tile, *refs):
-    pieces, gate_pieces, refs = refs[:4], refs[4:8], refs[8:]
-    down_mat, pre_gate, pre_up, gate_mat, up_mat = refs[:5]
-    d_gate, d_up, own, other, grads = refs[5:]
+        functools.partial(outputs_kernel, 256),
+        "outputs",
+        (gated, down_mat),
+        (sums, sums),
+        flops=2 * total * width * hidden,
+    )
+
+
+def hidden_grads_kernel(experts, tile, *refs):
+    pieces, gate_pieces, refs = refs[:8], refs[8:16], refs[16:]
+    down_mat, pre_gate, pre_up, d_gate, d_up, shares_out, grads = refs
     total, width = grads.shape
-    half = width // 2
     lay_out(pieces, grads, slice(0, width))
     gate = gate_column(experts, gate_pieces, width)
     shares = []
@@ -239,10 +267,29 @@
     lane = lax.broadcasted_iota(jnp.int32, (total, LANES), 1)
     high = 2 * lax.axis_index("expert") + lax.axis_index("helper")
     value = jnp.where((lane == high) | (lane == high + 2 * experts), value, 0.0)
-    value = hi_lo(value, lane < 2 * experts)
+    shares_out[...] = hi_lo(value, lane < 2 * experts)
+
+
+def hidden_grads(pieces, gate_pieces, pre_gate, pre_up, down_mat, experts):
+    hidden, width = down_mat.shape
+    total = pre_gate.shape[0]
+    act = jax.ShapeDtypeStruct((total, hidden), jnp.bfloat16)
+    return call(
+        functools.partial(hidden_grads_kernel, experts, 256),
+        "hidden_grads",
+        (*pieces, *gate_pieces, down_mat, pre_gate, pre_up),
+        (act, act, jax.ShapeDtypeStruct((total, LANES), jnp.bfloat16)),
+        [pltpu.VMEM((total, width), jnp.bfloat16)],
+        flops=2 * total * width * hidden,
+        mebibytes=12,
+    )
+
+
+def input_grads_kernel(tile, d_gate, d_up, shares, gate_mat, up_mat, own, other):
+    half = own.shape[2] - LANES
     for which in range(2):
-        own[which, :, half:] = half_at(value, 0)
-        other[which, :, half:] = half_at(value, 1)
+        own[which, :, half:] = half_at(shares, 0)
+        other[which, :, half:] = half_at(shares, 1)
     for which in range(2):
         stays = (lax.axis_index("helper") == which).astype(jnp.int32)
         for start in range(0, half, tile):
@@ -255,45 +302,39 @@
             other[stays, :, columns] = half_at(back, 1)
 
 
-def backward(pieces, gate_pieces, pre_gate, pre_up, gate_mat, up_mat, down_mat, experts):
+def input_grads_of(d_gate, d_up, shares, gate_mat, up_mat):
     width, hidden = gate_mat.shape
-    total = pre_gate.shape[0]
-    act = jax.ShapeDtypeStruct((total, hidden), jnp.bfloat16)
+    total = d_gate.shape[0]
     sums = jax.ShapeDtypeStruct((2, total // 2, width // 2 + LANES), jnp.bfloat16)
     return call(
-        functools.partial(backward_kernel, experts, 256),
-        "backward",
-        (*pieces, *gate_pieces, down_mat, pre_gate, pre_up, gate_mat, up_mat),
-        (act, act, sums, sums),
-        [pltpu.VMEM((total, width), jnp.bfloat16)],
-        flops=6 * total * width * hidden,
-    )
-
-
-def weights_kernel(width, hidden, tile, *refs):
-    pieces, refs = refs[:8], refs[8:]
-    first, second, grad, rows, acts = refs
+        functools.partial(input_grads_kernel, 256),
+        "input_grads",
+        (d_gate, d_up, shares, gate_mat, up_mat),
+        (sums, sums),
+        flops=0,
+        mebibytes=12,
+    )
+
+
+def weights_kernel(width, tile, *refs):
+    pieces, (acts, grad, rows) = refs[:8], refs[8:]
     lay_out(pieces, rows, slice(0, width))
-    lay_out((first, second), acts, slice(0, hidden))
-    left, right = (acts, rows) if grad.shape[0] == hidden else (rows, acts)
+    left, right = (acts, rows) if grad.shape[1] == width else (rows, acts)
     for start in range(0, grad.shape[0], tile):
         columns = slice(start, start + tile)
         grad[columns, :] = transposed_product(left[:, columns], right[...]).astype(jnp.bfloat16)
 
 
 def weights(name, pieces, acts, width, by_hidden):
-    rows, hidden = acts[0].shape
+    rows, hidden = acts.shape
     shape = (hidden, width) if by_hidden else (width, hidden)
     return call(
-        functools.partial(weights_kernel, width, hidden, 256),
+        functools.partial(weights_kernel, width, 256),
         name,
-        (*pieces, *acts),
+        (*pieces, acts),
         jax.ShapeDtypeStruct(shape, jnp.bfloat16),
-        [
-            pltpu.VMEM((2 * rows, width), jnp.bfloat16),
-            pltpu.VMEM((2 * rows, hidden), jnp.bfloat16),
-        ],
-        flops=4 * rows * width * hidden,
+        [pltpu.VMEM((rows, width), jnp.bfloat16)],
+        flops=2 * rows * width * hidden,
     )
 
 
@@ -313,9 +354,16 @@
     return kept + jnp.concatenate([other[half:], other[:half]], axis=0)
 
 
-def slots_kernel(own, received, arrived, first, second):
-    for slot, target in enumerate((first, second)):
-        target[...] = slot_sum(own, received, arrived, slot, slot * LANES).astype(target.dtype)
+def slots_kernel(own, received, arrived, own_slot, near_and_last, far_slot):
+    rows = own_slot.shape[0]
+    targets = (own_slot, near_and_last.at[:rows], far_slot, near_and_last.at[rows:])
+    for slot, target in enumerate(targets):
+        target[...] = slot_sum(own, received, arrived, slot, slot * rows).astype(target.dtype)
+
+
+def add_last_kernel(far_slot, arrived, total):
+    rows = far_slot.shape[0]
+    total[...] = far_slot[...] + arrived[rows:, :]
 
 
 def slot_kernel(slot, own, received, arrived, *refs):
@@ -325,9 +373,9 @@
     refs[-1][...] = whole.astype(refs[-1].dtype)
 
 
-def finish_outputs_kernel(*refs):
-    columns = refs[-1]
-    whole = total_of([ref[...].astype(jnp.float32) for ref in refs[:-1]])
+def finish_outputs_kernel(own, near_and_last, far, columns):
+    near = near_and_last[: own.shape[0], :]
+    whole = total_of([term.astype(jnp.float32) for term in (own[...], near, far[...])])
     whole = jnp.where(lax.axis_index("helper") == 0, whole, swap_halves(whole))
     columns[...] = whole.astype(jnp.bfloat16)
 
@@ -380,8 +428,13 @@
 
     def slots(self, own, received, arrived):
         rows, columns = arrived.shape
-        slot = jax.ShapeDtypeStruct((rows // 2, columns), arrived.dtype)
-        return call(slots_kernel, self.label + "_slots", (own, received, arrived), (slot, slot))
+        shape = lambda slots: jax.ShapeDtypeStruct((slots * rows // 4, columns), arrived.dtype)
+        return call(
+            slots_kernel,
+            self.label + "_slots",
+            (own, received, arrived),
+            (shape(1), shape(2), shape(1)),
+        )
 
     def slot(self, which, own, received, arrived, *others):
         return call(
@@ -416,7 +469,7 @@
     )(*(pltpu.with_memory_space_constraint(mat, pltpu.HBM) for mat in mats))
 
 
-def space(clock, flops=12 * 10**9):
+def space(clock, flops=36 * 10**9):
     return pl.pallas_call(
         lambda old, new: None,
         out_shape=jax.ShapeDtypeStruct(clock.shape, clock.dtype),
@@ -443,110 +496,104 @@
 
 def lined_up(tokens, expert_ids, pick_counts, gate_scores, gate_local, up_local, down_local, grad_out):
     experts = lax.axis_size("expert")
-    width, hidden = gate_local.shape
+    width = gate_local.shape[0]
     picks = (expert_ids.T, pick_counts[None, :], gate_scores.T)
     rows, grads, outs, ins = (FourChips(label) for label in ("rows", "grads", "out", "in"))
     order = Order()
     hold = lambda value, *tokens: lax.optimization_barrier((value, tokens))[0]
-    ahead = lambda *pieces: forward(pieces, *mats, experts, 24 * tokens.size * hidden)
-    back = lambda g, r, *pre: backward(g, r, *pre, *mats, experts)
-    product_of = lambda name, by_hidden: lambda r, *acts: weights(name, r, acts, width, by_hidden)
+    product_of = lambda name, by_hidden: lambda r, acts: weights(name, r, acts, width, by_hidden)
 
     own, pair, clock = order(lambda r: prepare_rows(*picks, r, experts), tokens)
     near = rows.line(own, rows.near)
     far = rows.line(own, rows.far)
     sibling_pair = rows.sibling(pair)
-    mats = order(load, gate_local, up_local, down_local)
-    near, sibling_pair = hold((near, sibling_pair), mats)
-    near_across = rows.across(near)
-    far = hold(far, near)
-    far_across = rows.across(far)
-    last = rows.line(far, rows.near)
-    near_first, near_sibling = pair, sibling_pair
-    own, pair = order(prepare_grads, grad_out, also=far)
-    sibling_pair = grads.sibling(pair)
-    near_pair = order(pair_up, near, near_across)
-    near_rows = [near_first, near_pair, near_sibling, rows.sibling(near_pair)]
+    gate_mat, up_mat, down_mat = order(load, gate_local, up_local, down_local)
+    sibling_pair = hold(sibling_pair, down_mat)
+    line_pair = order(pair_up, near, far, also=sibling_pair)
+    across_pair = rows.across(line_pair)
+    last = rows.line(hold(far, line_pair), rows.near)
+    sibling_line = rows.sibling(line_pair)
+    all_rows = [pair, line_pair]
+    sibling_rows = [sibling_pair, sibling_line]
+    own, pair = order(prepare_grads, grad_out)
+    far = grads.line(own, grads.far)
     last_across = rows.across(last)
     near = grads.line(hold(own, last), grads.near)
-    far_grad = grads.line(hold(own, last), grads.far)
-    near_gate, near_up, near_act, near_out, sent = order(
-        ahead, *near_rows, also=(last, sibling_pair)
-    )
-    near_received = outs.sibling(sent)
-
-    near = hold(near, near_act)
-    far_grad = hold(far_grad, near)
-    far_across, last_across = hold((far_across, last_across), far_grad)
-    far_pair = order(pair_up, far, far_across)
-    far_sibling = rows.sibling(far_pair)
-    last_pair = order(pair_up, last, last_across, also=far_sibling)
-    far_rows = [far_pair, last_pair, far_sibling, rows.sibling(last_pair)]
-    near_across = grads.across(near)
-    far_across = grads.across(far_grad)
-    last = grads.line(far_grad, grads.near)
-    far_gate, far_up, far_act, far_out, sent = order(ahead, *far_rows, also=(near, far_grad))
-    far_received = outs.sibling(sent)
-
-    last, near_across = hold((last, near_across), far_act)
-    far_across = hold(far_across, near_across)
-    last_across = grads.across(last)
-    near_pair = order(pair_up, near, near_across)
-    near_grads = [pair, near_pair, sibling_pair, grads.sibling(near_pair)]
-    far_pair = order(pair_up, far_grad, far_across)
-    far_sibling = grads.sibling(far_pair)
+    clock = order(space, clock, also=last)
+    across_pair = hold(across_pair, clock)
+    sibling_across = rows.sibling(across_pair)
+    far = hold(far, across_pair)
+    grads_last = grads.line(far, grads.near)
+    clock = order(lambda c: space(c, 2 * 10**9), clock, also=far)
+    line_pair = order(pair_up, near, far, also=sibling_across)
+    sibling_pair, sibling_line = grads.sibling(pair), grads.sibling(line_pair)
+    grads_across = grads.across(line_pair)
+    last_pair = order(pair_up, last, last_across, also=line_pair)
+    all_rows = all_rows + [across_pair, last_pair]
+    all_rows = all_rows + sibling_rows + [sibling_across, rows.sibling(last_pair)]
+    pre_gate, pre_up, gated = order(
+        lambda *r: hidden_units(r, gate_mat, up_mat, experts), *all_rows
+    )
+    grads_last, grads_across = hold((grads_last, grads_across), gated)
+    last_across = grads.across(grads_last)
+    sibling_across = grads.sibling(grads_across)
+    near_out, sent = order(
+        outputs_of, gated, down_mat, also=(grads_across, sibling_pair, sibling_line)
+    )
+    received = outs.sibling(sent)
+    last_pair = order(pair_up, grads_last, last_across)
+    clock = order(space, clock, also=sibling_across)
+    received = hold(received, clock)
+    (sent,) = order(outs.send, near_out, received)
+    arrived = outs.across(sent)
+    all_grads = [pair, line_pair, grads_across, last_pair]
+    all_grads = all_grads + [sibling_pair, sibling_line, sibling_across, grads.sibling(last_pair)]
+    d_gate, d_up, shares = order(
+        lambda g, r, *pre: hidden_grads(g, r, *pre, down_mat, experts),
+        all_grads,
+        all_rows,
+        pre_gate,
+        pre_up,
+    )
+    in_own, sent = order(
+        lambda *d: input_grads_of(*d, gate_mat, up_mat), d_gate, d_up, shares
+    )
+    in_received = ins.sibling(sent)
+    arrived = hold(arrived, in_own)
+    own_slot, near_slots, far_slot = order(outs.slots, near_out, received, arrived)
     clock = order(space, clock)
-    far_received, near_received = hold((far_received, near_received), clock)
-    (sent,) = order(outs.send, far_out, far_received, also=(far_sibling, near_grads))
-    far_arrived = outs.across(sent)
-    (near_sent,) = order(outs.send, near_out, near_received)
-    near_d_gate, near_d_up, near_in, sent = order(
-        back, near_grads, near_rows, near_gate, near_up
-    )
-    near_in_received = ins.sibling(sent)
-    near_arrived = outs.across(hold(near_sent, near_d_gate))
-    far_slot, last_slot = order(outs.slots, far_out, far_received, far_arrived)
-    last_sum = outs.line(last_slot, outs.near)
-    last_across = hold(last_across, near_d_gate)
-    last_pair = order(pair_up, last, last_across)
-    far_grads = [far_pair, last_pair, far_sibling, grads.sibling(last_pair)]
-    far_d_gate, far_d_up, far_in, sent = order(
-        back, far_grads, far_rows, far_gate, far_up
-    )
-    far_in_received = ins.sibling(sent)
-    near_arrived = hold(near_arrived, far_d_gate)
-    clock = order(space, clock, also=near_arrived)
-    far_in_received = hold(far_in_received, clock)
-    far_sent, last_sent = order(lambda *s: ins.send(*s, parts=2), far_in, far_in_received)
+    in_received = hold(in_received, clock)
+    sent = order(lambda *s: ins.send(*s, parts=4), in_own, in_received)
+    own_sent, near_sent, far_sent, last_sent = sent
     last_arrived = ins.across(last_sent)
-    far_in_arrived = ins.across(far_sent)
-    own_sent, near_sent = order(lambda *s: ins.send(*s, parts=2), near_in, near_in_received)
-    far_sum = outs.line(order(jnp.add, far_slot, last_sum), outs.far)
-    own_slot, near_slot = order(outs.slots, near_out, near_received, near_arrived)
-    near_sum = outs.line(near_slot, outs.near)
-    near_in_arrived = ins.across(hold(near_sent, own_slot))
-    grad_down = order(
-        product_of("grad_down", True), near_grads + far_grads, near_act, far_act
-    )
-    all_rows = near_rows + far_rows
-    slot = order(lambda *s: ins.slot(1, *s), far_in, far_in_received, last_arrived)
+    near_sums = outs.line(near_slots, outs.near)
+    grad_down = order(product_of("grad_down", True), all_grads, gated)
+    slot = order(lambda *s: ins.slot(3, *s), in_own, in_received, last_arrived)
     last_sum = ins.line(slot, ins.near)
-    own_in_arrived = ins.across(hold(own_sent, slot))
-    grad_gate = order(product_of("grad_gate", False), all_rows, near_d_gate, far_d_gate)
-    slot = order(lambda *s: ins.slot(0, *s), far_in, far_in_received, far_in_arrived, last_sum)
+    far_arrived = ins.across(hold(far_sent, slot))
+    far_slot = order(
+        lambda *s: call(add_last_kernel, "add_last", s, jax.ShapeDtypeStruct(s[0].shape, s[0].dtype)),
+        far_slot,
+        near_sums,
+    )
+    far_sum = outs.line(far_slot, outs.far)
+    grad_gate = order(product_of("grad_gate", False), all_rows, d_gate)
+    slot = order(lambda *s: ins.slot(2, *s), in_own, in_received, far_arrived, last_sum)
     far = ins.line(slot, ins.far)
+    near_arrived = ins.across(hold(near_sent, slot))
+    grad_up = order(product_of("grad_up", False), all_rows, d_up)
+    slot = order(lambda *s: ins.slot(1, *s), in_own, in_received, near_arrived)
+    near = ins.line(slot, ins.near)
+    own_arrived = ins.across(hold(own_sent, slot))
     columns = jax.ShapeDtypeStruct((tokens.shape[0], width // 2), jnp.bfloat16)
     output_cols = order(
         lambda *sums: call(finish_outputs_kernel, "finish_outputs", sums, columns),
         own_slot,
-        near_sum,
+        near_sums,
         far_sum,
     )
-    grad_up = order(product_of("grad_up", False), all_rows, near_d_up, far_d_up)
-    slot = order(lambda *s: ins.slot(1, *s), near_in, near_in_received, near_in_arrived)
-    near = ins.line(slot, ins.near)
     clock = order(lambda c: space(c, 2 * 10**9), clock, also=far)
-    near, own_in_arrived = hold((near, own_in_arrived), clock)
+    near, own_arrived = hold((near, own_arrived), clock)
     input_cols, d_scores = order(
         lambda *sums: call(
             functools.partial(finish_inputs_kernel, experts),
@@ -554,9 +601,9 @@
             (*picks, clock, *sums),
             (columns, jax.ShapeDtypeStruct(picks[2].shape, jnp.float32)),
         ),
-        near_in,
-        near_in_received,
-        own_in_arrived,
+        in_own,
+        in_received,
+        own_arrived,
         far,
         near,
     )

time: 150 us -> 151 us (level)
  waiting for transfers between devices: 56 us -> 63.7 us
  starting transfers between devices: 35.9 us -> 29.4 us
    ppermute x12 -> x11, waiting for transfers between devices: 30.5 us -> 38.4 us  [line(): return lax.ppermute(array, 'expert', pairs)]
    ppermute x12 -> x9, starting transfers between devices: 15.6 us -> 9.96 us  [across(): return lax.ppermute(array, 'helper', self.sides)]
    ppermute x12 -> x10, waiting for transfers between devices: 4.23 us -> 3.36 us  [sibling(): return lax.ppermute(array, 'expert', self.cores)]
    ppermute x12 -> x9, waiting for transfers between devices: 21.3 us -> 22 us  [across(): return lax.ppermute(array, 'helper', self.sides)]
    pallas_call x25 -> x21, Pallas kernels: 51.2 us -> 50.8 us  [call(): pl.pallas_call(kernel, out_shape=out_shape, in_specs=[VMEM] * len(operand...]
    ppermute x12 -> x11, starting transfers between devices: 17.6 us -> 17.8 us  [line(): return lax.ppermute(array, 'expert', pairs)]
  transfers between devices with their start and end apart: 36 -> 30, of which waited for: 17 -> 17; matrix products, arithmetic and copies ran while one was open for 0% -> 0% of each run, Pallas kernels for 36% -> 36%
where the time goes in v6:
time: 151 us
  waiting for transfers between devices  63.7 us (42%)
  Pallas kernels  56.9 us (38%)
  starting transfers between devices  29.4 us (19%)
    pallas_call x21, Pallas kernels, call(): pl.pallas_call(kernel, out_shape=out_shape, in_specs=[VMEM] * len(operand...  50.8 us
    ppermute x11, waiting for transfers between devices, line(): return lax.ppermute(array, 'expert', pairs)  38.4 us
    ppermute x9, waiting for transfers between devices, across(): return lax.ppermute(array, 'helper', self.sides)  22 us
    ppermute x11, starting transfers between devices, line(): return lax.ppermute(array, 'expert', pairs)  17.8 us
    ppermute x9, starting transfers between devices, across(): return lax.ppermute(array, 'helper', self.sides)  9.96 us
    pallas_call x1, Pallas kernels, load(): pl.pallas_call(load_kernel, out_shape=tuple((jax.ShapeDtypeStruct(mat.sha...  4.73 us
    ppermute x10, waiting for transfers between devices, sibling(): return lax.ppermute(array, 'expert', self.cores)  3.36 us
  transfers between devices with their start and end apart: 30, of which 17 were waited for; matrix products, arithmetic and copies ran while one was open for 0% of the time, Pallas kernels for 36%

profile of v6, /device:TPU:0, one launch (start us, length us, event | category | flops | bytes accessed | tf_op | source)
XLA Modules:
  0.0 150.8 jit_solution(2875575514955929384)
XLA Ops:
  0.6 1.3 prepare_rows.1
  1.9 0.5 collective-permute-start.2
  2.5 3.7 %collective-permute-start.1 = (bf16[64,2176]{1,0:T(8,128)(2,1)S(1)}, bf16[64,2176]{1,0:T(8,128)(2,1)S(1)}, u32[]{:S(2)}, u32[]{:S(2)}) collective-permute-start(bf16[64,2176]{1,0:T(8,128)(2,1)S(1)} %get-tuple-element.151), channel_id=1, source_target_pairs={{0,8},{2,10},{4,12},{6,14},{8,0},{10,2},{12,4},{14,6},{1,9},{3,11}... | collective-permute-start | bytes 835592 | tf_op jit(solution)/shard_map/rows_line/ppermute | solution.py:414
  6.1 1.6 %collective-permute-start = (bf16[64,2176]{1,0:T(8,128)(2,1)S(1)}, bf16[64,2176]{1,0:T(8,128)(2,1)S(1)}, u32[]{:S(2)}, u32[]{:S(2)}) collective-permute-start(bf16[64,2176]{1,0:T(8,128)(2,1)S(1)} %get-tuple-element.151), channel_id=1, source_target_pairs={{0,4},{2,6},{4,0},{6,2},{8,12},{10,14},{12,8},{14,10},{1,5},{3,7},... | collective-permute-start | bytes 835592 | tf_op jit(solution)/shard_map/rows_line/ppermute | solution.py:414
  7.7 4.7 %load.1 = (bf16[2048,1024]{1,0:T(8,128)(2,1)S(1)}, bf16[2048,1024]{1,0:T(8,128)(2,1)S(1)}, bf16[1024,2048]{1,0:T(8,128)(2,1)S(1)}) custom-call(bf16[2048,1024]{1,0:T(8,128)(2,1)} %bitcast.16, bf16[2048,1024]{1,0:T(8,128)(2,1)} %bitcast.17, bf16[1024,2048]{1,0:T(8,128)(2,1)} %bitcast.18), custom_call_target="tpu_custom_call" | custom-call | tf_op jit(solution)/shard_map/load/pallas_call | solution.py:461
  12.4 7.0 %collective-permute-done.1.second = bf16[64,2176]{1,0:T(8,128)(2,1)S(1)} collective-permute-done((bf16[64,2176]{1,0:T(8,128)(2,1)S(1)}, bf16[64,2176]{1,0:T(8,128)(2,1)S(1)}, u32[]{:S(2)}, u32[]{:S(2)}) %collective-permute-start.1) | collective-permute-done | bytes 278560 | tf_op jit(solution)/shard_map/rows_line/ppermute | solution.py:414
  19.7 1.6 %collective-permute-start.4 = (bf16[64,2176]{1,0:T(8,128)(2,1)S(1)}, bf16[64,2176]{1,0:T(8,128)(2,1)S(1)}, u32[]{:S(2)}, u32[]{:S(2)}) collective-permute-start(bf16[64,2176]{1,0:T(8,128)(2,1)S(1)} %collective-permute-done.1.second), channel_id=1, source_target_pairs={{0,4},{2,6},{4,0},{6,2},{8,12},{10,14},{12,8},{14,10},{1,5},{3,7},... | collective-permute-start | bytes 835592 | tf_op jit(solution)/shard_map/rows_line/ppermute | solution.py:414
  21.2 1.5 %collective-permute-start.3 = (bf16[128,2176]{1,0:T(8,128)(2,1)S(1)}, bf16[128,2176]{1,0:T(8,128)(2,1)S(1)}, u32[]{:S(2)}, u32[]{:S(2)}) collective-permute-start(bf16[128,2176]{1,0:T(8,128)(2,1)S(1)} %pair.4.refs_1_.refs_9_), channel_id=1, source_target_pairs={{0,1},{1,0},{2,3},{3,2},{4,5},{5,4},{6,7},{7,6},{8,9},{9,8},{10,11... | collective-permute-start | bytes 1671176 | tf_op jit(solution)/shard_map/rows_across/ppermute | solution.py:422
  22.8 5.1 %collective-permute-done.4.first = bf16[64,2176]{1,0:T(8,128)(2,1)S(1)} collective-permute-done((bf16[64,2176]{1,0:T(8,128)(2,1)S(1)}, bf16[64,2176]{1,0:T(8,128)(2,1)S(1)}, u32[]{:S(2)}, u32[]{:S(2)}) %collective-permute-start.4) | collective-permute-done | bytes 278560 | tf_op jit(solution)/shard_map/rows_line/ppermute | solution.py:414
  27.9 7.2 %collective-permute-done.3.refs_2_.refs_10_ = bf16[128,2176]{1,0:T(8,128)(2,1)S(1)} collective-permute-done((bf16[128,2176]{1,0:T(8,128)(2,1)S(1)}, bf16[128,2176]{1,0:T(8,128)(2,1)S(1)}, u32[]{:S(2)}, u32[]{:S(2)}) %collective-permute-start.3) | collective-permute-done | bytes 557088 | tf_op jit(solution)/shard_map/rows_across/ppermute | solution.py:422
  35.2 2.7 %collective-permute-start.7 = (bf16[64,2048]{1,0:T(8,128)(2,1)S(1)}, bf16[64,2048]{1,0:T(8,128)(2,1)S(1)}, u32[]{:S(2)}, u32[]{:S(2)}) collective-permute-start(bf16[64,2048]{1,0:T(8,128)(2,1)S(1)} %get-tuple-element.168), channel_id=1, source_target_pairs={{0,8},{2,10},{4,12},{6,14},{8,0},{10,2},{12,4},{14,6},{1,9},{3,11}... | collective-permute-start | bytes 786440 | tf_op jit(solution)/shard_map/grads_line/ppermute | solution.py:414
  37.9 1.5 %collective-permute-start.5 = (bf16[64,2176]{1,0:T(8,128)(2,1)S(1)}, bf16[64,2176]{1,0:T(8,128)(2,1)S(1)}, u32[]{:S(2)}, u32[]{:S(2)}) collective-permute-start(bf16[64,2176]{1,0:T(8,128)(2,1)S(1)} %collective-permute-done.4.first), channel_id=1, source_target_pairs={{0,1},{1,0},{2,3},{3,2},{4,5},{5,4},{6,7},{7,6},{8,9},{9,8},{10,11... | collective-permute-start | bytes 835592 | tf_op jit(solution)/shard_map/rows_across/ppermute | solution.py:422
  39.4 0.4 collective-permute-start.6
  39.8 10.6 %collective-permute-done.7.second = bf16[64,2048]{1,0:T(8,128)(2,1)S(1)} collective-permute-done((bf16[64,2048]{1,0:T(8,128)(2,1)S(1)}, bf16[64,2048]{1,0:T(8,128)(2,1)S(1)}, u32[]{:S(2)}, u32[]{:S(2)}) %collective-permute-start.7) | collective-permute-done | bytes 262176 | tf_op jit(solution)/shard_map/grads_line/ppermute | solution.py:414
  50.4 2.7 %collective-permute-done.6.first = bf16[64,2048]{1,0:T(8,128)(2,1)S(1)} collective-permute-done((bf16[64,2048]{1,0:T(8,128)(2,1)S(1)}, bf16[64,2048]{1,0:T(8,128)(2,1)S(1)}, u32[]{:S(2)}, u32[]{:S(2)}) %collective-permute-start.6) | collective-permute-done | bytes 262176 | tf_op jit(solution)/shard_map/grads_line/ppermute | solution.py:414
  53.3 0.5 collective-permute-start.13
  53.8 0.6 collective-permute-start.12
  54.5 0.7 collective-permute-done.10.refs_7_.refs_15_
  55.2 8.8 %hidden_units.1 = (f32[1024,1024]{1,0:T(8,128)S(1)}, f32[1024,1024]{1,0:T(8,128)S(1)}, bf16[1024,1024]{1,0:T(8,128)(2,1)S(1)}) custom-call(bf16[128,2176]{1,0:T(8,128)(2,1)S(1)} %get-tuple-element.268.refs_0_.refs_8_, bf16[128,2176]{1,0:T(8,128)(2,1)S(1)} %pair.4.refs_1_.refs_9_, bf16[128,2176]{1,0:T(8,128)(2,1)S(1)} %collective-permute-done.3.refs_2_.refs_10_, ...), custom_call_target="tpu_custom_call" | custom-call | flops 8589934592 | tf_op jit(solution)/shard_map/hidden_units/pallas_call | solution.py:40
  64.0 4.1 %collective-permute-done.12.refs_2_ = bf16[128,2048]{1,0:T(8,128)(2,1)S(1)} collective-permute-done((bf16[128,2048]{1,0:T(8,128)(2,1)S(1)}, bf16[128,2048]{1,0:T(8,128)(2,1)S(1)}, u32[]{:S(2)}, u32[]{:S(2)}) %collective-permute-start.12) | collective-permute-done | bytes 524320 | tf_op jit(solution)/shard_map/grads_across/ppermute | solution.py:422
  68.1 0.8 collective-permute-start.16
  68.9 4.5 %outputs.1 = (bf16[2,512,1024]{2,1,0:T(8,128)(2,1)S(1)}, bf16[2,512,1024]{2,1,0:T(8,128)(2,1)S(1)}) custom-call(bf16[1024,1024]{1,0:T(8,128)(2,1)S(1)} %get-tuple-element.247.gated.refs_8_, bf16[1024,2048]{1,0:T(8,128)(2,1)S(1)} %get-tuple-element.188.down_mat.refs_16_), custom_call_target="tpu_custom_call" | custom-call | flops 4294967296 | tf_op jit(solution)/shard_map/outputs/pallas_call | solution.py:40
  73.6 3.2 %collective-permute-done.16.second = bf16[64,2048]{1,0:T(8,128)(2,1)S(1)} collective-permute-done((bf16[64,2048]{1,0:T(8,128)(2,1)S(1)}, bf16[64,2048]{1,0:T(8,128)(2,1)S(1)}, u32[]{:S(2)}, u32[]{:S(2)}) %collective-permute-start.16) | collective-permute-done | bytes 262176 | tf_op jit(solution)/shard_map/grads_across/ppermute | solution.py:422
  76.9 0.7 collective-permute-done.15.received
  77.7 1.4 collective-permute-start.18
  79.1 1.9 %collective-permute-done.19.refs_7_ = bf16[128,2048]{1,0:T(8,128)(2,1)S(1)} collective-permute-done((bf16[128,2048]{1,0:T(8,128)(2,1)S(1)}, bf16[128,2048]{1,0:T(8,128)(2,1)S(1)}, u32[]{:S(2)}, u32[]{:S(2)}) %collective-permute-start.19) | collective-permute-done | bytes 524320 | tf_op jit(solution)/shard_map/grads_cores/ppermute | solution.py:418
  81.0 5.7 %hidden_grads.1 = (bf16[1024,1024]{1,0:T(8,128)(2,1)S(1)}, bf16[1024,1024]{1,0:T(8,128)(2,1)S(1)}, bf16[1024,128]{1,0:T(8,128)(2,1)S(1)}) custom-call(bf16[128,2048]{1,0:T(8,128)(2,1)S(1)} %get-tuple-element.239.refs_0_, bf16[128,2048]{1,0:T(8,128)(2,1)S(1)} %pair.5.refs_1_, bf16[128,2048]{1,0:T(8,128)(2,1)S(1)} %collective-permute-done.12.refs_2_, ...), custom_call_target="tpu_custom_call" | custom-call | flops 4294967296 | tf_op jit(solution)/shard_map/hidden_grads/pallas_call | solution.py:40
  86.7 8.9 %input_grads.1 = (bf16[2,512,1152]{2,1,0:T(8,128)(2,1)S(1)}, bf16[2,512,1152]{2,1,0:T(8,128)(2,1)S(1)}) custom-call(bf16[1024,1024]{1,0:T(8,128)(2,1)S(1)} %get-tuple-element.262.d_gate.refs_8_, bf16[1024,1024]{1,0:T(8,128)(2,1)S(1)} %get-tuple-element.276.d_up.refs_8_, bf16[1024,128]{1,0:T(8,128)(2,1)S(1)} %get-tuple-element.221.shares, ...), custom_call_target="tpu_custom_call" | custom-call | tf_op jit(solution)/shard_map/input_grads/pallas_call | solution.py:40
  95.8 7.2 %collective-permute-done.18.arrived = bf16[512,1024]{1,0:T(8,128)(2,1)S(1)} collective-permute-done((bf16[512,1024]{1,0:T(8,128)(2,1)S(1)}, bf16[512,1024]{1,0:T(8,128)(2,1)S(1)}, u32[]{:S(2)}, u32[]{:S(2)}) %collective-permute-start.18) | collective-permute-done | bytes 1048608 | tf_op jit(solution)/shard_map/out_across/ppermute | solution.py:422
  103.0 0.4 out_slots.1
  103.4 1.9 %collective-permute-start.20 = (bf16[256,1024]{1,0:T(8,128)(2,1)S(1)}, bf16[256,1024]{1,0:T(8,128)(2,1)S(1)}, u32[]{:S(2)}, u32[]{:S(2)}) collective-permute-start(bf16[256,1024]{1,0:T(8,128)(2,1)S(1)} %get-tuple-element.229), channel_id=1, source_target_pairs={{0,4},{2,6},{4,0},{6,2},{8,12},{10,14},{12,8},{14,10},{1,5},{3,7},... | collective-permute-start | bytes 1572872 | tf_op jit(solution)/shard_map/out_line/ppermute | solution.py:414
  105.4 1.6 %collective-permute-start.22 = (bf16[128,1152]{1,0:T(8,128)(2,1)S(1)}, bf16[128,1152]{1,0:T(8,128)(2,1)S(1)}, u32[]{:S(2)}, u32[]{:S(2)}) collective-permute-start(bf16[128,1152]{1,0:T(8,128)(2,1)S(1)} %get-tuple-element.235), channel_id=1, source_target_pairs={{0,1},{1,0},{2,3},{3,2},{4,5},{5,4},{6,7},{7,6},{8,9},{9,8},{10,11... | collective-permute-start | bytes 884744 | tf_op jit(solution)/shard_map/in_across/ppermute | solution.py:422
  107.0 6.6 %grad_down.1 = bf16[1024,2048]{1,0:T(8,128)(2,1)} custom-call(bf16[128,2048]{1,0:T(8,128)(2,1)S(1)} %get-tuple-element.239.refs_0_, bf16[128,2048]{1,0:T(8,128)(2,1)S(1)} %pair.5.refs_1_, bf16[128,2048]{1,0:T(8,128)(2,1)S(1)} %collective-permute-done.12.refs_2_, bf16[128,2048]{1,0:T(8,128)(2,1)S(1)} %pair.7.refs_3_, ...), custom_call_target="tpu_custom_call" | custom-call | flops 4294967296 | tf_op jit(solution)/shard_map/grad_down/pallas_call | solution.py:40
  113.7 0.3 collective-permute-start.25
  114.0 4.3 %collective-permute-done.20.arrived.near_and_last = bf16[256,1024]{1,0:T(8,128)(2,1)S(1)} collective-permute-done((bf16[256,1024]{1,0:T(8,128)(2,1)S(1)}, bf16[256,1024]{1,0:T(8,128)(2,1)S(1)}, u32[]{:S(2)}, u32[]{:S(2)}) %collective-permute-start.20) | collective-permute-done | bytes 524320 | tf_op jit(solution)/shard_map/out_line/ppermute | solution.py:414
  118.3 1.4 collective-permute-start.23
  119.7 0.5 collective-permute-start.24
  120.1 6.8 %grad_gate.1 = bf16[2048,1024]{1,0:T(8,128)(2,1)} custom-call(bf16[128,2176]{1,0:T(8,128)(2,1)S(1)} %get-tuple-element.268.refs_0_.refs_8_, bf16[128,2176]{1,0:T(8,128)(2,1)S(1)} %pair.4.refs_1_.refs_9_, bf16[128,2176]{1,0:T(8,128)(2,1)S(1)} %collective-permute-done.3.refs_2_.refs_10_, bf16[128,2176]{1,0:T(8,128)(2,1)S(1)} %pair.6.refs_3_.refs_11_, ...), custom_call_target="tpu_custom_call" | custom-call | flops 4294967296 | tf_op jit(solution)/shard_map/grad_gate/pallas_call | solution.py:40
  126.9 0.3 collective-permute-done.25.refs_0_
  127.4 2.3 %collective-permute-start.27 = (bf16[128,1152]{1,0:T(8,128)(2,1)S(1)}, bf16[128,1152]{1,0:T(8,128)(2,1)S(1)}, u32[]{:S(2)}, u32[]{:S(2)}) collective-permute-start(bf16[128,1152]{1,0:T(8,128)(2,1)S(1)} %in_slot.4), channel_id=1, source_target_pairs={{0,8},{2,10},{4,12},{6,14},{8,0},{10,2},{12,4},{14,6},{1,9},{3,11}... | collective-permute-start | bytes 884744 | tf_op jit(solution)/shard_map/in_line/ppermute | solution.py:414
  129.7 0.6 collective-permute-start.26
  130.3 6.5 %grad_up.1 = bf16[2048,1024]{1,0:T(8,128)(2,1)} custom-call(bf16[128,2176]{1,0:T(8,128)(2,1)S(1)} %get-tuple-element.268.refs_0_.refs_8_, bf16[128,2176]{1,0:T(8,128)(2,1)S(1)} %pair.4.refs_1_.refs_9_, bf16[128,2176]{1,0:T(8,128)(2,1)S(1)} %collective-permute-done.3.refs_2_.refs_10_, bf16[128,2176]{1,0:T(8,128)(2,1)S(1)} %pair.6.refs_3_.refs_11_, ...), custom_call_target="tpu_custom_call" | custom-call | flops 4294967296 | tf_op jit(solution)/shard_map/grad_up/pallas_call | solution.py:40
  137.0 1.5 collective-permute-start.29
  138.4 2.0 %collective-permute-start.28 = (bf16[128,1152]{1,0:T(8,128)(2,1)S(1)}, bf16[128,1152]{1,0:T(8,128)(2,1)S(1)}, u32[]{:S(2)}, u32[]{:S(2)}) collective-permute-start(bf16[128,1152]{1,0:T(8,128)(2,1)S(1)} %in_slot.5), channel_id=1, source_target_pairs={{0,4},{2,6},{4,0},{6,2},{8,12},{10,14},{12,8},{14,10},{1,5},{3,7},... | collective-permute-start | bytes 884744 | tf_op jit(solution)/shard_map/in_line/ppermute | solution.py:414
  140.5 0.8 finish_outputs.1
  141.3 2.2 %collective-permute-done.27.refs_0_ = bf16[128,1152]{1,0:T(8,128)(2,1)S(1)} collective-permute-done((bf16[128,1152]{1,0:T(8,128)(2,1)S(1)}, bf16[128,1152]{1,0:T(8,128)(2,1)S(1)}, u32[]{:S(2)}, u32[]{:S(2)}) %collective-permute-start.27) | collective-permute-done | bytes 294944 | tf_op jit(solution)/shard_map/in_line/ppermute | solution.py:414
  143.7 6.0 %collective-permute-done.28.refs_1_ = bf16[128,1152]{1,0:T(8,128)(2,1)S(1)} collective-permute-done((bf16[128,1152]{1,0:T(8,128)(2,1)S(1)}, bf16[128,1152]{1,0:T(8,128)(2,1)S(1)}, u32[]{:S(2)}, u32[]{:S(2)}) %collective-permute-start.28) | collective-permute-done | bytes 294944 | tf_op jit(solution)/shard_map/in_line/ppermute | solution.py:414
  149.8 1.1 finish_inputs.1
  (48 shorter events, 1.9 us)
Async XLA Ops:
  1.9 10.5 %collective-permute-start.2 = (bf16[128,2176]{1,0:T(8,128)(2,1)S(1)}, bf16[128,2176]{1,0:T(8,128)(2,1)S(1)}, u32[]{:S(2)}, u32[]{:S(2)}) collective-permute-start(bf16[128,2176]{1,0:T(8,128)(2,1)S(1)} %get-tuple-element.268.refs_0_.refs_8_), channel_id=1, source_target_pairs={{0,2},{2,0},{4,6},{6,4},{8,10},{10,8},{12,14},{14,12},{1,3},{3,1},... | collective-permute-start | bytes 1671176 | tf_op jit(solution)/shard_map/rows_cores/ppermute | solution.py:418
  2.5 17.0 %collective-permute-start.1 = (bf16[64,2176]{1,0:T(8,128)(2,1)S(1)}, bf16[64,2176]{1,0:T(8,128)(2,1)S(1)}, u32[]{:S(2)}, u32[]{:S(2)}) collective-permute-start(bf16[64,2176]{1,0:T(8,128)(2,1)S(1)} %get-tuple-element.151), channel_id=1, source_target_pairs={{0,8},{2,10},{4,12},{6,14},{8,0},{10,2},{12,4},{14,6},{1,9},{3,11}... | collective-permute-start | bytes 835592 | tf_op jit(solution)/shard_map/rows_line/ppermute | solution.py:414
  6.1 13.5 %collective-permute-start = (bf16[64,2176]{1,0:T(8,128)(2,1)S(1)}, bf16[64,2176]{1,0:T(8,128)(2,1)S(1)}, u32[]{:S(2)}, u32[]{:S(2)}) collective-permute-start(bf16[64,2176]{1,0:T(8,128)(2,1)S(1)} %get-tuple-element.151), channel_id=1, source_target_pairs={{0,4},{2,6},{4,0},{6,2},{8,12},{10,14},{12,8},{14,10},{1,5},{3,7},... | collective-permute-start | bytes 835592 | tf_op jit(solution)/shard_map/rows_line/ppermute | solution.py:414
  7.7 15.1 %copy-start = (bf16[128,2048]{1,0:T(8,128)(2,1)S(1)}, bf16[128,2048]{1,0:T(8,128)(2,1)}, u32[]{:S(2)}) copy-start(bf16[128,2048]{1,0:T(8,128)(2,1)} %rows) | copy-start | bytes 1572868
  19.7 8.2 %collective-permute-start.4 = (bf16[64,2176]{1,0:T(8,128)(2,1)S(1)}, bf16[64,2176]{1,0:T(8,128)(2,1)S(1)}, u32[]{:S(2)}, u32[]{:S(2)}) collective-permute-start(bf16[64,2176]{1,0:T(8,128)(2,1)S(1)} %collective-permute-done.1.second), channel_id=1, source_target_pairs={{0,4},{2,6},{4,0},{6,2},{8,12},{10,14},{12,8},{14,10},{1,5},{3,7},... | collective-permute-start | bytes 835592 | tf_op jit(solution)/shard_map/rows_line/ppermute | solution.py:414
  21.2 13.9 %collective-permute-start.3 = (bf16[128,2176]{1,0:T(8,128)(2,1)S(1)}, bf16[128,2176]{1,0:T(8,128)(2,1)S(1)}, u32[]{:S(2)}, u32[]{:S(2)}) collective-permute-start(bf16[128,2176]{1,0:T(8,128)(2,1)S(1)} %pair.4.refs_1_.refs_9_), channel_id=1, source_target_pairs={{0,1},{1,0},{2,3},{3,2},{4,5},{5,4},{6,7},{7,6},{8,9},{9,8},{10,11... | collective-permute-start | bytes 1671176 | tf_op jit(solution)/shard_map/rows_across/ppermute | solution.py:422
  35.2 17.9 %collective-permute-start.8 = (bf16[128,2176]{1,0:T(8,128)(2,1)S(1)}, bf16[128,2176]{1,0:T(8,128)(2,1)S(1)}, u32[]{:S(2)}, u32[]{:S(2)}) collective-permute-start(bf16[128,2176]{1,0:T(8,128)(2,1)S(1)} %collective-permute-done.3.refs_2_.refs_10_), channel_id=1, source_target_pairs={{0,2},{2,0},{4,6},{6,4},{8,10},{10,8},{12,14},{14,12},{1,3},{3,1},... | collective-permute-start | bytes 1671176 | tf_op jit(solution)/shard_map/rows_cores/ppermute | solution.py:418
  35.2 15.2 %collective-permute-start.7 = (bf16[64,2048]{1,0:T(8,128)(2,1)S(1)}, bf16[64,2048]{1,0:T(8,128)(2,1)S(1)}, u32[]{:S(2)}, u32[]{:S(2)}) collective-permute-start(bf16[64,2048]{1,0:T(8,128)(2,1)S(1)} %get-tuple-element.168), channel_id=1, source_target_pairs={{0,8},{2,10},{4,12},{6,14},{8,0},{10,2},{12,4},{14,6},{1,9},{3,11}... | collective-permute-start | bytes 786440 | tf_op jit(solution)/shard_map/grads_line/ppermute | solution.py:414
  37.9 15.2 %collective-permute-start.5 = (bf16[64,2176]{1,0:T(8,128)(2,1)S(1)}, bf16[64,2176]{1,0:T(8,128)(2,1)S(1)}, u32[]{:S(2)}, u32[]{:S(2)}) collective-permute-start(bf16[64,2176]{1,0:T(8,128)(2,1)S(1)} %collective-permute-done.4.first), channel_id=1, source_target_pairs={{0,1},{1,0},{2,3},{3,2},{4,5},{5,4},{6,7},{7,6},{8,9},{9,8},{10,11... | collective-permute-start | bytes 835592 | tf_op jit(solution)/shard_map/rows_across/ppermute | solution.py:422
  39.4 13.7 %collective-permute-start.6 = (bf16[64,2048]{1,0:T(8,128)(2,1)S(1)}, bf16[64,2048]{1,0:T(8,128)(2,1)S(1)}, u32[]{:S(2)}, u32[]{:S(2)}) collective-permute-start(bf16[64,2048]{1,0:T(8,128)(2,1)S(1)} %get-tuple-element.168), channel_id=1, source_target_pairs={{0,4},{2,6},{4,0},{6,2},{8,12},{10,14},{12,8},{14,10},{1,5},{3,7},... | collective-permute-start | bytes 786440 | tf_op jit(solution)/shard_map/grads_line/ppermute | solution.py:414
  39.8 14.1 %collective-permute-start.9 = (bf16[128,2176]{1,0:T(8,128)(2,1)S(1)}, bf16[128,2176]{1,0:T(8,128)(2,1)S(1)}, u32[]{:S(2)}, u32[]{:S(2)}) collective-permute-start(bf16[128,2176]{1,0:T(8,128)(2,1)S(1)} %pair.4.refs_1_.refs_9_), channel_id=1, source_target_pairs={{0,2},{2,0},{4,6},{6,4},{8,10},{10,8},{12,14},{14,12},{1,3},{3,1},... | collective-permute-start | bytes 1671176 | tf_op jit(solution)/shard_map/rows_cores/ppermute | solution.py:418
  53.2 2.0 %collective-permute-start.10 = (bf16[128,2176]{1,0:T(8,128)(2,1)S(1)}, bf16[128,2176]{1,0:T(8,128)(2,1)S(1)}, u32[]{:S(2)}, u32[]{:S(2)}) collective-permute-start(bf16[128,2176]{1,0:T(8,128)(2,1)S(1)} %pair.6.refs_3_.refs_11_), channel_id=1, source_target_pairs={{0,2},{2,0},{4,6},{6,4},{8,10},{10,8},{12,14},{14,12},{1,3},{3,1},... | collective-permute-start | bytes 1671176 | tf_op jit(solution)/shard_map/rows_cores/ppermute | solution.py:418
  53.3 14.9 %collective-permute-start.13 = (bf16[128,2048]{1,0:T(8,128)(2,1)S(1)}, bf16[128,2048]{1,0:T(8,128)(2,1)S(1)}, u32[]{:S(2)}, u32[]{:S(2)}) collective-permute-start(bf16[128,2048]{1,0:T(8,128)(2,1)S(1)} %get-tuple-element.239.refs_0_), channel_id=1, source_target_pairs={{0,2},{2,0},{4,6},{6,4},{8,10},{10,8},{12,14},{14,12},{1,3},{3,1},... | collective-permute-start | bytes 1572872 | tf_op jit(solution)/shard_map/grads_cores/ppermute | solution.py:418
  53.8 10.3 %collective-permute-start.11 = (bf16[64,2048]{1,0:T(8,128)(2,1)S(1)}, bf16[64,2048]{1,0:T(8,128)(2,1)S(1)}, u32[]{:S(2)}, u32[]{:S(2)}) collective-permute-start(bf16[64,2048]{1,0:T(8,128)(2,1)S(1)} %collective-permute-done.7.second), channel_id=1, source_target_pairs={{0,4},{2,6},{4,0},{6,2},{8,12},{10,14},{12,8},{14,10},{1,5},{3,7},... | collective-permute-start | bytes 786440 | tf_op jit(solution)/shard_map/grads_line/ppermute | solution.py:414
  53.8 14.4 %collective-permute-start.14 = (bf16[128,2048]{1,0:T(8,128)(2,1)S(1)}, bf16[128,2048]{1,0:T(8,128)(2,1)S(1)}, u32[]{:S(2)}, u32[]{:S(2)}) collective-permute-start(bf16[128,2048]{1,0:T(8,128)(2,1)S(1)} %pair.5.refs_1_), channel_id=1, source_target_pairs={{0,2},{2,0},{4,6},{6,4},{8,10},{10,8},{12,14},{14,12},{1,3},{3,1},... | collective-permute-start | bytes 1572872 | tf_op jit(solution)/shard_map/grads_cores/ppermute | solution.py:418
  53.8 14.3 %collective-permute-start.12 = (bf16[128,2048]{1,0:T(8,128)(2,1)S(1)}, bf16[128,2048]{1,0:T(8,128)(2,1)S(1)}, u32[]{:S(2)}, u32[]{:S(2)}) collective-permute-start(bf16[128,2048]{1,0:T(8,128)(2,1)S(1)} %pair.5.refs_1_), channel_id=1, source_target_pairs={{0,1},{1,0},{2,3},{3,2},{4,5},{5,4},{6,7},{7,6},{8,9},{9,8},{10,11... | collective-permute-start | bytes 1572872 | tf_op jit(solution)/shard_map/grads_across/ppermute | solution.py:422
  68.1 8.8 %collective-permute-start.17 = (bf16[128,2048]{1,0:T(8,128)(2,1)S(1)}, bf16[128,2048]{1,0:T(8,128)(2,1)S(1)}, u32[]{:S(2)}, u32[]{:S(2)}) collective-permute-start(bf16[128,2048]{1,0:T(8,128)(2,1)S(1)} %collective-permute-done.12.refs_2_), channel_id=1, source_target_pairs={{0,2},{2,0},{4,6},{6,4},{8,10},{10,8},{12,14},{14,12},{1,3},{3,1},... | collective-permute-start | bytes 1572872 | tf_op jit(solution)/shard_map/grads_cores/ppermute | solution.py:418
  68.1 8.7 %collective-permute-start.16 = (bf16[64,2048]{1,0:T(8,128)(2,1)S(1)}, bf16[64,2048]{1,0:T(8,128)(2,1)S(1)}, u32[]{:S(2)}, u32[]{:S(2)}) collective-permute-start(bf16[64,2048]{1,0:T(8,128)(2,1)S(1)} %collective-permute-done.11.first), channel_id=1, source_target_pairs={{0,1},{1,0},{2,3},{3,2},{4,5},{5,4},{6,7},{7,6},{8,9},{9,8},{10,11... | collective-permute-start | bytes 786440 | tf_op jit(solution)/shard_map/grads_across/ppermute | solution.py:422
  73.4 4.2 %collective-permute-start.15 = (bf16[2,512,1024]{2,1,0:T(8,128)(2,1)S(1)}, bf16[2,512,1024]{2,1,0:T(8,128)(2,1)S(1)}, u32[]{:S(2)}, u32[]{:S(2)}) collective-permute-start(bf16[2,512,1024]{2,1,0:T(8,128)(2,1)S(1)} %get-tuple-element.190), channel_id=1, source_target_pairs={{0,2},{2,0},{4,6},{6,4},{8,10},{10,8},{12,14},{14,12},{1,3},{3,1},... | collective-permute-start | bytes 6291464 | tf_op jit(solution)/shard_map/out_cores/ppermute | solution.py:418
  77.7 25.3 %collective-permute-start.18 = (bf16[512,1024]{1,0:T(8,128)(2,1)S(1)}, bf16[512,1024]{1,0:T(8,128)(2,1)S(1)}, u32[]{:S(2)}, u32[]{:S(2)}) collective-permute-start(bf16[512,1024]{1,0:T(8,128)(2,1)S(1)} %out_send.1), channel_id=1, source_target_pairs={{0,1},{1,0},{2,3},{3,2},{4,5},{5,4},{6,7},{7,6},{8,9},{9,8},{10,11... | collective-permute-start | bytes 3145736 | tf_op jit(solution)/shard_map/out_across/ppermute | solution.py:422
  79.1 1.9 %collective-permute-start.19 = (bf16[128,2048]{1,0:T(8,128)(2,1)S(1)}, bf16[128,2048]{1,0:T(8,128)(2,1)S(1)}, u32[]{:S(2)}, u32[]{:S(2)}) collective-permute-start(bf16[128,2048]{1,0:T(8,128)(2,1)S(1)} %pair.7.refs_3_), channel_id=1, source_target_pairs={{0,2},{2,0},{4,6},{6,4},{8,10},{10,8},{12,14},{14,12},{1,3},{3,1},... | collective-permute-start | bytes 1572872 | tf_op jit(solution)/shard_map/grads_cores/ppermute | solution.py:418
  95.6 9.7 %collective-permute-start.21 = (bf16[2,512,1152]{2,1,0:T(8,128)(2,1)S(1)}, bf16[2,512,1152]{2,1,0:T(8,128)(2,1)S(1)}, u32[]{:S(2)}, u32[]{:S(2)}) collective-permute-start(bf16[2,512,1152]{2,1,0:T(8,128)(2,1)S(1)} %get-tuple-element.224), channel_id=1, source_target_pairs={{0,2},{2,0},{4,6},{6,4},{8,10},{10,8},{12,14},{14,12},{1,3},{3,1},... | collective-permute-start | bytes 7077896 | tf_op jit(solution)/shard_map/in_cores/ppermute | solution.py:418
  103.4 14.8 %collective-permute-start.20 = (bf16[256,1024]{1,0:T(8,128)(2,1)S(1)}, bf16[256,1024]{1,0:T(8,128)(2,1)S(1)}, u32[]{:S(2)}, u32[]{:S(2)}) collective-permute-start(bf16[256,1024]{1,0:T(8,128)(2,1)S(1)} %get-tuple-element.229), channel_id=1, source_target_pairs={{0,4},{2,6},{4,0},{6,2},{8,12},{10,14},{12,8},{14,10},{1,5},{3,7},... | collective-permute-start | bytes 1572872 | tf_op jit(solution)/shard_map/out_line/ppermute | solution.py:414
  105.4 8.1 %collective-permute-start.22 = (bf16[128,1152]{1,0:T(8,128)(2,1)S(1)}, bf16[128,1152]{1,0:T(8,128)(2,1)S(1)}, u32[]{:S(2)}, u32[]{:S(2)}) collective-permute-start(bf16[128,1152]{1,0:T(8,128)(2,1)S(1)} %get-tuple-element.235), channel_id=1, source_target_pairs={{0,1},{1,0},{2,3},{3,2},{4,5},{5,4},{6,7},{7,6},{8,9},{9,8},{10,11... | collective-permute-start | bytes 884744 | tf_op jit(solution)/shard_map/in_across/ppermute | solution.py:422
  113.7 13.5 %collective-permute-start.25 = (bf16[128,1152]{1,0:T(8,128)(2,1)S(1)}, bf16[128,1152]{1,0:T(8,128)(2,1)S(1)}, u32[]{:S(2)}, u32[]{:S(2)}) collective-permute-start(bf16[128,1152]{1,0:T(8,128)(2,1)S(1)} %in_slot.3), channel_id=1, source_target_pairs={{0,4},{2,6},{4,0},{6,2},{8,12},{10,14},{12,8},{14,10},{1,5},{3,7},... | collective-permute-start | bytes 884744 | tf_op jit(solution)/shard_map/in_line/ppermute | solution.py:414
  118.3 22.2 %collective-permute-start.23 = (bf16[128,1024]{1,0:T(8,128)(2,1)S(1)}, bf16[128,1024]{1,0:T(8,128)(2,1)S(1)}, u32[]{:S(2)}, u32[]{:S(2)}) collective-permute-start(bf16[128,1024]{1,0:T(8,128)(2,1)S(1)} %add_last.1), channel_id=1, source_target_pairs={{0,8},{2,10},{4,12},{6,14},{8,0},{10,2},{12,4},{14,6},{1,9},{3,11}... | collective-permute-start | bytes 786440 | tf_op jit(solution)/shard_map/out_line/ppermute | solution.py:414
  119.7 7.2 %collective-permute-start.24 = (bf16[128,1152]{1,0:T(8,128)(2,1)S(1)}, bf16[128,1152]{1,0:T(8,128)(2,1)S(1)}, u32[]{:S(2)}, u32[]{:S(2)}) collective-permute-start(bf16[128,1152]{1,0:T(8,128)(2,1)S(1)} %get-tuple-element.253), channel_id=1, source_target_pairs={{0,1},{1,0},{2,3},{3,2},{4,5},{5,4},{6,7},{7,6},{8,9},{9,8},{10,11... | collective-permute-start | bytes 884744 | tf_op jit(solution)/shard_map/in_across/ppermute | solution.py:422
  127.4 16.2 %collective-permute-start.27 = (bf16[128,1152]{1,0:T(8,128)(2,1)S(1)}, bf16[128,1152]{1,0:T(8,128)(2,1)S(1)}, u32[]{:S(2)}, u32[]{:S(2)}) collective-permute-start(bf16[128,1152]{1,0:T(8,128)(2,1)S(1)} %in_slot.4), channel_id=1, source_target_pairs={{0,8},{2,10},{4,12},{6,14},{8,0},{10,2},{12,4},{14,6},{1,9},{3,11}... | collective-permute-start | bytes 884744 | tf_op jit(solution)/shard_map/in_line/ppermute | solution.py:414
  129.7 7.1 %collective-permute-start.26 = (bf16[128,1152]{1,0:T(8,128)(2,1)S(1)}, bf16[128,1152]{1,0:T(8,128)(2,1)S(1)}, u32[]{:S(2)}, u32[]{:S(2)}) collective-permute-start(bf16[128,1152]{1,0:T(8,128)(2,1)S(1)} %get-tuple-element.267), channel_id=1, source_target_pairs={{0,1},{1,0},{2,3},{3,2},{4,5},{5,4},{6,7},{7,6},{8,9},{9,8},{10,11... | collective-permute-start | bytes 884744 | tf_op jit(solution)/shard_map/in_across/ppermute | solution.py:422
  136.9 12.8 %copy-start.1 = (s32[128,4]{0,1:T(4,128)S(1)}, s32[128,4]{0,1:T(4,128)}, u32[]{:S(2)}) copy-start(s32[128,4]{0,1:T(4,128)} %param.9) | copy-start | bytes 6148
  136.9 12.8 %copy-start.2 = (f32[128,4]{0,1:T(4,128)S(1)}, f32[128,4]{0,1:T(4,128)}, u32[]{:S(2)}) copy-start(f32[128,4]{0,1:T(4,128)} %param.11) | copy-start | bytes 6148
  136.9 12.8 %copy-start.3 = (s32[128]{0:T(128)S(1)}, s32[128]{0:T(128)}, u32[]{:S(2)}) copy-start(s32[128]{0:T(128)} %param.10) | copy-start | bytes 1540
  137.0 6.8 %collective-permute-start.29 = (bf16[128,1152]{1,0:T(8,128)(2,1)S(1)}, bf16[128,1152]{1,0:T(8,128)(2,1)S(1)}, u32[]{:S(2)}, u32[]{:S(2)}) collective-permute-start(bf16[128,1152]{1,0:T(8,128)(2,1)S(1)} %get-tuple-element.284), channel_id=1, source_target_pairs={{0,1},{1,0},{2,3},{3,2},{4,5},{5,4},{6,7},{7,6},{8,9},{9,8},{10,11... | collective-permute-start | bytes 884744 | tf_op jit(solution)/shard_map/in_across/ppermute | solution.py:422
  138.4 11.3 %collective-permute-start.28 = (bf16[128,1152]{1,0:T(8,128)(2,1)S(1)}, bf16[128,1152]{1,0:T(8,128)(2,1)S(1)}, u32[]{:S(2)}, u32[]{:S(2)}) collective-permute-start(bf16[128,1152]{1,0:T(8,128)(2,1)S(1)} %in_slot.5), channel_id=1, source_target_pairs={{0,4},{2,6},{4,0},{6,2},{8,12},{10,14},{12,8},{14,10},{1,5},{3,7},... | collective-permute-start | bytes 884744 | tf_op jit(solution)/shard_map/in_line/ppermute | solution.py:414

commit v7 on v6

--- a/solution.py
+++ b/solution.py
@@ -149,37 +149,37 @@
     )
 
 
-def pair_kernel(first, second, pair):
-    half = first.shape[0]
-    pair[:half, :] = first[...]
-    pair[half:, :] = second[...]
-
-
-def pair_up(first, second):
-    rows, width = first.shape
-    shape = jax.ShapeDtypeStruct((2 * rows, width), first.dtype)
-    return call(pair_kernel, "pair", (first, second), shape)
-
-
-def parts_of(pieces):
-    pair, line_pair, across_pair, last_pair = pieces
+def join_kernel(*refs):
+    at = 0
+    for piece in refs[:-1]:
+        refs[-1][at : at + piece.shape[0], :] = piece[...]
+        at = at + piece.shape[0]
+
+
+def join(*pieces):
+    total = sum(piece.shape[0] for piece in pieces)
+    shape = jax.ShapeDtypeStruct((total, pieces[0].shape[1]), pieces[0].dtype)
+    return call(join_kernel, "join", pieces, shape)
+
+
+def parts_of(pair, rest):
     rows = pair.shape[0]
     half = rows // 2
     parts = [(pair, 0, rows)]
     for slot in range(2):
-        parts = parts + [(line_pair, slot * half, half), (across_pair, slot * half, half)]
-    return parts + [(last_pair, 0, rows)]
+        parts = parts + [(rest, slot * half, half), (rest, rows + slot * half, half)]
+    return parts + [(rest, 2 * rows, rows)]
 
 
 def lay_out(pieces, target, columns):
     at = 0
-    for piece, start, rows in parts_of(pieces[:4]) + parts_of(pieces[4:]):
+    for piece, start, rows in parts_of(*pieces[:2]) + parts_of(*pieces[2:]):
         target[at : at + rows, :] = piece[start : start + rows, columns]
         at = at + rows
 
 
 def gate_column(experts, pieces, width):
-    parts = parts_of(pieces[:4]) + parts_of(pieces[4:])
+    parts = parts_of(*pieces[:2]) + parts_of(*pieces[2:])
     table = jnp.concatenate(
         [piece[start : start + rows, width:] for piece, start, rows in parts], axis=0
     )
@@ -190,7 +190,7 @@
 
 
 def hidden_kernel(experts, tile, *refs):
-    pieces, refs = refs[:8], refs[8:]
+    pieces, refs = refs[:4], refs[4:]
     gate_mat, up_mat, pre_gate, pre_up, gated, rows = refs
     width = rows.shape[1]
     lay_out(pieces, rows, slice(0, width))
@@ -247,7 +247,7 @@
 
 
 def hidden_grads_kernel(experts, tile, *refs):
-    pieces, gate_pieces, refs = refs[:8], refs[8:16], refs[16:]
+    pieces, gate_pieces, refs = refs[:4], refs[4:8], refs[8:]
     down_mat, pre_gate, pre_up, d_gate, d_up, shares_out, grads = refs
     total, width = grads.shape
     lay_out(pieces, grads, slice(0, width))
@@ -317,7 +317,7 @@
 
 
 def weights_kernel(width, tile, *refs):
-    pieces, (acts, grad, rows) = refs[:8], refs[8:]
+    pieces, (acts, grad, rows) = refs[:4], refs[4:]
     lay_out(pieces, rows, slice(0, width))
     left, right = (acts, rows) if grad.shape[1] == width else (rows, acts)
     for start in range(0, grad.shape[0], tile):
@@ -509,45 +509,34 @@
     sibling_pair = rows.sibling(pair)
     gate_mat, up_mat, down_mat = order(load, gate_local, up_local, down_local)
     sibling_pair = hold(sibling_pair, down_mat)
-    line_pair = order(pair_up, near, far, also=sibling_pair)
+    line_pair = order(join, near, far, also=sibling_pair)
+    last = rows.line(hold(far, line_pair), rows.near)
     across_pair = rows.across(line_pair)
-    last = rows.line(hold(far, line_pair), rows.near)
-    sibling_line = rows.sibling(line_pair)
-    all_rows = [pair, line_pair]
-    sibling_rows = [sibling_pair, sibling_line]
-    own, pair = order(prepare_grads, grad_out)
+    own, grads_pair = order(prepare_grads, grad_out)
     far = grads.line(own, grads.far)
     last_across = rows.across(last)
     near = grads.line(hold(own, last), grads.near)
-    clock = order(space, clock, also=last)
-    across_pair = hold(across_pair, clock)
-    sibling_across = rows.sibling(across_pair)
-    far = hold(far, across_pair)
+    far = hold(far, last)
     grads_last = grads.line(far, grads.near)
     clock = order(lambda c: space(c, 2 * 10**9), clock, also=far)
-    line_pair = order(pair_up, near, far, also=sibling_across)
-    sibling_pair, sibling_line = grads.sibling(pair), grads.sibling(line_pair)
-    grads_across = grads.across(line_pair)
-    last_pair = order(pair_up, last, last_across, also=line_pair)
-    all_rows = all_rows + [across_pair, last_pair]
-    all_rows = all_rows + sibling_rows + [sibling_across, rows.sibling(last_pair)]
+    grads_line = order(join, near, far)
+    grads_across = grads.across(grads_line)
+    grads_sibling = grads.sibling(grads_pair)
+    rest = order(join, line_pair, across_pair, last, last_across)
+    all_rows = [pair, rest, sibling_pair, rows.sibling(rest)]
     pre_gate, pre_up, gated = order(
         lambda *r: hidden_units(r, gate_mat, up_mat, experts), *all_rows
     )
-    grads_last, grads_across = hold((grads_last, grads_across), gated)
+    grads_last = hold(grads_last, gated)
     last_across = grads.across(grads_last)
-    sibling_across = grads.sibling(grads_across)
-    near_out, sent = order(
-        outputs_of, gated, down_mat, also=(grads_across, sibling_pair, sibling_line)
-    )
+    near_out, sent = order(outputs_of, gated, down_mat, also=(grads_last, grads_sibling))
     received = outs.sibling(sent)
-    last_pair = order(pair_up, grads_last, last_across)
-    clock = order(space, clock, also=sibling_across)
+    clock = order(space, clock, also=(grads_across, last_across))
     received = hold(received, clock)
     (sent,) = order(outs.send, near_out, received)
     arrived = outs.across(sent)
-    all_grads = [pair, line_pair, grads_across, last_pair]
-    all_grads = all_grads + [sibling_pair, sibling_line, sibling_across, grads.sibling(last_pair)]
+    rest = order(join, grads_line, grads_across, grads_last, last_across)
+    all_grads = [grads_pair, rest, grads_sibling, grads.sibling(rest)]
     d_gate, d_up, shares = order(
         lambda g, r, *pre: hidden_grads(g, r, *pre, down_mat, experts),
         all_grads,
@@ -571,13 +560,13 @@
     slot = order(lambda *s: ins.slot(3, *s), in_own, in_received, last_arrived)
     last_sum = ins.line(slot, ins.near)
     far_arrived = ins.across(hold(far_sent, slot))
+    grad_gate = order(product_of("grad_gate", False), all_rows, d_gate)
     far_slot = order(
         lambda *s: call(add_last_kernel, "add_last", s, jax.ShapeDtypeStruct(s[0].shape, s[0].dtype)),
         far_slot,
         near_sums,
     )
     far_sum = outs.line(far_slot, outs.far)
-    grad_gate = order(product_of("grad_gate", False), all_rows, d_gate)
     slot = order(lambda *s: ins.slot(2, *s), in_own, in_received, far_arrived, last_sum)
     far = ins.line(slot, ins.far)
     near_arrived = ins.across(hold(near_sent, slot))

time: 151 us -> 144 us (0.954)
  waiting for transfers between devices: 63.7 us -> 56.9 us
    ppermute x9, waiting for transfers between devices: 22 us -> 12 us  [across(): return lax.ppermute(array, 'helper', self.sides)]
    ppermute x10 -> x6, waiting for transfers between devices: 3.36 us -> 7.87 us  [sibling(): return lax.ppermute(array, 'expert', self.cores)]
    ppermute x11, starting transfers between devices: 17.8 us -> 15.8 us  [line(): return lax.ppermute(array, 'expert', pairs)]
    ppermute x9, starting transfers between devices: 9.96 us -> 11.6 us  [across(): return lax.ppermute(array, 'helper', self.sides)]
  transfers between devices with their start and end apart: 30 -> 26, of which waited for: 17 -> 15; matrix products, arithmetic and copies ran while one was open for 0% -> 0% of each run, Pallas kernels for 36% -> 38%
where the time goes in v7:
time: 144 us; the launch traced here: 143 us
  Pallas kernels  57 us (40%)
  waiting for transfers between devices  56.9 us (40%)
  starting transfers between devices  28.8 us (20%)
    pallas_call x21, Pallas kernels, call(): pl.pallas_call(kernel, out_shape=out_shape, in_specs=[VMEM] * len(operand...  51 us
    ppermute x11, waiting for transfers between devices, line(): return lax.ppermute(array, 'expert', pairs)  37 us
    ppermute x11, starting transfers between devices, line(): return lax.ppermute(array, 'expert', pairs)  15.8 us
    ppermute x9, waiting for transfers between devices, across(): return lax.ppermute(array, 'helper', self.sides)  12 us
    ppermute x9, starting transfers between devices, across(): return lax.ppermute(array, 'helper', self.sides)  11.6 us
    ppermute x6, waiting for transfers between devices, sibling(): return lax.ppermute(array, 'expert', self.cores)  7.87 us
    pallas_call x1, Pallas kernels, load(): pl.pallas_call(load_kernel, out_shape=tuple((jax.ShapeDtypeStruct(mat.sha...  4.73 us
  transfers between devices with their start and end apart: 26, of which 15 were waited for; matrix products, arithmetic and copies ran while one was open for 0% of the time, Pallas kernels for 38%

profile of v7, /device:TPU:0, one launch (start us, length us, event | category | flops | bytes accessed | tf_op | source)
XLA Modules:
  0.0 143.5 jit_solution(9722387079435826660)
XLA Ops:
  0.6 1.3 prepare_rows.1
  1.9 0.5 collective-permute-start.2
  2.5 3.7 %collective-permute-start.1 = (bf16[64,2176]{1,0:T(8,128)(2,1)S(1)}, bf16[64,2176]{1,0:T(8,128)(2,1)S(1)}, u32[]{:S(2)}, u32[]{:S(2)}) collective-permute-start(bf16[64,2176]{1,0:T(8,128)(2,1)S(1)} %get-tuple-element.128), channel_id=1, source_target_pairs={{0,8},{2,10},{4,12},{6,14},{8,0},{10,2},{12,4},{14,6},{1,9},{3,11}... | collective-permute-start | bytes 835592 | tf_op jit(solution)/shard_map/rows_line/ppermute | solution.py:414
  6.1 1.6 %collective-permute-start = (bf16[64,2176]{1,0:T(8,128)(2,1)S(1)}, bf16[64,2176]{1,0:T(8,128)(2,1)S(1)}, u32[]{:S(2)}, u32[]{:S(2)}) collective-permute-start(bf16[64,2176]{1,0:T(8,128)(2,1)S(1)} %get-tuple-element.128), channel_id=1, source_target_pairs={{0,4},{2,6},{4,0},{6,2},{8,12},{10,14},{12,8},{14,10},{1,5},{3,7},... | collective-permute-start | bytes 835592 | tf_op jit(solution)/shard_map/rows_line/ppermute | solution.py:414
  7.7 4.7 %load.1 = (bf16[2048,1024]{1,0:T(8,128)(2,1)S(1)}, bf16[2048,1024]{1,0:T(8,128)(2,1)S(1)}, bf16[1024,2048]{1,0:T(8,128)(2,1)S(1)}) custom-call(bf16[2048,1024]{1,0:T(8,128)(2,1)} %bitcast.16, bf16[2048,1024]{1,0:T(8,128)(2,1)} %bitcast.17, bf16[1024,2048]{1,0:T(8,128)(2,1)} %bitcast.18), custom_call_target="tpu_custom_call" | custom-call | tf_op jit(solution)/shard_map/load/pallas_call | solution.py:461
  12.4 7.0 %collective-permute-done.1.refs_1_ = bf16[64,2176]{1,0:T(8,128)(2,1)S(1)} collective-permute-done((bf16[64,2176]{1,0:T(8,128)(2,1)S(1)}, bf16[64,2176]{1,0:T(8,128)(2,1)S(1)}, u32[]{:S(2)}, u32[]{:S(2)}) %collective-permute-start.1) | collective-permute-done | bytes 278560 | tf_op jit(solution)/shard_map/rows_line/ppermute | solution.py:414
  19.4 0.2 collective-permute-done.refs_0_
  19.7 1.6 %collective-permute-start.4 = (bf16[64,2176]{1,0:T(8,128)(2,1)S(1)}, bf16[64,2176]{1,0:T(8,128)(2,1)S(1)}, u32[]{:S(2)}, u32[]{:S(2)}) collective-permute-start(bf16[64,2176]{1,0:T(8,128)(2,1)S(1)} %collective-permute-done.1.refs_1_), channel_id=1, source_target_pairs={{0,4},{2,6},{4,0},{6,2},{8,12},{10,14},{12,8},{14,10},{1,5},{3,7},... | collective-permute-start | bytes 835592 | tf_op jit(solution)/shard_map/rows_line/ppermute | solution.py:414
  21.2 1.5 %collective-permute-start.3 = (bf16[128,2176]{1,0:T(8,128)(2,1)S(1)}, bf16[128,2176]{1,0:T(8,128)(2,1)S(1)}, u32[]{:S(2)}, u32[]{:S(2)}) collective-permute-start(bf16[128,2176]{1,0:T(8,128)(2,1)S(1)} %join.4.refs_0_), channel_id=1, source_target_pairs={{0,1},{1,0},{2,3},{3,2},{4,5},{5,4},{6,7},{7,6},{8,9},{9,8},{10,11... | collective-permute-start | bytes 1671176 | tf_op jit(solution)/shard_map/rows_across/ppermute | solution.py:422
  22.8 2.4 %collective-permute-start.7 = (bf16[64,2048]{1,0:T(8,128)(2,1)S(1)}, bf16[64,2048]{1,0:T(8,128)(2,1)S(1)}, u32[]{:S(2)}, u32[]{:S(2)}) collective-permute-start(bf16[64,2048]{1,0:T(8,128)(2,1)S(1)} %get-tuple-element.142), channel_id=1, source_target_pairs={{0,8},{2,10},{4,12},{6,14},{8,0},{10,2},{12,4},{14,6},{1,9},{3,11}... | collective-permute-start | bytes 786440 | tf_op jit(solution)/shard_map/grads_line/ppermute | solution.py:414
  25.2 7.1 %collective-permute-done.4.refs_2_ = bf16[64,2176]{1,0:T(8,128)(2,1)S(1)} collective-permute-done((bf16[64,2176]{1,0:T(8,128)(2,1)S(1)}, bf16[64,2176]{1,0:T(8,128)(2,1)S(1)}, u32[]{:S(2)}, u32[]{:S(2)}) %collective-permute-start.4) | collective-permute-done | bytes 278560 | tf_op jit(solution)/shard_map/rows_line/ppermute | solution.py:414
  32.3 2.4 %collective-permute-start.5 = (bf16[64,2176]{1,0:T(8,128)(2,1)S(1)}, bf16[64,2176]{1,0:T(8,128)(2,1)S(1)}, u32[]{:S(2)}, u32[]{:S(2)}) collective-permute-start(bf16[64,2176]{1,0:T(8,128)(2,1)S(1)} %collective-permute-done.4.refs_2_), channel_id=1, source_target_pairs={{0,1},{1,0},{2,3},{3,2},{4,5},{5,4},{6,7},{7,6},{8,9},{9,8},{10,11... | collective-permute-start | bytes 835592 | tf_op jit(solution)/shard_map/rows_across/ppermute | solution.py:422
  34.7 2.3 %collective-permute-done.7.refs_1_ = bf16[64,2048]{1,0:T(8,128)(2,1)S(1)} collective-permute-done((bf16[64,2048]{1,0:T(8,128)(2,1)S(1)}, bf16[64,2048]{1,0:T(8,128)(2,1)S(1)}, u32[]{:S(2)}, u32[]{:S(2)}) %collective-permute-start.7) | collective-permute-done | bytes 262176 | tf_op jit(solution)/shard_map/grads_line/ppermute | solution.py:414
  37.0 5.4 %collective-permute-done.6.refs_0_ = bf16[64,2048]{1,0:T(8,128)(2,1)S(1)} collective-permute-done((bf16[64,2048]{1,0:T(8,128)(2,1)S(1)}, bf16[64,2048]{1,0:T(8,128)(2,1)S(1)}, u32[]{:S(2)}, u32[]{:S(2)}) %collective-permute-start.6) | collective-permute-done | bytes 262176 | tf_op jit(solution)/shard_map/grads_line/ppermute | solution.py:414
  42.6 0.5 collective-permute-start.10
  43.1 0.6 collective-permute-start.12
  43.7 2.4 %collective-permute-done.8.refs_3_.refs_7_ = bf16[384,2176]{1,0:T(8,128)(2,1)S(1)} collective-permute-done((bf16[384,2176]{1,0:T(8,128)(2,1)S(1)}, bf16[384,2176]{1,0:T(8,128)(2,1)S(1)}, u32[]{:S(2)}, u32[]{:S(2)}) %collective-permute-start.8) | collective-permute-done | bytes 1671200 | tf_op jit(solution)/shard_map/rows_cores/ppermute | solution.py:418
  46.1 8.8 %hidden_units.1 = (f32[1024,1024]{1,0:T(8,128)S(1)}, f32[1024,1024]{1,0:T(8,128)S(1)}, bf16[1024,1024]{1,0:T(8,128)(2,1)S(1)}) custom-call(bf16[128,2176]{1,0:T(8,128)(2,1)S(1)} %get-tuple-element.226.refs_0_.refs_4_, bf16[384,2176]{1,0:T(8,128)(2,1)S(1)} %join.6.refs_1_.refs_5_, bf16[128,2176]{1,0:T(8,128)(2,1)S(1)} %collective-permute-done.2.refs_2_.refs_6_, ...), custom_call_target="tpu_custom_call" | custom-call | flops 8589934592 | tf_op jit(solution)/shard_map/hidden_units/pallas_call | solution.py:40
  55.0 0.3 collective-permute-start.13
  55.3 4.5 %outputs.1 = (bf16[2,512,1024]{2,1,0:T(8,128)(2,1)S(1)}, bf16[2,512,1024]{2,1,0:T(8,128)(2,1)S(1)}) custom-call(bf16[1024,1024]{1,0:T(8,128)(2,1)S(1)} %get-tuple-element.209.gated.refs_4_, bf16[1024,2048]{1,0:T(8,128)(2,1)S(1)} %get-tuple-element.161.down_mat.refs_8_), custom_call_target="tpu_custom_call" | custom-call | flops 4294967296 | tf_op jit(solution)/shard_map/outputs/pallas_call | solution.py:40
  59.9 3.5 %collective-permute-done.13.refs_3_ = bf16[64,2048]{1,0:T(8,128)(2,1)S(1)} collective-permute-done((bf16[64,2048]{1,0:T(8,128)(2,1)S(1)}, bf16[64,2048]{1,0:T(8,128)(2,1)S(1)}, u32[]{:S(2)}, u32[]{:S(2)}) %collective-permute-start.13) | collective-permute-done | bytes 262176 | tf_op jit(solution)/shard_map/grads_across/ppermute | solution.py:422
  63.4 0.6 collective-permute-done.11.received
  64.2 0.2 collective-permute-start.15
  64.4 1.8 %collective-permute-start.14 = (bf16[512,1024]{1,0:T(8,128)(2,1)S(1)}, bf16[512,1024]{1,0:T(8,128)(2,1)S(1)}, u32[]{:S(2)}, u32[]{:S(2)}) collective-permute-start(bf16[512,1024]{1,0:T(8,128)(2,1)S(1)} %out_send.1), channel_id=1, source_target_pairs={{0,1},{1,0},{2,3},{3,2},{4,5},{5,4},{6,7},{7,6},{8,9},{9,8},{10,11... | collective-permute-start | bytes 3145736 | tf_op jit(solution)/shard_map/out_across/ppermute | solution.py:422
  66.2 1.5 %collective-permute-done.15.refs_3_ = bf16[384,2048]{1,0:T(8,128)(2,1)S(1)} collective-permute-done((bf16[384,2048]{1,0:T(8,128)(2,1)S(1)}, bf16[384,2048]{1,0:T(8,128)(2,1)S(1)}, u32[]{:S(2)}, u32[]{:S(2)}) %collective-permute-start.15) | collective-permute-done | bytes 1572896 | tf_op jit(solution)/shard_map/grads_cores/ppermute | solution.py:418
  67.7 5.6 %hidden_grads.1 = (bf16[1024,1024]{1,0:T(8,128)(2,1)S(1)}, bf16[1024,1024]{1,0:T(8,128)(2,1)S(1)}, bf16[1024,128]{1,0:T(8,128)(2,1)S(1)}) custom-call(bf16[128,2048]{1,0:T(8,128)(2,1)S(1)} %get-tuple-element.205.refs_0_, bf16[384,2048]{1,0:T(8,128)(2,1)S(1)} %join.7.refs_1_, bf16[128,2048]{1,0:T(8,128)(2,1)S(1)} %collective-permute-done.10.refs_2_, ...), custom_call_target="tpu_custom_call" | custom-call | flops 4294967296 | tf_op jit(solution)/shard_map/hidden_grads/pallas_call | solution.py:40
  73.4 8.9 %input_grads.1 = (bf16[2,512,1152]{2,1,0:T(8,128)(2,1)S(1)}, bf16[2,512,1152]{2,1,0:T(8,128)(2,1)S(1)}) custom-call(bf16[1024,1024]{1,0:T(8,128)(2,1)S(1)} %get-tuple-element.217.d_gate.refs_4_, bf16[1024,1024]{1,0:T(8,128)(2,1)S(1)} %get-tuple-element.230.d_up.refs_4_, bf16[1024,128]{1,0:T(8,128)(2,1)S(1)} %get-tuple-element.187.shares, ...), custom_call_target="tpu_custom_call" | custom-call | tf_op jit(solution)/shard_map/input_grads/pallas_call | solution.py:40
  82.3 7.7 %collective-permute-done.14.arrived = bf16[512,1024]{1,0:T(8,128)(2,1)S(1)} collective-permute-done((bf16[512,1024]{1,0:T(8,128)(2,1)S(1)}, bf16[512,1024]{1,0:T(8,128)(2,1)S(1)}, u32[]{:S(2)}, u32[]{:S(2)}) %collective-permute-start.14) | collective-permute-done | bytes 1048608 | tf_op jit(solution)/shard_map/out_across/ppermute | solution.py:422
  89.9 0.4 out_slots.1
  90.3 0.8 collective-permute-start.16
  91.1 3.3 %collective-permute-done.17.received = bf16[2,512,1152]{2,1,0:T(8,128)(2,1)S(1)} collective-permute-done((bf16[2,512,1152]{2,1,0:T(8,128)(2,1)S(1)}, bf16[2,512,1152]{2,1,0:T(8,128)(2,1)S(1)}, u32[]{:S(2)}, u32[]{:S(2)}) %collective-permute-start.17) | collective-permute-done | bytes 2359328 | tf_op jit(solution)/shard_map/in_cores/ppermute | solution.py:418
  94.6 1.8 %collective-permute-start.18 = (bf16[128,1152]{1,0:T(8,128)(2,1)S(1)}, bf16[128,1152]{1,0:T(8,128)(2,1)S(1)}, u32[]{:S(2)}, u32[]{:S(2)}) collective-permute-start(bf16[128,1152]{1,0:T(8,128)(2,1)S(1)} %get-tuple-element.201), channel_id=1, source_target_pairs={{0,1},{1,0},{2,3},{3,2},{4,5},{5,4},{6,7},{7,6},{8,9},{9,8},{10,11... | collective-permute-start | bytes 884744 | tf_op jit(solution)/shard_map/in_across/ppermute | solution.py:422
  96.4 6.6 %grad_down.1 = bf16[1024,2048]{1,0:T(8,128)(2,1)} custom-call(bf16[128,2048]{1,0:T(8,128)(2,1)S(1)} %get-tuple-element.205.refs_0_, bf16[384,2048]{1,0:T(8,128)(2,1)S(1)} %join.7.refs_1_, bf16[128,2048]{1,0:T(8,128)(2,1)S(1)} %collective-permute-done.10.refs_2_, bf16[384,2048]{1,0:T(8,128)(2,1)S(1)} %collective-permute-done.15.refs_3_, ...), custom_call_target="tpu_custom_call" | custom-call | flops 4294967296 | tf_op jit(solution)/shard_map/grad_down/pallas_call | solution.py:40
  103.0 0.8 collective-permute-done.18.arrived
  103.8 0.8 collective-permute-start.21
  104.6 1.1 collective-permute-start.20
  105.7 6.8 %grad_gate.1 = bf16[2048,1024]{1,0:T(8,128)(2,1)} custom-call(bf16[128,2176]{1,0:T(8,128)(2,1)S(1)} %get-tuple-element.226.refs_0_.refs_4_, bf16[384,2176]{1,0:T(8,128)(2,1)S(1)} %join.6.refs_1_.refs_5_, bf16[128,2176]{1,0:T(8,128)(2,1)S(1)} %collective-permute-done.2.refs_2_.refs_6_, bf16[384,2176]{1,0:T(8,128)(2,1)S(1)} %collective-permute-done.8.refs_3_.refs_7_, ...), custom_call_target="tpu_custom_call" | custom-call | flops 4294967296 | tf_op jit(solution)/shard_map/grad_gate/pallas_call | solution.py:40
  112.5 3.1 %collective-permute-start.19 = (bf16[128,1024]{1,0:T(8,128)(2,1)S(1)}, bf16[128,1024]{1,0:T(8,128)(2,1)S(1)}, u32[]{:S(2)}, u32[]{:S(2)}) collective-permute-start(bf16[128,1024]{1,0:T(8,128)(2,1)S(1)} %add_last.1), channel_id=1, source_target_pairs={{0,8},{2,10},{4,12},{6,14},{8,0},{10,2},{12,4},{14,6},{1,9},{3,11}... | collective-permute-start | bytes 786440 | tf_op jit(solution)/shard_map/out_line/ppermute | solution.py:414
  115.6 0.1 in_slot.4
  115.9 1.0 collective-permute-start.22
  116.9 6.5 %grad_up.1 = bf16[2048,1024]{1,0:T(8,128)(2,1)} custom-call(bf16[128,2176]{1,0:T(8,128)(2,1)S(1)} %get-tuple-element.226.refs_0_.refs_4_, bf16[384,2176]{1,0:T(8,128)(2,1)S(1)} %join.6.refs_1_.refs_5_, bf16[128,2176]{1,0:T(8,128)(2,1)S(1)} %collective-permute-done.2.refs_2_.refs_6_, bf16[384,2176]{1,0:T(8,128)(2,1)S(1)} %collective-permute-done.8.refs_3_.refs_7_, ...), custom_call_target="tpu_custom_call" | custom-call | flops 4294967296 | tf_op jit(solution)/shard_map/grad_up/pallas_call | solution.py:40
  123.6 1.1 collective-permute-start.25
  124.7 1.8 %collective-permute-start.24 = (bf16[128,1152]{1,0:T(8,128)(2,1)S(1)}, bf16[128,1152]{1,0:T(8,128)(2,1)S(1)}, u32[]{:S(2)}, u32[]{:S(2)}) collective-permute-start(bf16[128,1152]{1,0:T(8,128)(2,1)S(1)} %in_slot.5), channel_id=1, source_target_pairs={{0,4},{2,6},{4,0},{6,2},{8,12},{10,14},{12,8},{14,10},{1,5},{3,7},... | collective-permute-start | bytes 884744 | tf_op jit(solution)/shard_map/in_line/ppermute | solution.py:414
  126.4 7.6 %collective-permute-done.19.far = bf16[128,1024]{1,0:T(8,128)(2,1)S(1)} collective-permute-done((bf16[128,1024]{1,0:T(8,128)(2,1)S(1)}, bf16[128,1024]{1,0:T(8,128)(2,1)S(1)}, u32[]{:S(2)}, u32[]{:S(2)}) %collective-permute-start.19) | collective-permute-done | bytes 262176 | tf_op jit(solution)/shard_map/out_line/ppermute | solution.py:414
  134.0 0.8 finish_outputs.1
  134.9 4.4 %collective-permute-done.23.refs_0_ = bf16[128,1152]{1,0:T(8,128)(2,1)S(1)} collective-permute-done((bf16[128,1152]{1,0:T(8,128)(2,1)S(1)}, bf16[128,1152]{1,0:T(8,128)(2,1)S(1)}, u32[]{:S(2)}, u32[]{:S(2)}) %collective-permute-start.23) | collective-permute-done | bytes 294944 | tf_op jit(solution)/shard_map/in_line/ppermute | solution.py:414
  139.2 3.1 %collective-permute-done.24.refs_1_ = bf16[128,1152]{1,0:T(8,128)(2,1)S(1)} collective-permute-done((bf16[128,1152]{1,0:T(8,128)(2,1)S(1)}, bf16[128,1152]{1,0:T(8,128)(2,1)S(1)}, u32[]{:S(2)}, u32[]{:S(2)}) %collective-permute-start.24) | collective-permute-done | bytes 294944 | tf_op jit(solution)/shard_map/in_line/ppermute | solution.py:414
  142.4 1.1 finish_inputs.1
  (39 shorter events, 1.1 us)
Async XLA Ops:
  1.9 10.5 %collective-permute-start.2 = (bf16[128,2176]{1,0:T(8,128)(2,1)S(1)}, bf16[128,2176]{1,0:T(8,128)(2,1)S(1)}, u32[]{:S(2)}, u32[]{:S(2)}) collective-permute-start(bf16[128,2176]{1,0:T(8,128)(2,1)S(1)} %get-tuple-element.226.refs_0_.refs_4_), channel_id=1, source_target_pairs={{0,2},{2,0},{4,6},{6,4},{8,10},{10,8},{12,14},{14,12},{1,3},{3,1},... | collective-permute-start | bytes 1671176 | tf_op jit(solution)/shard_map/rows_cores/ppermute | solution.py:418
  2.5 17.0 %collective-permute-start.1 = (bf16[64,2176]{1,0:T(8,128)(2,1)S(1)}, bf16[64,2176]{1,0:T(8,128)(2,1)S(1)}, u32[]{:S(2)}, u32[]{:S(2)}) collective-permute-start(bf16[64,2176]{1,0:T(8,128)(2,1)S(1)} %get-tuple-element.128), channel_id=1, source_target_pairs={{0,8},{2,10},{4,12},{6,14},{8,0},{10,2},{12,4},{14,6},{1,9},{3,11}... | collective-permute-start | bytes 835592 | tf_op jit(solution)/shard_map/rows_line/ppermute | solution.py:414
  6.1 13.5 %collective-permute-start = (bf16[64,2176]{1,0:T(8,128)(2,1)S(1)}, bf16[64,2176]{1,0:T(8,128)(2,1)S(1)}, u32[]{:S(2)}, u32[]{:S(2)}) collective-permute-start(bf16[64,2176]{1,0:T(8,128)(2,1)S(1)} %get-tuple-element.128), channel_id=1, source_target_pairs={{0,4},{2,6},{4,0},{6,2},{8,12},{10,14},{12,8},{14,10},{1,5},{3,7},... | collective-permute-start | bytes 835592 | tf_op jit(solution)/shard_map/rows_line/ppermute | solution.py:414
  7.7 15.1 %copy-start = (bf16[128,2048]{1,0:T(8,128)(2,1)S(1)}, bf16[128,2048]{1,0:T(8,128)(2,1)}, u32[]{:S(2)}) copy-start(bf16[128,2048]{1,0:T(8,128)(2,1)} %rows) | copy-start | bytes 1572868
  19.7 12.6 %collective-permute-start.4 = (bf16[64,2176]{1,0:T(8,128)(2,1)S(1)}, bf16[64,2176]{1,0:T(8,128)(2,1)S(1)}, u32[]{:S(2)}, u32[]{:S(2)}) collective-permute-start(bf16[64,2176]{1,0:T(8,128)(2,1)S(1)} %collective-permute-done.1.refs_1_), channel_id=1, source_target_pairs={{0,4},{2,6},{4,0},{6,2},{8,12},{10,14},{12,8},{14,10},{1,5},{3,7},... | collective-permute-start | bytes 835592 | tf_op jit(solution)/shard_map/rows_line/ppermute | solution.py:414
  21.2 21.2 %collective-permute-start.3 = (bf16[128,2176]{1,0:T(8,128)(2,1)S(1)}, bf16[128,2176]{1,0:T(8,128)(2,1)S(1)}, u32[]{:S(2)}, u32[]{:S(2)}) collective-permute-start(bf16[128,2176]{1,0:T(8,128)(2,1)S(1)} %join.4.refs_0_), channel_id=1, source_target_pairs={{0,1},{1,0},{2,3},{3,2},{4,5},{5,4},{6,7},{7,6},{8,9},{9,8},{10,11... | collective-permute-start | bytes 1671176 | tf_op jit(solution)/shard_map/rows_across/ppermute | solution.py:422
  22.8 14.1 %collective-permute-start.7 = (bf16[64,2048]{1,0:T(8,128)(2,1)S(1)}, bf16[64,2048]{1,0:T(8,128)(2,1)S(1)}, u32[]{:S(2)}, u32[]{:S(2)}) collective-permute-start(bf16[64,2048]{1,0:T(8,128)(2,1)S(1)} %get-tuple-element.142), channel_id=1, source_target_pairs={{0,8},{2,10},{4,12},{6,14},{8,0},{10,2},{12,4},{14,6},{1,9},{3,11}... | collective-permute-start | bytes 786440 | tf_op jit(solution)/shard_map/grads_line/ppermute | solution.py:414
  32.3 10.1 %collective-permute-start.5 = (bf16[64,2176]{1,0:T(8,128)(2,1)S(1)}, bf16[64,2176]{1,0:T(8,128)(2,1)S(1)}, u32[]{:S(2)}, u32[]{:S(2)}) collective-permute-start(bf16[64,2176]{1,0:T(8,128)(2,1)S(1)} %collective-permute-done.4.refs_2_), channel_id=1, source_target_pairs={{0,1},{1,0},{2,3},{3,2},{4,5},{5,4},{6,7},{7,6},{8,9},{9,8},{10,11... | collective-permute-start | bytes 835592 | tf_op jit(solution)/shard_map/rows_across/ppermute | solution.py:422
  34.7 7.7 %collective-permute-start.6 = (bf16[64,2048]{1,0:T(8,128)(2,1)S(1)}, bf16[64,2048]{1,0:T(8,128)(2,1)S(1)}, u32[]{:S(2)}, u32[]{:S(2)}) collective-permute-start(bf16[64,2048]{1,0:T(8,128)(2,1)S(1)} %get-tuple-element.142), channel_id=1, source_target_pairs={{0,4},{2,6},{4,0},{6,2},{8,12},{10,14},{12,8},{14,10},{1,5},{3,7},... | collective-permute-start | bytes 786440 | tf_op jit(solution)/shard_map/grads_line/ppermute | solution.py:414
  42.5 3.6 %collective-permute-start.8 = (bf16[384,2176]{1,0:T(8,128)(2,1)S(1)}, bf16[384,2176]{1,0:T(8,128)(2,1)S(1)}, u32[]{:S(2)}, u32[]{:S(2)}) collective-permute-start(bf16[384,2176]{1,0:T(8,128)(2,1)S(1)} %join.6.refs_1_.refs_5_), channel_id=1, source_target_pairs={{0,2},{2,0},{4,6},{6,4},{8,10},{10,8},{12,14},{14,12},{1,3},{3,1},... | collective-permute-start | bytes 5013512 | tf_op jit(solution)/shard_map/rows_cores/ppermute | solution.py:418
  42.6 12.7 %collective-permute-start.10 = (bf16[128,2048]{1,0:T(8,128)(2,1)S(1)}, bf16[128,2048]{1,0:T(8,128)(2,1)S(1)}, u32[]{:S(2)}, u32[]{:S(2)}) collective-permute-start(bf16[128,2048]{1,0:T(8,128)(2,1)S(1)} %get-tuple-element.205.refs_0_), channel_id=1, source_target_pairs={{0,2},{2,0},{4,6},{6,4},{8,10},{10,8},{12,14},{14,12},{1,3},{3,1},... | collective-permute-start | bytes 1572872 | tf_op jit(solution)/shard_map/grads_cores/ppermute | solution.py:418
  43.1 11.9 %collective-permute-start.9 = (bf16[64,2048]{1,0:T(8,128)(2,1)S(1)}, bf16[64,2048]{1,0:T(8,128)(2,1)S(1)}, u32[]{:S(2)}, u32[]{:S(2)}) collective-permute-start(bf16[64,2048]{1,0:T(8,128)(2,1)S(1)} %collective-permute-done.7.refs_1_), channel_id=1, source_target_pairs={{0,4},{2,6},{4,0},{6,2},{8,12},{10,14},{12,8},{14,10},{1,5},{3,7},... | collective-permute-start | bytes 786440 | tf_op jit(solution)/shard_map/grads_line/ppermute | solution.py:414
  43.1 16.8 %collective-permute-start.12 = (bf16[128,2048]{1,0:T(8,128)(2,1)S(1)}, bf16[128,2048]{1,0:T(8,128)(2,1)S(1)}, u32[]{:S(2)}, u32[]{:S(2)}) collective-permute-start(bf16[128,2048]{1,0:T(8,128)(2,1)S(1)} %join.5.refs_0_), channel_id=1, source_target_pairs={{0,1},{1,0},{2,3},{3,2},{4,5},{5,4},{6,7},{7,6},{8,9},{9,8},{10,11... | collective-permute-start | bytes 1572872 | tf_op jit(solution)/shard_map/grads_across/ppermute | solution.py:422
  55.0 8.4 %collective-permute-start.13 = (bf16[64,2048]{1,0:T(8,128)(2,1)S(1)}, bf16[64,2048]{1,0:T(8,128)(2,1)S(1)}, u32[]{:S(2)}, u32[]{:S(2)}) collective-permute-start(bf16[64,2048]{1,0:T(8,128)(2,1)S(1)} %collective-permute-done.9.refs_2_), channel_id=1, source_target_pairs={{0,1},{1,0},{2,3},{3,2},{4,5},{5,4},{6,7},{7,6},{8,9},{9,8},{10,11... | collective-permute-start | bytes 786440 | tf_op jit(solution)/shard_map/grads_across/ppermute | solution.py:422
  59.8 4.2 %collective-permute-start.11 = (bf16[2,512,1024]{2,1,0:T(8,128)(2,1)S(1)}, bf16[2,512,1024]{2,1,0:T(8,128)(2,1)S(1)}, u32[]{:S(2)}, u32[]{:S(2)}) collective-permute-start(bf16[2,512,1024]{2,1,0:T(8,128)(2,1)S(1)} %get-tuple-element.163), channel_id=1, source_target_pairs={{0,2},{2,0},{4,6},{6,4},{8,10},{10,8},{12,14},{14,12},{1,3},{3,1},... | collective-permute-start | bytes 6291464 | tf_op jit(solution)/shard_map/out_cores/ppermute | solution.py:418
  64.2 3.5 %collective-permute-start.15 = (bf16[384,2048]{1,0:T(8,128)(2,1)S(1)}, bf16[384,2048]{1,0:T(8,128)(2,1)S(1)}, u32[]{:S(2)}, u32[]{:S(2)}) collective-permute-start(bf16[384,2048]{1,0:T(8,128)(2,1)S(1)} %join.7.refs_1_), channel_id=1, source_target_pairs={{0,2},{2,0},{4,6},{6,4},{8,10},{10,8},{12,14},{14,12},{1,3},{3,1},... | collective-permute-start | bytes 4718600 | tf_op jit(solution)/shard_map/grads_cores/ppermute | solution.py:418
  64.4 25.5 %collective-permute-start.14 = (bf16[512,1024]{1,0:T(8,128)(2,1)S(1)}, bf16[512,1024]{1,0:T(8,128)(2,1)S(1)}, u32[]{:S(2)}, u32[]{:S(2)}) collective-permute-start(bf16[512,1024]{1,0:T(8,128)(2,1)S(1)} %out_send.1), channel_id=1, source_target_pairs={{0,1},{1,0},{2,3},{3,2},{4,5},{5,4},{6,7},{7,6},{8,9},{9,8},{10,11... | collective-permute-start | bytes 3145736 | tf_op jit(solution)/shard_map/out_across/ppermute | solution.py:422
  89.9 4.5 %collective-permute-start.17 = (bf16[2,512,1152]{2,1,0:T(8,128)(2,1)S(1)}, bf16[2,512,1152]{2,1,0:T(8,128)(2,1)S(1)}, u32[]{:S(2)}, u32[]{:S(2)}) collective-permute-start(bf16[2,512,1152]{2,1,0:T(8,128)(2,1)S(1)} %get-tuple-element.190), channel_id=1, source_target_pairs={{0,2},{2,0},{4,6},{6,4},{8,10},{10,8},{12,14},{14,12},{1,3},{3,1},... | collective-permute-start | bytes 7077896 | tf_op jit(solution)/shard_map/in_cores/ppermute | solution.py:418
  90.3 22.2 %collective-permute-start.16 = (bf16[256,1024]{1,0:T(8,128)(2,1)S(1)}, bf16[256,1024]{1,0:T(8,128)(2,1)S(1)}, u32[]{:S(2)}, u32[]{:S(2)}) collective-permute-start(bf16[256,1024]{1,0:T(8,128)(2,1)S(1)} %get-tuple-element.195), channel_id=1, source_target_pairs={{0,4},{2,6},{4,0},{6,2},{8,12},{10,14},{12,8},{14,10},{1,5},{3,7},... | collective-permute-start | bytes 1572872 | tf_op jit(solution)/shard_map/out_line/ppermute | solution.py:414
  94.6 9.1 %collective-permute-start.18 = (bf16[128,1152]{1,0:T(8,128)(2,1)S(1)}, bf16[128,1152]{1,0:T(8,128)(2,1)S(1)}, u32[]{:S(2)}, u32[]{:S(2)}) collective-permute-start(bf16[128,1152]{1,0:T(8,128)(2,1)S(1)} %get-tuple-element.201), channel_id=1, source_target_pairs={{0,1},{1,0},{2,3},{3,2},{4,5},{5,4},{6,7},{7,6},{8,9},{9,8},{10,11... | collective-permute-start | bytes 884744 | tf_op jit(solution)/shard_map/in_across/ppermute | solution.py:422
  103.8 11.8 %collective-permute-start.21 = (bf16[128,1152]{1,0:T(8,128)(2,1)S(1)}, bf16[128,1152]{1,0:T(8,128)(2,1)S(1)}, u32[]{:S(2)}, u32[]{:S(2)}) collective-permute-start(bf16[128,1152]{1,0:T(8,128)(2,1)S(1)} %in_slot.3), channel_id=1, source_target_pairs={{0,4},{2,6},{4,0},{6,2},{8,12},{10,14},{12,8},{14,10},{1,5},{3,7},... | collective-permute-start | bytes 884744 | tf_op jit(solution)/shard_map/in_line/ppermute | solution.py:414
  104.6 11.0 %collective-permute-start.20 = (bf16[128,1152]{1,0:T(8,128)(2,1)S(1)}, bf16[128,1152]{1,0:T(8,128)(2,1)S(1)}, u32[]{:S(2)}, u32[]{:S(2)}) collective-permute-start(bf16[128,1152]{1,0:T(8,128)(2,1)S(1)} %get-tuple-element.220), channel_id=1, source_target_pairs={{0,1},{1,0},{2,3},{3,2},{4,5},{5,4},{6,7},{7,6},{8,9},{9,8},{10,11... | collective-permute-start | bytes 884744 | tf_op jit(solution)/shard_map/in_across/ppermute | solution.py:422
  112.5 21.5 %collective-permute-start.19 = (bf16[128,1024]{1,0:T(8,128)(2,1)S(1)}, bf16[128,1024]{1,0:T(8,128)(2,1)S(1)}, u32[]{:S(2)}, u32[]{:S(2)}) collective-permute-start(bf16[128,1024]{1,0:T(8,128)(2,1)S(1)} %add_last.1), channel_id=1, source_target_pairs={{0,8},{2,10},{4,12},{6,14},{8,0},{10,2},{12,4},{14,6},{1,9},{3,11}... | collective-permute-start | bytes 786440 | tf_op jit(solution)/shard_map/out_line/ppermute | solution.py:414
  115.8 23.4 %collective-permute-start.23 = (bf16[128,1152]{1,0:T(8,128)(2,1)S(1)}, bf16[128,1152]{1,0:T(8,128)(2,1)S(1)}, u32[]{:S(2)}, u32[]{:S(2)}) collective-permute-start(bf16[128,1152]{1,0:T(8,128)(2,1)S(1)} %in_slot.4), channel_id=1, source_target_pairs={{0,8},{2,10},{4,12},{6,14},{8,0},{10,2},{12,4},{14,6},{1,9},{3,11}... | collective-permute-start | bytes 884744 | tf_op jit(solution)/shard_map/in_line/ppermute | solution.py:414
  115.9 7.6 %collective-permute-start.22 = (bf16[128,1152]{1,0:T(8,128)(2,1)S(1)}, bf16[128,1152]{1,0:T(8,128)(2,1)S(1)}, u32[]{:S(2)}, u32[]{:S(2)}) collective-permute-start(bf16[128,1152]{1,0:T(8,128)(2,1)S(1)} %get-tuple-element.225), channel_id=1, source_target_pairs={{0,1},{1,0},{2,3},{3,2},{4,5},{5,4},{6,7},{7,6},{8,9},{9,8},{10,11... | collective-permute-start | bytes 884744 | tf_op jit(solution)/shard_map/in_across/ppermute | solution.py:422
  123.6 15.6 %collective-permute-start.25 = (bf16[128,1152]{1,0:T(8,128)(2,1)S(1)}, bf16[128,1152]{1,0:T(8,128)(2,1)S(1)}, u32[]{:S(2)}, u32[]{:S(2)}) collective-permute-start(bf16[128,1152]{1,0:T(8,128)(2,1)S(1)} %get-tuple-element.238), channel_id=1, source_target_pairs={{0,1},{1,0},{2,3},{3,2},{4,5},{5,4},{6,7},{7,6},{8,9},{9,8},{10,11... | collective-permute-start | bytes 884744 | tf_op jit(solution)/shard_map/in_across/ppermute | solution.py:422
  124.7 17.7 %collective-permute-start.24 = (bf16[128,1152]{1,0:T(8,128)(2,1)S(1)}, bf16[128,1152]{1,0:T(8,128)(2,1)S(1)}, u32[]{:S(2)}, u32[]{:S(2)}) collective-permute-start(bf16[128,1152]{1,0:T(8,128)(2,1)S(1)} %in_slot.5), channel_id=1, source_target_pairs={{0,4},{2,6},{4,0},{6,2},{8,12},{10,14},{12,8},{14,10},{1,5},{3,7},... | collective-permute-start | bytes 884744 | tf_op jit(solution)/shard_map/in_line/ppermute | solution.py:414
  134.9 7.5 %copy-start.1 = (s32[128,4]{0,1:T(4,128)S(1)}, s32[128,4]{0,1:T(4,128)}, u32[]{:S(2)}) copy-start(s32[128,4]{0,1:T(4,128)} %param.9) | copy-start | bytes 6148
  134.9 7.5 %copy-start.2 = (f32[128,4]{0,1:T(4,128)S(1)}, f32[128,4]{0,1:T(4,128)}, u32[]{:S(2)}) copy-start(f32[128,4]{0,1:T(4,128)} %param.11) | copy-start | bytes 6148
  134.9 7.5 %copy-start.3 = (s32[128]{0:T(128)S(1)}, s32[128]{0:T(128)}, u32[]{:S(2)}) copy-start(s32[128]{0:T(128)} %param.10) | copy-start | bytes 1540

commit v8 on v7

--- a/solution.py
+++ b/solution.py
@@ -221,27 +221,28 @@
     )
 
 
-def outputs_kernel(tile, gated, down_mat, own, other):
+def outputs_kernel(tile, gated, down_mat, own, *other):
     half = own.shape[2]
-    for which in range(2):
-        stays = (lax.axis_index("helper") == which).astype(jnp.int32)
+    for keep in range(2):
+        side = lax.axis_index("helper")
+        side = side if keep else 1 - side
         for start in range(0, half, tile):
             columns = slice(start, start + tile)
-            first = which * half + start
-            out = product(gated[...], down_mat[:, first : first + tile]).astype(jnp.bfloat16)
-            own[stays, :, columns] = half_at(out, 0)
-            other[stays, :, columns] = half_at(out, 1)
+            here = pl.ds(pl.multiple_of(side * half + start, tile), tile)
+            out = product(gated[...], down_mat[:, here]).astype(jnp.bfloat16)
+            own[keep, :, columns] = half_at(out, 0)
+            other[keep][:, columns] = half_at(out, 1)
 
 
 def outputs_of(gated, down_mat):
     total, hidden = gated.shape
     width = down_mat.shape[1]
-    sums = jax.ShapeDtypeStruct((2, total // 2, width // 2), jnp.bfloat16)
+    sums = lambda *rows: jax.ShapeDtypeStruct((*rows, width // 2), jnp.bfloat16)
     return call(
         functools.partial(outputs_kernel, 256),
         "outputs",
         (gated, down_mat),
-        (sums, sums),
+        (sums(2, total // 2), *(sums(total // 2),) * 2),
         flops=2 * total * width * hidden,
     )
 
@@ -285,33 +286,34 @@
     )
 
 
-def input_grads_kernel(tile, d_gate, d_up, shares, gate_mat, up_mat, own, other):
+def input_grads_kernel(tile, d_gate, d_up, shares, gate_mat, up_mat, own, *other):
     half = own.shape[2] - LANES
-    for which in range(2):
-        own[which, :, half:] = half_at(shares, 0)
-        other[which, :, half:] = half_at(shares, 1)
-    for which in range(2):
-        stays = (lax.axis_index("helper") == which).astype(jnp.int32)
+
+    def put(keep, columns, values):
+        own[keep, :, columns] = half_at(values, 0)
+        for i in range(2):
+            other[2 * keep + i][:, columns] = half_at(half_at(values, 1), i)
+
+    for keep in range(2):
+        put(keep, slice(half, half + LANES), shares[...])
+        side = lax.axis_index("helper")
+        side = side if keep else 1 - side
         for start in range(0, half, tile):
-            columns = slice(start, start + tile)
-            first = which * half + start
-            back = right_transposed(d_gate[...], gate_mat[first : first + tile, :])
-            back = back + right_transposed(d_up[...], up_mat[first : first + tile, :])
-            back = back.astype(jnp.bfloat16)
-            own[stays, :, columns] = half_at(back, 0)
-            other[stays, :, columns] = half_at(back, 1)
+            here = pl.ds(pl.multiple_of(side * half + start, tile), tile)
+            back = right_transposed(d_gate[...], gate_mat[here, :])
+            back = back + right_transposed(d_up[...], up_mat[here, :])
+            put(keep, slice(start, start + tile), back.astype(jnp.bfloat16))
 
 
 def input_grads_of(d_gate, d_up, shares, gate_mat, up_mat):
     width, hidden = gate_mat.shape
     total = d_gate.shape[0]
-    sums = jax.ShapeDtypeStruct((2, total // 2, width // 2 + LANES), jnp.bfloat16)
+    sums = lambda *rows: jax.ShapeDtypeStruct((*rows, width // 2 + LANES), jnp.bfloat16)
     return call(
         functools.partial(input_grads_kernel, 256),
         "input_grads",
         (d_gate, d_up, shares, gate_mat, up_mat),
-        (sums, sums),
-        flops=0,
+        (sums(2, total // 2), *(sums(total // 4),) * 4),
         mebibytes=12,
     )
 
@@ -338,19 +340,20 @@
     )
 
 
-def send_kernel(own, received, *sent):
+def send_kernel(first, own, received, *sent):
     rows = sent[0].shape[0]
     for i, target in enumerate(sent):
-        here = slice(i * rows, (i + 1) * rows)
-        target[...] = own[0, here, :] + received[0, here, :]
-
-
-def slot_sum(own, received, arrived, slot, offset):
+        here = slice(first + i * rows, first + (i + 1) * rows)
+        target[...] = own[0, here, :] + received[i * rows : (i + 1) * rows, :]
+
+
+def slot_sum(own, received, arrived, slot, offset, received_slot):
     rows = LANES
     half = rows // 2
     here = slice(slot * rows, (slot + 1) * rows)
     other = arrived[offset : offset + rows, :].astype(jnp.float32)
-    kept = own[1, here, :].astype(jnp.float32) + received[1, here, :].astype(jnp.float32)
+    there = slice(received_slot * rows, (received_slot + 1) * rows)
+    kept = own[1, here, :].astype(jnp.float32) + received[there, :].astype(jnp.float32)
     return kept + jnp.concatenate([other[half:], other[:half]], axis=0)
 
 
@@ -358,7 +361,7 @@
     rows = own_slot.shape[0]
     targets = (own_slot, near_and_last.at[:rows], far_slot, near_and_last.at[rows:])
     for slot, target in enumerate(targets):
-        target[...] = slot_sum(own, received, arrived, slot, slot * rows).astype(target.dtype)
+        target[...] = slot_sum(own, received, arrived, slot, slot * rows, slot).astype(target.dtype)
 
 
 def add_last_kernel(far_slot, arrived, total):
@@ -367,7 +370,7 @@
 
 
 def slot_kernel(slot, own, received, arrived, *refs):
-    whole = slot_sum(own, received, arrived, slot, 0)
+    whole = slot_sum(own, received, arrived, slot, 0, slot % 2)
     if len(refs) > 1:
         whole = whole + refs[0][...].astype(jnp.float32)
     refs[-1][...] = whole.astype(refs[-1].dtype)
@@ -383,7 +386,7 @@
 def finish_inputs_kernel(experts, ids, counts, scores, clock, own, received, arrived, *refs):
     columns, d_scores = refs[-2:]
     width = columns.shape[1]
-    whole = slot_sum(own, received, arrived, 0, 0)
+    whole = slot_sum(own, received, arrived, 0, 0, 0)
     whole = total_of([whole] + [ref[...].astype(jnp.float32) for ref in refs[:-2]])
     whole = jnp.where(lax.axis_index("helper") == 0, whole, swap_halves(whole))
     columns[...] = whole[:, :width].astype(jnp.bfloat16)
@@ -421,10 +424,15 @@
         with jax.named_scope(self.label + "_across"):
             return lax.ppermute(array, "helper", self.sides)
 
-    def send(self, own, received, parts=1):
-        _, rows, columns = own.shape
+    def send(self, first, own, received, parts):
+        rows, columns = received.shape
         part = jax.ShapeDtypeStruct((rows // parts, columns), own.dtype)
-        return call(send_kernel, self.label + "_send", (own, received), (part,) * parts)
+        return call(
+            functools.partial(send_kernel, first),
+            self.label + "_send",
+            (own, received),
+            (part,) * parts,
+        )
 
     def slots(self, own, received, arrived):
         rows, columns = arrived.shape
@@ -529,11 +537,11 @@
     )
     grads_last = hold(grads_last, gated)
     last_across = grads.across(grads_last)
-    near_out, sent = order(outputs_of, gated, down_mat, also=(grads_last, grads_sibling))
-    received = outs.sibling(sent)
+    near_out, sent, kept = order(outputs_of, gated, down_mat, also=(grads_last, grads_sibling))
+    received, kept = outs.sibling(sent), outs.sibling(kept)
     clock = order(space, clock, also=(grads_across, last_across))
     received = hold(received, clock)
-    (sent,) = order(outs.send, near_out, received)
+    (sent,) = order(lambda *s: outs.send(0, *s, 1), near_out, received)
     arrived = outs.across(sent)
     rest = order(join, grads_line, grads_across, grads_last, last_across)
     all_grads = [grads_pair, rest, grads_sibling, grads.sibling(rest)]
@@ -544,34 +552,34 @@
         pre_gate,
         pre_up,
     )
-    in_own, sent = order(
+    in_own, near_sent, far_sent, near_kept, far_kept = order(
         lambda *d: input_grads_of(*d, gate_mat, up_mat), d_gate, d_up, shares
     )
-    in_received = ins.sibling(sent)
-    arrived = hold(arrived, in_own)
-    own_slot, near_slots, far_slot = order(outs.slots, near_out, received, arrived)
-    clock = order(space, clock)
-    in_received = hold(in_received, clock)
-    sent = order(lambda *s: ins.send(*s, parts=4), in_own, in_received)
-    own_sent, near_sent, far_sent, last_sent = sent
+    far_received, far_kept = ins.sibling(far_sent), ins.sibling(far_kept)
+    near_received, near_kept = ins.sibling(near_sent), ins.sibling(near_kept)
+    first = 2 * tokens.shape[0]
+    far_sent, last_sent = order(lambda *s: ins.send(first, *s, 2), in_own, far_received)
     last_arrived = ins.across(last_sent)
-    near_sums = outs.line(near_slots, outs.near)
     grad_down = order(product_of("grad_down", True), all_grads, gated)
-    slot = order(lambda *s: ins.slot(3, *s), in_own, in_received, last_arrived)
+    slot = order(lambda *s: ins.slot(3, *s), in_own, far_kept, last_arrived)
     last_sum = ins.line(slot, ins.near)
     far_arrived = ins.across(hold(far_sent, slot))
-    grad_gate = order(product_of("grad_gate", False), all_rows, d_gate)
+    arrived = hold(arrived, slot)
+    own_slot, near_slots, far_slot = order(outs.slots, near_out, kept, arrived)
+    near_sums = outs.line(near_slots, outs.near)
+    own_sent, near_sent = order(lambda *s: ins.send(0, *s, 2), in_own, near_received)
     far_slot = order(
         lambda *s: call(add_last_kernel, "add_last", s, jax.ShapeDtypeStruct(s[0].shape, s[0].dtype)),
         far_slot,
         near_sums,
     )
     far_sum = outs.line(far_slot, outs.far)
-    slot = order(lambda *s: ins.slot(2, *s), in_own, in_received, far_arrived, last_sum)
+    grad_gate = order(product_of("grad_gate", False), all_rows, d_gate)
+    slot = order(lambda *s: ins.slot(2, *s), in_own, far_kept, far_arrived, last_sum)
     far = ins.line(slot, ins.far)
     near_arrived = ins.across(hold(near_sent, slot))
     grad_up = order(product_of("grad_up", False), all_rows, d_up)
-    slot = order(lambda *s: ins.slot(1, *s), in_own, in_received, near_arrived)
+    slot = order(lambda *s: ins.slot(1, *s), in_own, near_kept, near_arrived)
     near = ins.line(slot, ins.near)
     own_arrived = ins.across(hold(own_sent, slot))
     columns = jax.ShapeDtypeStruct((tokens.shape[0], width // 2), jnp.bfloat16)
@@ -591,7 +599,7 @@
             (columns, jax.ShapeDtypeStruct(picks[2].shape, jnp.float32)),
         ),
         in_own,
-        in_received,
+        near_kept,
         own_arrived,
         far,
         near,

time: 144 us -> 144 us (level)
    ppermute x11, waiting for transfers between devices: 37 us -> 44.4 us  [line(): return lax.ppermute(array, 'expert', pairs)]
    ppermute x9, waiting for transfers between devices: 12 us -> 7.6 us  [across(): return lax.ppermute(array, 'helper', self.sides)]
    ppermute x6 -> x10, waiting for transfers between devices: 7.87 us -> 5.78 us  [sibling(): return lax.ppermute(array, 'expert', self.cores)]
    ppermute x9, starting transfers between devices: 11.6 us -> 9.83 us  [across(): return lax.ppermute(array, 'helper', self.sides)]
    pallas_call x21 -> x22, Pallas kernels: 51 us -> 51 us  [call(): pl.pallas_call(kernel, out_shape=out_shape, in_specs=[VMEM] * len(operand...]
  transfers between devices with their start and end apart: 26 -> 30, of which waited for: 15 -> 14; matrix products, arithmetic and copies ran while one was open for 0% -> 0% of each run, Pallas kernels for 38% -> 38%
where the time goes in v8:
time: 144 us
  waiting for transfers between devices  57.8 us (40%)
  Pallas kernels  57 us (40%)
  starting transfers between devices  28.2 us (20%)
    pallas_call x22, Pallas kernels, call(): pl.pallas_call(kernel, out_shape=out_shape, in_specs=[VMEM] * len(operand...  51 us
    ppermute x11, waiting for transfers between devices, line(): return lax.ppermute(array, 'expert', pairs)  44.4 us
    ppermute x11, starting transfers between devices, line(): return lax.ppermute(array, 'expert', pairs)  16 us
    ppermute x9, starting transfers between devices, across(): return lax.ppermute(array, 'helper', self.sides)  9.83 us
    ppermute x9, waiting for transfers between devices, across(): return lax.ppermute(array, 'helper', self.sides)  7.6 us
    ppermute x10, waiting for transfers between devices, sibling(): return lax.ppermute(array, 'expert', self.cores)  5.78 us
    pallas_call x1, Pallas kernels, load(): pl.pallas_call(load_kernel, out_shape=tuple((jax.ShapeDtypeStruct(mat.sha...  4.73 us
  transfers between devices with their start and end apart: 30, of which 14 were waited for; matrix products, arithmetic and copies ran while one was open for 0% of the time, Pallas kernels for 38%

profile of v8, /device:TPU:0, one launch (start us, length us, event | category | flops | bytes accessed | tf_op | source)
XLA Modules:
  0.0 144.0 jit_solution(16316911110910842860)
XLA Ops:
  0.6 1.3 prepare_rows.1
  1.9 0.5 collective-permute-start.2
  2.5 3.7 %collective-permute-start.1 = (bf16[64,2176]{1,0:T(8,128)(2,1)S(1)}, bf16[64,2176]{1,0:T(8,128)(2,1)S(1)}, u32[]{:S(2)}, u32[]{:S(2)}) collective-permute-start(bf16[64,2176]{1,0:T(8,128)(2,1)S(1)} %get-tuple-element.132), channel_id=1, source_target_pairs={{0,8},{2,10},{4,12},{6,14},{8,0},{10,2},{12,4},{14,6},{1,9},{3,11}... | collective-permute-start | bytes 835592 | tf_op jit(solution)/shard_map/rows_line/ppermute | solution.py:417
  6.1 1.6 %collective-permute-start = (bf16[64,2176]{1,0:T(8,128)(2,1)S(1)}, bf16[64,2176]{1,0:T(8,128)(2,1)S(1)}, u32[]{:S(2)}, u32[]{:S(2)}) collective-permute-start(bf16[64,2176]{1,0:T(8,128)(2,1)S(1)} %get-tuple-element.132), channel_id=1, source_target_pairs={{0,4},{2,6},{4,0},{6,2},{8,12},{10,14},{12,8},{14,10},{1,5},{3,7},... | collective-permute-start | bytes 835592 | tf_op jit(solution)/shard_map/rows_line/ppermute | solution.py:417
  7.7 4.7 %load.1 = (bf16[2048,1024]{1,0:T(8,128)(2,1)S(1)}, bf16[2048,1024]{1,0:T(8,128)(2,1)S(1)}, bf16[1024,2048]{1,0:T(8,128)(2,1)S(1)}) custom-call(bf16[2048,1024]{1,0:T(8,128)(2,1)} %bitcast.16, bf16[2048,1024]{1,0:T(8,128)(2,1)} %bitcast.17, bf16[1024,2048]{1,0:T(8,128)(2,1)} %bitcast.18), custom_call_target="tpu_custom_call" | custom-call | tf_op jit(solution)/shard_map/load/pallas_call | solution.py:469
  12.4 7.0 %collective-permute-done.1.refs_1_ = bf16[64,2176]{1,0:T(8,128)(2,1)S(1)} collective-permute-done((bf16[64,2176]{1,0:T(8,128)(2,1)S(1)}, bf16[64,2176]{1,0:T(8,128)(2,1)S(1)}, u32[]{:S(2)}, u32[]{:S(2)}) %collective-permute-start.1) | collective-permute-done | bytes 278560 | tf_op jit(solution)/shard_map/rows_line/ppermute | solution.py:417
  19.7 1.6 %collective-permute-start.4 = (bf16[64,2176]{1,0:T(8,128)(2,1)S(1)}, bf16[64,2176]{1,0:T(8,128)(2,1)S(1)}, u32[]{:S(2)}, u32[]{:S(2)}) collective-permute-start(bf16[64,2176]{1,0:T(8,128)(2,1)S(1)} %collective-permute-done.1.refs_1_), channel_id=1, source_target_pairs={{0,4},{2,6},{4,0},{6,2},{8,12},{10,14},{12,8},{14,10},{1,5},{3,7},... | collective-permute-start | bytes 835592 | tf_op jit(solution)/shard_map/rows_line/ppermute | solution.py:417
  21.2 1.5 %collective-permute-start.3 = (bf16[128,2176]{1,0:T(8,128)(2,1)S(1)}, bf16[128,2176]{1,0:T(8,128)(2,1)S(1)}, u32[]{:S(2)}, u32[]{:S(2)}) collective-permute-start(bf16[128,2176]{1,0:T(8,128)(2,1)S(1)} %join.4.refs_0_), channel_id=1, source_target_pairs={{0,1},{1,0},{2,3},{3,2},{4,5},{5,4},{6,7},{7,6},{8,9},{9,8},{10,11... | collective-permute-start | bytes 1671176 | tf_op jit(solution)/shard_map/rows_across/ppermute | solution.py:425
  22.8 2.4 %collective-permute-start.7 = (bf16[64,2048]{1,0:T(8,128)(2,1)S(1)}, bf16[64,2048]{1,0:T(8,128)(2,1)S(1)}, u32[]{:S(2)}, u32[]{:S(2)}) collective-permute-start(bf16[64,2048]{1,0:T(8,128)(2,1)S(1)} %get-tuple-element.146), channel_id=1, source_target_pairs={{0,8},{2,10},{4,12},{6,14},{8,0},{10,2},{12,4},{14,6},{1,9},{3,11}... | collective-permute-start | bytes 786440 | tf_op jit(solution)/shard_map/grads_line/ppermute | solution.py:417
  25.2 7.1 %collective-permute-done.4.refs_2_ = bf16[64,2176]{1,0:T(8,128)(2,1)S(1)} collective-permute-done((bf16[64,2176]{1,0:T(8,128)(2,1)S(1)}, bf16[64,2176]{1,0:T(8,128)(2,1)S(1)}, u32[]{:S(2)}, u32[]{:S(2)}) %collective-permute-start.4) | collective-permute-done | bytes 278560 | tf_op jit(solution)/shard_map/rows_line/ppermute | solution.py:417
  32.3 2.4 %collective-permute-start.5 = (bf16[64,2176]{1,0:T(8,128)(2,1)S(1)}, bf16[64,2176]{1,0:T(8,128)(2,1)S(1)}, u32[]{:S(2)}, u32[]{:S(2)}) collective-permute-start(bf16[64,2176]{1,0:T(8,128)(2,1)S(1)} %collective-permute-done.4.refs_2_), channel_id=1, source_target_pairs={{0,1},{1,0},{2,3},{3,2},{4,5},{5,4},{6,7},{7,6},{8,9},{9,8},{10,11... | collective-permute-start | bytes 835592 | tf_op jit(solution)/shard_map/rows_across/ppermute | solution.py:425
  34.7 2.3 %collective-permute-done.7.refs_1_ = bf16[64,2048]{1,0:T(8,128)(2,1)S(1)} collective-permute-done((bf16[64,2048]{1,0:T(8,128)(2,1)S(1)}, bf16[64,2048]{1,0:T(8,128)(2,1)S(1)}, u32[]{:S(2)}, u32[]{:S(2)}) %collective-permute-start.7) | collective-permute-done | bytes 262176 | tf_op jit(solution)/shard_map/grads_line/ppermute | solution.py:417
  37.0 5.4 %collective-permute-done.6.refs_0_ = bf16[64,2048]{1,0:T(8,128)(2,1)S(1)} collective-permute-done((bf16[64,2048]{1,0:T(8,128)(2,1)S(1)}, bf16[64,2048]{1,0:T(8,128)(2,1)S(1)}, u32[]{:S(2)}, u32[]{:S(2)}) %collective-permute-start.6) | collective-permute-done | bytes 262176 | tf_op jit(solution)/shard_map/grads_line/ppermute | solution.py:417
  42.6 0.5 collective-permute-start.10
  43.1 0.6 collective-permute-start.13
  43.7 2.4 %collective-permute-done.8.refs_3_.refs_7_ = bf16[384,2176]{1,0:T(8,128)(2,1)S(1)} collective-permute-done((bf16[384,2176]{1,0:T(8,128)(2,1)S(1)}, bf16[384,2176]{1,0:T(8,128)(2,1)S(1)}, u32[]{:S(2)}, u32[]{:S(2)}) %collective-permute-start.8) | collective-permute-done | bytes 1671200 | tf_op jit(solution)/shard_map/rows_cores/ppermute | solution.py:421
  46.1 8.8 %hidden_units.1 = (f32[1024,1024]{1,0:T(8,128)S(1)}, f32[1024,1024]{1,0:T(8,128)S(1)}, bf16[1024,1024]{1,0:T(8,128)(2,1)S(1)}) custom-call(bf16[128,2176]{1,0:T(8,128)(2,1)S(1)} %get-tuple-element.234.refs_0_.refs_4_, bf16[384,2176]{1,0:T(8,128)(2,1)S(1)} %join.6.refs_1_.refs_5_, bf16[128,2176]{1,0:T(8,128)(2,1)S(1)} %collective-permute-done.2.refs_2_.refs_6_, ...), custom_call_target="tpu_custom_call" | custom-call | flops 8589934592 | tf_op jit(solution)/shard_map/hidden_units/pallas_call | solution.py:40
  55.0 0.3 collective-permute-start.14
  55.3 4.5 %outputs.1 = (bf16[2,512,1024]{2,1,0:T(8,128)(2,1)S(1)}, bf16[512,1024]{1,0:T(8,128)(2,1)S(1)}, bf16[512,1024]{1,0:T(8,128)(2,1)S(1)}) custom-call(bf16[1024,1024]{1,0:T(8,128)(2,1)S(1)} %get-tuple-element.206.gated.refs_4_, bf16[1024,2048]{1,0:T(8,128)(2,1)S(1)} %get-tuple-element.165.down_mat.refs_8_), custom_call_target="tpu_custom_call" | custom-call | flops 4294967296 | tf_op jit(solution)/shard_map/outputs/pallas_call | solution.py:40
  59.9 3.5 %collective-permute-done.14.refs_3_ = bf16[64,2048]{1,0:T(8,128)(2,1)S(1)} collective-permute-done((bf16[64,2048]{1,0:T(8,128)(2,1)S(1)}, bf16[64,2048]{1,0:T(8,128)(2,1)S(1)}, u32[]{:S(2)}, u32[]{:S(2)}) %collective-permute-start.14) | collective-permute-done | bytes 262176 | tf_op jit(solution)/shard_map/grads_across/ppermute | solution.py:425
  63.7 0.5 collective-permute-start.11
  64.2 0.9 collective-permute-start.15
  65.1 2.0 %collective-permute-done.16.refs_3_ = bf16[384,2048]{1,0:T(8,128)(2,1)S(1)} collective-permute-done((bf16[384,2048]{1,0:T(8,128)(2,1)S(1)}, bf16[384,2048]{1,0:T(8,128)(2,1)S(1)}, u32[]{:S(2)}, u32[]{:S(2)}) %collective-permute-start.16) | collective-permute-done | bytes 1572896 | tf_op jit(solution)/shard_map/grads_cores/ppermute | solution.py:421
  67.1 5.7 %hidden_grads.1 = (bf16[1024,1024]{1,0:T(8,128)(2,1)S(1)}, bf16[1024,1024]{1,0:T(8,128)(2,1)S(1)}, bf16[1024,128]{1,0:T(8,128)(2,1)S(1)}) custom-call(bf16[128,2048]{1,0:T(8,128)(2,1)S(1)} %get-tuple-element.202.refs_0_, bf16[384,2048]{1,0:T(8,128)(2,1)S(1)} %join.7.refs_1_, bf16[128,2048]{1,0:T(8,128)(2,1)S(1)} %collective-permute-done.10.refs_2_, ...), custom_call_target="tpu_custom_call" | custom-call | flops 4294967296 | tf_op jit(solution)/shard_map/hidden_grads/pallas_call | solution.py:40
  72.8 8.9 %input_grads.1 = (bf16[2,512,1152]{2,1,0:T(8,128)(2,1)S(1)}, bf16[256,1152]{1,0:T(8,128)(2,1)S(1)}, bf16[256,1152]{1,0:T(8,128)(2,1)S(1)}, bf16[256,1152]{1,0:T(8,128)(2,1)S(1)}, bf16[256,1152]{1,0:T(8,128)(2,1)S(1)}) custom-call(bf16[1024,1024]{1,0:T(8,128)(2,1)S(1)} %get-tuple-element.228.d_gate.refs_4_, ...), custom_call_target="tpu_custom_call" | custom-call | tf_op jit(solution)/shard_map/input_grads/pallas_call | solution.py:40
  81.6 0.2 collective-permute-start.18
  81.8 0.4 collective-permute-start.17
  82.3 1.4 collective-permute-done.18.received
  83.8 1.0 collective-permute-start.19
  84.8 6.8 %grad_down.1 = bf16[1024,2048]{1,0:T(8,128)(2,1)} custom-call(bf16[128,2048]{1,0:T(8,128)(2,1)S(1)} %get-tuple-element.202.refs_0_, bf16[384,2048]{1,0:T(8,128)(2,1)S(1)} %join.7.refs_1_, bf16[128,2048]{1,0:T(8,128)(2,1)S(1)} %collective-permute-done.10.refs_2_, bf16[384,2048]{1,0:T(8,128)(2,1)S(1)} %collective-permute-done.16.refs_3_, ...), custom_call_target="tpu_custom_call" | custom-call | flops 4294967296 | tf_op jit(solution)/shard_map/grad_down/pallas_call | solution.py:40
  91.6 4.1 %collective-permute-done.19.arrived = bf16[128,1152]{1,0:T(8,128)(2,1)S(1)} collective-permute-done((bf16[128,1152]{1,0:T(8,128)(2,1)S(1)}, bf16[128,1152]{1,0:T(8,128)(2,1)S(1)}, u32[]{:S(2)}, u32[]{:S(2)}) %collective-permute-start.19) | collective-permute-done | bytes 294944 | tf_op jit(solution)/shard_map/in_across/ppermute | solution.py:425
  95.8 0.4 out_slots.1
  96.2 1.0 collective-permute-start.20
  97.2 1.0 collective-permute-start.25
  98.3 1.0 collective-permute-start.24
  99.3 11.8 %collective-permute-done.20.arrived.near_and_last = bf16[256,1024]{1,0:T(8,128)(2,1)S(1)} collective-permute-done((bf16[256,1024]{1,0:T(8,128)(2,1)S(1)}, bf16[256,1024]{1,0:T(8,128)(2,1)S(1)}, u32[]{:S(2)}, u32[]{:S(2)}) %collective-permute-start.20) | collective-permute-done | bytes 524320 | tf_op jit(solution)/shard_map/out_line/ppermute | solution.py:417
  111.1 2.1 %collective-permute-start.22 = (bf16[128,1024]{1,0:T(8,128)(2,1)S(1)}, bf16[128,1024]{1,0:T(8,128)(2,1)S(1)}, u32[]{:S(2)}, u32[]{:S(2)}) collective-permute-start(bf16[128,1024]{1,0:T(8,128)(2,1)S(1)} %add_last.1), channel_id=1, source_target_pairs={{0,8},{2,10},{4,12},{6,14},{8,0},{10,2},{12,4},{14,6},{1,9},{3,11}... | collective-permute-start | bytes 786440 | tf_op jit(solution)/shard_map/out_line/ppermute | solution.py:417
  113.3 6.5 %grad_gate.1 = bf16[2048,1024]{1,0:T(8,128)(2,1)} custom-call(bf16[128,2176]{1,0:T(8,128)(2,1)S(1)} %get-tuple-element.234.refs_0_.refs_4_, bf16[384,2176]{1,0:T(8,128)(2,1)S(1)} %join.6.refs_1_.refs_5_, bf16[128,2176]{1,0:T(8,128)(2,1)S(1)} %collective-permute-done.2.refs_2_.refs_6_, bf16[384,2176]{1,0:T(8,128)(2,1)S(1)} %collective-permute-done.8.refs_3_.refs_7_, ...), custom_call_target="tpu_custom_call" | custom-call | flops 4294967296 | tf_op jit(solution)/shard_map/grad_gate/pallas_call | solution.py:40
  119.8 0.4 collective-permute-done.25.refs_0_
  120.3 0.6 collective-permute-start.27
  120.9 1.0 collective-permute-start.26
  121.9 6.5 %grad_up.1 = bf16[2048,1024]{1,0:T(8,128)(2,1)} custom-call(bf16[128,2176]{1,0:T(8,128)(2,1)S(1)} %get-tuple-element.234.refs_0_.refs_4_, bf16[384,2176]{1,0:T(8,128)(2,1)S(1)} %join.6.refs_1_.refs_5_, bf16[128,2176]{1,0:T(8,128)(2,1)S(1)} %collective-permute-done.2.refs_2_.refs_6_, bf16[384,2176]{1,0:T(8,128)(2,1)S(1)} %collective-permute-done.8.refs_3_.refs_7_, ...), custom_call_target="tpu_custom_call" | custom-call | flops 4294967296 | tf_op jit(solution)/shard_map/grad_up/pallas_call | solution.py:40
  128.6 1.1 collective-permute-start.29
  129.7 2.0 %collective-permute-start.28 = (bf16[128,1152]{1,0:T(8,128)(2,1)S(1)}, bf16[128,1152]{1,0:T(8,128)(2,1)S(1)}, u32[]{:S(2)}, u32[]{:S(2)}) collective-permute-start(bf16[128,1152]{1,0:T(8,128)(2,1)S(1)} %in_slot.5), channel_id=1, source_target_pairs={{0,4},{2,6},{4,0},{6,2},{8,12},{10,14},{12,8},{14,10},{1,5},{3,7},... | collective-permute-start | bytes 884744 | tf_op jit(solution)/shard_map/in_line/ppermute | solution.py:417
  131.7 0.8 finish_outputs.1
  132.5 4.2 %collective-permute-done.27.refs_0_ = bf16[128,1152]{1,0:T(8,128)(2,1)S(1)} collective-permute-done((bf16[128,1152]{1,0:T(8,128)(2,1)S(1)}, bf16[128,1152]{1,0:T(8,128)(2,1)S(1)}, u32[]{:S(2)}, u32[]{:S(2)}) %collective-permute-start.27) | collective-permute-done | bytes 294944 | tf_op jit(solution)/shard_map/in_line/ppermute | solution.py:417
  136.7 6.2 %collective-permute-done.28.refs_1_ = bf16[128,1152]{1,0:T(8,128)(2,1)S(1)} collective-permute-done((bf16[128,1152]{1,0:T(8,128)(2,1)S(1)}, bf16[128,1152]{1,0:T(8,128)(2,1)S(1)}, u32[]{:S(2)}, u32[]{:S(2)}) %collective-permute-start.28) | collective-permute-done | bytes 294944 | tf_op jit(solution)/shard_map/in_line/ppermute | solution.py:417
  142.9 1.1 finish_inputs.1
  (47 shorter events, 1.6 us)
Async XLA Ops:
  1.9 10.5 %collective-permute-start.2 = (bf16[128,2176]{1,0:T(8,128)(2,1)S(1)}, bf16[128,2176]{1,0:T(8,128)(2,1)S(1)}, u32[]{:S(2)}, u32[]{:S(2)}) collective-permute-start(bf16[128,2176]{1,0:T(8,128)(2,1)S(1)} %get-tuple-element.234.refs_0_.refs_4_), channel_id=1, source_target_pairs={{0,2},{2,0},{4,6},{6,4},{8,10},{10,8},{12,14},{14,12},{1,3},{3,1},... | collective-permute-start | bytes 1671176 | tf_op jit(solution)/shard_map/rows_cores/ppermute | solution.py:421
  2.5 17.0 %collective-permute-start.1 = (bf16[64,2176]{1,0:T(8,128)(2,1)S(1)}, bf16[64,2176]{1,0:T(8,128)(2,1)S(1)}, u32[]{:S(2)}, u32[]{:S(2)}) collective-permute-start(bf16[64,2176]{1,0:T(8,128)(2,1)S(1)} %get-tuple-element.132), channel_id=1, source_target_pairs={{0,8},{2,10},{4,12},{6,14},{8,0},{10,2},{12,4},{14,6},{1,9},{3,11}... | collective-permute-start | bytes 835592 | tf_op jit(solution)/shard_map/rows_line/ppermute | solution.py:417
  6.1 13.5 %collective-permute-start = (bf16[64,2176]{1,0:T(8,128)(2,1)S(1)}, bf16[64,2176]{1,0:T(8,128)(2,1)S(1)}, u32[]{:S(2)}, u32[]{:S(2)}) collective-permute-start(bf16[64,2176]{1,0:T(8,128)(2,1)S(1)} %get-tuple-element.132), channel_id=1, source_target_pairs={{0,4},{2,6},{4,0},{6,2},{8,12},{10,14},{12,8},{14,10},{1,5},{3,7},... | collective-permute-start | bytes 835592 | tf_op jit(solution)/shard_map/rows_line/ppermute | solution.py:417
  7.7 15.1 %copy-start = (bf16[128,2048]{1,0:T(8,128)(2,1)S(1)}, bf16[128,2048]{1,0:T(8,128)(2,1)}, u32[]{:S(2)}) copy-start(bf16[128,2048]{1,0:T(8,128)(2,1)} %rows) | copy-start | bytes 1572868
  19.7 12.6 %collective-permute-start.4 = (bf16[64,2176]{1,0:T(8,128)(2,1)S(1)}, bf16[64,2176]{1,0:T(8,128)(2,1)S(1)}, u32[]{:S(2)}, u32[]{:S(2)}) collective-permute-start(bf16[64,2176]{1,0:T(8,128)(2,1)S(1)} %collective-permute-done.1.refs_1_), channel_id=1, source_target_pairs={{0,4},{2,6},{4,0},{6,2},{8,12},{10,14},{12,8},{14,10},{1,5},{3,7},... | collective-permute-start | bytes 835592 | tf_op jit(solution)/shard_map/rows_line/ppermute | solution.py:417
  21.2 21.2 %collective-permute-start.3 = (bf16[128,2176]{1,0:T(8,128)(2,1)S(1)}, bf16[128,2176]{1,0:T(8,128)(2,1)S(1)}, u32[]{:S(2)}, u32[]{:S(2)}) collective-permute-start(bf16[128,2176]{1,0:T(8,128)(2,1)S(1)} %join.4.refs_0_), channel_id=1, source_target_pairs={{0,1},{1,0},{2,3},{3,2},{4,5},{5,4},{6,7},{7,6},{8,9},{9,8},{10,11... | collective-permute-start | bytes 1671176 | tf_op jit(solution)/shard_map/rows_across/ppermute | solution.py:425
  22.8 14.1 %collective-permute-start.7 = (bf16[64,2048]{1,0:T(8,128)(2,1)S(1)}, bf16[64,2048]{1,0:T(8,128)(2,1)S(1)}, u32[]{:S(2)}, u32[]{:S(2)}) collective-permute-start(bf16[64,2048]{1,0:T(8,128)(2,1)S(1)} %get-tuple-element.146), channel_id=1, source_target_pairs={{0,8},{2,10},{4,12},{6,14},{8,0},{10,2},{12,4},{14,6},{1,9},{3,11}... | collective-permute-start | bytes 786440 | tf_op jit(solution)/shard_map/grads_line/ppermute | solution.py:417
  32.3 10.1 %collective-permute-start.5 = (bf16[64,2176]{1,0:T(8,128)(2,1)S(1)}, bf16[64,2176]{1,0:T(8,128)(2,1)S(1)}, u32[]{:S(2)}, u32[]{:S(2)}) collective-permute-start(bf16[64,2176]{1,0:T(8,128)(2,1)S(1)} %collective-permute-done.4.refs_2_), channel_id=1, source_target_pairs={{0,1},{1,0},{2,3},{3,2},{4,5},{5,4},{6,7},{7,6},{8,9},{9,8},{10,11... | collective-permute-start | bytes 835592 | tf_op jit(solution)/shard_map/rows_across/ppermute | solution.py:425
  34.7 7.7 %collective-permute-start.6 = (bf16[64,2048]{1,0:T(8,128)(2,1)S(1)}, bf16[64,2048]{1,0:T(8,128)(2,1)S(1)}, u32[]{:S(2)}, u32[]{:S(2)}) collective-permute-start(bf16[64,2048]{1,0:T(8,128)(2,1)S(1)} %get-tuple-element.146), channel_id=1, source_target_pairs={{0,4},{2,6},{4,0},{6,2},{8,12},{10,14},{12,8},{14,10},{1,5},{3,7},... | collective-permute-start | bytes 786440 | tf_op jit(solution)/shard_map/grads_line/ppermute | solution.py:417
  42.5 3.6 %collective-permute-start.8 = (bf16[384,2176]{1,0:T(8,128)(2,1)S(1)}, bf16[384,2176]{1,0:T(8,128)(2,1)S(1)}, u32[]{:S(2)}, u32[]{:S(2)}) collective-permute-start(bf16[384,2176]{1,0:T(8,128)(2,1)S(1)} %join.6.refs_1_.refs_5_), channel_id=1, source_target_pairs={{0,2},{2,0},{4,6},{6,4},{8,10},{10,8},{12,14},{14,12},{1,3},{3,1},... | collective-permute-start | bytes 5013512 | tf_op jit(solution)/shard_map/rows_cores/ppermute | solution.py:421
  42.6 12.7 %collective-permute-start.10 = (bf16[128,2048]{1,0:T(8,128)(2,1)S(1)}, bf16[128,2048]{1,0:T(8,128)(2,1)S(1)}, u32[]{:S(2)}, u32[]{:S(2)}) collective-permute-start(bf16[128,2048]{1,0:T(8,128)(2,1)S(1)} %get-tuple-element.202.refs_0_), channel_id=1, source_target_pairs={{0,2},{2,0},{4,6},{6,4},{8,10},{10,8},{12,14},{14,12},{1,3},{3,1},... | collective-permute-start | bytes 1572872 | tf_op jit(solution)/shard_map/grads_cores/ppermute | solution.py:421
  43.1 11.9 %collective-permute-start.9 = (bf16[64,2048]{1,0:T(8,128)(2,1)S(1)}, bf16[64,2048]{1,0:T(8,128)(2,1)S(1)}, u32[]{:S(2)}, u32[]{:S(2)}) collective-permute-start(bf16[64,2048]{1,0:T(8,128)(2,1)S(1)} %collective-permute-done.7.refs_1_), channel_id=1, source_target_pairs={{0,4},{2,6},{4,0},{6,2},{8,12},{10,14},{12,8},{14,10},{1,5},{3,7},... | collective-permute-start | bytes 786440 | tf_op jit(solution)/shard_map/grads_line/ppermute | solution.py:417
  43.1 16.8 %collective-permute-start.13 = (bf16[128,2048]{1,0:T(8,128)(2,1)S(1)}, bf16[128,2048]{1,0:T(8,128)(2,1)S(1)}, u32[]{:S(2)}, u32[]{:S(2)}) collective-permute-start(bf16[128,2048]{1,0:T(8,128)(2,1)S(1)} %join.5.refs_0_), channel_id=1, source_target_pairs={{0,1},{1,0},{2,3},{3,2},{4,5},{5,4},{6,7},{7,6},{8,9},{9,8},{10,11... | collective-permute-start | bytes 1572872 | tf_op jit(solution)/shard_map/grads_across/ppermute | solution.py:425
  55.0 8.4 %collective-permute-start.14 = (bf16[64,2048]{1,0:T(8,128)(2,1)S(1)}, bf16[64,2048]{1,0:T(8,128)(2,1)S(1)}, u32[]{:S(2)}, u32[]{:S(2)}) collective-permute-start(bf16[64,2048]{1,0:T(8,128)(2,1)S(1)} %collective-permute-done.9.refs_2_), channel_id=1, source_target_pairs={{0,1},{1,0},{2,3},{3,2},{4,5},{5,4},{6,7},{7,6},{8,9},{9,8},{10,11... | collective-permute-start | bytes 786440 | tf_op jit(solution)/shard_map/grads_across/ppermute | solution.py:425
  59.8 3.6 %collective-permute-start.12 = (bf16[512,1024]{1,0:T(8,128)(2,1)S(1)}, bf16[512,1024]{1,0:T(8,128)(2,1)S(1)}, u32[]{:S(2)}, u32[]{:S(2)}) collective-permute-start(bf16[512,1024]{1,0:T(8,128)(2,1)S(1)} %get-tuple-element.168), channel_id=1, source_target_pairs={{0,2},{2,0},{4,6},{6,4},{8,10},{10,8},{12,14},{14,12},{1,3},{3,1},... | collective-permute-start | bytes 3145736 | tf_op jit(solution)/shard_map/out_cores/ppermute | solution.py:421
  63.6 3.5 %collective-permute-start.16 = (bf16[384,2048]{1,0:T(8,128)(2,1)S(1)}, bf16[384,2048]{1,0:T(8,128)(2,1)S(1)}, u32[]{:S(2)}, u32[]{:S(2)}) collective-permute-start(bf16[384,2048]{1,0:T(8,128)(2,1)S(1)} %join.7.refs_1_), channel_id=1, source_target_pairs={{0,2},{2,0},{4,6},{6,4},{8,10},{10,8},{12,14},{14,12},{1,3},{3,1},... | collective-permute-start | bytes 4718600 | tf_op jit(solution)/shard_map/grads_cores/ppermute | solution.py:421
  63.7 32.1 %collective-permute-start.11 = (bf16[512,1024]{1,0:T(8,128)(2,1)S(1)}, bf16[512,1024]{1,0:T(8,128)(2,1)S(1)}, u32[]{:S(2)}, u32[]{:S(2)}) collective-permute-start(bf16[512,1024]{1,0:T(8,128)(2,1)S(1)} %get-tuple-element.167), channel_id=1, source_target_pairs={{0,2},{2,0},{4,6},{6,4},{8,10},{10,8},{12,14},{14,12},{1,3},{3,1},... | collective-permute-start | bytes 3145736 | tf_op jit(solution)/shard_map/out_cores/ppermute | solution.py:421
  64.2 31.6 %collective-permute-start.15 = (bf16[512,1024]{1,0:T(8,128)(2,1)S(1)}, bf16[512,1024]{1,0:T(8,128)(2,1)S(1)}, u32[]{:S(2)}, u32[]{:S(2)}) collective-permute-start(bf16[512,1024]{1,0:T(8,128)(2,1)S(1)} %out_send.1), channel_id=1, source_target_pairs={{0,1},{1,0},{2,3},{3,2},{4,5},{5,4},{6,7},{7,6},{8,9},{9,8},{10,11... | collective-permute-start | bytes 3145736 | tf_op jit(solution)/shard_map/out_across/ppermute | solution.py:425
  81.6 2.1 %collective-permute-start.18 = (bf16[256,1152]{1,0:T(8,128)(2,1)S(1)}, bf16[256,1152]{1,0:T(8,128)(2,1)S(1)}, u32[]{:S(2)}, u32[]{:S(2)}) collective-permute-start(bf16[256,1152]{1,0:T(8,128)(2,1)S(1)} %get-tuple-element.195), channel_id=1, source_target_pairs={{0,2},{2,0},{4,6},{6,4},{8,10},{10,8},{12,14},{14,12},{1,3},{3,1},... | collective-permute-start | bytes 1769480 | tf_op jit(solution)/shard_map/in_cores/ppermute | solution.py:421
  81.8 9.7 %collective-permute-start.17 = (bf16[256,1152]{1,0:T(8,128)(2,1)S(1)}, bf16[256,1152]{1,0:T(8,128)(2,1)S(1)}, u32[]{:S(2)}, u32[]{:S(2)}) collective-permute-start(bf16[256,1152]{1,0:T(8,128)(2,1)S(1)} %get-tuple-element.194), channel_id=1, source_target_pairs={{0,2},{2,0},{4,6},{6,4},{8,10},{10,8},{12,14},{14,12},{1,3},{3,1},... | collective-permute-start | bytes 1769480 | tf_op jit(solution)/shard_map/in_cores/ppermute | solution.py:421
  82.2 17.1 %collective-permute-start.21 = (bf16[256,1152]{1,0:T(8,128)(2,1)S(1)}, bf16[256,1152]{1,0:T(8,128)(2,1)S(1)}, u32[]{:S(2)}, u32[]{:S(2)}) collective-permute-start(bf16[256,1152]{1,0:T(8,128)(2,1)S(1)} %get-tuple-element.196), channel_id=1, source_target_pairs={{0,2},{2,0},{4,6},{6,4},{8,10},{10,8},{12,14},{14,12},{1,3},{3,1},... | collective-permute-start | bytes 1769480 | tf_op jit(solution)/shard_map/in_cores/ppermute | solution.py:421
  83.8 11.9 %collective-permute-start.19 = (bf16[128,1152]{1,0:T(8,128)(2,1)S(1)}, bf16[128,1152]{1,0:T(8,128)(2,1)S(1)}, u32[]{:S(2)}, u32[]{:S(2)}) collective-permute-start(bf16[128,1152]{1,0:T(8,128)(2,1)S(1)} %get-tuple-element.200), channel_id=1, source_target_pairs={{0,1},{1,0},{2,3},{3,2},{4,5},{5,4},{6,7},{7,6},{8,9},{9,8},{10,11... | collective-permute-start | bytes 884744 | tf_op jit(solution)/shard_map/in_across/ppermute | solution.py:425
  96.2 14.9 %collective-permute-start.20 = (bf16[256,1024]{1,0:T(8,128)(2,1)S(1)}, bf16[256,1024]{1,0:T(8,128)(2,1)S(1)}, u32[]{:S(2)}, u32[]{:S(2)}) collective-permute-start(bf16[256,1024]{1,0:T(8,128)(2,1)S(1)} %get-tuple-element.215), channel_id=1, source_target_pairs={{0,4},{2,6},{4,0},{6,2},{8,12},{10,14},{12,8},{14,10},{1,5},{3,7},... | collective-permute-start | bytes 1572872 | tf_op jit(solution)/shard_map/out_line/ppermute | solution.py:417
  97.2 31.2 %collective-permute-start.23 = (bf16[256,1152]{1,0:T(8,128)(2,1)S(1)}, bf16[256,1152]{1,0:T(8,128)(2,1)S(1)}, u32[]{:S(2)}, u32[]{:S(2)}) collective-permute-start(bf16[256,1152]{1,0:T(8,128)(2,1)S(1)} %get-tuple-element.197), channel_id=1, source_target_pairs={{0,2},{2,0},{4,6},{6,4},{8,10},{10,8},{12,14},{14,12},{1,3},{3,1},... | collective-permute-start | bytes 1769480 | tf_op jit(solution)/shard_map/in_cores/ppermute | solution.py:421
  97.2 23.0 %collective-permute-start.25 = (bf16[128,1152]{1,0:T(8,128)(2,1)S(1)}, bf16[128,1152]{1,0:T(8,128)(2,1)S(1)}, u32[]{:S(2)}, u32[]{:S(2)}) collective-permute-start(bf16[128,1152]{1,0:T(8,128)(2,1)S(1)} %in_slot.3), channel_id=1, source_target_pairs={{0,4},{2,6},{4,0},{6,2},{8,12},{10,14},{12,8},{14,10},{1,5},{3,7},... | collective-permute-start | bytes 884744 | tf_op jit(solution)/shard_map/in_line/ppermute | solution.py:417
  98.3 21.6 %collective-permute-start.24 = (bf16[128,1152]{1,0:T(8,128)(2,1)S(1)}, bf16[128,1152]{1,0:T(8,128)(2,1)S(1)}, u32[]{:S(2)}, u32[]{:S(2)}) collective-permute-start(bf16[128,1152]{1,0:T(8,128)(2,1)S(1)} %get-tuple-element.223), channel_id=1, source_target_pairs={{0,1},{1,0},{2,3},{3,2},{4,5},{5,4},{6,7},{7,6},{8,9},{9,8},{10,11... | collective-permute-start | bytes 884744 | tf_op jit(solution)/shard_map/in_across/ppermute | solution.py:425
  111.1 20.5 %collective-permute-start.22 = (bf16[128,1024]{1,0:T(8,128)(2,1)S(1)}, bf16[128,1024]{1,0:T(8,128)(2,1)S(1)}, u32[]{:S(2)}, u32[]{:S(2)}) collective-permute-start(bf16[128,1024]{1,0:T(8,128)(2,1)S(1)} %add_last.1), channel_id=1, source_target_pairs={{0,8},{2,10},{4,12},{6,14},{8,0},{10,2},{12,4},{14,6},{1,9},{3,11}... | collective-permute-start | bytes 786440 | tf_op jit(solution)/shard_map/out_line/ppermute | solution.py:417
  120.3 16.3 %collective-permute-start.27 = (bf16[128,1152]{1,0:T(8,128)(2,1)S(1)}, bf16[128,1152]{1,0:T(8,128)(2,1)S(1)}, u32[]{:S(2)}, u32[]{:S(2)}) collective-permute-start(bf16[128,1152]{1,0:T(8,128)(2,1)S(1)} %in_slot.4), channel_id=1, source_target_pairs={{0,8},{2,10},{4,12},{6,14},{8,0},{10,2},{12,4},{14,6},{1,9},{3,11}... | collective-permute-start | bytes 884744 | tf_op jit(solution)/shard_map/in_line/ppermute | solution.py:417
  120.9 7.5 %collective-permute-start.26 = (bf16[128,1152]{1,0:T(8,128)(2,1)S(1)}, bf16[128,1152]{1,0:T(8,128)(2,1)S(1)}, u32[]{:S(2)}, u32[]{:S(2)}) collective-permute-start(bf16[128,1152]{1,0:T(8,128)(2,1)S(1)} %get-tuple-element.233), channel_id=1, source_target_pairs={{0,1},{1,0},{2,3},{3,2},{4,5},{5,4},{6,7},{7,6},{8,9},{9,8},{10,11... | collective-permute-start | bytes 884744 | tf_op jit(solution)/shard_map/in_across/ppermute | solution.py:425
  128.6 14.3 %copy-start.1 = (s32[128,4]{0,1:T(4,128)S(1)}, s32[128,4]{0,1:T(4,128)}, u32[]{:S(2)}) copy-start(s32[128,4]{0,1:T(4,128)} %param.9) | copy-start | bytes 6148
  128.6 14.3 %copy-start.2 = (f32[128,4]{0,1:T(4,128)S(1)}, f32[128,4]{0,1:T(4,128)}, u32[]{:S(2)}) copy-start(f32[128,4]{0,1:T(4,128)} %param.11) | copy-start | bytes 6148
  128.6 14.3 %copy-start.3 = (s32[128]{0:T(128)S(1)}, s32[128]{0:T(128)}, u32[]{:S(2)}) copy-start(s32[128]{0:T(128)} %param.10) | copy-start | bytes 1540
  128.6 8.1 %collective-permute-start.29 = (bf16[128,1152]{1,0:T(8,128)(2,1)S(1)}, bf16[128,1152]{1,0:T(8,128)(2,1)S(1)}, u32[]{:S(2)}, u32[]{:S(2)}) collective-permute-start(bf16[128,1152]{1,0:T(8,128)(2,1)S(1)} %get-tuple-element.246), channel_id=1, source_target_pairs={{0,1},{1,0},{2,3},{3,2},{4,5},{5,4},{6,7},{7,6},{8,9},{9,8},{10,11... | collective-permute-start | bytes 884744 | tf_op jit(solution)/shard_map/in_across/ppermute | solution.py:425
  129.7 13.2 %collective-permute-start.28 = (bf16[128,1152]{1,0:T(8,128)(2,1)S(1)}, bf16[128,1152]{1,0:T(8,128)(2,1)S(1)}, u32[]{:S(2)}, u32[]{:S(2)}) collective-permute-start(bf16[128,1152]{1,0:T(8,128)(2,1)S(1)} %in_slot.5), channel_id=1, source_target_pairs={{0,4},{2,6},{4,0},{6,2},{8,12},{10,14},{12,8},{14,10},{1,5},{3,7},... | collective-permute-start | bytes 884744 | tf_op jit(solution)/shard_map/in_line/ppermute | solution.py:417

commit v9 on v8

--- a/solution.py
+++ b/solution.py
@@ -341,10 +341,12 @@
 
 
 def send_kernel(first, own, received, *sent):
-    rows = sent[0].shape[0]
-    for i, target in enumerate(sent):
-        here = slice(first + i * rows, first + (i + 1) * rows)
-        target[...] = own[0, here, :] + received[i * rows : (i + 1) * rows, :]
+    at = 0
+    for target in sent:
+        rows = target.shape[0]
+        here = slice(first + at, first + at + rows)
+        target[...] = own[0, here, :] + received[at : at + rows, :]
+        at = at + rows
 
 
 def slot_sum(own, received, arrived, slot, offset, received_slot):
@@ -357,11 +359,12 @@
     return kept + jnp.concatenate([other[half:], other[:half]], axis=0)
 
 
-def slots_kernel(own, received, arrived, own_slot, near_and_last, far_slot):
-    rows = own_slot.shape[0]
-    targets = (own_slot, near_and_last.at[:rows], far_slot, near_and_last.at[rows:])
-    for slot, target in enumerate(targets):
-        target[...] = slot_sum(own, received, arrived, slot, slot * rows, slot).astype(target.dtype)
+def slots_kernel(own, received, arrived, near_and_last, far_slot):
+    rows = far_slot.shape[0]
+    targets = (near_and_last.at[:rows], far_slot, near_and_last.at[rows:])
+    for i, target in enumerate(targets):
+        whole = slot_sum(own, received, arrived, i + 1, i * rows, i + 1)
+        target[...] = whole.astype(target.dtype)
 
 
 def add_last_kernel(far_slot, arrived, total):
@@ -376,9 +379,10 @@
     refs[-1][...] = whole.astype(refs[-1].dtype)
 
 
-def finish_outputs_kernel(own, near_and_last, far, columns):
-    near = near_and_last[: own.shape[0], :]
-    whole = total_of([term.astype(jnp.float32) for term in (own[...], near, far[...])])
+def finish_outputs_kernel(own, received, arrived, near_and_last, far, columns):
+    near = near_and_last[: far.shape[0], :]
+    whole = slot_sum(own, received, arrived, 0, 0, 0)
+    whole = total_of([whole, near.astype(jnp.float32), far[...].astype(jnp.float32)])
     whole = jnp.where(lax.axis_index("helper") == 0, whole, swap_halves(whole))
     columns[...] = whole.astype(jnp.bfloat16)
 
@@ -425,23 +429,22 @@
             return lax.ppermute(array, "helper", self.sides)
 
     def send(self, first, own, received, parts):
-        rows, columns = received.shape
-        part = jax.ShapeDtypeStruct((rows // parts, columns), own.dtype)
+        shape = lambda rows: jax.ShapeDtypeStruct((rows, received.shape[1]), own.dtype)
         return call(
             functools.partial(send_kernel, first),
             self.label + "_send",
             (own, received),
-            (part,) * parts,
+            tuple(shape(rows) for rows in parts),
         )
 
     def slots(self, own, received, arrived):
         rows, columns = arrived.shape
-        shape = lambda slots: jax.ShapeDtypeStruct((slots * rows // 4, columns), arrived.dtype)
+        shape = lambda slots: jax.ShapeDtypeStruct((slots * rows // 3, columns), arrived.dtype)
         return call(
             slots_kernel,
             self.label + "_slots",
             (own, received, arrived),
-            (shape(1), shape(2), shape(1)),
+            (shape(2), shape(1)),
         )
 
     def slot(self, which, own, received, arrived, *others):
@@ -541,7 +544,10 @@
     received, kept = outs.sibling(sent), outs.sibling(kept)
     clock = order(space, clock, also=(grads_across, last_across))
     received = hold(received, clock)
-    (sent,) = order(lambda *s: outs.send(0, *s, 1), near_out, received)
+    size = tokens.shape[0]
+    own_sent, sent = order(
+        lambda *s: outs.send(0, *s, (size, 3 * size)), near_out, received
+    )
     arrived = outs.across(sent)
     rest = order(join, grads_line, grads_across, grads_last, last_across)
     all_grads = [grads_pair, rest, grads_sibling, grads.sibling(rest)]
@@ -557,17 +563,20 @@
     )
     far_received, far_kept = ins.sibling(far_sent), ins.sibling(far_kept)
     near_received, near_kept = ins.sibling(near_sent), ins.sibling(near_kept)
-    first = 2 * tokens.shape[0]
-    far_sent, last_sent = order(lambda *s: ins.send(first, *s, 2), in_own, far_received)
+    far_sent, last_sent = order(
+        lambda *s: ins.send(2 * size, *s, (size, size)), in_own, far_received
+    )
     last_arrived = ins.across(last_sent)
+    near_slots, far_slot = order(outs.slots, near_out, kept, hold(arrived, far_sent))
+    near_sums = outs.line(near_slots, outs.near)
+    out_arrived = outs.across(hold(own_sent, near_slots))
     grad_down = order(product_of("grad_down", True), all_grads, gated)
     slot = order(lambda *s: ins.slot(3, *s), in_own, far_kept, last_arrived)
     last_sum = ins.line(slot, ins.near)
     far_arrived = ins.across(hold(far_sent, slot))
-    arrived = hold(arrived, slot)
-    own_slot, near_slots, far_slot = order(outs.slots, near_out, kept, arrived)
-    near_sums = outs.line(near_slots, outs.near)
-    own_sent, near_sent = order(lambda *s: ins.send(0, *s, 2), in_own, near_received)
+    own_sent, near_sent = order(
+        lambda *s: ins.send(0, *s, (size, size)), in_own, near_received, also=out_arrived
+    )
     far_slot = order(
         lambda *s: call(add_last_kernel, "add_last", s, jax.ShapeDtypeStruct(s[0].shape, s[0].dtype)),
         far_slot,
@@ -582,10 +591,12 @@
     slot = order(lambda *s: ins.slot(1, *s), in_own, near_kept, near_arrived)
     near = ins.line(slot, ins.near)
     own_arrived = ins.across(hold(own_sent, slot))
-    columns = jax.ShapeDtypeStruct((tokens.shape[0], width // 2), jnp.bfloat16)
+    columns = jax.ShapeDtypeStruct((size, width // 2), jnp.bfloat16)
     output_cols = order(
         lambda *sums: call(finish_outputs_kernel, "finish_outputs", sums, columns),
-        own_slot,
+        near_out,
+        kept,
+        out_arrived,
         near_sums,
         far_sum,
     )

time: 144 us -> 134 us (0.931)
  waiting for transfers between devices: 57.8 us -> 47.1 us
    ppermute x11, waiting for transfers between devices: 44.4 us -> 33.5 us  [line(): return lax.ppermute(array, 'expert', pairs)]
    ppermute x9 -> x10, starting transfers between devices: 9.83 us -> 10.3 us  [across(): return lax.ppermute(array, 'helper', self.sides)]
    ppermute x9 -> x10, waiting for transfers between devices: 7.6 us -> 7.85 us  [across(): return lax.ppermute(array, 'helper', self.sides)]
  transfers between devices with their start and end apart: 30 -> 31, of which waited for: 14 -> 14; matrix products, arithmetic and copies ran while one was open for 0% -> 0% of each run, Pallas kernels for 38% -> 41%
where the time goes in v9:
time: 134 us
  Pallas kernels  57 us (43%)
  waiting for transfers between devices  47.1 us (35%)
  starting transfers between devices  28.7 us (21%)
    pallas_call x22, Pallas kernels, call(): pl.pallas_call(kernel, out_shape=out_shape, in_specs=[VMEM] * len(operand...  51 us
    ppermute x11, waiting for transfers between devices, line(): return lax.ppermute(array, 'expert', pairs)  33.5 us
    ppermute x11, starting transfers between devices, line(): return lax.ppermute(array, 'expert', pairs)  16 us
    ppermute x10, starting transfers between devices, across(): return lax.ppermute(array, 'helper', self.sides)  10.3 us
    ppermute x10, waiting for transfers between devices, across(): return lax.ppermute(array, 'helper', self.sides)  7.85 us
    ppermute x10, waiting for transfers between devices, sibling(): return lax.ppermute(array, 'expert', self.cores)  5.79 us
    pallas_call x1, Pallas kernels, load(): pl.pallas_call(load_kernel, out_shape=tuple((jax.ShapeDtypeStruct(mat.sha...  4.73 us
  transfers between devices with their start and end apart: 31, of which 14 were waited for; matrix products, arithmetic and copies ran while one was open for 0% of the time, Pallas kernels for 41%

profile of v9, /device:TPU:0, one launch (start us, length us, event | category | flops | bytes accessed | tf_op | source)
XLA Modules:
  0.0 133.7 jit_solution(14187771718991364335)
XLA Ops:
  0.6 1.3 prepare_rows.1
  1.9 0.5 collective-permute-start.2
  2.5 3.7 %collective-permute-start.1 = (bf16[64,2176]{1,0:T(8,128)(2,1)S(1)}, bf16[64,2176]{1,0:T(8,128)(2,1)S(1)}, u32[]{:S(2)}, u32[]{:S(2)}) collective-permute-start(bf16[64,2176]{1,0:T(8,128)(2,1)S(1)} %get-tuple-element.136), channel_id=1, source_target_pairs={{0,8},{2,10},{4,12},{6,14},{8,0},{10,2},{12,4},{14,6},{1,9},{3,11}... | collective-permute-start | bytes 835592 | tf_op jit(solution)/shard_map/rows_line/ppermute | solution.py:421
  6.1 1.6 %collective-permute-start = (bf16[64,2176]{1,0:T(8,128)(2,1)S(1)}, bf16[64,2176]{1,0:T(8,128)(2,1)S(1)}, u32[]{:S(2)}, u32[]{:S(2)}) collective-permute-start(bf16[64,2176]{1,0:T(8,128)(2,1)S(1)} %get-tuple-element.136), channel_id=1, source_target_pairs={{0,4},{2,6},{4,0},{6,2},{8,12},{10,14},{12,8},{14,10},{1,5},{3,7},... | collective-permute-start | bytes 835592 | tf_op jit(solution)/shard_map/rows_line/ppermute | solution.py:421
  7.7 4.7 %load.1 = (bf16[2048,1024]{1,0:T(8,128)(2,1)S(1)}, bf16[2048,1024]{1,0:T(8,128)(2,1)S(1)}, bf16[1024,2048]{1,0:T(8,128)(2,1)S(1)}) custom-call(bf16[2048,1024]{1,0:T(8,128)(2,1)} %bitcast.16, bf16[2048,1024]{1,0:T(8,128)(2,1)} %bitcast.17, bf16[1024,2048]{1,0:T(8,128)(2,1)} %bitcast.18), custom_call_target="tpu_custom_call" | custom-call | tf_op jit(solution)/shard_map/load/pallas_call | solution.py:472
  12.4 7.0 %collective-permute-done.1.refs_1_ = bf16[64,2176]{1,0:T(8,128)(2,1)S(1)} collective-permute-done((bf16[64,2176]{1,0:T(8,128)(2,1)S(1)}, bf16[64,2176]{1,0:T(8,128)(2,1)S(1)}, u32[]{:S(2)}, u32[]{:S(2)}) %collective-permute-start.1) | collective-permute-done | bytes 278560 | tf_op jit(solution)/shard_map/rows_line/ppermute | solution.py:421
  19.7 1.6 %collective-permute-start.4 = (bf16[64,2176]{1,0:T(8,128)(2,1)S(1)}, bf16[64,2176]{1,0:T(8,128)(2,1)S(1)}, u32[]{:S(2)}, u32[]{:S(2)}) collective-permute-start(bf16[64,2176]{1,0:T(8,128)(2,1)S(1)} %collective-permute-done.1.refs_1_), channel_id=1, source_target_pairs={{0,4},{2,6},{4,0},{6,2},{8,12},{10,14},{12,8},{14,10},{1,5},{3,7},... | collective-permute-start | bytes 835592 | tf_op jit(solution)/shard_map/rows_line/ppermute | solution.py:421
  21.2 1.5 %collective-permute-start.3 = (bf16[128,2176]{1,0:T(8,128)(2,1)S(1)}, bf16[128,2176]{1,0:T(8,128)(2,1)S(1)}, u32[]{:S(2)}, u32[]{:S(2)}) collective-permute-start(bf16[128,2176]{1,0:T(8,128)(2,1)S(1)} %join.4.refs_0_), channel_id=1, source_target_pairs={{0,1},{1,0},{2,3},{3,2},{4,5},{5,4},{6,7},{7,6},{8,9},{9,8},{10,11... | collective-permute-start | bytes 1671176 | tf_op jit(solution)/shard_map/rows_across/ppermute | solution.py:429
  22.8 2.4 %collective-permute-start.7 = (bf16[64,2048]{1,0:T(8,128)(2,1)S(1)}, bf16[64,2048]{1,0:T(8,128)(2,1)S(1)}, u32[]{:S(2)}, u32[]{:S(2)}) collective-permute-start(bf16[64,2048]{1,0:T(8,128)(2,1)S(1)} %get-tuple-element.150), channel_id=1, source_target_pairs={{0,8},{2,10},{4,12},{6,14},{8,0},{10,2},{12,4},{14,6},{1,9},{3,11}... | collective-permute-start | bytes 786440 | tf_op jit(solution)/shard_map/grads_line/ppermute | solution.py:421
  25.2 7.1 %collective-permute-done.4.refs_2_ = bf16[64,2176]{1,0:T(8,128)(2,1)S(1)} collective-permute-done((bf16[64,2176]{1,0:T(8,128)(2,1)S(1)}, bf16[64,2176]{1,0:T(8,128)(2,1)S(1)}, u32[]{:S(2)}, u32[]{:S(2)}) %collective-permute-start.4) | collective-permute-done | bytes 278560 | tf_op jit(solution)/shard_map/rows_line/ppermute | solution.py:421
  32.3 2.4 %collective-permute-start.5 = (bf16[64,2176]{1,0:T(8,128)(2,1)S(1)}, bf16[64,2176]{1,0:T(8,128)(2,1)S(1)}, u32[]{:S(2)}, u32[]{:S(2)}) collective-permute-start(bf16[64,2176]{1,0:T(8,128)(2,1)S(1)} %collective-permute-done.4.refs_2_), channel_id=1, source_target_pairs={{0,1},{1,0},{2,3},{3,2},{4,5},{5,4},{6,7},{7,6},{8,9},{9,8},{10,11... | collective-permute-start | bytes 835592 | tf_op jit(solution)/shard_map/rows_across/ppermute | solution.py:429
  34.7 2.3 %collective-permute-done.7.refs_1_ = bf16[64,2048]{1,0:T(8,128)(2,1)S(1)} collective-permute-done((bf16[64,2048]{1,0:T(8,128)(2,1)S(1)}, bf16[64,2048]{1,0:T(8,128)(2,1)S(1)}, u32[]{:S(2)}, u32[]{:S(2)}) %collective-permute-start.7) | collective-permute-done | bytes 262176 | tf_op jit(solution)/shard_map/grads_line/ppermute | solution.py:421
  37.0 5.4 %collective-permute-done.6.refs_0_ = bf16[64,2048]{1,0:T(8,128)(2,1)S(1)} collective-permute-done((bf16[64,2048]{1,0:T(8,128)(2,1)S(1)}, bf16[64,2048]{1,0:T(8,128)(2,1)S(1)}, u32[]{:S(2)}, u32[]{:S(2)}) %collective-permute-start.6) | collective-permute-done | bytes 262176 | tf_op jit(solution)/shard_map/grads_line/ppermute | solution.py:421
  42.6 0.5 collective-permute-start.10
  43.1 0.6 collective-permute-start.13
  43.7 2.4 %collective-permute-done.8.refs_3_.refs_7_ = bf16[384,2176]{1,0:T(8,128)(2,1)S(1)} collective-permute-done((bf16[384,2176]{1,0:T(8,128)(2,1)S(1)}, bf16[384,2176]{1,0:T(8,128)(2,1)S(1)}, u32[]{:S(2)}, u32[]{:S(2)}) %collective-permute-start.8) | collective-permute-done | bytes 1671200 | tf_op jit(solution)/shard_map/rows_cores/ppermute | solution.py:425
  46.1 8.8 %hidden_units.1 = (f32[1024,1024]{1,0:T(8,128)S(1)}, f32[1024,1024]{1,0:T(8,128)S(1)}, bf16[1024,1024]{1,0:T(8,128)(2,1)S(1)}) custom-call(bf16[128,2176]{1,0:T(8,128)(2,1)S(1)} %get-tuple-element.240.refs_0_.refs_4_, bf16[384,2176]{1,0:T(8,128)(2,1)S(1)} %join.6.refs_1_.refs_5_, bf16[128,2176]{1,0:T(8,128)(2,1)S(1)} %collective-permute-done.2.refs_2_.refs_6_, ...), custom_call_target="tpu_custom_call" | custom-call | flops 8589934592 | tf_op jit(solution)/shard_map/hidden_units/pallas_call | solution.py:40
  55.0 0.3 collective-permute-start.14
  55.3 4.5 %outputs.1 = (bf16[2,512,1024]{2,1,0:T(8,128)(2,1)S(1)}, bf16[512,1024]{1,0:T(8,128)(2,1)S(1)}, bf16[512,1024]{1,0:T(8,128)(2,1)S(1)}) custom-call(bf16[1024,1024]{1,0:T(8,128)(2,1)S(1)} %get-tuple-element.219.gated.refs_4_, bf16[1024,2048]{1,0:T(8,128)(2,1)S(1)} %get-tuple-element.169.down_mat.refs_8_), custom_call_target="tpu_custom_call" | custom-call | flops 4294967296 | tf_op jit(solution)/shard_map/outputs/pallas_call | solution.py:40
  59.9 3.5 %collective-permute-done.14.refs_3_ = bf16[64,2048]{1,0:T(8,128)(2,1)S(1)} collective-permute-done((bf16[64,2048]{1,0:T(8,128)(2,1)S(1)}, bf16[64,2048]{1,0:T(8,128)(2,1)S(1)}, u32[]{:S(2)}, u32[]{:S(2)}) %collective-permute-start.14) | collective-permute-done | bytes 262176 | tf_op jit(solution)/shard_map/grads_across/ppermute | solution.py:429
  63.7 0.5 collective-permute-start.11
  64.2 0.9 collective-permute-start.15
  65.1 2.0 %collective-permute-done.16.refs_3_ = bf16[384,2048]{1,0:T(8,128)(2,1)S(1)} collective-permute-done((bf16[384,2048]{1,0:T(8,128)(2,1)S(1)}, bf16[384,2048]{1,0:T(8,128)(2,1)S(1)}, u32[]{:S(2)}, u32[]{:S(2)}) %collective-permute-start.16) | collective-permute-done | bytes 1572896 | tf_op jit(solution)/shard_map/grads_cores/ppermute | solution.py:425
  67.1 5.7 %hidden_grads.1 = (bf16[1024,1024]{1,0:T(8,128)(2,1)S(1)}, bf16[1024,1024]{1,0:T(8,128)(2,1)S(1)}, bf16[1024,128]{1,0:T(8,128)(2,1)S(1)}) custom-call(bf16[128,2048]{1,0:T(8,128)(2,1)S(1)} %get-tuple-element.215.refs_0_, bf16[384,2048]{1,0:T(8,128)(2,1)S(1)} %join.7.refs_1_, bf16[128,2048]{1,0:T(8,128)(2,1)S(1)} %collective-permute-done.10.refs_2_, ...), custom_call_target="tpu_custom_call" | custom-call | flops 4294967296 | tf_op jit(solution)/shard_map/hidden_grads/pallas_call | solution.py:40
  72.8 8.9 %input_grads.1 = (bf16[2,512,1152]{2,1,0:T(8,128)(2,1)S(1)}, bf16[256,1152]{1,0:T(8,128)(2,1)S(1)}, bf16[256,1152]{1,0:T(8,128)(2,1)S(1)}, bf16[256,1152]{1,0:T(8,128)(2,1)S(1)}, bf16[256,1152]{1,0:T(8,128)(2,1)S(1)}) custom-call(bf16[1024,1024]{1,0:T(8,128)(2,1)S(1)} %get-tuple-element.234.d_gate.refs_4_, ...), custom_call_target="tpu_custom_call" | custom-call | tf_op jit(solution)/shard_map/input_grads/pallas_call | solution.py:40
  81.8 0.4 collective-permute-start.21
  82.3 1.4 %collective-permute-done.17.received = bf16[256,1152]{1,0:T(8,128)(2,1)S(1)} collective-permute-done((bf16[256,1152]{1,0:T(8,128)(2,1)S(1)}, bf16[256,1152]{1,0:T(8,128)(2,1)S(1)}, u32[]{:S(2)}, u32[]{:S(2)}) %collective-permute-start.17) | collective-permute-done | bytes 589856 | tf_op jit(solution)/shard_map/in_cores/ppermute | solution.py:425
  83.8 0.3 out_slots.1
  84.1 1.0 collective-permute-start.19
  85.1 0.3 collective-permute-start.22
  85.4 1.7 %collective-permute-start.18 = (bf16[128,1024]{1,0:T(8,128)(2,1)S(1)}, bf16[128,1024]{1,0:T(8,128)(2,1)S(1)}, u32[]{:S(2)}, u32[]{:S(2)}) collective-permute-start(bf16[128,1024]{1,0:T(8,128)(2,1)S(1)} %get-tuple-element.213), channel_id=1, source_target_pairs={{0,1},{1,0},{2,3},{3,2},{4,5},{5,4},{6,7},{7,6},{8,9},{9,8},{10,11... | collective-permute-start | bytes 786440 | tf_op jit(solution)/shard_map/out_across/ppermute | solution.py:429
  87.2 6.8 %grad_down.1 = bf16[1024,2048]{1,0:T(8,128)(2,1)} custom-call(bf16[128,2048]{1,0:T(8,128)(2,1)S(1)} %get-tuple-element.215.refs_0_, bf16[384,2048]{1,0:T(8,128)(2,1)S(1)} %join.7.refs_1_, bf16[128,2048]{1,0:T(8,128)(2,1)S(1)} %collective-permute-done.10.refs_2_, bf16[384,2048]{1,0:T(8,128)(2,1)S(1)} %collective-permute-done.16.refs_3_, ...), custom_call_target="tpu_custom_call" | custom-call | flops 4294967296 | tf_op jit(solution)/shard_map/grad_down/pallas_call | solution.py:40
  93.9 1.1 collective-permute-done.22.arrived
  95.1 1.1 collective-permute-start.26
  96.3 3.3 %collective-permute-done.18.arrived = bf16[128,1024]{1,0:T(8,128)(2,1)S(1)} collective-permute-done((bf16[128,1024]{1,0:T(8,128)(2,1)S(1)}, bf16[128,1024]{1,0:T(8,128)(2,1)S(1)}, u32[]{:S(2)}, u32[]{:S(2)}) %collective-permute-start.18) | collective-permute-done | bytes 262176 | tf_op jit(solution)/shard_map/out_across/ppermute | solution.py:429
  99.5 0.3 collective-permute-start.25
  100.0 2.8 %collective-permute-start.23 = (bf16[128,1024]{1,0:T(8,128)(2,1)S(1)}, bf16[128,1024]{1,0:T(8,128)(2,1)S(1)}, u32[]{:S(2)}, u32[]{:S(2)}) collective-permute-start(bf16[128,1024]{1,0:T(8,128)(2,1)S(1)} %add_last.1), channel_id=1, source_target_pairs={{0,8},{2,10},{4,12},{6,14},{8,0},{10,2},{12,4},{14,6},{1,9},{3,11}... | collective-permute-start | bytes 786440 | tf_op jit(solution)/shard_map/out_line/ppermute | solution.py:421
  102.8 6.5 %grad_gate.1 = bf16[2048,1024]{1,0:T(8,128)(2,1)} custom-call(bf16[128,2176]{1,0:T(8,128)(2,1)S(1)} %get-tuple-element.240.refs_0_.refs_4_, bf16[384,2176]{1,0:T(8,128)(2,1)S(1)} %join.6.refs_1_.refs_5_, bf16[128,2176]{1,0:T(8,128)(2,1)S(1)} %collective-permute-done.2.refs_2_.refs_6_, bf16[384,2176]{1,0:T(8,128)(2,1)S(1)} %collective-permute-done.8.refs_3_.refs_7_, ...), custom_call_target="tpu_custom_call" | custom-call | flops 4294967296 | tf_op jit(solution)/shard_map/grad_gate/pallas_call | solution.py:40
  109.5 0.3 collective-permute-start.28
  109.8 1.6 %collective-permute-start.27 = (bf16[128,1152]{1,0:T(8,128)(2,1)S(1)}, bf16[128,1152]{1,0:T(8,128)(2,1)S(1)}, u32[]{:S(2)}, u32[]{:S(2)}) collective-permute-start(bf16[128,1152]{1,0:T(8,128)(2,1)S(1)} %get-tuple-element.239), channel_id=1, source_target_pairs={{0,1},{1,0},{2,3},{3,2},{4,5},{5,4},{6,7},{7,6},{8,9},{9,8},{10,11... | collective-permute-start | bytes 884744 | tf_op jit(solution)/shard_map/in_across/ppermute | solution.py:429
  111.4 6.5 %grad_up.1 = bf16[2048,1024]{1,0:T(8,128)(2,1)} custom-call(bf16[128,2176]{1,0:T(8,128)(2,1)S(1)} %get-tuple-element.240.refs_0_.refs_4_, bf16[384,2176]{1,0:T(8,128)(2,1)S(1)} %join.6.refs_1_.refs_5_, bf16[128,2176]{1,0:T(8,128)(2,1)S(1)} %collective-permute-done.2.refs_2_.refs_6_, bf16[384,2176]{1,0:T(8,128)(2,1)S(1)} %collective-permute-done.8.refs_3_.refs_7_, ...), custom_call_target="tpu_custom_call" | custom-call | flops 4294967296 | tf_op jit(solution)/shard_map/grad_up/pallas_call | solution.py:40
  118.1 0.6 collective-permute-start.30
  118.7 1.5 %collective-permute-start.29 = (bf16[128,1152]{1,0:T(8,128)(2,1)S(1)}, bf16[128,1152]{1,0:T(8,128)(2,1)S(1)}, u32[]{:S(2)}, u32[]{:S(2)}) collective-permute-start(bf16[128,1152]{1,0:T(8,128)(2,1)S(1)} %in_slot.5), channel_id=1, source_target_pairs={{0,4},{2,6},{4,0},{6,2},{8,12},{10,14},{12,8},{14,10},{1,5},{3,7},... | collective-permute-start | bytes 884744 | tf_op jit(solution)/shard_map/in_line/ppermute | solution.py:421
  120.1 1.8 %collective-permute-done.23.far = bf16[128,1024]{1,0:T(8,128)(2,1)S(1)} collective-permute-done((bf16[128,1024]{1,0:T(8,128)(2,1)S(1)}, bf16[128,1024]{1,0:T(8,128)(2,1)S(1)}, u32[]{:S(2)}, u32[]{:S(2)}) %collective-permute-start.23) | collective-permute-done | bytes 262176 | tf_op jit(solution)/shard_map/out_line/ppermute | solution.py:421
  121.9 0.9 finish_outputs.1
  122.8 3.5 %collective-permute-done.28.refs_0_ = bf16[128,1152]{1,0:T(8,128)(2,1)S(1)} collective-permute-done((bf16[128,1152]{1,0:T(8,128)(2,1)S(1)}, bf16[128,1152]{1,0:T(8,128)(2,1)S(1)}, u32[]{:S(2)}, u32[]{:S(2)}) %collective-permute-start.28) | collective-permute-done | bytes 294944 | tf_op jit(solution)/shard_map/in_line/ppermute | solution.py:421
  126.4 6.2 %collective-permute-done.29.refs_1_ = bf16[128,1152]{1,0:T(8,128)(2,1)S(1)} collective-permute-done((bf16[128,1152]{1,0:T(8,128)(2,1)S(1)}, bf16[128,1152]{1,0:T(8,128)(2,1)S(1)}, u32[]{:S(2)}, u32[]{:S(2)}) %collective-permute-start.29) | collective-permute-done | bytes 294944 | tf_op jit(solution)/shard_map/in_line/ppermute | solution.py:421
  132.6 1.1 finish_inputs.1
  (49 shorter events, 1.8 us)
Async XLA Ops:
  1.9 10.5 %collective-permute-start.2 = (bf16[128,2176]{1,0:T(8,128)(2,1)S(1)}, bf16[128,2176]{1,0:T(8,128)(2,1)S(1)}, u32[]{:S(2)}, u32[]{:S(2)}) collective-permute-start(bf16[128,2176]{1,0:T(8,128)(2,1)S(1)} %get-tuple-element.240.refs_0_.refs_4_), channel_id=1, source_target_pairs={{0,2},{2,0},{4,6},{6,4},{8,10},{10,8},{12,14},{14,12},{1,3},{3,1},... | collective-permute-start | bytes 1671176 | tf_op jit(solution)/shard_map/rows_cores/ppermute | solution.py:425
  2.5 17.0 %collective-permute-start.1 = (bf16[64,2176]{1,0:T(8,128)(2,1)S(1)}, bf16[64,2176]{1,0:T(8,128)(2,1)S(1)}, u32[]{:S(2)}, u32[]{:S(2)}) collective-permute-start(bf16[64,2176]{1,0:T(8,128)(2,1)S(1)} %get-tuple-element.136), channel_id=1, source_target_pairs={{0,8},{2,10},{4,12},{6,14},{8,0},{10,2},{12,4},{14,6},{1,9},{3,11}... | collective-permute-start | bytes 835592 | tf_op jit(solution)/shard_map/rows_line/ppermute | solution.py:421
  6.1 13.5 %collective-permute-start = (bf16[64,2176]{1,0:T(8,128)(2,1)S(1)}, bf16[64,2176]{1,0:T(8,128)(2,1)S(1)}, u32[]{:S(2)}, u32[]{:S(2)}) collective-permute-start(bf16[64,2176]{1,0:T(8,128)(2,1)S(1)} %get-tuple-element.136), channel_id=1, source_target_pairs={{0,4},{2,6},{4,0},{6,2},{8,12},{10,14},{12,8},{14,10},{1,5},{3,7},... | collective-permute-start | bytes 835592 | tf_op jit(solution)/shard_map/rows_line/ppermute | solution.py:421
  7.7 15.1 %copy-start = (bf16[128,2048]{1,0:T(8,128)(2,1)S(1)}, bf16[128,2048]{1,0:T(8,128)(2,1)}, u32[]{:S(2)}) copy-start(bf16[128,2048]{1,0:T(8,128)(2,1)} %rows) | copy-start | bytes 1572868
  19.7 12.6 %collective-permute-start.4 = (bf16[64,2176]{1,0:T(8,128)(2,1)S(1)}, bf16[64,2176]{1,0:T(8,128)(2,1)S(1)}, u32[]{:S(2)}, u32[]{:S(2)}) collective-permute-start(bf16[64,2176]{1,0:T(8,128)(2,1)S(1)} %collective-permute-done.1.refs_1_), channel_id=1, source_target_pairs={{0,4},{2,6},{4,0},{6,2},{8,12},{10,14},{12,8},{14,10},{1,5},{3,7},... | collective-permute-start | bytes 835592 | tf_op jit(solution)/shard_map/rows_line/ppermute | solution.py:421
  21.2 21.2 %collective-permute-start.3 = (bf16[128,2176]{1,0:T(8,128)(2,1)S(1)}, bf16[128,2176]{1,0:T(8,128)(2,1)S(1)}, u32[]{:S(2)}, u32[]{:S(2)}) collective-permute-start(bf16[128,2176]{1,0:T(8,128)(2,1)S(1)} %join.4.refs_0_), channel_id=1, source_target_pairs={{0,1},{1,0},{2,3},{3,2},{4,5},{5,4},{6,7},{7,6},{8,9},{9,8},{10,11... | collective-permute-start | bytes 1671176 | tf_op jit(solution)/shard_map/rows_across/ppermute | solution.py:429
  22.8 14.1 %collective-permute-start.7 = (bf16[64,2048]{1,0:T(8,128)(2,1)S(1)}, bf16[64,2048]{1,0:T(8,128)(2,1)S(1)}, u32[]{:S(2)}, u32[]{:S(2)}) collective-permute-start(bf16[64,2048]{1,0:T(8,128)(2,1)S(1)} %get-tuple-element.150), channel_id=1, source_target_pairs={{0,8},{2,10},{4,12},{6,14},{8,0},{10,2},{12,4},{14,6},{1,9},{3,11}... | collective-permute-start | bytes 786440 | tf_op jit(solution)/shard_map/grads_line/ppermute | solution.py:421
  32.3 10.1 %collective-permute-start.5 = (bf16[64,2176]{1,0:T(8,128)(2,1)S(1)}, bf16[64,2176]{1,0:T(8,128)(2,1)S(1)}, u32[]{:S(2)}, u32[]{:S(2)}) collective-permute-start(bf16[64,2176]{1,0:T(8,128)(2,1)S(1)} %collective-permute-done.4.refs_2_), channel_id=1, source_target_pairs={{0,1},{1,0},{2,3},{3,2},{4,5},{5,4},{6,7},{7,6},{8,9},{9,8},{10,11... | collective-permute-start | bytes 835592 | tf_op jit(solution)/shard_map/rows_across/ppermute | solution.py:429
  34.7 7.7 %collective-permute-start.6 = (bf16[64,2048]{1,0:T(8,128)(2,1)S(1)}, bf16[64,2048]{1,0:T(8,128)(2,1)S(1)}, u32[]{:S(2)}, u32[]{:S(2)}) collective-permute-start(bf16[64,2048]{1,0:T(8,128)(2,1)S(1)} %get-tuple-element.150), channel_id=1, source_target_pairs={{0,4},{2,6},{4,0},{6,2},{8,12},{10,14},{12,8},{14,10},{1,5},{3,7},... | collective-permute-start | bytes 786440 | tf_op jit(solution)/shard_map/grads_line/ppermute | solution.py:421
  42.5 3.6 %collective-permute-start.8 = (bf16[384,2176]{1,0:T(8,128)(2,1)S(1)}, bf16[384,2176]{1,0:T(8,128)(2,1)S(1)}, u32[]{:S(2)}, u32[]{:S(2)}) collective-permute-start(bf16[384,2176]{1,0:T(8,128)(2,1)S(1)} %join.6.refs_1_.refs_5_), channel_id=1, source_target_pairs={{0,2},{2,0},{4,6},{6,4},{8,10},{10,8},{12,14},{14,12},{1,3},{3,1},... | collective-permute-start | bytes 5013512 | tf_op jit(solution)/shard_map/rows_cores/ppermute | solution.py:425
  42.6 12.7 %collective-permute-start.10 = (bf16[128,2048]{1,0:T(8,128)(2,1)S(1)}, bf16[128,2048]{1,0:T(8,128)(2,1)S(1)}, u32[]{:S(2)}, u32[]{:S(2)}) collective-permute-start(bf16[128,2048]{1,0:T(8,128)(2,1)S(1)} %get-tuple-element.215.refs_0_), channel_id=1, source_target_pairs={{0,2},{2,0},{4,6},{6,4},{8,10},{10,8},{12,14},{14,12},{1,3},{3,1},... | collective-permute-start | bytes 1572872 | tf_op jit(solution)/shard_map/grads_cores/ppermute | solution.py:425
  43.1 11.9 %collective-permute-start.9 = (bf16[64,2048]{1,0:T(8,128)(2,1)S(1)}, bf16[64,2048]{1,0:T(8,128)(2,1)S(1)}, u32[]{:S(2)}, u32[]{:S(2)}) collective-permute-start(bf16[64,2048]{1,0:T(8,128)(2,1)S(1)} %collective-permute-done.7.refs_1_), channel_id=1, source_target_pairs={{0,4},{2,6},{4,0},{6,2},{8,12},{10,14},{12,8},{14,10},{1,5},{3,7},... | collective-permute-start | bytes 786440 | tf_op jit(solution)/shard_map/grads_line/ppermute | solution.py:421
  43.1 16.8 %collective-permute-start.13 = (bf16[128,2048]{1,0:T(8,128)(2,1)S(1)}, bf16[128,2048]{1,0:T(8,128)(2,1)S(1)}, u32[]{:S(2)}, u32[]{:S(2)}) collective-permute-start(bf16[128,2048]{1,0:T(8,128)(2,1)S(1)} %join.5.refs_0_), channel_id=1, source_target_pairs={{0,1},{1,0},{2,3},{3,2},{4,5},{5,4},{6,7},{7,6},{8,9},{9,8},{10,11... | collective-permute-start | bytes 1572872 | tf_op jit(solution)/shard_map/grads_across/ppermute | solution.py:429
  55.0 8.4 %collective-permute-start.14 = (bf16[64,2048]{1,0:T(8,128)(2,1)S(1)}, bf16[64,2048]{1,0:T(8,128)(2,1)S(1)}, u32[]{:S(2)}, u32[]{:S(2)}) collective-permute-start(bf16[64,2048]{1,0:T(8,128)(2,1)S(1)} %collective-permute-done.9.refs_2_), channel_id=1, source_target_pairs={{0,1},{1,0},{2,3},{3,2},{4,5},{5,4},{6,7},{7,6},{8,9},{9,8},{10,11... | collective-permute-start | bytes 786440 | tf_op jit(solution)/shard_map/grads_across/ppermute | solution.py:429
  59.8 3.6 %collective-permute-start.12 = (bf16[512,1024]{1,0:T(8,128)(2,1)S(1)}, bf16[512,1024]{1,0:T(8,128)(2,1)S(1)}, u32[]{:S(2)}, u32[]{:S(2)}) collective-permute-start(bf16[512,1024]{1,0:T(8,128)(2,1)S(1)} %get-tuple-element.172), channel_id=1, source_target_pairs={{0,2},{2,0},{4,6},{6,4},{8,10},{10,8},{12,14},{14,12},{1,3},{3,1},... | collective-permute-start | bytes 3145736 | tf_op jit(solution)/shard_map/out_cores/ppermute | solution.py:425
  63.6 3.5 %collective-permute-start.16 = (bf16[384,2048]{1,0:T(8,128)(2,1)S(1)}, bf16[384,2048]{1,0:T(8,128)(2,1)S(1)}, u32[]{:S(2)}, u32[]{:S(2)}) collective-permute-start(bf16[384,2048]{1,0:T(8,128)(2,1)S(1)} %join.7.refs_1_), channel_id=1, source_target_pairs={{0,2},{2,0},{4,6},{6,4},{8,10},{10,8},{12,14},{14,12},{1,3},{3,1},... | collective-permute-start | bytes 4718600 | tf_op jit(solution)/shard_map/grads_cores/ppermute | solution.py:425
  63.7 20.1 %collective-permute-start.11 = (bf16[512,1024]{1,0:T(8,128)(2,1)S(1)}, bf16[512,1024]{1,0:T(8,128)(2,1)S(1)}, u32[]{:S(2)}, u32[]{:S(2)}) collective-permute-start(bf16[512,1024]{1,0:T(8,128)(2,1)S(1)} %get-tuple-element.171), channel_id=1, source_target_pairs={{0,2},{2,0},{4,6},{6,4},{8,10},{10,8},{12,14},{14,12},{1,3},{3,1},... | collective-permute-start | bytes 3145736 | tf_op jit(solution)/shard_map/out_cores/ppermute | solution.py:425
  64.2 19.6 %collective-permute-start.15 = (bf16[384,1024]{1,0:T(8,128)(2,1)S(1)}, bf16[384,1024]{1,0:T(8,128)(2,1)S(1)}, u32[]{:S(2)}, u32[]{:S(2)}) collective-permute-start(bf16[384,1024]{1,0:T(8,128)(2,1)S(1)} %get-tuple-element.178), channel_id=1, source_target_pairs={{0,1},{1,0},{2,3},{3,2},{4,5},{5,4},{6,7},{7,6},{8,9},{9,8},{10,11... | collective-permute-start | bytes 2359304 | tf_op jit(solution)/shard_map/out_across/ppermute | solution.py:429
  81.6 2.1 %collective-permute-start.17 = (bf16[256,1152]{1,0:T(8,128)(2,1)S(1)}, bf16[256,1152]{1,0:T(8,128)(2,1)S(1)}, u32[]{:S(2)}, u32[]{:S(2)}) collective-permute-start(bf16[256,1152]{1,0:T(8,128)(2,1)S(1)} %get-tuple-element.200), channel_id=1, source_target_pairs={{0,2},{2,0},{4,6},{6,4},{8,10},{10,8},{12,14},{14,12},{1,3},{3,1},... | collective-permute-start | bytes 1769480 | tf_op jit(solution)/shard_map/in_cores/ppermute | solution.py:425
  81.8 12.1 %collective-permute-start.21 = (bf16[256,1152]{1,0:T(8,128)(2,1)S(1)}, bf16[256,1152]{1,0:T(8,128)(2,1)S(1)}, u32[]{:S(2)}, u32[]{:S(2)}) collective-permute-start(bf16[256,1152]{1,0:T(8,128)(2,1)S(1)} %get-tuple-element.203), channel_id=1, source_target_pairs={{0,2},{2,0},{4,6},{6,4},{8,10},{10,8},{12,14},{14,12},{1,3},{3,1},... | collective-permute-start | bytes 1769480 | tf_op jit(solution)/shard_map/in_cores/ppermute | solution.py:425
  82.2 14.0 %collective-permute-start.20 = (bf16[256,1152]{1,0:T(8,128)(2,1)S(1)}, bf16[256,1152]{1,0:T(8,128)(2,1)S(1)}, u32[]{:S(2)}, u32[]{:S(2)}) collective-permute-start(bf16[256,1152]{1,0:T(8,128)(2,1)S(1)} %get-tuple-element.201), channel_id=1, source_target_pairs={{0,2},{2,0},{4,6},{6,4},{8,10},{10,8},{12,14},{14,12},{1,3},{3,1},... | collective-permute-start | bytes 1769480 | tf_op jit(solution)/shard_map/in_cores/ppermute | solution.py:425
  84.1 15.8 %collective-permute-start.19 = (bf16[256,1024]{1,0:T(8,128)(2,1)S(1)}, bf16[256,1024]{1,0:T(8,128)(2,1)S(1)}, u32[]{:S(2)}, u32[]{:S(2)}) collective-permute-start(bf16[256,1024]{1,0:T(8,128)(2,1)S(1)} %get-tuple-element.212), channel_id=1, source_target_pairs={{0,4},{2,6},{4,0},{6,2},{8,12},{10,14},{12,8},{14,10},{1,5},{3,7},... | collective-permute-start | bytes 1572872 | tf_op jit(solution)/shard_map/out_line/ppermute | solution.py:421
  85.1 9.9 %collective-permute-start.22 = (bf16[128,1152]{1,0:T(8,128)(2,1)S(1)}, bf16[128,1152]{1,0:T(8,128)(2,1)S(1)}, u32[]{:S(2)}, u32[]{:S(2)}) collective-permute-start(bf16[128,1152]{1,0:T(8,128)(2,1)S(1)} %get-tuple-element.208), channel_id=1, source_target_pairs={{0,1},{1,0},{2,3},{3,2},{4,5},{5,4},{6,7},{7,6},{8,9},{9,8},{10,11... | collective-permute-start | bytes 884744 | tf_op jit(solution)/shard_map/in_across/ppermute | solution.py:429
  85.4 14.1 %collective-permute-start.18 = (bf16[128,1024]{1,0:T(8,128)(2,1)S(1)}, bf16[128,1024]{1,0:T(8,128)(2,1)S(1)}, u32[]{:S(2)}, u32[]{:S(2)}) collective-permute-start(bf16[128,1024]{1,0:T(8,128)(2,1)S(1)} %get-tuple-element.213), channel_id=1, source_target_pairs={{0,1},{1,0},{2,3},{3,2},{4,5},{5,4},{6,7},{7,6},{8,9},{9,8},{10,11... | collective-permute-start | bytes 786440 | tf_op jit(solution)/shard_map/out_across/ppermute | solution.py:429
  93.9 24.0 %collective-permute-start.24 = (bf16[256,1152]{1,0:T(8,128)(2,1)S(1)}, bf16[256,1152]{1,0:T(8,128)(2,1)S(1)}, u32[]{:S(2)}, u32[]{:S(2)}) collective-permute-start(bf16[256,1152]{1,0:T(8,128)(2,1)S(1)} %get-tuple-element.202), channel_id=1, source_target_pairs={{0,2},{2,0},{4,6},{6,4},{8,10},{10,8},{12,14},{14,12},{1,3},{3,1},... | collective-permute-start | bytes 1769480 | tf_op jit(solution)/shard_map/in_cores/ppermute | solution.py:425
  95.1 14.2 %collective-permute-start.26 = (bf16[128,1152]{1,0:T(8,128)(2,1)S(1)}, bf16[128,1152]{1,0:T(8,128)(2,1)S(1)}, u32[]{:S(2)}, u32[]{:S(2)}) collective-permute-start(bf16[128,1152]{1,0:T(8,128)(2,1)S(1)} %in_slot.3), channel_id=1, source_target_pairs={{0,4},{2,6},{4,0},{6,2},{8,12},{10,14},{12,8},{14,10},{1,5},{3,7},... | collective-permute-start | bytes 884744 | tf_op jit(solution)/shard_map/in_line/ppermute | solution.py:421
  99.5 9.8 %collective-permute-start.25 = (bf16[128,1152]{1,0:T(8,128)(2,1)S(1)}, bf16[128,1152]{1,0:T(8,128)(2,1)S(1)}, u32[]{:S(2)}, u32[]{:S(2)}) collective-permute-start(bf16[128,1152]{1,0:T(8,128)(2,1)S(1)} %get-tuple-element.229), channel_id=1, source_target_pairs={{0,1},{1,0},{2,3},{3,2},{4,5},{5,4},{6,7},{7,6},{8,9},{9,8},{10,11... | collective-permute-start | bytes 884744 | tf_op jit(solution)/shard_map/in_across/ppermute | solution.py:429
  100.0 22.0 %collective-permute-start.23 = (bf16[128,1024]{1,0:T(8,128)(2,1)S(1)}, bf16[128,1024]{1,0:T(8,128)(2,1)S(1)}, u32[]{:S(2)}, u32[]{:S(2)}) collective-permute-start(bf16[128,1024]{1,0:T(8,128)(2,1)S(1)} %add_last.1), channel_id=1, source_target_pairs={{0,8},{2,10},{4,12},{6,14},{8,0},{10,2},{12,4},{14,6},{1,9},{3,11}... | collective-permute-start | bytes 786440 | tf_op jit(solution)/shard_map/out_line/ppermute | solution.py:421
  109.5 16.9 %collective-permute-start.28 = (bf16[128,1152]{1,0:T(8,128)(2,1)S(1)}, bf16[128,1152]{1,0:T(8,128)(2,1)S(1)}, u32[]{:S(2)}, u32[]{:S(2)}) collective-permute-start(bf16[128,1152]{1,0:T(8,128)(2,1)S(1)} %in_slot.4), channel_id=1, source_target_pairs={{0,8},{2,10},{4,12},{6,14},{8,0},{10,2},{12,4},{14,6},{1,9},{3,11}... | collective-permute-start | bytes 884744 | tf_op jit(solution)/shard_map/in_line/ppermute | solution.py:421
  109.8 8.2 %collective-permute-start.27 = (bf16[128,1152]{1,0:T(8,128)(2,1)S(1)}, bf16[128,1152]{1,0:T(8,128)(2,1)S(1)}, u32[]{:S(2)}, u32[]{:S(2)}) collective-permute-start(bf16[128,1152]{1,0:T(8,128)(2,1)S(1)} %get-tuple-element.239), channel_id=1, source_target_pairs={{0,1},{1,0},{2,3},{3,2},{4,5},{5,4},{6,7},{7,6},{8,9},{9,8},{10,11... | collective-permute-start | bytes 884744 | tf_op jit(solution)/shard_map/in_across/ppermute | solution.py:429
  118.1 8.3 %collective-permute-start.30 = (bf16[128,1152]{1,0:T(8,128)(2,1)S(1)}, bf16[128,1152]{1,0:T(8,128)(2,1)S(1)}, u32[]{:S(2)}, u32[]{:S(2)}) collective-permute-start(bf16[128,1152]{1,0:T(8,128)(2,1)S(1)} %get-tuple-element.254), channel_id=1, source_target_pairs={{0,1},{1,0},{2,3},{3,2},{4,5},{5,4},{6,7},{7,6},{8,9},{9,8},{10,11... | collective-permute-start | bytes 884744 | tf_op jit(solution)/shard_map/in_across/ppermute | solution.py:429
  118.7 13.9 %collective-permute-start.29 = (bf16[128,1152]{1,0:T(8,128)(2,1)S(1)}, bf16[128,1152]{1,0:T(8,128)(2,1)S(1)}, u32[]{:S(2)}, u32[]{:S(2)}) collective-permute-start(bf16[128,1152]{1,0:T(8,128)(2,1)S(1)} %in_slot.5), channel_id=1, source_target_pairs={{0,4},{2,6},{4,0},{6,2},{8,12},{10,14},{12,8},{14,10},{1,5},{3,7},... | collective-permute-start | bytes 884744 | tf_op jit(solution)/shard_map/in_line/ppermute | solution.py:421
  122.8 9.8 %copy-start.1 = (s32[128,4]{0,1:T(4,128)S(1)}, s32[128,4]{0,1:T(4,128)}, u32[]{:S(2)}) copy-start(s32[128,4]{0,1:T(4,128)} %param.9) | copy-start | bytes 6148
  122.8 9.8 %copy-start.2 = (f32[128,4]{0,1:T(4,128)S(1)}, f32[128,4]{0,1:T(4,128)}, u32[]{:S(2)}) copy-start(f32[128,4]{0,1:T(4,128)} %param.11) | copy-start | bytes 6148
  122.8 9.8 %copy-start.3 = (s32[128]{0:T(128)S(1)}, s32[128]{0:T(128)}, u32[]{:S(2)}) copy-start(s32[128]{0:T(128)} %param.10) | copy-start | bytes 1540

commit v10 on v9

--- a/solution.py
+++ b/solution.py
@@ -516,24 +516,29 @@
 
     own, pair, clock = order(lambda r: prepare_rows(*picks, r, experts), tokens)
     near = rows.line(own, rows.near)
-    far = rows.line(own, rows.far)
     sibling_pair = rows.sibling(pair)
     gate_mat, up_mat, down_mat = order(load, gate_local, up_local, down_local)
-    sibling_pair = hold(sibling_pair, down_mat)
-    line_pair = order(join, near, far, also=sibling_pair)
-    last = rows.line(hold(far, line_pair), rows.near)
-    across_pair = rows.across(line_pair)
-    own, grads_pair = order(prepare_grads, grad_out)
-    far = grads.line(own, grads.far)
+    grads_own, grads_pair = order(prepare_grads, grad_out, also=sibling_pair)
+    near = hold(near, grads_own)
+    near_across = rows.across(near)
+    far = rows.line(hold(own, near), rows.far)
+    grads_near = grads.line(hold(grads_own, near), grads.near)
+    far = hold(far, near_across, grads_near)
+    far_across = rows.across(far)
+    last = rows.line(far, rows.near)
+    grads_far = grads.line(hold(grads_own, far), grads.far)
+    grads_near = hold(grads_near, far)
+    grads_near_across = grads.across(grads_near)
+    last = hold(last, grads_near_across)
     last_across = rows.across(last)
-    near = grads.line(hold(own, last), grads.near)
-    far = hold(far, last)
-    grads_last = grads.line(far, grads.near)
-    clock = order(lambda c: space(c, 2 * 10**9), clock, also=far)
-    grads_line = order(join, near, far)
-    grads_across = grads.across(grads_line)
+    grads_far, far_across = hold((grads_far, far_across), last)
+    clock = order(lambda c: space(c, 2 * 10**9), clock, also=(grads_far, far_across))
+    grads_far_across = grads.across(grads_far)
+    grads_last = grads.line(grads_far, grads.near)
     grads_sibling = grads.sibling(grads_pair)
-    rest = order(join, line_pair, across_pair, last, last_across)
+    rest = order(
+        join, near, far, near_across, far_across, last, last_across, also=grads_near_across
+    )
     all_rows = [pair, rest, sibling_pair, rows.sibling(rest)]
     pre_gate, pre_up, gated = order(
         lambda *r: hidden_units(r, gate_mat, up_mat, experts), *all_rows
@@ -542,14 +547,22 @@
     last_across = grads.across(grads_last)
     near_out, sent, kept = order(outputs_of, gated, down_mat, also=(grads_last, grads_sibling))
     received, kept = outs.sibling(sent), outs.sibling(kept)
-    clock = order(space, clock, also=(grads_across, last_across))
+    clock = order(space, clock, also=(grads_far_across, last_across))
     received = hold(received, clock)
     size = tokens.shape[0]
     own_sent, sent = order(
         lambda *s: outs.send(0, *s, (size, 3 * size)), near_out, received
     )
     arrived = outs.across(sent)
-    rest = order(join, grads_line, grads_across, grads_last, last_across)
+    rest = order(
+        join,
+        grads_near,
+        grads_far,
+        grads_near_across,
+        grads_far_across,
+        grads_last,
+        last_across,
+    )
     all_grads = [grads_pair, rest, grads_sibling, grads.sibling(rest)]
     d_gate, d_up, shares = order(
         lambda g, r, *pre: hidden_grads(g, r, *pre, down_mat, experts),
@@ -569,13 +582,14 @@
     last_arrived = ins.across(last_sent)
     near_slots, far_slot = order(outs.slots, near_out, kept, hold(arrived, far_sent))
     near_sums = outs.line(near_slots, outs.near)
-    out_arrived = outs.across(hold(own_sent, near_slots))
+    out_sent = own_sent
     grad_down = order(product_of("grad_down", True), all_grads, gated)
     slot = order(lambda *s: ins.slot(3, *s), in_own, far_kept, last_arrived)
     last_sum = ins.line(slot, ins.near)
     far_arrived = ins.across(hold(far_sent, slot))
+    out_arrived = outs.across(hold(out_sent, slot))
     own_sent, near_sent = order(
-        lambda *s: ins.send(0, *s, (size, size)), in_own, near_received, also=out_arrived
+        lambda *s: ins.send(0, *s, (size, size)), in_own, near_received
     )
     far_slot = order(
         lambda *s: call(add_last_kernel, "add_last", s, jax.ShapeDtypeStruct(s[0].shape, s[0].dtype)),
@@ -584,7 +598,9 @@
     )
     far_sum = outs.line(far_slot, outs.far)
     grad_gate = order(product_of("grad_gate", False), all_rows, d_gate)
-    slot = order(lambda *s: ins.slot(2, *s), in_own, far_kept, far_arrived, last_sum)
+    slot = order(
+        lambda *s: ins.slot(2, *s), in_own, far_kept, far_arrived, last_sum, also=out_arrived
+    )
     far = ins.line(slot, ins.far)
     near_arrived = ins.across(hold(near_sent, slot))
     grad_up = order(product_of("grad_up", False), all_rows, d_up)

time: 134 us -> 139 us (1.037)
  starting transfers between devices: 28.7 us -> 36.1 us
  waiting for transfers between devices: 47.1 us -> 45.4 us
    ppermute x11, waiting for transfers between devices: 33.5 us -> 26.1 us  [line(): return lax.ppermute(array, 'expert', pairs)]
    ppermute x10 -> x12, waiting for transfers between devices: 7.85 us -> 14.6 us  [across(): return lax.ppermute(array, 'helper', self.sides)]
    ppermute x10 -> x12, starting transfers between devices: 10.3 us -> 14.2 us  [across(): return lax.ppermute(array, 'helper', self.sides)]
    ppermute x11, starting transfers between devices: 16 us -> 19.5 us  [line(): return lax.ppermute(array, 'expert', pairs)]
    pallas_call x22 -> x20, Pallas kernels: 51 us -> 50.9 us  [call(): pl.pallas_call(kernel, out_shape=out_shape, in_specs=[VMEM] * len(operand...]
  transfers between devices with their start and end apart: 31 -> 33, of which waited for: 14 -> 18; matrix products, arithmetic and copies ran while one was open for 0% -> 0% of each run, Pallas kernels for 41% -> 39%
where the time goes in v10:
time: 139 us
  Pallas kernels  56.9 us (41%)
  waiting for transfers between devices  45.4 us (33%)
  starting transfers between devices  36.1 us (26%)
    pallas_call x20, Pallas kernels, call(): pl.pallas_call(kernel, out_shape=out_shape, in_specs=[VMEM] * len(operand...  50.9 us
    ppermute x11, waiting for transfers between devices, line(): return lax.ppermute(array, 'expert', pairs)  26.1 us
    ppermute x11, starting transfers between devices, line(): return lax.ppermute(array, 'expert', pairs)  19.5 us
    ppermute x12, waiting for transfers between devices, across(): return lax.ppermute(array, 'helper', self.sides)  14.6 us
    ppermute x12, starting transfers between devices, across(): return lax.ppermute(array, 'helper', self.sides)  14.2 us
    ppermute x10, waiting for transfers between devices, sibling(): return lax.ppermute(array, 'expert', self.cores)  4.78 us
    pallas_call x1, Pallas kernels, load(): pl.pallas_call(load_kernel, out_shape=tuple((jax.ShapeDtypeStruct(mat.sha...  4.73 us
  transfers between devices with their start and end apart: 33, of which 18 were waited for; matrix products, arithmetic and copies ran while one was open for 0% of the time, Pallas kernels for 39%

profile of v10, /device:TPU:0, one launch (start us, length us, event | category | flops | bytes accessed | tf_op | source)
XLA Modules:
  0.0 139.3 jit_solution(15870915655768866478)
XLA Ops:
  0.6 1.3 prepare_rows.1
  1.9 0.5 collective-permute-start.1
  2.5 2.6 %collective-permute-start = (bf16[64,2176]{1,0:T(8,128)(2,1)S(1)}, bf16[64,2176]{1,0:T(8,128)(2,1)S(1)}, u32[]{:S(2)}, u32[]{:S(2)}) collective-permute-start(bf16[64,2176]{1,0:T(8,128)(2,1)S(1)} %get-tuple-element.152), channel_id=1, source_target_pairs={{0,4},{2,6},{4,0},{6,2},{8,12},{10,14},{12,8},{14,10},{1,5},{3,7},... | collective-permute-start | bytes 835592 | tf_op jit(solution)/shard_map/rows_line/ppermute | solution.py:421
  5.1 4.7 %load.1 = (bf16[2048,1024]{1,0:T(8,128)(2,1)S(1)}, bf16[2048,1024]{1,0:T(8,128)(2,1)S(1)}, bf16[1024,2048]{1,0:T(8,128)(2,1)S(1)}) custom-call(bf16[2048,1024]{1,0:T(8,128)(2,1)} %bitcast.16, bf16[2048,1024]{1,0:T(8,128)(2,1)} %bitcast.17, bf16[1024,2048]{1,0:T(8,128)(2,1)} %bitcast.18), custom_call_target="tpu_custom_call" | custom-call | tf_op jit(solution)/shard_map/load/pallas_call | solution.py:472
  9.9 2.4 %collective-permute-done.refs_0_ = bf16[64,2176]{1,0:T(8,128)(2,1)S(1)} collective-permute-done((bf16[64,2176]{1,0:T(8,128)(2,1)S(1)}, bf16[64,2176]{1,0:T(8,128)(2,1)S(1)}, u32[]{:S(2)}, u32[]{:S(2)}) %collective-permute-start) | collective-permute-done | bytes 278560 | tf_op jit(solution)/shard_map/rows_line/ppermute | solution.py:421
  12.4 2.8 %collective-permute-start.2 = (bf16[64,2176]{1,0:T(8,128)(2,1)S(1)}, bf16[64,2176]{1,0:T(8,128)(2,1)S(1)}, u32[]{:S(2)}, u32[]{:S(2)}) collective-permute-start(bf16[64,2176]{1,0:T(8,128)(2,1)S(1)} %get-tuple-element.152), channel_id=1, source_target_pairs={{0,8},{2,10},{4,12},{6,14},{8,0},{10,2},{12,4},{14,6},{1,9},{3,11}... | collective-permute-start | bytes 835592 | tf_op jit(solution)/shard_map/rows_line/ppermute | solution.py:421
  15.1 1.5 %collective-permute-start.3 = (bf16[64,2176]{1,0:T(8,128)(2,1)S(1)}, bf16[64,2176]{1,0:T(8,128)(2,1)S(1)}, u32[]{:S(2)}, u32[]{:S(2)}) collective-permute-start(bf16[64,2176]{1,0:T(8,128)(2,1)S(1)} %collective-permute-done.refs_0_), channel_id=1, source_target_pairs={{0,1},{1,0},{2,3},{3,2},{4,5},{5,4},{6,7},{7,6},{8,9},{9,8},{10,11... | collective-permute-start | bytes 835592 | tf_op jit(solution)/shard_map/rows_across/ppermute | solution.py:429
  16.6 1.6 %collective-permute-start.4 = (bf16[64,2048]{1,0:T(8,128)(2,1)S(1)}, bf16[64,2048]{1,0:T(8,128)(2,1)S(1)}, u32[]{:S(2)}, u32[]{:S(2)}) collective-permute-start(bf16[64,2048]{1,0:T(8,128)(2,1)S(1)} %get-tuple-element.155), channel_id=1, source_target_pairs={{0,4},{2,6},{4,0},{6,2},{8,12},{10,14},{12,8},{14,10},{1,5},{3,7},... | collective-permute-start | bytes 786440 | tf_op jit(solution)/shard_map/grads_line/ppermute | solution.py:421
  18.2 10.6 %collective-permute-done.4.refs_0_ = bf16[64,2048]{1,0:T(8,128)(2,1)S(1)} collective-permute-done((bf16[64,2048]{1,0:T(8,128)(2,1)S(1)}, bf16[64,2048]{1,0:T(8,128)(2,1)S(1)}, u32[]{:S(2)}, u32[]{:S(2)}) %collective-permute-start.4) | collective-permute-done | bytes 262176 | tf_op jit(solution)/shard_map/grads_line/ppermute | solution.py:421
  29.0 1.5 %collective-permute-start.8 = (bf16[64,2048]{1,0:T(8,128)(2,1)S(1)}, bf16[64,2048]{1,0:T(8,128)(2,1)S(1)}, u32[]{:S(2)}, u32[]{:S(2)}) collective-permute-start(bf16[64,2048]{1,0:T(8,128)(2,1)S(1)} %collective-permute-done.4.refs_0_), channel_id=1, source_target_pairs={{0,1},{1,0},{2,3},{3,2},{4,5},{5,4},{6,7},{7,6},{8,9},{9,8},{10,11... | collective-permute-start | bytes 786440 | tf_op jit(solution)/shard_map/grads_across/ppermute | solution.py:429
  30.5 0.5 collective-permute-start.6
  31.0 2.8 %collective-permute-start.5 = (bf16[64,2048]{1,0:T(8,128)(2,1)S(1)}, bf16[64,2048]{1,0:T(8,128)(2,1)S(1)}, u32[]{:S(2)}, u32[]{:S(2)}) collective-permute-start(bf16[64,2048]{1,0:T(8,128)(2,1)S(1)} %get-tuple-element.155), channel_id=1, source_target_pairs={{0,8},{2,10},{4,12},{6,14},{8,0},{10,2},{12,4},{14,6},{1,9},{3,11}... | collective-permute-start | bytes 786440 | tf_op jit(solution)/shard_map/grads_line/ppermute | solution.py:421
  33.8 4.4 %collective-permute-done.8.refs_2_ = bf16[64,2048]{1,0:T(8,128)(2,1)S(1)} collective-permute-done((bf16[64,2048]{1,0:T(8,128)(2,1)S(1)}, bf16[64,2048]{1,0:T(8,128)(2,1)S(1)}, u32[]{:S(2)}, u32[]{:S(2)}) %collective-permute-start.8) | collective-permute-done | bytes 262176 | tf_op jit(solution)/shard_map/grads_across/ppermute | solution.py:429
  38.3 1.4 collective-permute-done.7.refs_4_
  39.6 1.3 collective-permute-start.9
  41.0 4.1 %collective-permute-done.5.refs_1_ = bf16[64,2048]{1,0:T(8,128)(2,1)S(1)} collective-permute-done((bf16[64,2048]{1,0:T(8,128)(2,1)S(1)}, bf16[64,2048]{1,0:T(8,128)(2,1)S(1)}, u32[]{:S(2)}, u32[]{:S(2)}) %collective-permute-start.5) | collective-permute-done | bytes 262176 | tf_op jit(solution)/shard_map/grads_line/ppermute | solution.py:421
  45.1 3.2 %collective-permute-done.9.refs_5_ = bf16[64,2176]{1,0:T(8,128)(2,1)S(1)} collective-permute-done((bf16[64,2176]{1,0:T(8,128)(2,1)S(1)}, bf16[64,2176]{1,0:T(8,128)(2,1)S(1)}, u32[]{:S(2)}, u32[]{:S(2)}) %collective-permute-start.9) | collective-permute-done | bytes 278560 | tf_op jit(solution)/shard_map/rows_across/ppermute | solution.py:429
  48.4 0.5 collective-permute-start.12
  48.9 1.5 %collective-permute-start.15 = (bf16[64,2048]{1,0:T(8,128)(2,1)S(1)}, bf16[64,2048]{1,0:T(8,128)(2,1)S(1)}, u32[]{:S(2)}, u32[]{:S(2)}) collective-permute-start(bf16[64,2048]{1,0:T(8,128)(2,1)S(1)} %collective-permute-done.5.refs_1_), channel_id=1, source_target_pairs={{0,1},{1,0},{2,3},{3,2},{4,5},{5,4},{6,7},{7,6},{8,9},{9,8},{10,11... | collective-permute-start | bytes 786440 | tf_op jit(solution)/shard_map/grads_across/ppermute | solution.py:429
  50.7 1.2 collective-permute-done.10.refs_3_.refs_7_
  52.0 8.8 %hidden_units.1 = (f32[1024,1024]{1,0:T(8,128)S(1)}, f32[1024,1024]{1,0:T(8,128)S(1)}, bf16[1024,1024]{1,0:T(8,128)(2,1)S(1)}) custom-call(bf16[128,2176]{1,0:T(8,128)(2,1)S(1)} %get-tuple-element.250.refs_0_.refs_4_, bf16[384,2176]{1,0:T(8,128)(2,1)S(1)} %join.2.refs_1_.refs_5_, bf16[128,2176]{1,0:T(8,128)(2,1)S(1)} %collective-permute-done.1.refs_2_.refs_6_, ...), custom_call_target="tpu_custom_call" | custom-call | flops 8589934592 | tf_op jit(solution)/shard_map/hidden_units/pallas_call | solution.py:40
  60.8 1.5 %collective-permute-start.16 = (bf16[64,2048]{1,0:T(8,128)(2,1)S(1)}, bf16[64,2048]{1,0:T(8,128)(2,1)S(1)}, u32[]{:S(2)}, u32[]{:S(2)}) collective-permute-start(bf16[64,2048]{1,0:T(8,128)(2,1)S(1)} %collective-permute-done.11.refs_4_), channel_id=1, source_target_pairs={{0,1},{1,0},{2,3},{3,2},{4,5},{5,4},{6,7},{7,6},{8,9},{9,8},{10,11... | collective-permute-start | bytes 786440 | tf_op jit(solution)/shard_map/grads_across/ppermute | solution.py:429
  62.3 4.5 %outputs.1 = (bf16[2,512,1024]{2,1,0:T(8,128)(2,1)S(1)}, bf16[512,1024]{1,0:T(8,128)(2,1)S(1)}, bf16[512,1024]{1,0:T(8,128)(2,1)S(1)}) custom-call(bf16[1024,1024]{1,0:T(8,128)(2,1)S(1)} %get-tuple-element.228.gated.refs_4_, bf16[1024,2048]{1,0:T(8,128)(2,1)S(1)} %get-tuple-element.177.down_mat.refs_8_), custom_call_target="tpu_custom_call" | custom-call | flops 4294967296 | tf_op jit(solution)/shard_map/outputs/pallas_call | solution.py:40
  67.0 2.2 %collective-permute-done.16.refs_5_ = bf16[64,2048]{1,0:T(8,128)(2,1)S(1)} collective-permute-done((bf16[64,2048]{1,0:T(8,128)(2,1)S(1)}, bf16[64,2048]{1,0:T(8,128)(2,1)S(1)}, u32[]{:S(2)}, u32[]{:S(2)}) %collective-permute-start.16) | collective-permute-done | bytes 262176 | tf_op jit(solution)/shard_map/grads_across/ppermute | solution.py:429
  70.4 1.1 collective-permute-start.21
  71.5 1.8 %collective-permute-done.17.refs_3_ = bf16[384,2048]{1,0:T(8,128)(2,1)S(1)} collective-permute-done((bf16[384,2048]{1,0:T(8,128)(2,1)S(1)}, bf16[384,2048]{1,0:T(8,128)(2,1)S(1)}, u32[]{:S(2)}, u32[]{:S(2)}) %collective-permute-start.17) | collective-permute-done | bytes 1572896 | tf_op jit(solution)/shard_map/grads_cores/ppermute | solution.py:425
  73.3 5.6 %hidden_grads.1 = (bf16[1024,1024]{1,0:T(8,128)(2,1)S(1)}, bf16[1024,1024]{1,0:T(8,128)(2,1)S(1)}, bf16[1024,128]{1,0:T(8,128)(2,1)S(1)}) custom-call(bf16[128,2048]{1,0:T(8,128)(2,1)S(1)} %get-tuple-element.224.refs_0_, bf16[384,2048]{1,0:T(8,128)(2,1)S(1)} %join.3.refs_1_, bf16[128,2048]{1,0:T(8,128)(2,1)S(1)} %collective-permute-done.12.refs_2_, ...), custom_call_target="tpu_custom_call" | custom-call | flops 4294967296 | tf_op jit(solution)/shard_map/hidden_grads/pallas_call | solution.py:40
  78.9 8.9 %input_grads.1 = (bf16[2,512,1152]{2,1,0:T(8,128)(2,1)S(1)}, bf16[256,1152]{1,0:T(8,128)(2,1)S(1)}, bf16[256,1152]{1,0:T(8,128)(2,1)S(1)}, bf16[256,1152]{1,0:T(8,128)(2,1)S(1)}, bf16[256,1152]{1,0:T(8,128)(2,1)S(1)}) custom-call(bf16[1024,1024]{1,0:T(8,128)(2,1)S(1)} %get-tuple-element.244.d_gate.refs_4_, ...), custom_call_target="tpu_custom_call" | custom-call | tf_op jit(solution)/shard_map/input_grads/pallas_call | solution.py:40
  88.5 1.4 collective-permute-done.19.received
  90.7 1.1 collective-permute-start.20
  91.8 6.8 %grad_down.1 = bf16[1024,2048]{1,0:T(8,128)(2,1)} custom-call(bf16[128,2048]{1,0:T(8,128)(2,1)S(1)} %get-tuple-element.224.refs_0_, bf16[384,2048]{1,0:T(8,128)(2,1)S(1)} %join.3.refs_1_, bf16[128,2048]{1,0:T(8,128)(2,1)S(1)} %collective-permute-done.12.refs_2_, bf16[384,2048]{1,0:T(8,128)(2,1)S(1)} %collective-permute-done.17.refs_3_, ...), custom_call_target="tpu_custom_call" | custom-call | flops 4294967296 | tf_op jit(solution)/shard_map/grad_down/pallas_call | solution.py:40
  98.6 1.6 %collective-permute-done.20.arrived = bf16[128,1152]{1,0:T(8,128)(2,1)S(1)} collective-permute-done((bf16[128,1152]{1,0:T(8,128)(2,1)S(1)}, bf16[128,1152]{1,0:T(8,128)(2,1)S(1)}, u32[]{:S(2)}, u32[]{:S(2)}) %collective-permute-start.20) | collective-permute-done | bytes 294944 | tf_op jit(solution)/shard_map/in_across/ppermute | solution.py:429
  100.2 1.7 %collective-permute-start.28 = (bf16[128,1152]{1,0:T(8,128)(2,1)S(1)}, bf16[128,1152]{1,0:T(8,128)(2,1)S(1)}, u32[]{:S(2)}, u32[]{:S(2)}) collective-permute-start(bf16[128,1152]{1,0:T(8,128)(2,1)S(1)} %in_slot.3), channel_id=1, source_target_pairs={{0,4},{2,6},{4,0},{6,2},{8,12},{10,14},{12,8},{14,10},{1,5},{3,7},... | collective-permute-start | bytes 884744 | tf_op jit(solution)/shard_map/in_line/ppermute | solution.py:421
  102.0 1.1 collective-permute-start.22
  103.1 0.9 collective-permute-start.27
  104.1 1.0 collective-permute-done.23.arrived.near_and_last
  105.1 3.5 %collective-permute-start.25 = (bf16[128,1024]{1,0:T(8,128)(2,1)S(1)}, bf16[128,1024]{1,0:T(8,128)(2,1)S(1)}, u32[]{:S(2)}, u32[]{:S(2)}) collective-permute-start(bf16[128,1024]{1,0:T(8,128)(2,1)S(1)} %add_last.1), channel_id=1, source_target_pairs={{0,8},{2,10},{4,12},{6,14},{8,0},{10,2},{12,4},{14,6},{1,9},{3,11}... | collective-permute-start | bytes 786440 | tf_op jit(solution)/shard_map/out_line/ppermute | solution.py:421
  108.6 6.5 %grad_gate.1 = bf16[2048,1024]{1,0:T(8,128)(2,1)} custom-call(bf16[128,2176]{1,0:T(8,128)(2,1)S(1)} %get-tuple-element.250.refs_0_.refs_4_, bf16[384,2176]{1,0:T(8,128)(2,1)S(1)} %join.2.refs_1_.refs_5_, bf16[128,2176]{1,0:T(8,128)(2,1)S(1)} %collective-permute-done.1.refs_2_.refs_6_, bf16[384,2176]{1,0:T(8,128)(2,1)S(1)} %collective-permute-done.10.refs_3_.refs_7_, ...), custom_call_target="tpu_custom_call" | custom-call | flops 4294967296 | tf_op jit(solution)/shard_map/grad_gate/pallas_call | solution.py:40
  115.1 0.8 collective-permute-done.27.arrived
  116.3 3.2 %collective-permute-start.30 = (bf16[128,1152]{1,0:T(8,128)(2,1)S(1)}, bf16[128,1152]{1,0:T(8,128)(2,1)S(1)}, u32[]{:S(2)}, u32[]{:S(2)}) collective-permute-start(bf16[128,1152]{1,0:T(8,128)(2,1)S(1)} %in_slot.4), channel_id=1, source_target_pairs={{0,8},{2,10},{4,12},{6,14},{8,0},{10,2},{12,4},{14,6},{1,9},{3,11}... | collective-permute-start | bytes 884744 | tf_op jit(solution)/shard_map/in_line/ppermute | solution.py:421
  119.6 1.1 collective-permute-start.29
  120.6 6.5 %grad_up.1 = bf16[2048,1024]{1,0:T(8,128)(2,1)} custom-call(bf16[128,2176]{1,0:T(8,128)(2,1)S(1)} %get-tuple-element.250.refs_0_.refs_4_, bf16[384,2176]{1,0:T(8,128)(2,1)S(1)} %join.2.refs_1_.refs_5_, bf16[128,2176]{1,0:T(8,128)(2,1)S(1)} %collective-permute-done.1.refs_2_.refs_6_, bf16[384,2176]{1,0:T(8,128)(2,1)S(1)} %collective-permute-done.10.refs_3_.refs_7_, ...), custom_call_target="tpu_custom_call" | custom-call | flops 4294967296 | tf_op jit(solution)/shard_map/grad_up/pallas_call | solution.py:40
  127.3 1.0 collective-permute-start.32
  128.7 0.9 finish_outputs.1
  129.6 2.4 %collective-permute-done.30.refs_0_ = bf16[128,1152]{1,0:T(8,128)(2,1)S(1)} collective-permute-done((bf16[128,1152]{1,0:T(8,128)(2,1)S(1)}, bf16[128,1152]{1,0:T(8,128)(2,1)S(1)}, u32[]{:S(2)}, u32[]{:S(2)}) %collective-permute-start.30) | collective-permute-done | bytes 294944 | tf_op jit(solution)/shard_map/in_line/ppermute | solution.py:421
  131.9 2.3 %collective-permute-done.32.arrived = bf16[128,1152]{1,0:T(8,128)(2,1)S(1)} collective-permute-done((bf16[128,1152]{1,0:T(8,128)(2,1)S(1)}, bf16[128,1152]{1,0:T(8,128)(2,1)S(1)}, u32[]{:S(2)}, u32[]{:S(2)}) %collective-permute-start.32) | collective-permute-done | bytes 294944 | tf_op jit(solution)/shard_map/in_across/ppermute | solution.py:429
  134.2 3.9 %collective-permute-done.31.refs_1_ = bf16[128,1152]{1,0:T(8,128)(2,1)S(1)} collective-permute-done((bf16[128,1152]{1,0:T(8,128)(2,1)S(1)}, bf16[128,1152]{1,0:T(8,128)(2,1)S(1)}, u32[]{:S(2)}, u32[]{:S(2)}) %collective-permute-start.31) | collective-permute-done | bytes 294944 | tf_op jit(solution)/shard_map/in_line/ppermute | solution.py:421
  138.2 1.1 finish_inputs.1
  (51 shorter events, 4.7 us)
Async XLA Ops:
  1.9 7.9 %collective-permute-start.1 = (bf16[128,2176]{1,0:T(8,128)(2,1)S(1)}, bf16[128,2176]{1,0:T(8,128)(2,1)S(1)}, u32[]{:S(2)}, u32[]{:S(2)}) collective-permute-start(bf16[128,2176]{1,0:T(8,128)(2,1)S(1)} %get-tuple-element.250.refs_0_.refs_4_), channel_id=1, source_target_pairs={{0,2},{2,0},{4,6},{6,4},{8,10},{10,8},{12,14},{14,12},{1,3},{3,1},... | collective-permute-start | bytes 1671176 | tf_op jit(solution)/shard_map/rows_cores/ppermute | solution.py:425
  2.5 9.9 %collective-permute-start = (bf16[64,2176]{1,0:T(8,128)(2,1)S(1)}, bf16[64,2176]{1,0:T(8,128)(2,1)S(1)}, u32[]{:S(2)}, u32[]{:S(2)}) collective-permute-start(bf16[64,2176]{1,0:T(8,128)(2,1)S(1)} %get-tuple-element.152), channel_id=1, source_target_pairs={{0,4},{2,6},{4,0},{6,2},{8,12},{10,14},{12,8},{14,10},{1,5},{3,7},... | collective-permute-start | bytes 835592 | tf_op jit(solution)/shard_map/rows_line/ppermute | solution.py:421
  5.1 4.8 %copy-start = (bf16[128,2048]{1,0:T(8,128)(2,1)S(1)}, bf16[128,2048]{1,0:T(8,128)(2,1)}, u32[]{:S(2)}) copy-start(bf16[128,2048]{1,0:T(8,128)(2,1)} %rows) | copy-start | bytes 1572868
  12.4 16.5 %collective-permute-start.2 = (bf16[64,2176]{1,0:T(8,128)(2,1)S(1)}, bf16[64,2176]{1,0:T(8,128)(2,1)S(1)}, u32[]{:S(2)}, u32[]{:S(2)}) collective-permute-start(bf16[64,2176]{1,0:T(8,128)(2,1)S(1)} %get-tuple-element.152), channel_id=1, source_target_pairs={{0,8},{2,10},{4,12},{6,14},{8,0},{10,2},{12,4},{14,6},{1,9},{3,11}... | collective-permute-start | bytes 835592 | tf_op jit(solution)/shard_map/rows_line/ppermute | solution.py:421
  15.1 13.7 %collective-permute-start.3 = (bf16[64,2176]{1,0:T(8,128)(2,1)S(1)}, bf16[64,2176]{1,0:T(8,128)(2,1)S(1)}, u32[]{:S(2)}, u32[]{:S(2)}) collective-permute-start(bf16[64,2176]{1,0:T(8,128)(2,1)S(1)} %collective-permute-done.refs_0_), channel_id=1, source_target_pairs={{0,1},{1,0},{2,3},{3,2},{4,5},{5,4},{6,7},{7,6},{8,9},{9,8},{10,11... | collective-permute-start | bytes 835592 | tf_op jit(solution)/shard_map/rows_across/ppermute | solution.py:429
  16.6 12.2 %collective-permute-start.4 = (bf16[64,2048]{1,0:T(8,128)(2,1)S(1)}, bf16[64,2048]{1,0:T(8,128)(2,1)S(1)}, u32[]{:S(2)}, u32[]{:S(2)}) collective-permute-start(bf16[64,2048]{1,0:T(8,128)(2,1)S(1)} %get-tuple-element.155), channel_id=1, source_target_pairs={{0,4},{2,6},{4,0},{6,2},{8,12},{10,14},{12,8},{14,10},{1,5},{3,7},... | collective-permute-start | bytes 786440 | tf_op jit(solution)/shard_map/grads_line/ppermute | solution.py:421
  28.8 10.8 %collective-permute-start.7 = (bf16[64,2176]{1,0:T(8,128)(2,1)S(1)}, bf16[64,2176]{1,0:T(8,128)(2,1)S(1)}, u32[]{:S(2)}, u32[]{:S(2)}) collective-permute-start(bf16[64,2176]{1,0:T(8,128)(2,1)S(1)} %collective-permute-done.2.refs_1_), channel_id=1, source_target_pairs={{0,4},{2,6},{4,0},{6,2},{8,12},{10,14},{12,8},{14,10},{1,5},{3,7},... | collective-permute-start | bytes 835592 | tf_op jit(solution)/shard_map/rows_line/ppermute | solution.py:421
  29.0 9.2 %collective-permute-start.8 = (bf16[64,2048]{1,0:T(8,128)(2,1)S(1)}, bf16[64,2048]{1,0:T(8,128)(2,1)S(1)}, u32[]{:S(2)}, u32[]{:S(2)}) collective-permute-start(bf16[64,2048]{1,0:T(8,128)(2,1)S(1)} %collective-permute-done.4.refs_0_), channel_id=1, source_target_pairs={{0,1},{1,0},{2,3},{3,2},{4,5},{5,4},{6,7},{7,6},{8,9},{9,8},{10,11... | collective-permute-start | bytes 786440 | tf_op jit(solution)/shard_map/grads_across/ppermute | solution.py:429
  30.5 14.5 %collective-permute-start.6 = (bf16[64,2176]{1,0:T(8,128)(2,1)S(1)}, bf16[64,2176]{1,0:T(8,128)(2,1)S(1)}, u32[]{:S(2)}, u32[]{:S(2)}) collective-permute-start(bf16[64,2176]{1,0:T(8,128)(2,1)S(1)} %collective-permute-done.2.refs_1_), channel_id=1, source_target_pairs={{0,1},{1,0},{2,3},{3,2},{4,5},{5,4},{6,7},{7,6},{8,9},{9,8},{10,11... | collective-permute-start | bytes 835592 | tf_op jit(solution)/shard_map/rows_across/ppermute | solution.py:429
  31.0 14.0 %collective-permute-start.5 = (bf16[64,2048]{1,0:T(8,128)(2,1)S(1)}, bf16[64,2048]{1,0:T(8,128)(2,1)S(1)}, u32[]{:S(2)}, u32[]{:S(2)}) collective-permute-start(bf16[64,2048]{1,0:T(8,128)(2,1)S(1)} %get-tuple-element.155), channel_id=1, source_target_pairs={{0,8},{2,10},{4,12},{6,14},{8,0},{10,2},{12,4},{14,6},{1,9},{3,11}... | collective-permute-start | bytes 786440 | tf_op jit(solution)/shard_map/grads_line/ppermute | solution.py:421
  39.6 8.6 %collective-permute-start.9 = (bf16[64,2176]{1,0:T(8,128)(2,1)S(1)}, bf16[64,2176]{1,0:T(8,128)(2,1)S(1)}, u32[]{:S(2)}, u32[]{:S(2)}) collective-permute-start(bf16[64,2176]{1,0:T(8,128)(2,1)S(1)} %collective-permute-done.7.refs_4_), channel_id=1, source_target_pairs={{0,1},{1,0},{2,3},{3,2},{4,5},{5,4},{6,7},{7,6},{8,9},{9,8},{10,11... | collective-permute-start | bytes 835592 | tf_op jit(solution)/shard_map/rows_across/ppermute | solution.py:429
  48.4 3.6 %collective-permute-start.10 = (bf16[384,2176]{1,0:T(8,128)(2,1)S(1)}, bf16[384,2176]{1,0:T(8,128)(2,1)S(1)}, u32[]{:S(2)}, u32[]{:S(2)}) collective-permute-start(bf16[384,2176]{1,0:T(8,128)(2,1)S(1)} %join.2.refs_1_.refs_5_), channel_id=1, source_target_pairs={{0,2},{2,0},{4,6},{6,4},{8,10},{10,8},{12,14},{14,12},{1,3},{3,1},... | collective-permute-start | bytes 5013512 | tf_op jit(solution)/shard_map/rows_cores/ppermute | solution.py:425
  48.4 13.9 %collective-permute-start.12 = (bf16[128,2048]{1,0:T(8,128)(2,1)S(1)}, bf16[128,2048]{1,0:T(8,128)(2,1)S(1)}, u32[]{:S(2)}, u32[]{:S(2)}) collective-permute-start(bf16[128,2048]{1,0:T(8,128)(2,1)S(1)} %get-tuple-element.224.refs_0_), channel_id=1, source_target_pairs={{0,2},{2,0},{4,6},{6,4},{8,10},{10,8},{12,14},{14,12},{1,3},{3,1},... | collective-permute-start | bytes 1572872 | tf_op jit(solution)/shard_map/grads_cores/ppermute | solution.py:425
  48.9 18.0 %collective-permute-start.15 = (bf16[64,2048]{1,0:T(8,128)(2,1)S(1)}, bf16[64,2048]{1,0:T(8,128)(2,1)S(1)}, u32[]{:S(2)}, u32[]{:S(2)}) collective-permute-start(bf16[64,2048]{1,0:T(8,128)(2,1)S(1)} %collective-permute-done.5.refs_1_), channel_id=1, source_target_pairs={{0,1},{1,0},{2,3},{3,2},{4,5},{5,4},{6,7},{7,6},{8,9},{9,8},{10,11... | collective-permute-start | bytes 786440 | tf_op jit(solution)/shard_map/grads_across/ppermute | solution.py:429
  50.4 10.4 %collective-permute-start.11 = (bf16[64,2048]{1,0:T(8,128)(2,1)S(1)}, bf16[64,2048]{1,0:T(8,128)(2,1)S(1)}, u32[]{:S(2)}, u32[]{:S(2)}) collective-permute-start(bf16[64,2048]{1,0:T(8,128)(2,1)S(1)} %collective-permute-done.5.refs_1_), channel_id=1, source_target_pairs={{0,4},{2,6},{4,0},{6,2},{8,12},{10,14},{12,8},{14,10},{1,5},{3,7},... | collective-permute-start | bytes 786440 | tf_op jit(solution)/shard_map/grads_line/ppermute | solution.py:421
  60.8 8.4 %collective-permute-start.16 = (bf16[64,2048]{1,0:T(8,128)(2,1)S(1)}, bf16[64,2048]{1,0:T(8,128)(2,1)S(1)}, u32[]{:S(2)}, u32[]{:S(2)}) collective-permute-start(bf16[64,2048]{1,0:T(8,128)(2,1)S(1)} %collective-permute-done.11.refs_4_), channel_id=1, source_target_pairs={{0,1},{1,0},{2,3},{3,2},{4,5},{5,4},{6,7},{7,6},{8,9},{9,8},{10,11... | collective-permute-start | bytes 786440 | tf_op jit(solution)/shard_map/grads_across/ppermute | solution.py:429
  66.9 2.7 %collective-permute-start.14 = (bf16[512,1024]{1,0:T(8,128)(2,1)S(1)}, bf16[512,1024]{1,0:T(8,128)(2,1)S(1)}, u32[]{:S(2)}, u32[]{:S(2)}) collective-permute-start(bf16[512,1024]{1,0:T(8,128)(2,1)S(1)} %get-tuple-element.180), channel_id=1, source_target_pairs={{0,2},{2,0},{4,6},{6,4},{8,10},{10,8},{12,14},{14,12},{1,3},{3,1},... | collective-permute-start | bytes 3145736 | tf_op jit(solution)/shard_map/out_cores/ppermute | solution.py:425
  69.8 3.5 %collective-permute-start.17 = (bf16[384,2048]{1,0:T(8,128)(2,1)S(1)}, bf16[384,2048]{1,0:T(8,128)(2,1)S(1)}, u32[]{:S(2)}, u32[]{:S(2)}) collective-permute-start(bf16[384,2048]{1,0:T(8,128)(2,1)S(1)} %join.3.refs_1_), channel_id=1, source_target_pairs={{0,2},{2,0},{4,6},{6,4},{8,10},{10,8},{12,14},{14,12},{1,3},{3,1},... | collective-permute-start | bytes 4718600 | tf_op jit(solution)/shard_map/grads_cores/ppermute | solution.py:425
  70.0 20.0 %collective-permute-start.13 = (bf16[512,1024]{1,0:T(8,128)(2,1)S(1)}, bf16[512,1024]{1,0:T(8,128)(2,1)S(1)}, u32[]{:S(2)}, u32[]{:S(2)}) collective-permute-start(bf16[512,1024]{1,0:T(8,128)(2,1)S(1)} %get-tuple-element.179), channel_id=1, source_target_pairs={{0,2},{2,0},{4,6},{6,4},{8,10},{10,8},{12,14},{14,12},{1,3},{3,1},... | collective-permute-start | bytes 3145736 | tf_op jit(solution)/shard_map/out_cores/ppermute | solution.py:425
  70.4 19.6 %collective-permute-start.21 = (bf16[384,1024]{1,0:T(8,128)(2,1)S(1)}, bf16[384,1024]{1,0:T(8,128)(2,1)S(1)}, u32[]{:S(2)}, u32[]{:S(2)}) collective-permute-start(bf16[384,1024]{1,0:T(8,128)(2,1)S(1)} %get-tuple-element.186), channel_id=1, source_target_pairs={{0,1},{1,0},{2,3},{3,2},{4,5},{5,4},{6,7},{7,6},{8,9},{9,8},{10,11... | collective-permute-start | bytes 2359304 | tf_op jit(solution)/shard_map/out_across/ppermute | solution.py:429
  87.8 2.1 %collective-permute-start.19 = (bf16[256,1152]{1,0:T(8,128)(2,1)S(1)}, bf16[256,1152]{1,0:T(8,128)(2,1)S(1)}, u32[]{:S(2)}, u32[]{:S(2)}) collective-permute-start(bf16[256,1152]{1,0:T(8,128)(2,1)S(1)} %get-tuple-element.211), channel_id=1, source_target_pairs={{0,2},{2,0},{4,6},{6,4},{8,10},{10,8},{12,14},{14,12},{1,3},{3,1},... | collective-permute-start | bytes 1769480 | tf_op jit(solution)/shard_map/in_cores/ppermute | solution.py:425
  88.0 10.6 %collective-permute-start.18 = (bf16[256,1152]{1,0:T(8,128)(2,1)S(1)}, bf16[256,1152]{1,0:T(8,128)(2,1)S(1)}, u32[]{:S(2)}, u32[]{:S(2)}) collective-permute-start(bf16[256,1152]{1,0:T(8,128)(2,1)S(1)} %get-tuple-element.210), channel_id=1, source_target_pairs={{0,2},{2,0},{4,6},{6,4},{8,10},{10,8},{12,14},{14,12},{1,3},{3,1},... | collective-permute-start | bytes 1769480 | tf_op jit(solution)/shard_map/in_cores/ppermute | solution.py:425
  88.4 14.7 %collective-permute-start.24 = (bf16[256,1152]{1,0:T(8,128)(2,1)S(1)}, bf16[256,1152]{1,0:T(8,128)(2,1)S(1)}, u32[]{:S(2)}, u32[]{:S(2)}) collective-permute-start(bf16[256,1152]{1,0:T(8,128)(2,1)S(1)} %get-tuple-element.212), channel_id=1, source_target_pairs={{0,2},{2,0},{4,6},{6,4},{8,10},{10,8},{12,14},{14,12},{1,3},{3,1},... | collective-permute-start | bytes 1769480 | tf_op jit(solution)/shard_map/in_cores/ppermute | solution.py:425
  90.3 14.8 %collective-permute-start.23 = (bf16[256,1024]{1,0:T(8,128)(2,1)S(1)}, bf16[256,1024]{1,0:T(8,128)(2,1)S(1)}, u32[]{:S(2)}, u32[]{:S(2)}) collective-permute-start(bf16[256,1024]{1,0:T(8,128)(2,1)S(1)} %get-tuple-element.222), channel_id=1, source_target_pairs={{0,4},{2,6},{4,0},{6,2},{8,12},{10,14},{12,8},{14,10},{1,5},{3,7},... | collective-permute-start | bytes 1572872 | tf_op jit(solution)/shard_map/out_line/ppermute | solution.py:421
  90.7 36.5 %collective-permute-start.26 = (bf16[256,1152]{1,0:T(8,128)(2,1)S(1)}, bf16[256,1152]{1,0:T(8,128)(2,1)S(1)}, u32[]{:S(2)}, u32[]{:S(2)}) collective-permute-start(bf16[256,1152]{1,0:T(8,128)(2,1)S(1)} %get-tuple-element.213), channel_id=1, source_target_pairs={{0,2},{2,0},{4,6},{6,4},{8,10},{10,8},{12,14},{14,12},{1,3},{3,1},... | collective-permute-start | bytes 1769480 | tf_op jit(solution)/shard_map/in_cores/ppermute | solution.py:425
  90.7 9.4 %collective-permute-start.20 = (bf16[128,1152]{1,0:T(8,128)(2,1)S(1)}, bf16[128,1152]{1,0:T(8,128)(2,1)S(1)}, u32[]{:S(2)}, u32[]{:S(2)}) collective-permute-start(bf16[128,1152]{1,0:T(8,128)(2,1)S(1)} %get-tuple-element.216), channel_id=1, source_target_pairs={{0,1},{1,0},{2,3},{3,2},{4,5},{5,4},{6,7},{7,6},{8,9},{9,8},{10,11... | collective-permute-start | bytes 884744 | tf_op jit(solution)/shard_map/in_across/ppermute | solution.py:429
  100.2 16.0 %collective-permute-start.28 = (bf16[128,1152]{1,0:T(8,128)(2,1)S(1)}, bf16[128,1152]{1,0:T(8,128)(2,1)S(1)}, u32[]{:S(2)}, u32[]{:S(2)}) collective-permute-start(bf16[128,1152]{1,0:T(8,128)(2,1)S(1)} %in_slot.3), channel_id=1, source_target_pairs={{0,4},{2,6},{4,0},{6,2},{8,12},{10,14},{12,8},{14,10},{1,5},{3,7},... | collective-permute-start | bytes 884744 | tf_op jit(solution)/shard_map/in_line/ppermute | solution.py:421
  102.0 13.2 %collective-permute-start.22 = (bf16[128,1024]{1,0:T(8,128)(2,1)S(1)}, bf16[128,1024]{1,0:T(8,128)(2,1)S(1)}, u32[]{:S(2)}, u32[]{:S(2)}) collective-permute-start(bf16[128,1024]{1,0:T(8,128)(2,1)S(1)} %get-tuple-element.232), channel_id=1, source_target_pairs={{0,1},{1,0},{2,3},{3,2},{4,5},{5,4},{6,7},{7,6},{8,9},{9,8},{10,11... | collective-permute-start | bytes 786440 | tf_op jit(solution)/shard_map/out_across/ppermute | solution.py:429
  103.1 12.9 %collective-permute-start.27 = (bf16[128,1152]{1,0:T(8,128)(2,1)S(1)}, bf16[128,1152]{1,0:T(8,128)(2,1)S(1)}, u32[]{:S(2)}, u32[]{:S(2)}) collective-permute-start(bf16[128,1152]{1,0:T(8,128)(2,1)S(1)} %get-tuple-element.239), channel_id=1, source_target_pairs={{0,1},{1,0},{2,3},{3,2},{4,5},{5,4},{6,7},{7,6},{8,9},{9,8},{10,11... | collective-permute-start | bytes 884744 | tf_op jit(solution)/shard_map/in_across/ppermute | solution.py:429
  105.1 23.5 %collective-permute-start.25 = (bf16[128,1024]{1,0:T(8,128)(2,1)S(1)}, bf16[128,1024]{1,0:T(8,128)(2,1)S(1)}, u32[]{:S(2)}, u32[]{:S(2)}) collective-permute-start(bf16[128,1024]{1,0:T(8,128)(2,1)S(1)} %add_last.1), channel_id=1, source_target_pairs={{0,8},{2,10},{4,12},{6,14},{8,0},{10,2},{12,4},{14,6},{1,9},{3,11}... | collective-permute-start | bytes 786440 | tf_op jit(solution)/shard_map/out_line/ppermute | solution.py:421
  116.3 15.6 %collective-permute-start.30 = (bf16[128,1152]{1,0:T(8,128)(2,1)S(1)}, bf16[128,1152]{1,0:T(8,128)(2,1)S(1)}, u32[]{:S(2)}, u32[]{:S(2)}) collective-permute-start(bf16[128,1152]{1,0:T(8,128)(2,1)S(1)} %in_slot.4), channel_id=1, source_target_pairs={{0,8},{2,10},{4,12},{6,14},{8,0},{10,2},{12,4},{14,6},{1,9},{3,11}... | collective-permute-start | bytes 884744 | tf_op jit(solution)/shard_map/in_line/ppermute | solution.py:421
  119.6 7.6 %collective-permute-start.29 = (bf16[128,1152]{1,0:T(8,128)(2,1)S(1)}, bf16[128,1152]{1,0:T(8,128)(2,1)S(1)}, u32[]{:S(2)}, u32[]{:S(2)}) collective-permute-start(bf16[128,1152]{1,0:T(8,128)(2,1)S(1)} %get-tuple-element.249), channel_id=1, source_target_pairs={{0,1},{1,0},{2,3},{3,2},{4,5},{5,4},{6,7},{7,6},{8,9},{9,8},{10,11... | collective-permute-start | bytes 884744 | tf_op jit(solution)/shard_map/in_across/ppermute | solution.py:429
  127.3 6.9 %collective-permute-start.32 = (bf16[128,1152]{1,0:T(8,128)(2,1)S(1)}, bf16[128,1152]{1,0:T(8,128)(2,1)S(1)}, u32[]{:S(2)}, u32[]{:S(2)}) collective-permute-start(bf16[128,1152]{1,0:T(8,128)(2,1)S(1)} %get-tuple-element.264), channel_id=1, source_target_pairs={{0,1},{1,0},{2,3},{3,2},{4,5},{5,4},{6,7},{7,6},{8,9},{9,8},{10,11... | collective-permute-start | bytes 884744 | tf_op jit(solution)/shard_map/in_across/ppermute | solution.py:429
  128.3 9.9 %collective-permute-start.31 = (bf16[128,1152]{1,0:T(8,128)(2,1)S(1)}, bf16[128,1152]{1,0:T(8,128)(2,1)S(1)}, u32[]{:S(2)}, u32[]{:S(2)}) collective-permute-start(bf16[128,1152]{1,0:T(8,128)(2,1)S(1)} %in_slot.5), channel_id=1, source_target_pairs={{0,4},{2,6},{4,0},{6,2},{8,12},{10,14},{12,8},{14,10},{1,5},{3,7},... | collective-permute-start | bytes 884744 | tf_op jit(solution)/shard_map/in_line/ppermute | solution.py:421
  129.6 8.6 %copy-start.1 = (s32[128,4]{0,1:T(4,128)S(1)}, s32[128,4]{0,1:T(4,128)}, u32[]{:S(2)}) copy-start(s32[128,4]{0,1:T(4,128)} %param.9) | copy-start | bytes 6148
  129.6 8.6 %copy-start.2 = (f32[128,4]{0,1:T(4,128)S(1)}, f32[128,4]{0,1:T(4,128)}, u32[]{:S(2)}) copy-start(f32[128,4]{0,1:T(4,128)} %param.11) | copy-start | bytes 6148
  129.6 8.6 %copy-start.3 = (s32[128]{0:T(128)S(1)}, s32[128]{0:T(128)}, u32[]{:S(2)}) copy-start(s32[128]{0:T(128)} %param.10) | copy-start | bytes 1540
